TPU v7x, 128 devices: a whole 4x4x4 slice. The times are simulated.
128 devices in a mesh: tensor: 8 (over z_hi, y), seq: 16 (over x, z_lo, core).
Axes of the slice: x: 4, y: 4, z: 4 (z_hi: 2, z_lo: 2; z = z_hi * 2 + z_lo), core: 2. Of those that a mesh axis runs over, the one named last changes fastest.
Arguments:
- inputs: bfloat16 [4096, 4096], P('seq', 'tensor'), may hold values from -60 to 60
- gain: bfloat16 [4096], P('tensor'), may hold values from 0.099609375 to 1.8984375
- weights: bfloat16 [4096, 3, 6144], P(None, None, 'tensor'), may hold values from -0.09375 to 0.09375
- d_out: bfloat16 [4096, 4096], P('seq', 'tensor'), may hold values from -18 to 18
Outputs:
- output: bfloat16 [4096, 4096], P('seq', 'tensor')
- d_input: bfloat16 [4096, 4096], P('seq', 'tensor')
- d_gain: float32 [4096], P('tensor')
- d_weights: bfloat16 [4096, 3, 6144], P('seq', None, 'tensor')
All inputs are finite; a program needn't handle non-finite values.
Results may differ from a plain program's by a relative error of at most 0.018.
Values may be sent and summed in bfloat16 or wider, within the bound.
No kernel may reach another device: no remote copies, remote signals or barrier semaphores. Data moves between devices by JAX's collectives and lax.ppermute only.
A program may use at most 128 MiB of HBM per device.

v0:
```python
import jax
import jax.numpy as jnp
from jax import lax
from jax.sharding import PartitionSpec as P

norm_eps = 1e-05


def local(inputs, gain, weights, d_out):
    width = weights.shape[0]
    shard = inputs.shape[1]
    inputs_full, gain_full = (
        lax.all_gather(inputs, "tensor", axis=1, tiled=True),
        lax.all_gather(gain.reshape(1, shard), "tensor", axis=1, tiled=True),
    )
    x_full = inputs_full.astype(jnp.float32)
    inv_rms = lax.rsqrt(jnp.mean(x_full * x_full, axis=1, keepdims=True) + norm_eps)
    gain_row = gain_full.astype(jnp.float32)
    normed = (x_full * inv_rms * gain_row).astype(jnp.bfloat16)
    pair_weights = weights[:, 0:2, :]
    gate_up = jnp.einsum("td,dkf->tkf", normed, pair_weights, preferred_element_type=jnp.float32)
    gate = gate_up[:, 0, :]
    up_val = gate_up[:, 1, :]
    sigma = jax.nn.sigmoid(gate)
    hidden = (gate * sigma * up_val).astype(jnp.bfloat16)
    down_rows = weights[:, 2, :]
    partial_value = lax.dot_general(
        hidden, down_rows, (((1,), (1,)), ((), ())), preferred_element_type=jnp.float32
    )
    branch = lax.psum_scatter(
        partial_value.astype(jnp.bfloat16), "tensor", scatter_dimension=1, tiled=True
    )
    cot_full = lax.all_gather(d_out, "tensor", axis=1, tiled=True)
    d_hidden = jnp.dot(cot_full, down_rows, preferred_element_type=jnp.float32)
    d_gate = (d_hidden * up_val * sigma * (1.0 + gate * (1.0 - sigma))).astype(jnp.bfloat16)
    d_up = (d_hidden * gate * sigma).astype(jnp.bfloat16)
    d_pair = jnp.stack([d_gate, d_up], axis=1)
    d_partial = jnp.einsum("tkf,dkf->td", d_pair, pair_weights, preferred_element_type=jnp.float32)
    x_own = inputs.astype(jnp.float32)
    gain_own = gain.astype(jnp.float32)
    d_normed = lax.psum_scatter(
        d_partial.astype(jnp.bfloat16), "tensor", scatter_dimension=1, tiled=True
    ).astype(jnp.float32)
    products = lax.psum(jnp.sum(d_normed * gain_own * x_own, axis=1, keepdims=True), "tensor")
    mean_prod = products / width
    d_input = (inv_rms * d_normed * gain_own - inv_rms**3 * mean_prod * x_own).astype(jnp.bfloat16)
    d_gain = lax.psum(jnp.sum(d_normed * x_own * inv_rms, axis=0), "seq")
    pair_term = jnp.einsum("tc,tkf->ckf", normed, d_pair, preferred_element_type=jnp.float32)
    down_term = jnp.einsum("tc,tf->cf", cot_full, hidden, preferred_element_type=jnp.float32)
    d_weights = lax.psum_scatter(
        jnp.concatenate([pair_term, down_term[:, None, :]], axis=1).astype(jnp.bfloat16),
        "seq",
        scatter_dimension=0,
        tiled=True,
    )
    return (branch, d_input, d_gain, d_weights)


def solution(mesh):
    in_specs = (P("seq", "tensor"), P("tensor"), P(None, None, "tensor"), P("seq", "tensor"))
    out_specs = (P("seq", "tensor"), P("seq", "tensor"), P("tensor"), P("seq", None, "tensor"))
    return jax.shard_map(local, mesh=mesh, in_specs=in_specs, out_specs=out_specs, check_vma=False)
```

profile of v0, /device:TPU:0, one launch (start us, length us, event | category | flops | bytes accessed | tf_op | source)
XLA Modules:
  0.0 501.5 jit_solution(4299503231717451491)
XLA Ops:
  7.2 0.0 all-gather.5.cloned.1.call-start
  7.2 0.7 all-gather.5.cloned.1.call-update
  7.9 0.0 all-gather.7.cloned.1.call-start
  7.9 0.7 all-gather.7.cloned.1.call-update
  8.6 0.0 reduce-scatter.6.cloned.1.call-start
  8.7 0.7 reshape.49
  9.4 31.2 %all-gather.1 = bf16[8,1,512]{2,1,0:T(2,128)(2,1)S(1)} all-gather(bf16[1,1,512]{2,1,0:T(2,128)(2,1)S(1)} %reshape.49), channel_id=2, replica_groups=mesh['tensor'=8,'seq'=16] {'tensor'}, dimensions={0}, use_global_device_ids=true | all-gather | bytes 9216 | tf_op jit(solution)/shard_map/all_gather | solution.py:14
  40.6 29.8 %all-gather.5.cloned.1.call-done = bf16[256,4096]{1,0:T(8,128)(2,1)} async-done(((bf16[256,512]{1,0:T(8,128)(2,1)}), bf16[256,4096]{1,0:T(8,128)(2,1)}) %all-gather.5.cloned.1.call-update) | async-done | bytes 2097168 | tf_op jit(solution)/shard_map/all_gather | solution.py:13
  70.3 2.1 fusion.20
  72.4 7.3 %fusion.2 = f32[256,2,768]{2,0,1:T(8,128)S(1)} fusion(bf16[4096,3,768]{2,0,1:T(8,128)(2,1)} %param.6, bf16[256,4096]{1,0:T(8,128)(2,1)} %all-gather.5.cloned.1.call-done, f32[4096]{0:T(1024)S(1)} %bitcast.82, f32[256]{0:T(256)S(1)} %add_rsqrt_fusion), kind=kOutput, calls=%fused_computation.3 | convolution fusion | flops 3225419776 | bytes 16270336 | tf_op jit(solution)/shard_map/td,dkf->tkf/dot_general | solution.py:21
  79.7 0.0 copy-start.2
  79.7 49.1 %all-gather.7.cloned.1.call-done = bf16[256,4096]{1,0:T(8,128)(2,1)} async-done(((bf16[256,512]{1,0:T(8,128)(2,1)}), bf16[256,4096]{1,0:T(8,128)(2,1)}) %all-gather.7.cloned.1.call-update) | async-done | bytes 2097168 | tf_op jit(solution)/shard_map/all_gather | solution.py:33
  128.8 5.3 %fusion.47 = (bf16[256,1,768]{2,0,1:T(8,128)(2,1)S(1)}, bf16[256,1,768]{2,0,1:T(8,128)(2,1)S(1)}) fusion(f32[256,2,768]{2,0,1:T(8,128)S(1)} %fusion.2, bf16[256,4096]{1,0:T(8,128)(2,1)} %all-gather.7.cloned.1.call-done, bf16[4096,3,768]{2,0,1:T(8,128)(2,1)} %param.6), kind=kOutput, calls=%fused_computation.55 | convolution fusion | flops 1613168640 | bytes 10747904 | tf_op jit(solution)/shard_map/dot_general | solution.py:34
  134.2 9.3 %fusion.14 = bf16[256,4096]{1,0:T(8,128)(2,1)} fusion(bf16[4096,3,768]{2,0,1:T(8,128)(2,1)} %param.6, bf16[256,1,768]{2,0,1:T(8,128)(2,1)S(1)} %get-tuple-element.7, bf16[256,1,768]{2,0,1:T(8,128)(2,1)S(1)} %get-tuple-element.6), kind=kOutput, calls=%fused_computation.17 | convolution fusion | flops 3222667264 | bytes 15466496 | tf_op jit(solution)/shard_map/tkf,dkf->td/dot_general | solution.py:38
  143.5 0.0 reduce-scatter.6.cloned.1.call-update
  143.5 0.0 reduce-scatter.4.cloned.1.call-start
  143.6 0.0 copy-done.2
  143.6 5.9 %fusion.17 = bf16[256,4096]{1,0:T(8,128)(2,1)} fusion(bf16[4096,3,768]{2,0,1:T(8,128)(2,1)} %param.6, f32[256,2,768]{2,0,1:T(8,128)S(1)} %fusion.2), kind=kOutput, calls=%fused_computation.18 | convolution fusion | flops 1612840960 | bytes 9961472 | tf_op jit(solution)/shard_map/dot_general | solution.py:27
  149.5 0.0 reduce-scatter.4.cloned.1.call-update
  149.6 0.0 copy-start.1
  149.6 0.2 reduce-scatter.8.cloned.1.call-start
  149.8 4.3 fusion.8
  154.1 0.0 copy-done.1
  154.1 6.7 %convolution_convert_fusion = bf16[4096,2,768]{2,0,1:T(8,128)(2,1)} fusion(bf16[256,4096]{1,0:T(8,128)(2,1)S(1)} %copy-done.1, f32[4096]{0:T(1024)S(1)} %bitcast.83, f32[256]{0:T(256)S(1)} %add_rsqrt_fusion, bf16[256,1,768]{2,0,1:T(8,128)(2,1)S(1)} %get-tuple-element.7, bf16[256,1,768]{2,0,1:T(8,128)(2,1)S(1)} %get-tuple-element.6), kind=kOutput, calls=%fused_computation.5 | convolution fusion | flops 3233284096 | bytes 15483904 | tf_op jit(solution)/shard_map/tc,tkf->ckf/dot_general | solution.py:48
  160.9 13.8 %pad_maximum_fusion = bf16[4096,3,768]{2,0,1:T(8,128)(2,1)} fusion(bf16[4096,1,768]{2,0,1:T(8,128)(2,1)S(1)} %fusion.8, bf16[4096,2,768]{2,0,1:T(8,128)(2,1)} %convolution_convert_fusion), kind=kLoop, calls=%fused_computation | loop fusion | flops 9437184 | bytes 37748736 | tf_op jit(solution)/shard_map/concatenate | solution.py:51
  174.7 0.0 copy-start.3
  174.7 0.0 copy-start
  174.7 0.0 reduce-scatter.8.cloned.1.call-update
  174.7 0.7 copy-done.3
  175.4 42.6 %reduce-scatter.6.cloned.1.call-done = bf16[256,512]{1,0:T(8,128)(2,1)} async-done(((bf16[256,4096]{1,0:T(8,128)(2,1)}), bf16[256,512]{1,0:T(8,128)(2,1)}) %reduce-scatter.6.cloned.1.call-update) | async-done | bytes 262160 | tf_op jit(solution)/shard_map/reduce_scatter | solution.py:41
  218.0 0.0 copy-done
  218.0 1.2 fusion.42
  219.1 21.1 %psum.14 = f32[256,1]{0,1:T(1,128)S(1)} all-reduce(f32[256,1]{0,1:T(1,128)S(1)} %bitcast.85), channel_id=1, replica_groups=mesh['tensor'=8,'seq'=16] {'tensor'}, use_global_device_ids=true, to_apply=%region_4.0 | all-reduce | flops 256 | bytes 2048 | tf_op jit(solution)/shard_map/psum | solution.py:44
  240.3 27.8 %psum.15 = f32[512]{0:T(512)} all-reduce(f32[512]{0:T(512)S(1)} %get-tuple-element.4), channel_id=1, replica_groups=mesh['tensor'=8,'seq'=16] {'seq'}, use_global_device_ids=true, to_apply=%region_6.0 | all-reduce | flops 512 | bytes 4096 | tf_op jit(solution)/shard_map/psum | solution.py:47
  268.1 1.8 fusion.39
  269.9 26.9 %reduce-scatter.4.cloned.1.call-done = bf16[256,512]{1,0:T(8,128)(2,1)} async-done(((bf16[256,4096]{1,0:T(8,128)(2,1)}), bf16[256,512]{1,0:T(8,128)(2,1)}) %reduce-scatter.4.cloned.1.call-update) | async-done | bytes 262160 | tf_op jit(solution)/shard_map/reduce_scatter | solution.py:30
  296.8 198.2 %reduce-scatter.8.cloned.1.call-done = bf16[256,3,768]{2,0,1:T(8,128)(2,1)} async-done(((bf16[4096,3,768]{2,0,1:T(8,128)(2,1)}), bf16[256,3,768]{2,0,1:T(8,128)(2,1)}) %reduce-scatter.8.cloned.1.call-update) | async-done | bytes 1179664 | tf_op jit(solution)/shard_map/reduce_scatter | solution.py:50
  (4 shorter events, 0.0 us)
Async XLA Ops:
  7.2 63.2 %all-gather.5.cloned.1.call-start = ((), (), s32[]{:S(2)}) async-start(), calls=%async_computation.3 | async-start | bytes 2359296 | tf_op jit(solution)/shard_map/all_gather | solution.py:13
  7.9 120.9 %all-gather.7.cloned.1.call-start = ((), (), s32[]{:S(2)}) async-start(), calls=%async_computation.5 | async-start | bytes 2359296 | tf_op jit(solution)/shard_map/all_gather | solution.py:33
  8.6 209.3 %reduce-scatter.6.cloned.1.call-start = ((), (), s32[]{:S(2)}) async-start(), calls=%async_computation.6 | async-start | bytes 2359296 | tf_op jit(solution)/shard_map/reduce_scatter | solution.py:41
  79.7 63.9 %copy-start.2 = (f32[256,2,768]{2,0,1:T(8,128)}, f32[256,2,768]{2,0,1:T(8,128)S(1)}, u32[]{:S(2)}) copy-start(f32[256,2,768]{2,0,1:T(8,128)S(1)} %fusion.2) | copy-start | bytes 4718596
  143.5 153.3 %reduce-scatter.4.cloned.1.call-start = ((), (), s32[]{:S(2)}) async-start(), calls=%async_computation.4 | async-start | bytes 2359296 | tf_op jit(solution)/shard_map/reduce_scatter | solution.py:30
  149.6 4.6 copy-start.1
  149.6 345.4 %reduce-scatter.8.cloned.1.call-start = ((), (), s32[]{:S(2)}) async-start(), calls=%async_computation.7 | async-start | bytes 20054016 | tf_op jit(solution)/shard_map/reduce_scatter | solution.py:50
  174.7 0.7 copy-start.3
  174.7 43.3 %copy-start = (bf16[256,512]{1,0:T(8,128)(2,1)S(1)}, bf16[256,512]{1,0:T(8,128)(2,1)}, u32[]{:S(2)}) copy-start(bf16[256,512]{1,0:T(8,128)(2,1)} %param.4) | copy-start | bytes 786436
Sparse Core Ops, SparseCore 0:
  10.2 60.1 all-gather.4
  72.5 56.2 all-gather.6
  143.6 74.2 reduce-scatter.5
  222.6 74.1 reduce-scatter.3
  299.7 195.2 reduce-scatter.7
where the time goes:
time: 508 us; the launch traced here: 502 us
  waiting for transfers between devices  348 us (69%)
  blocking collectives  80.1 us (16%)
  matrix products  38.9 us (8%)
  other arithmetic  19 us (4%)
  between operations  13.8 us (3%)
    reduce_scatter x1, waiting for transfers between devices, local(): lax.psum_scatter(jnp.concatenate([pair_term, down_term[:, None, :]], axis...  198 us
    all_gather x1, waiting for transfers between devices, local(): cot_full = lax.all_gather(d_out, 'tensor', axis=1, tiled=True)  49.1 us
    reduce_scatter x1, waiting for transfers between devices, local(): lax.psum_scatter(d_partial.astype(jnp.bfloat16), 'tensor', scatter_dimens...  42.6 us
    all_gather x1, blocking collectives, local(): lax.all_gather(gain.reshape(1, shard), 'tensor', axis=1, tiled=True)  31.2 us
    all_gather x1, waiting for transfers between devices, local(): lax.all_gather(inputs, 'tensor', axis=1, tiled=True)  29.8 us
    psum x1, blocking collectives, local(): d_gain = lax.psum(jnp.sum(d_normed * x_own * inv_rms, axis=0), 'seq')  27.8 us
    reduce_scatter x1, waiting for transfers between devices, local(): lax.psum_scatter(partial_value.astype(jnp.bfloat16), 'tensor', scatter_di...  26.9 us
    psum x1, blocking collectives, local(): lax.psum(jnp.sum(d_normed * gain_own * x_own, axis=1, keepdims=True), 'te...  21.1 us
  transfers between devices with their start and end apart: 5, of which 5 were waited for; matrix products, arithmetic and copies ran while one was open for 9% of the time, Pallas kernels for 0%

commit v1 on v0

v1 whole, which is shorter than its diff:
```python
import functools
import jax
import jax.numpy as jnp
from jax import lax
from jax.experimental import pallas as pl
from jax.experimental.pallas import tpu as pltpu
from jax.sharding import PartitionSpec as P

norm_eps = 1e-05
AXES = ("tensor", "seq")
f32 = jnp.float32
bf16 = jnp.bfloat16
MiB = 1 << 20


def flat(x, y, z, c):
    x, y, z = x % 4, y % 4, z % 4
    return ((z // 2) * 4 + y) * 16 + (x * 2 + z % 2) * 2 + c


def pairs(move):
    places = [(x, y, z, c) for x in range(4) for y in range(4) for z in range(4) for c in range(2)]
    return [(flat(*place), flat(*move(*place))) for place in places]


moves = {
    "x^1": lambda x, y, z, c: (x ^ 1, y, z, c),
    "x^3": lambda x, y, z, c: (x ^ 3, y, z, c),
    "x+2": lambda x, y, z, c: (x + 2, y, z, c),
    "y+": lambda x, y, z, c: (x, y + 1, z, c),
    "y-": lambda x, y, z, c: (x, y - 1, z, c),
    "y^1": lambda x, y, z, c: (x, y ^ 1, z, c),
    "y^3": lambda x, y, z, c: (x, y ^ 3, z, c),
    "z+2": lambda x, y, z, c: (x, y, z + 2, c),
    "z^1": lambda x, y, z, c: (x, y, z ^ 1, c),
    "z^3": lambda x, y, z, c: (x, y, z ^ 3, c),
    "z^3c": lambda x, y, z, c: (x, y, z ^ 3, 1 - c),
    "c": lambda x, y, z, c: (x, y, z, 1 - c),
}


def send(value, move):
    return lax.ppermute(value, AXES, pairs(moves[move]))


def after(value, *done):
    return lax.optimization_barrier((value, *done))[0]


def rows_cat(*parts):
    return jnp.concatenate(parts, axis=0)


def dot(a, b):
    return jnp.dot(a, b, preferred_element_type=f32)


def dot_nt(a, b):
    return lax.dot_general(a, b, (((1,), (1,)), ((), ())), preferred_element_type=f32)


def dot_tn(a, b):
    return lax.dot_general(a, b, (((0,), (0,)), ((), ())), preferred_element_type=f32)


def call(body, name, shapes, scratch, limit, flops, size, args, hbm=()):
    spaces = [pltpu.SMEM] + [pltpu.HBM if i in hbm else pltpu.VMEM for i in range(1, len(args))]
    return pl.pallas_call(
        body,
        in_specs=[pl.BlockSpec(memory_space=space) for space in spaces],
        out_specs=[pl.BlockSpec(memory_space=pltpu.VMEM) for _ in shapes],
        out_shape=[jax.ShapeDtypeStruct(shape, dtype) for shape, dtype in shapes],
        scratch_shapes=scratch,
        compiler_params=pltpu.CompilerParams(vmem_limit_bytes=limit * MiB),
        cost_estimate=pl.CostEstimate(flops=flops, bytes_accessed=size, transcendentals=0),
        name=name,
    )(*args)


def lane(at, size, unit):
    return pl.ds(pl.multiple_of(at, unit), size)


def put(buf, spot, pieces):
    for dz, dy, row, ref, first, rows in pieces:
        buf[row:row + rows, lane(spot[dz * 4 + dy] * 512, 512, 512)] = ref[first:first + rows, :]


def fetch(w, held, sems, first, count, block_of):
    copies = []
    for k in range(8):
        rows = pl.ds(pl.multiple_of(block_of(k) * 512, 512), 512)
        copies.append(pltpu.make_async_copy(w.at[pl.ds(first, count), rows, :], held.at[k], sems.at[k]))
        copies[-1].start()
    return copies


def forward_body(spot, own, below, above, other, up2, dn2, up3, dn3, w, gate, up, hidden, inv, gains, keep, core_out,
                 z_out, cross_out, buf, held, sems):
    copies = fetch(w, held, sems, 0, 2, lambda k: k)
    put(buf, spot, [
        (0, 0, 0, own, 0, 272), (0, 3, 0, below, 0, 272), (0, 1, 0, above, 0, 272), (1, 0, 0, other, 0, 272),
        (0, 2, 0, up2, 0, 128), (1, 3, 0, up2, 128, 272), (0, 2, 128, dn2, 0, 144), (1, 1, 0, dn2, 144, 272),
        (1, 2, 0, up3, 0, 128), (1, 2, 128, dn3, 0, 144),
    ])
    z_lo, core = spot[8], spot[9]
    for i in range(4):
        for ref, zl, c in ((keep, z_lo, core), (core_out, z_lo, 1 - core), (z_out, 1 - z_lo, core),
                           (cross_out, 1 - z_lo, 1 - core)):
            ref[:, i * 256:(i + 1) * 256] = buf[0:256, lane((2 * i + zl) * 512 + c * 256, 256, 256)]
    gains[...] = buf[256:272, :]
    squares = jnp.zeros((256, 1), f32)
    for k in range(8):
        copies[k].wait()
        cols = slice(k * 512, (k + 1) * 512)
        x = buf[0:256, cols].astype(f32)
        squares = squares + jnp.sum(x * x, axis=1, keepdims=True)
        scaled = (x * buf[256:272, cols][0:1].astype(f32)).astype(bf16)
        for ref, j in ((gate, 0), (up, 1)):
            value = dot(scaled, held[k, j])
            ref[...] = value if k == 0 else ref[...] + value
    inv_rms = lax.rsqrt(squares / 4096 + norm_eps)
    g = gate[...] * inv_rms
    u = up[...] * inv_rms
    gate[...] = g
    up[...] = u
    hidden[...] = (g * jax.nn.sigmoid(g) * u).astype(bf16)
    inv[...] = jnp.broadcast_to(inv_rms, (256, 128))


def forward(spot, pieces, w3):
    shapes = [((256, 768), f32), ((256, 768), f32), ((256, 768), bf16), ((256, 128), f32), ((16, 4096), bf16)]
    shapes += [((256, 1024), bf16)] * 4
    scratch = [pltpu.VMEM((272, 4096), bf16), pltpu.VMEM((8, 2, 512, 768), bf16), pltpu.SemaphoreType.DMA((8,))]
    return call(forward_body, "forward", shapes, scratch, 46, 2 * 256 * 4096 * 1536, 16 * MiB,
                (spot, *pieces, w3), hbm=(len(pieces) + 1,))


def backward_body(spot, both, below, above, low, high, w, gate, up, inv, pair, products, mine, core_out, buf, acc,
                  held, sems):
    copies = fetch(w, held, sems, 2, 1, lambda k: k)
    put(buf, spot, [
        (0, 0, 0, both, 0, 256), (1, 0, 0, both, 256, 256), (0, 3, 0, below, 0, 256), (1, 3, 0, below, 256, 256),
        (0, 1, 0, above, 0, 256), (1, 1, 0, above, 256, 256), (0, 2, 0, low, 0, 128), (1, 2, 0, low, 128, 128),
        (0, 2, 128, high, 0, 128), (1, 2, 128, high, 128, 128),
    ])
    core = spot[9]
    for i in range(8):
        for ref, c in ((mine, core), (core_out, 1 - core)):
            ref[:, i * 256:(i + 1) * 256] = buf[:, lane(i * 512 + c * 256, 256, 256)]
    for k in range(8):
        copies[k].wait()
        value = dot(buf[:, k * 512:(k + 1) * 512], held[k, 0])
        acc[...] = value if k == 0 else acc[...] + value
    d_hidden = acc[...] * inv[:, 0:1]
    g, u = gate[...], up[...]
    sigma = jax.nn.sigmoid(g)
    d_gate = (d_hidden * u * sigma * (1.0 + g * (1.0 - sigma))).astype(bf16)
    d_up = (d_hidden * g * sigma).astype(bf16)
    pair[:, 0:768] = d_gate
    pair[:, 768:1536] = d_up
    total = jnp.sum(d_gate.astype(f32) * g + d_up.astype(f32) * u, axis=1, keepdims=True)
    products[...] = jnp.broadcast_to(total, (256, 128)).astype(bf16)


def backward(spot, pieces, w3, gate, up, inv):
    shapes = [((256, 1536), bf16), ((256, 128), bf16), ((256, 2048), bf16), ((256, 2048), bf16)]
    scratch = [pltpu.VMEM((256, 4096), bf16), pltpu.VMEM((256, 768), f32), pltpu.VMEM((8, 1, 512, 768), bf16),
               pltpu.SemaphoreType.DMA((8,))]
    return call(backward_body, "backward", shapes, scratch, 46, 2 * 256 * 4096 * 768, 8 * MiB,
                (spot, *pieces, w3, gate, up, inv), hbm=(len(pieces) + 1,))


def outer_body(count, rows, cols, order, *refs):
    a_refs, b_refs, out = refs[:count], refs[count:2 * count], refs[2 * count]

    def step(i, carry):
        at = lane(order[i] * rows, rows, rows)
        columns = lane(i // 4 * cols, cols, cols)
        total = dot_tn(a_refs[0][:, at], b_refs[0][:, columns])
        for a, b in zip(a_refs[1:], b_refs[1:]):
            total = total + dot_tn(a[:, at], b[:, columns])
        out[i] = total.astype(bf16)
        return carry

    lax.fori_loop(0, 8, step, 0)


def outer(name, order, a_list, b_list, rows):
    n = len(a_list)
    cols = b_list[0].shape[1] // 2
    return call(functools.partial(outer_body, n, rows, cols), name, [((8, rows, cols), bf16)], [], 24,
                2 * 256 * n * rows * 8 * cols, 8 * MiB, (order, *a_list, *b_list))[0]


def branch_rows_body(order, hidden, w, out, held, sems):
    copies = fetch(w, held, sems, 2, 1, lambda k: k // 4 * 4 + order[k])
    for k in range(8):
        copies[k].wait()
        out[k] = dot_nt(hidden[...], held[k, 0]).astype(bf16)


def branch_rows(order, hidden, w3):
    scratch = [pltpu.VMEM((8, 1, 512, 768), bf16), pltpu.SemaphoreType.DMA((8,))]
    return call(branch_rows_body, "branch_rows", [((8, 256, 512), bf16)], scratch, 46, 2 * 256 * 768 * 4096, 8 * MiB,
                (order, hidden, w3), hbm=(2,))[0]


def pair_rows_body(order, pair, products, w, out, held, sems):
    copies = fetch(w, held, sems, 0, 2, lambda k: k // 4 * 4 + order[k])
    for k in range(8):
        copies[k].wait()
        value = dot_nt(pair[:, 0:768], held[k, 0]) + dot_nt(pair[:, 768:1536], held[k, 1])
        out[k, :, 0:512] = value.astype(bf16)
        out[k, :, 512:640] = products[...]


def pair_rows(order, pair, products, w3):
    scratch = [pltpu.VMEM((8, 2, 512, 768), bf16), pltpu.SemaphoreType.DMA((8,))]
    return call(pair_rows_body, "pair_rows", [((8, 256, 640), bf16)], scratch, 46, 2 * 256 * 1536 * 4096, 16 * MiB,
                (order, pair, products, w3), hbm=(3,))[0]


def halve(terms, first, second, done=()):
    rows, cols = terms.shape[1:]
    got = send(terms[0:2].reshape(2 * rows, cols), first)
    later = after(got[rows:], *done)
    out = (terms[2].astype(f32) + later.astype(f32)).astype(bf16)
    last = send(out, second)
    return terms[3].astype(f32) + got[:rows].astype(f32) + last.astype(f32), got, out


def gather_inputs(own):
    below, above, other = send(own, "y+"), send(own, "y-"), send(own, "z+2")
    up2 = send(rows_cat(below[:128], other), "y+")
    dn2 = send(rows_cat(above[128:], other), "y-")
    up3 = send(up2[128:256], "y+")
    dn3 = send(dn2[272:], "y-")
    return (own, below, above, other, up2, dn2, up3, dn3)


def gather_cot(own, first, second):
    own = after(own, *first)
    other = send(own, "z+2")
    both = after(rows_cat(own, other), *second)
    below, above = send(both, "y+"), send(both, "y-")
    low = send(rows_cat(below[:128], below[256:384]), "y+")
    high = send(rows_cat(above[128:256], above[384:]), "y-")
    return (both, below, above, low, high)


def local(inputs, gain, weights, d_out):
    width = weights.shape[0]
    t, s = lax.axis_index("tensor"), lax.axis_index("seq")
    z_hi, y = t // 4, t % 4
    x, z_lo, core = s // 4, s // 2 % 2, s % 2
    w3 = jnp.transpose(weights, (1, 0, 2))
    spot = jnp.stack(
        [(z_hi + dz) % 2 * 4 + (y + dy) % 4 for dz in (0, 1) for dy in range(4)] + [z_lo, core]
    ).astype(jnp.int32)

    def order(at):
        return jnp.stack([at ^ 1, at ^ 2, at ^ 3, at, at ^ 3, at ^ 2, at ^ 1, at]).astype(jnp.int32)

    x_pieces = gather_inputs(rows_cat(inputs, jnp.broadcast_to(gain.reshape(1, 512), (16, 512))))
    cot_pieces = gather_cot(d_out, x_pieces[1:3], x_pieces[4:6])
    gate, up_val, hidden, inv, gains, x_keep, x_core, x_z, x_cross = forward(spot, x_pieces, w3)
    x_all = [x_keep, send(x_z, "z^3"), send(x_core, "c"), send(x_cross, "z^3c")]
    hidden_core = send(hidden, "c")

    d_pair, products, cot_mine, cot_core = backward(spot, cot_pieces, w3, gate, up_val, inv)
    cot_core = send(cot_core, "c")
    pair_z = send(d_pair, "z^1")
    pair_core = send(d_pair, "c")
    pair_cross = send(pair_z, "c")

    down_terms = outer("down_terms", order(x), [cot_mine, cot_core], [hidden, hidden_core], 512)
    d_w_low, down_one, _ = halve(down_terms[0:4], "x^1", "x^3")
    d_w_high, down_two, _ = halve(down_terms[4:8], "x^3", "x^1")
    d_w_down = jnp.concatenate([d_w_low, d_w_high], axis=1)
    lower = z_lo == 0
    theirs = jnp.where(lower, d_w_down[256:], d_w_down[:256]).astype(bf16)
    d_w_down = jnp.where(lower, d_w_down[:256], d_w_down[256:]) + send(theirs, "z^1").astype(f32)

    branch_terms = branch_rows(order(y), after(hidden, cot_mine), w3)
    low, _, _ = halve(branch_terms[0:4], "y^1", "y^3")
    high, _, _ = halve(branch_terms[4:8], "y^3", "y^1")
    upper = z_hi == 1
    theirs = jnp.where(upper, low, high).astype(bf16)
    branch = (jnp.where(upper, high, low) + send(theirs, "z+2").astype(f32)).astype(bf16)

    pair_terms = outer("pair_terms", order(x), x_all, [d_pair, pair_z, pair_core, pair_cross], 256)
    d_w_gate, pair_one, pair_out_one = halve(pair_terms[0:4], "x^1", "x^3")
    d_w_up, pair_two, pair_out_two = halve(pair_terms[4:8], "x^3", "x^1")

    d_terms = pair_rows(order(y), after(d_pair, pair_z, down_terms), products, w3)
    d_low, _, _ = halve(d_terms[0:4], "y^1", "y^3", (down_one, down_two))
    d_high, _, _ = halve(d_terms[4:8], "y^3", "y^1", (down_one, down_two))
    mine = jnp.where(upper, d_high, d_low)
    theirs = after(jnp.where(upper, d_low, d_high).astype(bf16), pair_one, pair_two)
    mine = mine + send(theirs, "z+2").astype(f32)
    d_normed, products = mine[:, :512], mine[:, 512:513] / width

    x_own = inputs.astype(f32)
    d_input = (d_normed * gain.astype(f32) - inv[:, :1] * products * x_own).astype(bf16)
    d_gain = jnp.sum(d_normed * x_own, axis=0, keepdims=True)
    d_gain = after(d_gain, pair_out_one, pair_out_two)
    for move in ("c", "z^1", "x^1", "x+2"):
        d_gain = d_gain + send(d_gain, move)

    gain_rows = lax.dynamic_slice(gains, (0, s * 256), (1, 256)).astype(f32).reshape(256, 1)
    d_weights = jnp.stack(
        [(d_w_gate * gain_rows).astype(bf16), (d_w_up * gain_rows).astype(bf16), d_w_down.astype(bf16)], axis=1
    )
    return (branch, d_input, d_gain.reshape(512), d_weights)


def solution(mesh):
    in_specs = (P("seq", "tensor"), P("tensor"), P(None, None, "tensor"), P("seq", "tensor"))
    out_specs = (P("seq", "tensor"), P("seq", "tensor"), P("tensor"), P("seq", None, "tensor"))
    return jax.shard_map(local, mesh=mesh, in_specs=in_specs, out_specs=out_specs, check_vma=False)
```

time: 508 us -> 177 us (0.35); the launches traced: 502 us -> 176 us
  waiting for transfers between devices: 348 us -> 75.8 us
  blocking collectives: 80.1 us -> 0 us
  starting transfers between devices: 0.38 us -> 51.8 us
  matrix products: 38.9 us -> 0 us
  Pallas kernels: 0 us -> 35 us
  between operations: 13.8 us -> 1.12 us
  other arithmetic: 19 us -> 7.75 us
    reduce_scatter x3 -> x0, waiting for transfers between devices: 268 us -> none  [the longest x1 198 us: local(): lax.psum_scatter(jnp.concatenate([pair_term, down_term[:, None, :]], axis...]
    all_gather x2 -> x0, waiting for transfers between devices: 78.9 us -> none  [the longest x1 49.1 us: local(): cot_full = lax.all_gather(d_out, 'tensor', axis=1, tiled=True)]
    ppermute x0 -> x43, waiting for transfers between devices: none -> 75.8 us  [send(): return lax.ppermute(value, AXES, pairs(moves[move]))]
    ppermute x0 -> x43, starting transfers between devices: none -> 51.8 us  [send(): return lax.ppermute(value, AXES, pairs(moves[move]))]
    psum x2 -> x0, blocking collectives: 48.9 us -> none  [the longest x1 27.8 us: local(): d_gain = lax.psum(jnp.sum(d_normed * x_own * inv_rms, axis=0), 'seq')]
    dot_general x6 -> x0, matrix products: 38.9 us -> none  [the longest x1 9.34 us: local(): jnp.einsum('tkf,dkf->td', d_pair, pair_weights, preferred_element_type=jn...]
    pallas_call x0 -> x6, Pallas kernels: none -> 35 us  [call(): pl.pallas_call(body, in_specs=[pl.BlockSpec(memory_space=space) for space...]
    all_gather x1 -> x0, blocking collectives: 31.2 us -> none  [local(): lax.all_gather(gain.reshape(1, shard), 'tensor', axis=1, tiled=True)]
  transfers between devices with their start and end apart: 5 -> 43, of which waited for: 5 -> 19; matrix products, arithmetic and copies ran while one was open for 9% -> 4% of each run, Pallas kernels for 0% -> 16%
where the time goes in v1:
time: 177 us; the launch traced here: 176 us
  waiting for transfers between devices  75.8 us (43%)
  starting transfers between devices  51.8 us (29%)
  Pallas kernels  35 us (20%)
  other arithmetic  7.75 us (4%)
  local copies, waits for them, and re-layouts  5.09 us (3%)
    ppermute x43, waiting for transfers between devices, send(): return lax.ppermute(value, AXES, pairs(moves[move]))  75.8 us
    ppermute x43, starting transfers between devices, send(): return lax.ppermute(value, AXES, pairs(moves[move]))  51.8 us
    pallas_call x6, Pallas kernels, call(): pl.pallas_call(body, in_specs=[pl.BlockSpec(memory_space=space) for space...  35 us
  transfers between devices with their start and end apart: 43, of which 19 were waited for; matrix products, arithmetic and copies ran while one was open for 4% of the time, Pallas kernels for 16%

profile of v1, /device:TPU:0, one launch (start us, length us, event | category | flops | bytes accessed | tf_op | source)
XLA Modules:
  0.0 176.5 jit_solution(8746280594587832323)
XLA Ops:
  0.6 0.7 broadcast_in_dim.4
  1.4 1.0 pad_maximum_fusion.5.own
  2.3 3.2 %collective-permute-start.1 = (bf16[272,512]{1,0:T(8,128)(2,1)S(1)}, bf16[272,512]{1,0:T(8,128)(2,1)S(1)}, u32[]{:S(2)}, u32[]{:S(2)}) collective-permute-start(bf16[272,512]{1,0:T(8,128)(2,1)S(1)} %pad_maximum_fusion.5.own), channel_id=1, source_target_pairs={{0,48},{1,49},{2,50},{3,51},{64,112},{65,113},{66,114},{67,115},{1... | collective-permute-start | bytes 835592 | tf_op jit(solution)/shard_map/ppermute | solution.py:43
  5.5 3.9 %collective-permute-start.2 = (bf16[272,512]{1,0:T(8,128)(2,1)S(1)}, bf16[272,512]{1,0:T(8,128)(2,1)S(1)}, u32[]{:S(2)}, u32[]{:S(2)}) collective-permute-start(bf16[272,512]{1,0:T(8,128)(2,1)S(1)} %pad_maximum_fusion.5.own), channel_id=1, source_target_pairs={{0,64},{1,65},{2,66},{3,67},{64,0},{65,1},{66,2},{67,3},{16,80},{1... | collective-permute-start | bytes 835592 | tf_op jit(solution)/shard_map/ppermute | solution.py:43
  9.4 2.0 %collective-permute-done.1.above = bf16[272,512]{1,0:T(8,128)(2,1)S(1)} collective-permute-done((bf16[272,512]{1,0:T(8,128)(2,1)S(1)}, bf16[272,512]{1,0:T(8,128)(2,1)S(1)}, u32[]{:S(2)}, u32[]{:S(2)}) %collective-permute-start.1) | collective-permute-done | bytes 278560 | tf_op jit(solution)/shard_map/ppermute | solution.py:43
  11.4 4.3 %collective-permute-done.2.other = bf16[272,512]{1,0:T(8,128)(2,1)S(1)} collective-permute-done((bf16[272,512]{1,0:T(8,128)(2,1)S(1)}, bf16[272,512]{1,0:T(8,128)(2,1)S(1)}, u32[]{:S(2)}, u32[]{:S(2)}) %collective-permute-start.2) | collective-permute-done | bytes 278560 | tf_op jit(solution)/shard_map/ppermute | solution.py:43
  15.8 0.8 collective-permute-start.4
  16.6 1.8 %collective-permute-done.below = bf16[272,512]{1,0:T(8,128)(2,1)S(1)} collective-permute-done((bf16[272,512]{1,0:T(8,128)(2,1)S(1)}, bf16[272,512]{1,0:T(8,128)(2,1)S(1)}, u32[]{:S(2)}, u32[]{:S(2)}) %collective-permute-start) | collective-permute-done | bytes 278560 | tf_op jit(solution)/shard_map/ppermute | solution.py:43
  18.6 2.7 %collective-permute-start.7 = (bf16[256,512]{1,0:T(8,128)(2,1)S(1)}, bf16[256,512]{1,0:T(8,128)(2,1)S(1)}, u32[]{:S(2)}, u32[]{:S(2)}) collective-permute-start(bf16[256,512]{1,0:T(8,128)(2,1)S(1)} %copy-done.16), channel_id=1, source_target_pairs={{0,64},{1,65},{2,66},{3,67},{64,0},{65,1},{66,2},{67,3},{16,80},{1... | collective-permute-start | bytes 786440 | tf_op jit(solution)/shard_map/ppermute | solution.py:43
  21.3 5.5 %collective-permute-done.7 = bf16[256,512]{1,0:T(8,128)(2,1)S(1)} collective-permute-done((bf16[256,512]{1,0:T(8,128)(2,1)S(1)}, bf16[256,512]{1,0:T(8,128)(2,1)S(1)}, u32[]{:S(2)}, u32[]{:S(2)}) %collective-permute-start.7) | collective-permute-done | bytes 262176 | tf_op jit(solution)/shard_map/ppermute | solution.py:43
  26.8 2.7 %collective-permute-done.3.up2 = bf16[400,512]{1,0:T(8,128)(2,1)S(1)} collective-permute-done((bf16[400,512]{1,0:T(8,128)(2,1)S(1)}, bf16[400,512]{1,0:T(8,128)(2,1)S(1)}, u32[]{:S(2)}, u32[]{:S(2)}) %collective-permute-start.3) | collective-permute-done | bytes 409632 | tf_op jit(solution)/shard_map/ppermute | solution.py:43
  29.8 1.7 collective-permute-start.8
  31.7 3.3 %collective-permute-start.6 = (bf16[144,512]{1,0:T(8,128)(2,1)S(1)}, bf16[144,512]{1,0:T(8,128)(2,1)S(1)}, u32[]{:S(2)}, u32[]{:S(2)}) collective-permute-start(bf16[144,512]{1,0:T(8,128)(2,1)S(1)} %slice.249), channel_id=1, source_target_pairs={{0,48},{1,49},{2,50},{3,51},{64,112},{65,113},{66,114},{67,115},{1... | collective-permute-start | bytes 442376 | tf_op jit(solution)/shard_map/ppermute | solution.py:43
  35.0 9.3 %collective-permute-done.9.above = bf16[512,512]{1,0:T(8,128)(2,1)S(1)} collective-permute-done((bf16[512,512]{1,0:T(8,128)(2,1)S(1)}, bf16[512,512]{1,0:T(8,128)(2,1)S(1)}, u32[]{:S(2)}, u32[]{:S(2)}) %collective-permute-start.9) | collective-permute-done | bytes 524320 | tf_op jit(solution)/shard_map/ppermute | solution.py:43
  44.4 0.7 collective-permute-start.11
  45.1 1.5 collective-permute-start.10
  47.0 5.9 %forward.1 = (f32[256,768]{1,0:T(8,128)S(1)}, f32[256,768]{1,0:T(8,128)S(1)}, bf16[256,768]{1,0:T(8,128)(2,1)S(1)}, f32[256,128]{1,0:T(8,128)S(1)}, bf16[16,4096...) custom-call(s32[10]{0:T(128)S(1)} %stack.116.spot, ...), custom_call_target="tpu_custom_call" | custom-call | flops 3221225472 | bytes 16777216 | tf_op jit(solution)/shard_map/forward/pallas_call | solution.py:68
  52.9 0.8 copy-done.5
  53.7 0.8 copy-done.7
  54.5 0.8 copy-done.9
  55.3 6.0 %backward.1 = (bf16[256,1536]{1,0:T(8,128)(2,1)}, bf16[256,128]{1,0:T(8,128)(2,1)S(1)}, bf16[256,2048]{1,0:T(8,128)(2,1)S(1)}, bf16[256,2048]{1,0:T(8,128)(2,1)}) custom-call(s32[10]{0:T(128)S(1)} %stack.116.spot, bf16[512,512]{1,0:T(8,128)(2,1)S(1)} %pad_maximum_fusion.2.both, bf16[512,512]{1,0:T(8,128)(2,1)S(1)} %collective-permute-done.8.below, ...), custom_call_target="tpu_custom_call" | custom-call | flops 1610612736 | bytes 8388608 | tf_op jit(solution)/shard_map/backward/pallas_call | solution.py:68
  61.4 1.1 collective-permute-start.17
  63.0 1.2 collective-permute-start.26
  64.3 5.0 %branch_rows.1 = bf16[8,256,512]{2,1,0:T(8,128)(2,1)S(1)} custom-call(s32[8]{0:T(128)S(1)} %stack.105.order, bf16[256,768]{1,0:T(8,128)(2,1)S(1)} %get-tuple-element.32.hidden.refs_2_, bf16[3,4096,768]{2,1,0:T(8,128)(2,1)} %bitcast.126), custom_call_target="tpu_custom_call" | custom-call | flops 1610612736 | bytes 8388608 | tf_op jit(solution)/shard_map/branch_rows/pallas_call | solution.py:68
  69.2 1.0 fusion.32
  70.3 2.1 %collective-permute-start.28 = (bf16[256,1024]{1,0:T(8,128)(2,1)S(1)}, bf16[256,1024]{1,0:T(8,128)(2,1)S(1)}, u32[]{:S(2)}, u32[]{:S(2)}) collective-permute-start(bf16[256,1024]{1,0:T(8,128)(2,1)S(1)} %copy-done.8), channel_id=1, source_target_pairs={{0,67},{1,66},{2,65},{3,64},{64,3},{65,2},{66,1},{67,0},{16,83},{1... | collective-permute-start | bytes 1572872 | tf_op jit(solution)/shard_map/ppermute | solution.py:43
  72.5 4.4 %down_terms.1 = bf16[8,512,384]{2,1,0:T(8,128)(2,1)S(1)} custom-call(s32[8]{0:T(128)S(1)} %stack.121.order, bf16[256,2048]{1,0:T(8,128)(2,1)S(1)} %get-tuple-element.31.refs_0_, bf16[256,2048]{1,0:T(8,128)(2,1)S(1)} %collective-permute-done.18.refs_1_, bf16[256,768]{1,0:T(8,128)(2,1)S(1)} %get-tuple-element.32.hidden.refs_2_, ...), custom_call_target="tpu_custom_call" | custom-call | flops 1610612736 | bytes 8388608 | tf_op jit(solution)/shard_map/down_terms/pallas_call | solution.py:68
  76.9 4.7 %collective-permute-done.17.refs_5_ = bf16[256,1536]{1,0:T(8,128)(2,1)S(1)} collective-permute-done((bf16[256,1536]{1,0:T(8,128)(2,1)}, bf16[256,1536]{1,0:T(8,128)(2,1)S(1)}, u32[]{:S(2)}, u32[]{:S(2)}) %collective-permute-start.17) | collective-permute-done | bytes 786464 | tf_op jit(solution)/shard_map/ppermute | solution.py:43
  81.6 1.4 collective-permute-start.12
  83.0 7.5 %pair_rows.1 = bf16[8,256,640]{2,1,0:T(8,128)(2,1)S(1)} custom-call(s32[8]{0:T(128)S(1)} %stack.105.order, bf16[256,1536]{1,0:T(8,128)(2,1)} %get-tuple-element.35.pair.refs_4_, bf16[256,128]{1,0:T(8,128)(2,1)S(1)} %get-tuple-element.36.products, bf16[3,4096,768]{2,1,0:T(8,128)(2,1)} %bitcast.127), custom_call_target="tpu_custom_call" | custom-call | flops 3221225472 | bytes 16777216 | tf_op jit(solution)/shard_map/pair_rows/pallas_call | solution.py:68
  90.8 1.6 collective-permute-start.21
  92.4 4.0 %collective-permute-done.12 = bf16[512,512]{1,0:T(8,128)(2,1)S(1)} collective-permute-done((bf16[512,512]{1,0:T(8,128)(2,1)}, bf16[512,512]{1,0:T(8,128)(2,1)S(1)}, u32[]{:S(2)}, u32[]{:S(2)}) %collective-permute-start.12) | collective-permute-done | bytes 524320 | tf_op jit(solution)/shard_map/ppermute | solution.py:43
  96.4 2.8 %collective-permute-start.22 = (bf16[1024,384]{1,0:T(8,128)(2,1)S(1)}, bf16[1024,384]{1,0:T(8,128)(2,1)S(1)}, u32[]{:S(2)}, u32[]{:S(2)}) collective-permute-start(bf16[1024,384]{1,0:T(8,128)(2,1)S(1)} %bitcast.128), channel_id=1, source_target_pairs={{0,12},{1,13},{2,14},{3,15},{64,76},{65,77},{66,78},{67,79},{16,28... | collective-permute-start | bytes 2359304 | tf_op jit(solution)/shard_map/ppermute | solution.py:43
  99.3 5.9 %collective-permute-done.14 = bf16[512,512]{1,0:T(8,128)(2,1)S(1)} collective-permute-done((bf16[512,512]{1,0:T(8,128)(2,1)}, bf16[512,512]{1,0:T(8,128)(2,1)S(1)}, u32[]{:S(2)}, u32[]{:S(2)}) %collective-permute-start.14) | collective-permute-done | bytes 524320 | tf_op jit(solution)/shard_map/ppermute | solution.py:43
  105.2 1.8 %collective-permute-start.20 = (bf16[512,640]{1,0:T(8,128)(2,1)S(1)}, bf16[512,640]{1,0:T(8,128)(2,1)S(1)}, u32[]{:S(2)}, u32[]{:S(2)}) collective-permute-start(bf16[512,640]{1,0:T(8,128)(2,1)S(1)} %bitcast.133), channel_id=1, source_target_pairs={{0,48},{1,49},{2,50},{3,51},{64,112},{65,113},{66,114},{67,115},{1... | collective-permute-start | bytes 1966088 | tf_op jit(solution)/shard_map/ppermute | solution.py:43
  107.0 0.7 dynamic-slice_convert_fusion
  107.7 6.2 %pair_terms.1 = bf16[8,256,768]{2,1,0:T(8,128)(2,1)S(1)} custom-call(s32[8]{0:T(128)S(1)} %stack.121.order, bf16[256,1024]{1,0:T(8,128)(2,1)S(1)} %copy-done.6, bf16[256,1024]{1,0:T(8,128)(2,1)S(1)} %collective-permute-done.26.refs_1_, bf16[256,1024]{1,0:T(8,128)(2,1)S(1)} %collective-permute-done.27.refs_2_, ...), custom_call_target="tpu_custom_call" | custom-call | flops 3221225472 | bytes 8388608 | tf_op jit(solution)/shard_map/pair_terms/pallas_call | solution.py:68
  114.0 1.6 collective-permute-start.31
  115.6 7.2 %collective-permute-done.20 = bf16[512,640]{1,0:T(8,128)(2,1)S(1)} collective-permute-done((bf16[512,640]{1,0:T(8,128)(2,1)S(1)}, bf16[512,640]{1,0:T(8,128)(2,1)S(1)}, u32[]{:S(2)}, u32[]{:S(2)}) %collective-permute-start.20) | collective-permute-done | bytes 655392 | tf_op jit(solution)/shard_map/ppermute | solution.py:43
  122.8 2.8 %collective-permute-start.32 = (bf16[512,768]{1,0:T(8,128)(2,1)S(1)}, bf16[512,768]{1,0:T(8,128)(2,1)S(1)}, u32[]{:S(2)}, u32[]{:S(2)}) collective-permute-start(bf16[512,768]{1,0:T(8,128)(2,1)S(1)} %bitcast.130), channel_id=1, source_target_pairs={{0,12},{1,13},{2,14},{3,15},{64,76},{65,77},{66,78},{67,79},{16,28... | collective-permute-start | bytes 2359304 | tf_op jit(solution)/shard_map/ppermute | solution.py:43
  125.8 1.9 %collective-permute-start.25 = (bf16[256,640]{1,0:T(8,128)(2,1)S(1)}, bf16[256,640]{1,0:T(8,128)(2,1)S(1)}, u32[]{:S(2)}, u32[]{:S(2)}) collective-permute-start(bf16[256,640]{1,0:T(8,128)(2,1)S(1)} %get-tuple-element.56), channel_id=1, source_target_pairs={{0,48},{1,49},{2,50},{3,51},{64,112},{65,113},{66,114},{67,115},{1... | collective-permute-start | bytes 983048 | tf_op jit(solution)/shard_map/ppermute | solution.py:43
  127.9 0.6 collective-permute-start.40
  128.6 6.7 %collective-permute-done.25 = bf16[256,640]{1,0:T(8,128)(2,1)S(1)} collective-permute-done((bf16[256,640]{1,0:T(8,128)(2,1)S(1)}, bf16[256,640]{1,0:T(8,128)(2,1)S(1)}, u32[]{:S(2)}, u32[]{:S(2)}) %collective-permute-start.25) | collective-permute-done | bytes 327712 | tf_op jit(solution)/shard_map/ppermute | solution.py:43
  135.3 1.8 %collective-permute-start.15 = (bf16[256,512]{1,0:T(8,128)(2,1)S(1)}, bf16[256,512]{1,0:T(8,128)(2,1)S(1)}, u32[]{:S(2)}, u32[]{:S(2)}) collective-permute-start(bf16[256,512]{1,0:T(8,128)(2,1)S(1)} %get-tuple-element.60), channel_id=1, source_target_pairs={{0,48},{1,49},{2,50},{3,51},{64,112},{65,113},{66,114},{67,115},{1... | collective-permute-start | bytes 786440 | tf_op jit(solution)/shard_map/ppermute | solution.py:43
  137.4 7.0 %collective-permute-done.32 = bf16[512,768]{1,0:T(8,128)(2,1)S(1)} collective-permute-done((bf16[512,768]{1,0:T(8,128)(2,1)S(1)}, bf16[512,768]{1,0:T(8,128)(2,1)S(1)}, u32[]{:S(2)}, u32[]{:S(2)}) %collective-permute-start.32) | collective-permute-done | bytes 786464 | tf_op jit(solution)/shard_map/ppermute | solution.py:43
  144.4 1.6 collective-permute-start.33
  146.1 4.6 %collective-permute-done.40 = bf16[512,384]{1,0:T(8,128)(2,1)S(1)} collective-permute-done((bf16[512,384]{1,0:T(8,128)(2,1)S(1)}, bf16[512,384]{1,0:T(8,128)(2,1)S(1)}, u32[]{:S(2)}, u32[]{:S(2)}) %collective-permute-start.40) | collective-permute-done | bytes 393248 | tf_op jit(solution)/shard_map/ppermute | solution.py:43
  150.9 0.4 collective-permute-start.41
  151.6 1.5 collective-permute-done.33
  153.4 0.9 fusion.19
  154.5 1.7 collective-permute-start.16
  156.3 0.6 collective-permute-start.39
  156.8 2.8 %collective-permute-start.38 = (bf16[256,768]{1,0:T(8,128)(2,1)S(1)}, bf16[256,768]{1,0:T(8,128)(2,1)S(1)}, u32[]{:S(2)}, u32[]{:S(2)}) collective-permute-start(bf16[256,768]{1,0:T(8,128)(2,1)S(1)} %get-tuple-element.51), channel_id=1, source_target_pairs={{0,12},{1,13},{2,14},{3,15},{64,76},{65,77},{66,78},{67,79},{16,28... | collective-permute-start | bytes 1179656 | tf_op jit(solution)/shard_map/ppermute | solution.py:43
  159.6 1.1 collective-permute-start.35
  160.9 3.1 %collective-permute-done.35 = f32[1,512]{1,0:T(1,128)S(1)} collective-permute-done((f32[1,512]{1,0:T(1,128)S(1)}, f32[1,512]{1,0:T(1,128)S(1)}, u32[]{:S(2)}, u32[]{:S(2)}) %collective-permute-start.35) | collective-permute-done | bytes 2080 | tf_op jit(solution)/shard_map/ppermute | solution.py:43
  164.0 0.6 collective-permute-start.36
  164.7 1.1 collective-permute-start.42
  165.8 2.6 %collective-permute-done.36 = f32[1,512]{1,0:T(1,128)S(1)} collective-permute-done((f32[1,512]{1,0:T(1,128)S(1)}, f32[1,512]{1,0:T(1,128)S(1)}, u32[]{:S(2)}, u32[]{:S(2)}) %collective-permute-start.36) | collective-permute-done | bytes 2080 | tf_op jit(solution)/shard_map/ppermute | solution.py:43
  168.4 2.5 %collective-permute-start.37 = (f32[1,512]{1,0:T(1,128)S(1)}, f32[1,512]{1,0:T(1,128)S(1)}, u32[]{:S(2)}, u32[]{:S(2)}) collective-permute-start(f32[1,512]{1,0:T(1,128)S(1)} %add.218), channel_id=1, source_target_pairs={{0,8},{1,9},{2,10},{3,11},{64,72},{65,73},{66,74},{67,75},{16,24},... | collective-permute-start | bytes 6152 | tf_op jit(solution)/shard_map/ppermute | solution.py:43
  170.9 0.9 add_convert_fusion.1
  171.8 1.7 collective-permute-done.37
  173.5 0.6 add.219
  174.4 0.8 collective-permute-done.42
  175.3 1.1 pad_maximum_fusion
  (116 shorter events, 5.1 us)
Async XLA Ops:
  0.6 17.9 %copy-start.16 = (bf16[256,512]{1,0:T(8,128)(2,1)S(1)}, bf16[256,512]{1,0:T(8,128)(2,1)}, u32[]{:S(2)}) copy-start(bf16[256,512]{1,0:T(8,128)(2,1)} %param.7) | copy-start | bytes 786436
  2.3 9.1 %collective-permute-start.1 = (bf16[272,512]{1,0:T(8,128)(2,1)S(1)}, bf16[272,512]{1,0:T(8,128)(2,1)S(1)}, u32[]{:S(2)}, u32[]{:S(2)}) collective-permute-start(bf16[272,512]{1,0:T(8,128)(2,1)S(1)} %pad_maximum_fusion.5.own), channel_id=1, source_target_pairs={{0,48},{1,49},{2,50},{3,51},{64,112},{65,113},{66,114},{67,115},{1... | collective-permute-start | bytes 835592 | tf_op jit(solution)/shard_map/ppermute | solution.py:43
  5.5 10.2 %collective-permute-start.2 = (bf16[272,512]{1,0:T(8,128)(2,1)S(1)}, bf16[272,512]{1,0:T(8,128)(2,1)S(1)}, u32[]{:S(2)}, u32[]{:S(2)}) collective-permute-start(bf16[272,512]{1,0:T(8,128)(2,1)S(1)} %pad_maximum_fusion.5.own), channel_id=1, source_target_pairs={{0,64},{1,65},{2,66},{3,67},{64,0},{65,1},{66,2},{67,3},{16,80},{1... | collective-permute-start | bytes 835592 | tf_op jit(solution)/shard_map/ppermute | solution.py:43
  9.4 9.0 %collective-permute-start = (bf16[272,512]{1,0:T(8,128)(2,1)S(1)}, bf16[272,512]{1,0:T(8,128)(2,1)S(1)}, u32[]{:S(2)}, u32[]{:S(2)}) collective-permute-start(bf16[272,512]{1,0:T(8,128)(2,1)S(1)} %pad_maximum_fusion.5.own), channel_id=1, source_target_pairs={{0,16},{1,17},{2,18},{3,19},{64,80},{65,81},{66,82},{67,83},{16,32... | collective-permute-start | bytes 835592 | tf_op jit(solution)/shard_map/ppermute | solution.py:43
  11.4 9.8 %copy-start = (bf16[272,512]{1,0:T(8,128)(2,1)}, bf16[272,512]{1,0:T(8,128)(2,1)S(1)}, u32[]{:S(2)}) copy-start(bf16[272,512]{1,0:T(8,128)(2,1)S(1)} %collective-permute-done.1.above) | copy-start | bytes 835588
  15.8 13.7 %collective-permute-start.4 = (bf16[416,512]{1,0:T(8,128)(2,1)S(1)}, bf16[416,512]{1,0:T(8,128)(2,1)S(1)}, u32[]{:S(2)}, u32[]{:S(2)}) collective-permute-start(bf16[416,512]{1,0:T(8,128)(2,1)S(1)} %pad_maximum_fusion.3), channel_id=1, source_target_pairs={{0,48},{1,49},{2,50},{3,51},{64,112},{65,113},{66,114},{67,115},{1... | collective-permute-start | bytes 1277960 | tf_op jit(solution)/shard_map/ppermute | solution.py:43
  18.4 2.8 %copy-start.2 = (bf16[272,512]{1,0:T(8,128)(2,1)}, bf16[272,512]{1,0:T(8,128)(2,1)S(1)}, u32[]{:S(2)}) copy-start(bf16[272,512]{1,0:T(8,128)(2,1)S(1)} %collective-permute-done.below) | copy-start | bytes 835588
  18.5 11.0 %collective-permute-start.3 = (bf16[400,512]{1,0:T(8,128)(2,1)S(1)}, bf16[400,512]{1,0:T(8,128)(2,1)S(1)}, u32[]{:S(2)}, u32[]{:S(2)}) collective-permute-start(bf16[400,512]{1,0:T(8,128)(2,1)S(1)} %pad_maximum_fusion.4), channel_id=1, source_target_pairs={{0,16},{1,17},{2,18},{3,19},{64,80},{65,81},{66,82},{67,83},{16,32... | collective-permute-start | bytes 1228808 | tf_op jit(solution)/shard_map/ppermute | solution.py:43
  18.6 8.1 %collective-permute-start.7 = (bf16[256,512]{1,0:T(8,128)(2,1)S(1)}, bf16[256,512]{1,0:T(8,128)(2,1)S(1)}, u32[]{:S(2)}, u32[]{:S(2)}) collective-permute-start(bf16[256,512]{1,0:T(8,128)(2,1)S(1)} %copy-done.16), channel_id=1, source_target_pairs={{0,64},{1,65},{2,66},{3,67},{64,0},{65,1},{66,2},{67,3},{16,80},{1... | collective-permute-start | bytes 786440 | tf_op jit(solution)/shard_map/ppermute | solution.py:43
  29.5 14.9 %collective-permute-start.9 = (bf16[512,512]{1,0:T(8,128)(2,1)S(1)}, bf16[512,512]{1,0:T(8,128)(2,1)S(1)}, u32[]{:S(2)}, u32[]{:S(2)}) collective-permute-start(bf16[512,512]{1,0:T(8,128)(2,1)S(1)} %pad_maximum_fusion.2.both), channel_id=1, source_target_pairs={{0,48},{1,49},{2,50},{3,51},{64,112},{65,113},{66,114},{67,115},{1... | collective-permute-start | bytes 1572872 | tf_op jit(solution)/shard_map/ppermute | solution.py:43
  29.8 15.3 %collective-permute-start.8 = (bf16[512,512]{1,0:T(8,128)(2,1)S(1)}, bf16[512,512]{1,0:T(8,128)(2,1)S(1)}, u32[]{:S(2)}, u32[]{:S(2)}) collective-permute-start(bf16[512,512]{1,0:T(8,128)(2,1)S(1)} %pad_maximum_fusion.2.both), channel_id=1, source_target_pairs={{0,16},{1,17},{2,18},{3,19},{64,80},{65,81},{66,82},{67,83},{16,32... | collective-permute-start | bytes 1572872 | tf_op jit(solution)/shard_map/ppermute | solution.py:43
  31.6 15.4 %copy-start.1 = (bf16[272,512]{1,0:T(8,128)(2,1)S(1)}, bf16[272,512]{1,0:T(8,128)(2,1)}, u32[]{:S(2)}) copy-start(bf16[272,512]{1,0:T(8,128)(2,1)} %copy-done) | copy-start | bytes 835588
  31.6 15.4 %copy-start.3 = (bf16[272,512]{1,0:T(8,128)(2,1)S(1)}, bf16[272,512]{1,0:T(8,128)(2,1)}, u32[]{:S(2)}) copy-start(bf16[272,512]{1,0:T(8,128)(2,1)} %copy-done.2) | copy-start | bytes 835588
  31.6 15.4 %collective-permute-start.5 = (bf16[128,512]{1,0:T(8,128)(2,1)S(1)}, bf16[128,512]{1,0:T(8,128)(2,1)S(1)}, u32[]{:S(2)}, u32[]{:S(2)}) collective-permute-start(bf16[128,512]{1,0:T(8,128)(2,1)S(1)} %slice.248), channel_id=1, source_target_pairs={{0,16},{1,17},{2,18},{3,19},{64,80},{65,81},{66,82},{67,83},{16,32... | collective-permute-start | bytes 393224 | tf_op jit(solution)/shard_map/ppermute | solution.py:43
  31.7 15.3 %collective-permute-start.6 = (bf16[144,512]{1,0:T(8,128)(2,1)S(1)}, bf16[144,512]{1,0:T(8,128)(2,1)S(1)}, u32[]{:S(2)}, u32[]{:S(2)}) collective-permute-start(bf16[144,512]{1,0:T(8,128)(2,1)S(1)} %slice.249), channel_id=1, source_target_pairs={{0,48},{1,49},{2,50},{3,51},{64,112},{65,113},{66,114},{67,115},{1... | collective-permute-start | bytes 442376 | tf_op jit(solution)/shard_map/ppermute | solution.py:43
  44.4 10.1 %collective-permute-start.11 = (bf16[256,512]{1,0:T(8,128)(2,1)S(1)}, bf16[256,512]{1,0:T(8,128)(2,1)S(1)}, u32[]{:S(2)}, u32[]{:S(2)}) collective-permute-start(bf16[256,512]{1,0:T(8,128)(2,1)S(1)} %pad_maximum_fusion.7), channel_id=1, source_target_pairs={{0,48},{1,49},{2,50},{3,51},{64,112},{65,113},{66,114},{67,115},{1... | collective-permute-start | bytes 786440 | tf_op jit(solution)/shard_map/ppermute | solution.py:43
  45.1 9.4 %collective-permute-start.10 = (bf16[256,512]{1,0:T(8,128)(2,1)S(1)}, bf16[256,512]{1,0:T(8,128)(2,1)S(1)}, u32[]{:S(2)}, u32[]{:S(2)}) collective-permute-start(bf16[256,512]{1,0:T(8,128)(2,1)S(1)} %pad_maximum_fusion.6), channel_id=1, source_target_pairs={{0,16},{1,17},{2,18},{3,19},{64,80},{65,81},{66,82},{67,83},{16,32... | collective-permute-start | bytes 786440 | tf_op jit(solution)/shard_map/ppermute | solution.py:43
  52.9 0.8 copy-start.5
  53.7 0.8 copy-start.7
  54.5 0.8 copy-start.9
  54.5 6.8 %copy-start.4 = (bf16[16,4096]{1,0:T(8,128)(2,1)}, bf16[16,4096]{1,0:T(8,128)(2,1)S(1)}, u32[]{:S(2)}) copy-start(bf16[16,4096]{1,0:T(8,128)(2,1)S(1)} %get-tuple-element.45) | copy-start | bytes 393220
  54.5 6.8 %copy-start.10 = (bf16[256,1024]{1,0:T(8,128)(2,1)}, bf16[256,1024]{1,0:T(8,128)(2,1)S(1)}, u32[]{:S(2)}) copy-start(bf16[256,1024]{1,0:T(8,128)(2,1)S(1)} %get-tuple-element.40) | copy-start | bytes 1572868
  55.3 7.2 %copy-start.17 = (bf16[512]{0:T(512)(128)(2,1)S(1)}, bf16[512]{0:T(512)(128)(2,1)}, u32[]{:S(2)}) copy-start(bf16[512]{0:T(512)(128)(2,1)} %param.5) | copy-start | bytes 3076
  61.3 11.1 %collective-permute-start.18 = (bf16[256,2048]{1,0:T(8,128)(2,1)}, bf16[256,2048]{1,0:T(8,128)(2,1)S(1)}, u32[]{:S(2)}, u32[]{:S(2)}) collective-permute-start(bf16[256,2048]{1,0:T(8,128)(2,1)} %get-tuple-element.34), channel_id=1, source_target_pairs={{0,1},{1,0},{2,3},{3,2},{64,65},{65,64},{66,67},{67,66},{16,17},{1... | collective-permute-start | bytes 3145736 | tf_op jit(solution)/shard_map/ppermute | solution.py:43
  61.4 20.2 %collective-permute-start.17 = (bf16[256,1536]{1,0:T(8,128)(2,1)}, bf16[256,1536]{1,0:T(8,128)(2,1)S(1)}, u32[]{:S(2)}, u32[]{:S(2)}) collective-permute-start(bf16[256,1536]{1,0:T(8,128)(2,1)} %get-tuple-element.35.pair.refs_4_), channel_id=1, source_target_pairs={{0,2},{1,3},{2,0},{3,1},{64,66},{65,67},{66,64},{67,65},{16,18},{1... | collective-permute-start | bytes 2359304 | tf_op jit(solution)/shard_map/ppermute | solution.py:43
  62.7 7.6 %collective-permute-start.19 = (bf16[256,768]{1,0:T(8,128)(2,1)S(1)}, bf16[256,768]{1,0:T(8,128)(2,1)S(1)}, u32[]{:S(2)}, u32[]{:S(2)}) collective-permute-start(bf16[256,768]{1,0:T(8,128)(2,1)S(1)} %get-tuple-element.32.hidden.refs_2_), channel_id=1, source_target_pairs={{0,1},{1,0},{2,3},{3,2},{64,65},{65,64},{66,67},{67,66},{16,17},{1... | collective-permute-start | bytes 1179656 | tf_op jit(solution)/shard_map/ppermute | solution.py:43
  63.0 20.0 %collective-permute-start.26 = (bf16[256,1024]{1,0:T(8,128)(2,1)}, bf16[256,1024]{1,0:T(8,128)(2,1)S(1)}, u32[]{:S(2)}, u32[]{:S(2)}) collective-permute-start(bf16[256,1024]{1,0:T(8,128)(2,1)} %copy-done.10), channel_id=1, source_target_pairs={{0,66},{1,67},{2,64},{3,65},{64,2},{65,3},{66,0},{67,1},{16,82},{1... | collective-permute-start | bytes 1572872 | tf_op jit(solution)/shard_map/ppermute | solution.py:43
  64.2 26.3 %collective-permute-start.27 = (bf16[256,1024]{1,0:T(8,128)(2,1)}, bf16[256,1024]{1,0:T(8,128)(2,1)S(1)}, u32[]{:S(2)}, u32[]{:S(2)}) collective-permute-start(bf16[256,1024]{1,0:T(8,128)(2,1)} %copy-done.9), channel_id=1, source_target_pairs={{0,1},{1,0},{2,3},{3,2},{64,65},{65,64},{66,67},{67,66},{16,17},{1... | collective-permute-start | bytes 1572872 | tf_op jit(solution)/shard_map/ppermute | solution.py:43
  64.3 6.0 %copy-start.8 = (bf16[256,1024]{1,0:T(8,128)(2,1)S(1)}, bf16[256,1024]{1,0:T(8,128)(2,1)}, u32[]{:S(2)}) copy-start(bf16[256,1024]{1,0:T(8,128)(2,1)} %copy-done.7) | copy-start | bytes 1572868
  70.3 20.5 %collective-permute-start.28 = (bf16[256,1024]{1,0:T(8,128)(2,1)S(1)}, bf16[256,1024]{1,0:T(8,128)(2,1)S(1)}, u32[]{:S(2)}, u32[]{:S(2)}) collective-permute-start(bf16[256,1024]{1,0:T(8,128)(2,1)S(1)} %copy-done.8), channel_id=1, source_target_pairs={{0,67},{1,66},{2,65},{3,64},{64,3},{65,2},{66,1},{67,0},{16,83},{1... | collective-permute-start | bytes 1572872 | tf_op jit(solution)/shard_map/ppermute | solution.py:43
  72.4 34.6 %collective-permute-start.29 = (bf16[256,1536]{1,0:T(8,128)(2,1)}, bf16[256,1536]{1,0:T(8,128)(2,1)S(1)}, u32[]{:S(2)}, u32[]{:S(2)}) collective-permute-start(bf16[256,1536]{1,0:T(8,128)(2,1)} %get-tuple-element.35.pair.refs_4_), channel_id=1, source_target_pairs={{0,1},{1,0},{2,3},{3,2},{64,65},{65,64},{66,67},{67,66},{16,17},{1... | collective-permute-start | bytes 2359304 | tf_op jit(solution)/shard_map/ppermute | solution.py:43
  81.6 14.9 %collective-permute-start.12 = (bf16[512,512]{1,0:T(8,128)(2,1)}, bf16[512,512]{1,0:T(8,128)(2,1)S(1)}, u32[]{:S(2)}, u32[]{:S(2)}) collective-permute-start(bf16[512,512]{1,0:T(8,128)(2,1)} %bitcast.16), channel_id=1, source_target_pairs={{0,48},{1,49},{2,50},{3,51},{64,112},{65,113},{66,114},{67,115},{1... | collective-permute-start | bytes 1572872 | tf_op jit(solution)/shard_map/ppermute | solution.py:43
  83.0 24.7 %collective-permute-start.30 = (bf16[256,1536]{1,0:T(8,128)(2,1)S(1)}, bf16[256,1536]{1,0:T(8,128)(2,1)S(1)}, u32[]{:S(2)}, u32[]{:S(2)}) collective-permute-start(bf16[256,1536]{1,0:T(8,128)(2,1)S(1)} %collective-permute-done.17.refs_5_), channel_id=1, source_target_pairs={{0,1},{1,0},{2,3},{3,2},{64,65},{65,64},{66,67},{67,66},{16,17},{1... | collective-permute-start | bytes 2359304 | tf_op jit(solution)/shard_map/ppermute | solution.py:43
  90.6 14.6 %collective-permute-start.14 = (bf16[512,512]{1,0:T(8,128)(2,1)}, bf16[512,512]{1,0:T(8,128)(2,1)S(1)}, u32[]{:S(2)}, u32[]{:S(2)}) collective-permute-start(bf16[512,512]{1,0:T(8,128)(2,1)} %bitcast.19), channel_id=1, source_target_pairs={{0,16},{1,17},{2,18},{3,19},{64,80},{65,81},{66,82},{67,83},{16,0}... | collective-permute-start | bytes 1572872 | tf_op jit(solution)/shard_map/ppermute | solution.py:43
  90.8 16.9 %copy-start.6 = (bf16[256,1024]{1,0:T(8,128)(2,1)S(1)}, bf16[256,1024]{1,0:T(8,128)(2,1)}, u32[]{:S(2)}) copy-start(bf16[256,1024]{1,0:T(8,128)(2,1)} %copy-done.5) | copy-start | bytes 1572868
  90.8 34.8 %collective-permute-start.21 = (bf16[1024,384]{1,0:T(8,128)(2,1)S(1)}, bf16[1024,384]{1,0:T(8,128)(2,1)S(1)}, u32[]{:S(2)}, u32[]{:S(2)}) collective-permute-start(bf16[1024,384]{1,0:T(8,128)(2,1)S(1)} %bitcast.129), channel_id=1, source_target_pairs={{0,4},{1,5},{2,6},{3,7},{64,68},{65,69},{66,70},{67,71},{16,20},{1... | collective-permute-start | bytes 2359304 | tf_op jit(solution)/shard_map/ppermute | solution.py:43
  96.4 17.4 %copy-start.11 = (bf16[512,512]{1,0:T(8,128)(2,1)}, bf16[512,512]{1,0:T(8,128)(2,1)S(1)}, u32[]{:S(2)}) copy-start(bf16[512,512]{1,0:T(8,128)(2,1)S(1)} %collective-permute-done.12) | copy-start | bytes 1572868
  96.4 29.2 %collective-permute-start.22 = (bf16[1024,384]{1,0:T(8,128)(2,1)S(1)}, bf16[1024,384]{1,0:T(8,128)(2,1)S(1)}, u32[]{:S(2)}, u32[]{:S(2)}) collective-permute-start(bf16[1024,384]{1,0:T(8,128)(2,1)S(1)} %bitcast.128), channel_id=1, source_target_pairs={{0,12},{1,13},{2,14},{3,15},{64,76},{65,77},{66,78},{67,79},{16,28... | collective-permute-start | bytes 2359304 | tf_op jit(solution)/shard_map/ppermute | solution.py:43
  105.2 8.7 %copy-start.13 = (bf16[512,512]{1,0:T(8,128)(2,1)}, bf16[512,512]{1,0:T(8,128)(2,1)S(1)}, u32[]{:S(2)}) copy-start(bf16[512,512]{1,0:T(8,128)(2,1)S(1)} %collective-permute-done.14) | copy-start | bytes 1572868
  105.2 17.6 %collective-permute-start.20 = (bf16[512,640]{1,0:T(8,128)(2,1)S(1)}, bf16[512,640]{1,0:T(8,128)(2,1)S(1)}, u32[]{:S(2)}, u32[]{:S(2)}) collective-permute-start(bf16[512,640]{1,0:T(8,128)(2,1)S(1)} %bitcast.133), channel_id=1, source_target_pairs={{0,48},{1,49},{2,50},{3,51},{64,112},{65,113},{66,114},{67,115},{1... | collective-permute-start | bytes 1966088 | tf_op jit(solution)/shard_map/ppermute | solution.py:43
  107.0 18.6 %collective-permute-start.24 = (bf16[512,640]{1,0:T(8,128)(2,1)S(1)}, bf16[512,640]{1,0:T(8,128)(2,1)S(1)}, u32[]{:S(2)}, u32[]{:S(2)}) collective-permute-start(bf16[512,640]{1,0:T(8,128)(2,1)S(1)} %bitcast.132), channel_id=1, source_target_pairs={{0,16},{1,17},{2,18},{3,19},{64,80},{65,81},{66,82},{67,83},{16,0}... | collective-permute-start | bytes 1966088 | tf_op jit(solution)/shard_map/ppermute | solution.py:43
  114.0 23.4 %collective-permute-start.31 = (bf16[512,768]{1,0:T(8,128)(2,1)S(1)}, bf16[512,768]{1,0:T(8,128)(2,1)S(1)}, u32[]{:S(2)}, u32[]{:S(2)}) collective-permute-start(bf16[512,768]{1,0:T(8,128)(2,1)S(1)} %bitcast.131), channel_id=1, source_target_pairs={{0,4},{1,5},{2,6},{3,7},{64,68},{65,69},{66,70},{67,71},{16,20},{1... | collective-permute-start | bytes 2359304 | tf_op jit(solution)/shard_map/ppermute | solution.py:43
  122.7 5.7 %slice-start = ((bf16[512,512]{1,0:T(8,128)(2,1)}), bf16[256,512]{1,0:T(8,128)(2,1)S(1)}, s32[]{:S(2)}) async-start(bf16[512,512]{1,0:T(8,128)(2,1)} %copy-done.11), calls=%async_computation | async-start | bytes 524288 | tf_op jit(solution)/shard_map/slice | solution.py:227
  122.7 5.7 %slice-start.1 = ((bf16[512,512]{1,0:T(8,128)(2,1)}), bf16[256,512]{1,0:T(8,128)(2,1)S(1)}, s32[]{:S(2)}) async-start(bf16[512,512]{1,0:T(8,128)(2,1)} %copy-done.13), calls=%async_computation.1 | async-start | bytes 524288 | tf_op jit(solution)/shard_map/slice | solution.py:227
  122.8 21.7 %collective-permute-start.32 = (bf16[512,768]{1,0:T(8,128)(2,1)S(1)}, bf16[512,768]{1,0:T(8,128)(2,1)S(1)}, u32[]{:S(2)}, u32[]{:S(2)}) collective-permute-start(bf16[512,768]{1,0:T(8,128)(2,1)S(1)} %bitcast.130), channel_id=1, source_target_pairs={{0,12},{1,13},{2,14},{3,15},{64,76},{65,77},{66,78},{67,79},{16,28... | collective-permute-start | bytes 2359304 | tf_op jit(solution)/shard_map/ppermute | solution.py:43
  125.8 9.5 %collective-permute-start.25 = (bf16[256,640]{1,0:T(8,128)(2,1)S(1)}, bf16[256,640]{1,0:T(8,128)(2,1)S(1)}, u32[]{:S(2)}, u32[]{:S(2)}) collective-permute-start(bf16[256,640]{1,0:T(8,128)(2,1)S(1)} %get-tuple-element.56), channel_id=1, source_target_pairs={{0,48},{1,49},{2,50},{3,51},{64,112},{65,113},{66,114},{67,115},{1... | collective-permute-start | bytes 983048 | tf_op jit(solution)/shard_map/ppermute | solution.py:43
  127.7 9.4 %collective-permute-start.23 = (bf16[256,640]{1,0:T(8,128)(2,1)S(1)}, bf16[256,640]{1,0:T(8,128)(2,1)S(1)}, u32[]{:S(2)}, u32[]{:S(2)}) collective-permute-start(bf16[256,640]{1,0:T(8,128)(2,1)S(1)} %get-tuple-element.57), channel_id=1, source_target_pairs={{0,16},{1,17},{2,18},{3,19},{64,80},{65,81},{66,82},{67,83},{16,0}... | collective-permute-start | bytes 983048 | tf_op jit(solution)/shard_map/ppermute | solution.py:43
  127.9 22.8 %collective-permute-start.40 = (bf16[512,384]{1,0:T(8,128)(2,1)S(1)}, bf16[512,384]{1,0:T(8,128)(2,1)S(1)}, u32[]{:S(2)}, u32[]{:S(2)}) collective-permute-start(bf16[512,384]{1,0:T(8,128)(2,1)S(1)} %fusion.3), channel_id=1, source_target_pairs={{0,12},{1,13},{2,14},{3,15},{64,76},{65,77},{66,78},{67,79},{16,28... | collective-permute-start | bytes 1179656 | tf_op jit(solution)/shard_map/ppermute | solution.py:43
  135.3 19.0 %collective-permute-start.15 = (bf16[256,512]{1,0:T(8,128)(2,1)S(1)}, bf16[256,512]{1,0:T(8,128)(2,1)S(1)}, u32[]{:S(2)}, u32[]{:S(2)}) collective-permute-start(bf16[256,512]{1,0:T(8,128)(2,1)S(1)} %get-tuple-element.60), channel_id=1, source_target_pairs={{0,48},{1,49},{2,50},{3,51},{64,112},{65,113},{66,114},{67,115},{1... | collective-permute-start | bytes 786440 | tf_op jit(solution)/shard_map/ppermute | solution.py:43
  137.1 17.2 %collective-permute-start.13 = (bf16[256,512]{1,0:T(8,128)(2,1)S(1)}, bf16[256,512]{1,0:T(8,128)(2,1)S(1)}, u32[]{:S(2)}, u32[]{:S(2)}) collective-permute-start(bf16[256,512]{1,0:T(8,128)(2,1)S(1)} %get-tuple-element.61), channel_id=1, source_target_pairs={{0,16},{1,17},{2,18},{3,19},{64,80},{65,81},{66,82},{67,83},{16,0}... | collective-permute-start | bytes 786440 | tf_op jit(solution)/shard_map/ppermute | solution.py:43
  144.4 8.6 %collective-permute-start.33 = (bf16[256,640]{1,0:T(8,128)(2,1)S(1)}, bf16[256,640]{1,0:T(8,128)(2,1)S(1)}, u32[]{:S(2)}, u32[]{:S(2)}) collective-permute-start(bf16[256,640]{1,0:T(8,128)(2,1)S(1)} %select_convert_fusion.1), channel_id=1, source_target_pairs={{0,64},{1,65},{2,66},{3,67},{64,0},{65,1},{66,2},{67,3},{16,80},{1... | collective-permute-start | bytes 983048 | tf_op jit(solution)/shard_map/ppermute | solution.py:43
  150.9 9.8 %collective-permute-start.41 = (bf16[512,384]{1,0:T(8,128)(2,1)S(1)}, bf16[512,384]{1,0:T(8,128)(2,1)S(1)}, u32[]{:S(2)}, u32[]{:S(2)}) collective-permute-start(bf16[512,384]{1,0:T(8,128)(2,1)S(1)} %get-tuple-element.49), channel_id=1, source_target_pairs={{0,4},{1,5},{2,6},{3,7},{64,68},{65,69},{66,70},{67,71},{16,20},{1... | collective-permute-start | bytes 1179656 | tf_op jit(solution)/shard_map/ppermute | solution.py:43
  151.3 2.1 %copy-start.15 = (bf16[256,512]{1,0:T(8,128)(2,1)S(1)}, bf16[256,512]{1,0:T(8,128)(2,1)}, u32[]{:S(2)}) copy-start(bf16[256,512]{1,0:T(8,128)(2,1)} %param.4) | copy-start | bytes 786436
  151.5 2.8 %copy-start.12 = (bf16[512,512]{1,0:T(8,128)(2,1)S(1)}, bf16[512,512]{1,0:T(8,128)(2,1)}, u32[]{:S(2)}) copy-start(bf16[512,512]{1,0:T(8,128)(2,1)} %copy-done.11) | copy-start | bytes 1572868
  151.6 2.8 %copy-start.14 = (bf16[512,512]{1,0:T(8,128)(2,1)S(1)}, bf16[512,512]{1,0:T(8,128)(2,1)}, u32[]{:S(2)}) copy-start(bf16[512,512]{1,0:T(8,128)(2,1)} %copy-done.13) | copy-start | bytes 1572868
  154.3 5.3 %collective-permute-start.34 = (f32[1,512]{1,0:T(1,128)S(1)}, f32[1,512]{1,0:T(1,128)S(1)}, u32[]{:S(2)}, u32[]{:S(2)}) collective-permute-start(f32[1,512]{1,0:T(1,128)S(1)} %bitcast.134), channel_id=1, source_target_pairs={{0,1},{1,0},{2,3},{3,2},{64,65},{65,64},{66,67},{67,66},{16,17},{1... | collective-permute-start | bytes 6152 | tf_op jit(solution)/shard_map/ppermute | solution.py:43
  154.5 16.3 %collective-permute-start.16 = (bf16[256,512]{1,0:T(8,128)(2,1)S(1)}, bf16[256,512]{1,0:T(8,128)(2,1)S(1)}, u32[]{:S(2)}, u32[]{:S(2)}) collective-permute-start(bf16[256,512]{1,0:T(8,128)(2,1)S(1)} %select_convert_fusion.2), channel_id=1, source_target_pairs={{0,64},{1,65},{2,66},{3,67},{64,0},{65,1},{66,2},{67,3},{16,80},{1... | collective-permute-start | bytes 786440 | tf_op jit(solution)/shard_map/ppermute | solution.py:43
  156.3 17.8 %collective-permute-start.39 = (bf16[256,768]{1,0:T(8,128)(2,1)S(1)}, bf16[256,768]{1,0:T(8,128)(2,1)S(1)}, u32[]{:S(2)}, u32[]{:S(2)}) collective-permute-start(bf16[256,768]{1,0:T(8,128)(2,1)S(1)} %get-tuple-element.50), channel_id=1, source_target_pairs={{0,4},{1,5},{2,6},{3,7},{64,68},{65,69},{66,70},{67,71},{16,20},{1... | collective-permute-start | bytes 1179656 | tf_op jit(solution)/shard_map/ppermute | solution.py:43
  156.8 17.2 %collective-permute-start.38 = (bf16[256,768]{1,0:T(8,128)(2,1)S(1)}, bf16[256,768]{1,0:T(8,128)(2,1)S(1)}, u32[]{:S(2)}, u32[]{:S(2)}) collective-permute-start(bf16[256,768]{1,0:T(8,128)(2,1)S(1)} %get-tuple-element.51), channel_id=1, source_target_pairs={{0,12},{1,13},{2,14},{3,15},{64,76},{65,77},{66,78},{67,79},{16,28... | collective-permute-start | bytes 1179656 | tf_op jit(solution)/shard_map/ppermute | solution.py:43
  159.6 4.4 %collective-permute-start.35 = (f32[1,512]{1,0:T(1,128)S(1)}, f32[1,512]{1,0:T(1,128)S(1)}, u32[]{:S(2)}, u32[]{:S(2)}) collective-permute-start(f32[1,512]{1,0:T(1,128)S(1)} %add.216), channel_id=1, source_target_pairs={{0,2},{1,3},{2,0},{3,1},{64,66},{65,67},{66,64},{67,65},{16,18},{1... | collective-permute-start | bytes 6152 | tf_op jit(solution)/shard_map/ppermute | solution.py:43
  164.0 4.4 %collective-permute-start.36 = (f32[1,512]{1,0:T(1,128)S(1)}, f32[1,512]{1,0:T(1,128)S(1)}, u32[]{:S(2)}, u32[]{:S(2)}) collective-permute-start(f32[1,512]{1,0:T(1,128)S(1)} %add.217), channel_id=1, source_target_pairs={{0,4},{1,5},{2,6},{3,7},{64,68},{65,69},{66,70},{67,71},{16,20},{1... | collective-permute-start | bytes 6152 | tf_op jit(solution)/shard_map/ppermute | solution.py:43
  164.7 10.5 %collective-permute-start.42 = (bf16[256,768]{1,0:T(8,128)(2,1)S(1)}, bf16[256,768]{1,0:T(8,128)(2,1)S(1)}, u32[]{:S(2)}, u32[]{:S(2)}) collective-permute-start(bf16[256,768]{1,0:T(8,128)(2,1)S(1)} %select_convert_fusion), channel_id=1, source_target_pairs={{0,2},{1,3},{2,0},{3,1},{64,66},{65,67},{66,64},{67,65},{16,18},{1... | collective-permute-start | bytes 1179656 | tf_op jit(solution)/shard_map/ppermute | solution.py:43
  168.4 5.1 %collective-permute-start.37 = (f32[1,512]{1,0:T(1,128)S(1)}, f32[1,512]{1,0:T(1,128)S(1)}, u32[]{:S(2)}, u32[]{:S(2)}) collective-permute-start(f32[1,512]{1,0:T(1,128)S(1)} %add.218), channel_id=1, source_target_pairs={{0,8},{1,9},{2,10},{3,11},{64,72},{65,73},{66,74},{67,75},{16,24},... | collective-permute-start | bytes 6152 | tf_op jit(solution)/shard_map/ppermute | solution.py:43

commit v2 on v1

--- a/solution.py
+++ b/solution.py
@@ -63,7 +63,7 @@
     return lax.dot_general(a, b, (((0,), (0,)), ((), ())), preferred_element_type=f32)
 
 
-def call(body, name, shapes, scratch, limit, flops, size, args, hbm=()):
+def call(body, name, shapes, scratch, limit, args, hbm=()):
     spaces = [pltpu.SMEM] + [pltpu.HBM if i in hbm else pltpu.VMEM for i in range(1, len(args))]
     return pl.pallas_call(
         body,
@@ -72,7 +72,7 @@
         out_shape=[jax.ShapeDtypeStruct(shape, dtype) for shape, dtype in shapes],
         scratch_shapes=scratch,
         compiler_params=pltpu.CompilerParams(vmem_limit_bytes=limit * MiB),
-        cost_estimate=pl.CostEstimate(flops=flops, bytes_accessed=size, transcendentals=0),
+        cost_estimate=pl.CostEstimate(flops=1, bytes_accessed=1, transcendentals=0),
         name=name,
     )(*args)
 
@@ -95,13 +95,13 @@
     return copies
 
 
-def forward_body(spot, own, below, above, other, up2, dn2, up3, dn3, w, gate, up, hidden, inv, gains, keep, core_out,
-                 z_out, cross_out, buf, held, sems):
+def forward_body(spot, own, below, above, far, other, other_below, other_above, other_far, w, gate, up, hidden, inv,
+                 gains, keep, core_out, z_out, cross_out, buf, held, sems):
     copies = fetch(w, held, sems, 0, 2, lambda k: k)
     put(buf, spot, [
-        (0, 0, 0, own, 0, 272), (0, 3, 0, below, 0, 272), (0, 1, 0, above, 0, 272), (1, 0, 0, other, 0, 272),
-        (0, 2, 0, up2, 0, 128), (1, 3, 0, up2, 128, 272), (0, 2, 128, dn2, 0, 144), (1, 1, 0, dn2, 144, 272),
-        (1, 2, 0, up3, 0, 128), (1, 2, 128, dn3, 0, 144),
+        (0, 0, 0, own, 0, 272), (0, 3, 0, below, 0, 272), (0, 1, 0, above, 0, 272), (0, 2, 0, far, 0, 272),
+        (1, 0, 0, other, 0, 272), (1, 3, 0, other_below, 0, 272), (1, 1, 0, other_above, 0, 272),
+        (1, 2, 0, other_far, 0, 272),
     ])
     z_lo, core = spot[8], spot[9]
     for i in range(4):
@@ -125,14 +125,15 @@
     gate[...] = g
     up[...] = u
     hidden[...] = (g * jax.nn.sigmoid(g) * u).astype(bf16)
+    core_out[:, 1024:1792] = hidden[...]
     inv[...] = jnp.broadcast_to(inv_rms, (256, 128))
 
 
 def forward(spot, pieces, w3):
     shapes = [((256, 768), f32), ((256, 768), f32), ((256, 768), bf16), ((256, 128), f32), ((16, 4096), bf16)]
-    shapes += [((256, 1024), bf16)] * 4
+    shapes += [((256, 1024), bf16), ((256, 1792), bf16), ((256, 1024), bf16), ((256, 1024), bf16)]
     scratch = [pltpu.VMEM((272, 4096), bf16), pltpu.VMEM((8, 2, 512, 768), bf16), pltpu.SemaphoreType.DMA((8,))]
-    return call(forward_body, "forward", shapes, scratch, 46, 2 * 256 * 4096 * 1536, 16 * MiB,
+    return call(forward_body, "forward", shapes, scratch, 20,
                 (spot, *pieces, w3), hbm=(len(pieces) + 1,))
 
 
@@ -159,38 +160,38 @@
     d_up = (d_hidden * g * sigma).astype(bf16)
     pair[:, 0:768] = d_gate
     pair[:, 768:1536] = d_up
+    core_out[:, 2048:2816] = d_gate
+    core_out[:, 2816:3584] = d_up
     total = jnp.sum(d_gate.astype(f32) * g + d_up.astype(f32) * u, axis=1, keepdims=True)
     products[...] = jnp.broadcast_to(total, (256, 128)).astype(bf16)
 
 
 def backward(spot, pieces, w3, gate, up, inv):
-    shapes = [((256, 1536), bf16), ((256, 128), bf16), ((256, 2048), bf16), ((256, 2048), bf16)]
+    shapes = [((256, 1536), bf16), ((256, 128), bf16), ((256, 2048), bf16), ((256, 3584), bf16)]
     scratch = [pltpu.VMEM((256, 4096), bf16), pltpu.VMEM((256, 768), f32), pltpu.VMEM((8, 1, 512, 768), bf16),
                pltpu.SemaphoreType.DMA((8,))]
-    return call(backward_body, "backward", shapes, scratch, 46, 2 * 256 * 4096 * 768, 8 * MiB,
+    return call(backward_body, "backward", shapes, scratch, 15,
                 (spot, *pieces, w3, gate, up, inv), hbm=(len(pieces) + 1,))
 
 
-def outer_body(count, rows, cols, order, *refs):
-    a_refs, b_refs, out = refs[:count], refs[count:2 * count], refs[2 * count]
+def outer_body(a_from, b_from, rows, cols, order, *refs):
+    n = len(a_from)
+    a_refs, b_refs, out = refs[:n], refs[n:2 * n], refs[2 * n]
 
     def step(i, carry):
-        at = lane(order[i] * rows, rows, rows)
-        columns = lane(i // 4 * cols, cols, cols)
-        total = dot_tn(a_refs[0][:, at], b_refs[0][:, columns])
-        for a, b in zip(a_refs[1:], b_refs[1:]):
-            total = total + dot_tn(a[:, at], b[:, columns])
+        total = None
+        for a, a0, b, b0 in zip(a_refs, a_from, b_refs, b_from):
+            value = dot_tn(a[:, lane(order[i] * rows + a0, rows, 256)], b[:, lane(i // 4 * cols + b0, cols, 128)])
+            total = value if total is None else total + value
         out[i] = total.astype(bf16)
         return carry
 
     lax.fori_loop(0, 8, step, 0)
 
 
-def outer(name, order, a_list, b_list, rows):
-    n = len(a_list)
-    cols = b_list[0].shape[1] // 2
-    return call(functools.partial(outer_body, n, rows, cols), name, [((8, rows, cols), bf16)], [], 24,
-                2 * 256 * n * rows * 8 * cols, 8 * MiB, (order, *a_list, *b_list))[0]
+def outer(name, order, a_list, b_list, rows, cols):
+    body = functools.partial(outer_body, [f for _, f in a_list], [f for _, f in b_list], rows, cols)
+    return call(body, name, [((8, rows, cols), bf16)], [], 10, (order, *[a for a, _ in a_list], *[b for b, _ in b_list]))[0]
 
 
 def branch_rows_body(order, hidden, w, out, held, sems):
@@ -202,7 +203,7 @@
 
 def branch_rows(order, hidden, w3):
     scratch = [pltpu.VMEM((8, 1, 512, 768), bf16), pltpu.SemaphoreType.DMA((8,))]
-    return call(branch_rows_body, "branch_rows", [((8, 256, 512), bf16)], scratch, 46, 2 * 256 * 768 * 4096, 8 * MiB,
+    return call(branch_rows_body, "branch_rows", [((8, 256, 512), bf16)], scratch, 8,
                 (order, hidden, w3), hbm=(2,))[0]
 
 
@@ -217,31 +218,31 @@
 
 def pair_rows(order, pair, products, w3):
     scratch = [pltpu.VMEM((8, 2, 512, 768), bf16), pltpu.SemaphoreType.DMA((8,))]
-    return call(pair_rows_body, "pair_rows", [((8, 256, 640), bf16)], scratch, 46, 2 * 256 * 1536 * 4096, 16 * MiB,
+    return call(pair_rows_body, "pair_rows", [((8, 256, 640), bf16)], scratch, 15,
                 (order, pair, products, w3), hbm=(3,))[0]
 
 
-def halve(terms, first, second, done=()):
+def halve(terms, axis, done=()):
     rows, cols = terms.shape[1:]
-    got = send(terms[0:2].reshape(2 * rows, cols), first)
-    later = after(got[rows:], *done)
-    out = (terms[2].astype(f32) + later.astype(f32)).astype(bf16)
-    last = send(out, second)
-    return terms[3].astype(f32) + got[:rows].astype(f32) + last.astype(f32), got, out
+    near, far = axis + "^1", axis + "^3"
+    got = [send(terms[4 * h:4 * h + 2].reshape(2 * rows, cols), move) for h, move in ((0, near), (1, far))]
+    two, six, *got = lax.optimization_barrier((terms[2], terms[6], *got, *done))[:4]
+    out = [(t.astype(f32) + g[rows:].astype(f32)).astype(bf16) for t, g in zip((two, six), got)]
+    last = [send(o, move) for o, move in zip(out, (far, near))]
+    sums = [terms[4 * h + 3].astype(f32) + got[h][:rows].astype(f32) + last[h].astype(f32) for h in (0, 1)]
+    return sums, got, out, last
 
 
 def gather_inputs(own):
     below, above, other = send(own, "y+"), send(own, "y-"), send(own, "z+2")
-    up2 = send(rows_cat(below[:128], other), "y+")
-    dn2 = send(rows_cat(above[128:], other), "y-")
-    up3 = send(up2[128:256], "y+")
-    dn3 = send(dn2[272:], "y-")
-    return (own, below, above, other, up2, dn2, up3, dn3)
+    far = rows_cat(send(below[:128], "y+"), send(above[128:], "y-"))
+    other = after(other, far)
+    other_below, other_above = send(other, "y+"), send(other, "y-")
+    return (own, below, above, far, other, other_below, other_above, send(far, "z+2"))
 
 
 def gather_cot(own, first, second):
-    own = after(own, *first)
-    other = send(own, "z+2")
+    other = send(after(own, *first), "z+2")
     both = after(rows_cat(own, other), *second)
     below, above = send(both, "y+"), send(both, "y-")
     low = send(rows_cat(below[:128], below[256:384]), "y+")
@@ -254,7 +255,7 @@
     t, s = lax.axis_index("tensor"), lax.axis_index("seq")
     z_hi, y = t // 4, t % 4
     x, z_lo, core = s // 4, s // 2 % 2, s % 2
-    w3 = jnp.transpose(weights, (1, 0, 2))
+    w3 = pltpu.with_memory_space_constraint(jnp.transpose(weights, (1, 0, 2)), pltpu.HBM)
     spot = jnp.stack(
         [(z_hi + dz) % 2 * 4 + (y + dy) % 4 for dz in (0, 1) for dy in range(4)] + [z_lo, core]
     ).astype(jnp.int32)
@@ -263,49 +264,47 @@
         return jnp.stack([at ^ 1, at ^ 2, at ^ 3, at, at ^ 3, at ^ 2, at ^ 1, at]).astype(jnp.int32)
 
     x_pieces = gather_inputs(rows_cat(inputs, jnp.broadcast_to(gain.reshape(1, 512), (16, 512))))
-    cot_pieces = gather_cot(d_out, x_pieces[1:3], x_pieces[4:6])
-    gate, up_val, hidden, inv, gains, x_keep, x_core, x_z, x_cross = forward(spot, x_pieces, w3)
-    x_all = [x_keep, send(x_z, "z^3"), send(x_core, "c"), send(x_cross, "z^3c")]
-    hidden_core = send(hidden, "c")
-
-    d_pair, products, cot_mine, cot_core = backward(spot, cot_pieces, w3, gate, up_val, inv)
-    cot_core = send(cot_core, "c")
+    cot_pieces = gather_cot(d_out, x_pieces[4:5], x_pieces[5:7])
+    gate, up_val, hidden, inv, gains, x_keep, core_one, x_same, x_cross = forward(spot, x_pieces, w3)
+    x_same = send(x_same, "z^3")
+    core_one = send(core_one, "c")
+    branch_terms = branch_rows(order(y), hidden, w3)
+    x_cross = send(x_cross, "z^1")
+    cot_pieces = (after(cot_pieces[0], core_one, x_same, x_cross, branch_terms), *cot_pieces[1:])
+    d_pair, products, cot_mine, core_two = backward(spot, cot_pieces, w3, gate, up_val, inv)
+    core_two = send(core_two, "c")
+    d_terms = pair_rows(order(y), d_pair, products, w3)
     pair_z = send(d_pair, "z^1")
-    pair_core = send(d_pair, "c")
-    pair_cross = send(pair_z, "c")
-
-    down_terms = outer("down_terms", order(x), [cot_mine, cot_core], [hidden, hidden_core], 512)
-    d_w_low, down_one, _ = halve(down_terms[0:4], "x^1", "x^3")
-    d_w_high, down_two, _ = halve(down_terms[4:8], "x^3", "x^1")
-    d_w_down = jnp.concatenate([d_w_low, d_w_high], axis=1)
+    down_terms = outer("down_terms", order(x), [(after(cot_mine, d_terms), 0), (core_two, 0)], [(hidden, 0), (core_one, 1024)], 512, 384)
+    down, down_got, _, down_last = halve(down_terms, "x")
+    core_three = send(jnp.concatenate([x_cross, after(pair_z, *down_got)], axis=1), "c")
+    d_w_down = jnp.concatenate(down, axis=1)
     lower = z_lo == 0
     theirs = jnp.where(lower, d_w_down[256:], d_w_down[:256]).astype(bf16)
     d_w_down = jnp.where(lower, d_w_down[:256], d_w_down[256:]) + send(theirs, "z^1").astype(f32)
 
-    branch_terms = branch_rows(order(y), after(hidden, cot_mine), w3)
-    low, _, _ = halve(branch_terms[0:4], "y^1", "y^3")
-    high, _, _ = halve(branch_terms[4:8], "y^3", "y^1")
+    pair_terms = outer(
+        "pair_terms", order(x), [(x_keep, 0), (x_same, 0), (core_one, 0), (core_three, 0)],
+        [(d_pair, 0), (pair_z, 0), (core_two, 2048), (core_three, 1024)], 256, 768,
+    )
+    (d_w_gate, d_w_up), _, pair_out, _ = halve(after(pair_terms, *down_last), "x")
+
+    (d_low, d_high), _, _, d_last = halve(d_terms, "y", down_got)
+    (low, high), _, _, _ = halve(after(branch_terms, *d_last), "y")
     upper = z_hi == 1
-    theirs = jnp.where(upper, low, high).astype(bf16)
-    branch = (jnp.where(upper, high, low) + send(theirs, "z+2").astype(f32)).astype(bf16)
-
-    pair_terms = outer("pair_terms", order(x), x_all, [d_pair, pair_z, pair_core, pair_cross], 256)
-    d_w_gate, pair_one, pair_out_one = halve(pair_terms[0:4], "x^1", "x^3")
-    d_w_up, pair_two, pair_out_two = halve(pair_terms[4:8], "x^3", "x^1")
-
-    d_terms = pair_rows(order(y), after(d_pair, pair_z, down_terms), products, w3)
-    d_low, _, _ = halve(d_terms[0:4], "y^1", "y^3", (down_one, down_two))
-    d_high, _, _ = halve(d_terms[4:8], "y^3", "y^1", (down_one, down_two))
     mine = jnp.where(upper, d_high, d_low)
-    theirs = after(jnp.where(upper, d_low, d_high).astype(bf16), pair_one, pair_two)
-    mine = mine + send(theirs, "z+2").astype(f32)
+    theirs = send(jnp.where(upper, d_low, d_high).astype(bf16), "z+2")
+    mine = mine + theirs.astype(f32)
+    theirs = send(after(jnp.where(upper, low, high).astype(bf16), theirs), "z+2")
+    branch = (jnp.where(upper, high, low) + theirs.astype(f32)).astype(bf16)
     d_normed, products = mine[:, :512], mine[:, 512:513] / width
 
     x_own = inputs.astype(f32)
     d_input = (d_normed * gain.astype(f32) - inv[:, :1] * products * x_own).astype(bf16)
     d_gain = jnp.sum(d_normed * x_own, axis=0, keepdims=True)
-    d_gain = after(d_gain, pair_out_one, pair_out_two)
     for move in ("c", "z^1", "x^1", "x+2"):
+        if move == "x^1":
+            d_gain = after(d_gain, *pair_out)
         d_gain = d_gain + send(d_gain, move)
 
     gain_rows = lax.dynamic_slice(gains, (0, s * 256), (1, 256)).astype(f32).reshape(256, 1)

time: 177 us -> 191 us (1.079)
  starting transfers between devices: 51.8 us -> 57 us
  local copies, waits for them, and re-layouts: 5.09 us -> 9.73 us
  other arithmetic: 7.75 us -> 11.3 us
  waiting for transfers between devices: 75.8 us -> 72.4 us
  Pallas kernels: 35 us -> 38.2 us
    unnamed x36 -> x53, local copies, waits for them, and re-layouts: 2.42 us -> 8.05 us
    ppermute x43 -> x42, starting transfers between devices: 51.8 us -> 57 us  [send(): return lax.ppermute(value, AXES, pairs(moves[move]))]
    ppermute x43 -> x42, waiting for transfers between devices: 75.8 us -> 72.4 us  [send(): return lax.ppermute(value, AXES, pairs(moves[move]))]
    pallas_call x6, Pallas kernels: 35 us -> 38.2 us  [call(): pl.pallas_call(body, in_specs=[pl.BlockSpec(memory_space=space) for space...]
    concatenate x6 -> x4, other arithmetic: 1.1 us -> 3.58 us  [rows_cat(): return jnp.concatenate(parts, axis=0)]
  transfers between devices with their start and end apart: 43 -> 42, of which waited for: 19 -> 19; matrix products, arithmetic and copies ran while one was open for 4% -> 5% of each run, Pallas kernels for 16% -> 17%
where the time goes in v2:
time: 191 us; the launch traced here: 190 us
  waiting for transfers between devices  72.4 us (38%)
  starting transfers between devices  57 us (30%)
  Pallas kernels  38.2 us (20%)
  other arithmetic  11.3 us (6%)
  local copies, waits for them, and re-layouts  9.73 us (5%)
    ppermute x42, waiting for transfers between devices, send(): return lax.ppermute(value, AXES, pairs(moves[move]))  72.4 us
    ppermute x42, starting transfers between devices, send(): return lax.ppermute(value, AXES, pairs(moves[move]))  57 us
    pallas_call x6, Pallas kernels, call(): pl.pallas_call(body, in_specs=[pl.BlockSpec(memory_space=space) for space...  38.2 us
    unnamed x53, local copies, waits for them, and re-layouts  8.05 us
  transfers between devices with their start and end apart: 42, of which 19 were waited for; matrix products, arithmetic and copies ran while one was open for 5% of the time, Pallas kernels for 17%

profile of v2, /device:TPU:0, one launch (start us, length us, event | category | flops | bytes accessed | tf_op | source)
XLA Modules:
  0.0 189.7 jit_solution(2473263985658953644)
XLA Ops:
  1.3 1.0 pad_maximum_fusion.4.own
  2.3 1.7 collective-permute-start
  4.0 1.6 collective-permute-start.1
  5.6 6.5 %collective-permute-done.below = bf16[272,512]{1,0:T(8,128)(2,1)S(1)} collective-permute-done((bf16[272,512]{1,0:T(8,128)(2,1)S(1)}, bf16[272,512]{1,0:T(8,128)(2,1)S(1)}, u32[]{:S(2)}, u32[]{:S(2)}) %collective-permute-start) | collective-permute-done | bytes 278560 | tf_op jit(solution)/shard_map/ppermute | solution.py:43
  12.5 3.9 %collective-permute-start.4 = (bf16[272,512]{1,0:T(8,128)(2,1)S(1)}, bf16[272,512]{1,0:T(8,128)(2,1)S(1)}, u32[]{:S(2)}, u32[]{:S(2)}) collective-permute-start(bf16[272,512]{1,0:T(8,128)(2,1)S(1)} %pad_maximum_fusion.4.own), channel_id=1, source_target_pairs={{0,64},{1,65},{2,66},{3,67},{64,0},{65,1},{66,2},{67,3},{16,80},{1... | collective-permute-start | bytes 835592 | tf_op jit(solution)/shard_map/ppermute | solution.py:43
  16.4 3.0 %collective-permute-start.3 = (bf16[144,512]{1,0:T(8,128)(2,1)S(1)}, bf16[144,512]{1,0:T(8,128)(2,1)S(1)}, u32[]{:S(2)}, u32[]{:S(2)}) collective-permute-start(bf16[144,512]{1,0:T(8,128)(2,1)S(1)} %slice.207), channel_id=1, source_target_pairs={{0,48},{1,49},{2,50},{3,51},{64,112},{65,113},{66,114},{67,115},{1... | collective-permute-start | bytes 442376 | tf_op jit(solution)/shard_map/ppermute | solution.py:43
  19.4 2.7 %collective-permute-done.3 = bf16[144,512]{1,0:T(8,128)(2,1)S(1)} collective-permute-done((bf16[144,512]{1,0:T(8,128)(2,1)S(1)}, bf16[144,512]{1,0:T(8,128)(2,1)S(1)}, u32[]{:S(2)}, u32[]{:S(2)}) %collective-permute-start.3) | collective-permute-done | bytes 147488 | tf_op jit(solution)/shard_map/ppermute | solution.py:43
  22.1 3.2 %collective-permute-start.8 = (bf16[256,512]{1,0:T(8,128)(2,1)}, bf16[256,512]{1,0:T(8,128)(2,1)S(1)}, u32[]{:S(2)}, u32[]{:S(2)}) collective-permute-start(bf16[256,512]{1,0:T(8,128)(2,1)} %param.7), channel_id=1, source_target_pairs={{0,64},{1,65},{2,66},{3,67},{64,0},{65,1},{66,2},{67,3},{16,80},{1... | collective-permute-start | bytes 786440 | tf_op jit(solution)/shard_map/ppermute | solution.py:43
  25.3 2.9 %collective-permute-start.6 = (bf16[272,512]{1,0:T(8,128)(2,1)S(1)}, bf16[272,512]{1,0:T(8,128)(2,1)S(1)}, u32[]{:S(2)}, u32[]{:S(2)}) collective-permute-start(bf16[272,512]{1,0:T(8,128)(2,1)S(1)} %collective-permute-done.4.other), channel_id=1, source_target_pairs={{0,48},{1,49},{2,50},{3,51},{64,112},{65,113},{66,114},{67,115},{1... | collective-permute-start | bytes 835592 | tf_op jit(solution)/shard_map/ppermute | solution.py:43
  28.1 2.1 %collective-permute-done.8 = bf16[256,512]{1,0:T(8,128)(2,1)S(1)} collective-permute-done((bf16[256,512]{1,0:T(8,128)(2,1)}, bf16[256,512]{1,0:T(8,128)(2,1)S(1)}, u32[]{:S(2)}, u32[]{:S(2)}) %collective-permute-start.8) | collective-permute-done | bytes 262176 | tf_op jit(solution)/shard_map/ppermute | solution.py:43
  30.3 1.0 pad_maximum_fusion.3.both
  31.2 0.9 collective-permute-done.6.other_above
  32.2 3.7 %collective-permute-done.5.other_below = bf16[272,512]{1,0:T(8,128)(2,1)S(1)} collective-permute-done((bf16[272,512]{1,0:T(8,128)(2,1)S(1)}, bf16[272,512]{1,0:T(8,128)(2,1)S(1)}, u32[]{:S(2)}, u32[]{:S(2)}) %collective-permute-start.5) | collective-permute-done | bytes 278560 | tf_op jit(solution)/shard_map/ppermute | solution.py:43
  35.9 1.4 collective-permute-start.7
  37.3 1.9 collective-permute-start.12
  39.3 4.8 %collective-permute-done.7.other_far = bf16[272,512]{1,0:T(8,128)(2,1)} collective-permute-done((bf16[272,512]{1,0:T(8,128)(2,1)S(1)}, bf16[272,512]{1,0:T(8,128)(2,1)}, u32[]{:S(2)}, u32[]{:S(2)}) %collective-permute-start.7) | collective-permute-done | bytes 278560 | tf_op jit(solution)/shard_map/ppermute | solution.py:43
  44.0 7.2 %forward.1 = (f32[256,768]{1,0:T(8,128)S(1)}, f32[256,768]{1,0:T(8,128)S(1)}, bf16[256,768]{1,0:T(8,128)(2,1)S(1)}, f32[256,128]{1,0:T(8,128)S(1)}, bf16[16,4096...) custom-call(s32[10]{0:T(128)S(1)} %stack.116.spot, ...), custom_call_target="tpu_custom_call" | custom-call | flops 1 | bytes 1 | tf_op jit(solution)/shard_map/forward/pallas_call | solution.py:68
  51.3 0.9 copy-done.12
  52.2 0.9 copy-done.14
  53.8 1.6 collective-permute-start.10
  56.7 0.8 pad_maximum_fusion.5
  57.5 1.6 collective-permute-start.14
  59.2 1.0 copy-done.4
  60.2 5.2 %branch_rows.1 = bf16[8,256,512]{2,1,0:T(8,128)(2,1)S(1)} custom-call(s32[8]{0:T(128)S(1)} %stack.105.order, bf16[256,768]{1,0:T(8,128)(2,1)S(1)} %copy-done.4, bf16[3,4096,768]{2,1,0:T(8,128)(2,1)} %bitcast.91), custom_call_target="tpu_custom_call" | custom-call | flops 1 | bytes 1 | tf_op jit(solution)/shard_map/branch_rows/pallas_call | solution.py:68
  65.5 2.0 %collective-permute-done.14.low = bf16[256,512]{1,0:T(8,128)(2,1)} collective-permute-done((bf16[256,512]{1,0:T(8,128)(2,1)}, bf16[256,512]{1,0:T(8,128)(2,1)}, u32[]{:S(2)}, u32[]{:S(2)}) %collective-permute-start.14) | collective-permute-done | bytes 262176 | tf_op jit(solution)/shard_map/ppermute | solution.py:43
  67.5 6.7 %backward.1 = (bf16[256,1536]{1,0:T(8,128)(2,1)S(1)}, bf16[256,128]{1,0:T(8,128)(2,1)S(1)}, bf16[256,2048]{1,0:T(8,128)(2,1)S(1)}, bf16[256,3584]{1,0:T(8,128)(2,1)}) custom-call(s32[10]{0:T(128)S(1)} %stack.116.spot, bf16[512,512]{1,0:T(8,128)(2,1)S(1)} %pad_maximum_fusion.3.both, bf16[512,512]{1,0:T(8,128)(2,1)S(1)} %copy-done.9, ...), custom_call_target="tpu_custom_call" | custom-call | flops 1 | bytes 1 | tf_op jit(solution)/shard_map/backward/pallas_call | solution.py:68
  74.3 0.9 copy-done
  75.2 1.0 copy-done.10
  76.9 2.0 %collective-permute-start.31 = (bf16[256,1536]{1,0:T(8,128)(2,1)}, bf16[256,1536]{1,0:T(8,128)(2,1)S(1)}, u32[]{:S(2)}, u32[]{:S(2)}) collective-permute-start(bf16[256,1536]{1,0:T(8,128)(2,1)} %copy-done), channel_id=1, source_target_pairs={{0,2},{1,3},{2,0},{3,1},{64,66},{65,67},{66,64},{67,65},{16,18},{1... | collective-permute-start | bytes 2359304 | tf_op jit(solution)/shard_map/ppermute | solution.py:43
  78.9 1.2 copy-done.1
  80.1 0.8 copy-done.22
  80.9 6.9 %pair_rows.1 = bf16[8,256,640]{2,1,0:T(8,128)(2,1)S(1)} custom-call(s32[8]{0:T(128)S(1)} %stack.105.order, bf16[256,1536]{1,0:T(8,128)(2,1)S(1)} %copy-done.1, bf16[256,128]{1,0:T(8,128)(2,1)S(1)} %copy-done.22, bf16[3,4096,768]{2,1,0:T(8,128)(2,1)} %bitcast.93), custom_call_target="tpu_custom_call" | custom-call | flops 1 | bytes 1 | tf_op jit(solution)/shard_map/pair_rows/pallas_call | solution.py:68
  87.9 5.3 %down_terms.1 = bf16[8,512,384]{2,1,0:T(8,128)(2,1)S(1)} custom-call(s32[8]{0:T(128)S(1)} %stack.121.order, bf16[256,2048]{1,0:T(8,128)(2,1)S(1)} %copy-done.11, bf16[256,3584]{1,0:T(8,128)(2,1)} %collective-permute-done.18.refs_1_.refs_6_, bf16[256,768]{1,0:T(8,128)(2,1)S(1)} %copy-done.5, bf16[256,1792]{1,0:T(8,128)(2,1)S(1)} %collective-permute-done.9.refs_3_.refs_2_), custom_call_target="tpu_custom_call" | custom-call | flops 1 | bytes 1 | tf_op jit(solution)/shard_map/down_terms/pallas_call | solution.py:68
  93.4 1.6 collective-permute-start.19
  95.0 2.1 %collective-permute-start.20 = (bf16[1024,384]{1,0:T(8,128)(2,1)S(1)}, bf16[1024,384]{1,0:T(8,128)(2,1)S(1)}, u32[]{:S(2)}, u32[]{:S(2)}) collective-permute-start(bf16[1024,384]{1,0:T(8,128)(2,1)S(1)} %bitcast.96), channel_id=1, source_target_pairs={{0,12},{1,13},{2,14},{3,15},{64,76},{65,77},{66,78},{67,79},{16,28... | collective-permute-start | bytes 2359304 | tf_op jit(solution)/shard_map/ppermute | solution.py:43
  98.5 2.3 %collective-permute-start.17 = (bf16[512,640]{1,0:T(8,128)(2,1)S(1)}, bf16[512,640]{1,0:T(8,128)(2,1)S(1)}, u32[]{:S(2)}, u32[]{:S(2)}) collective-permute-start(bf16[512,640]{1,0:T(8,128)(2,1)S(1)} %bitcast.98), channel_id=1, source_target_pairs={{0,48},{1,49},{2,50},{3,51},{64,112},{65,113},{66,114},{67,115},{1... | collective-permute-start | bytes 1966088 | tf_op jit(solution)/shard_map/ppermute | solution.py:43
  101.0 12.2 %collective-permute-done.19 = bf16[1024,384]{1,0:T(8,128)(2,1)S(1)} collective-permute-done((bf16[1024,384]{1,0:T(8,128)(2,1)S(1)}, bf16[1024,384]{1,0:T(8,128)(2,1)S(1)}, u32[]{:S(2)}, u32[]{:S(2)}) %collective-permute-start.19) | collective-permute-done | bytes 786464 | tf_op jit(solution)/shard_map/ppermute | solution.py:43
  113.2 2.4 %collective-permute-done.20 = bf16[1024,384]{1,0:T(8,128)(2,1)S(1)} collective-permute-done((bf16[1024,384]{1,0:T(8,128)(2,1)S(1)}, bf16[1024,384]{1,0:T(8,128)(2,1)S(1)}, u32[]{:S(2)}, u32[]{:S(2)}) %collective-permute-start.20) | collective-permute-done | bytes 786464 | tf_op jit(solution)/shard_map/ppermute | solution.py:43
  116.5 2.4 %collective-permute-start.21 = (bf16[256,640]{1,0:T(8,128)(2,1)S(1)}, bf16[256,640]{1,0:T(8,128)(2,1)S(1)}, u32[]{:S(2)}, u32[]{:S(2)}) collective-permute-start(bf16[256,640]{1,0:T(8,128)(2,1)S(1)} %add_convert_fusion.6), channel_id=1, source_target_pairs={{0,48},{1,49},{2,50},{3,51},{64,112},{65,113},{66,114},{67,115},{1... | collective-permute-start | bytes 983048 | tf_op jit(solution)/shard_map/ppermute | solution.py:43
  119.2 2.1 %collective-permute-start.33 = (bf16[512,384]{1,0:T(8,128)(2,1)S(1)}, bf16[512,384]{1,0:T(8,128)(2,1)S(1)}, u32[]{:S(2)}, u32[]{:S(2)}) collective-permute-start(bf16[512,384]{1,0:T(8,128)(2,1)S(1)} %add_convert_fusion.4), channel_id=1, source_target_pairs={{0,12},{1,13},{2,14},{3,15},{64,76},{65,77},{66,78},{67,79},{16,28... | collective-permute-start | bytes 1179656 | tf_op jit(solution)/shard_map/ppermute | solution.py:43
  121.3 1.1 pad_maximum_fusion
  122.7 1.8 collective-permute-done.22
  124.6 1.6 collective-permute-done.21
  126.5 1.8 collective-permute-start.27
  128.5 7.1 %collective-permute-done.27 = bf16[256,640]{1,0:T(8,128)(2,1)S(1)} collective-permute-done((bf16[256,640]{1,0:T(8,128)(2,1)S(1)}, bf16[256,640]{1,0:T(8,128)(2,1)S(1)}, u32[]{:S(2)}, u32[]{:S(2)}) %collective-permute-start.27) | collective-permute-done | bytes 327712 | tf_op jit(solution)/shard_map/ppermute | solution.py:43
  135.5 2.3 %collective-permute-start.24 = (bf16[512,512]{1,0:T(8,128)(2,1)S(1)}, bf16[512,512]{1,0:T(8,128)(2,1)S(1)}, u32[]{:S(2)}, u32[]{:S(2)}) collective-permute-start(bf16[512,512]{1,0:T(8,128)(2,1)S(1)} %bitcast.100), channel_id=1, source_target_pairs={{0,48},{1,49},{2,50},{3,51},{64,112},{65,113},{66,114},{67,115},{1... | collective-permute-start | bytes 1572872 | tf_op jit(solution)/shard_map/ppermute | solution.py:43
  138.2 0.9 fusion.13
  139.8 7.7 %collective-permute-done.24 = bf16[512,512]{1,0:T(8,128)(2,1)S(1)} collective-permute-done((bf16[512,512]{1,0:T(8,128)(2,1)S(1)}, bf16[512,512]{1,0:T(8,128)(2,1)S(1)}, u32[]{:S(2)}, u32[]{:S(2)}) %collective-permute-start.24) | collective-permute-done | bytes 524320 | tf_op jit(solution)/shard_map/ppermute | solution.py:43
  147.6 2.3 %collective-permute-start.26 = (bf16[256,512]{1,0:T(8,128)(2,1)S(1)}, bf16[256,512]{1,0:T(8,128)(2,1)S(1)}, u32[]{:S(2)}, u32[]{:S(2)}) collective-permute-start(bf16[256,512]{1,0:T(8,128)(2,1)S(1)} %add_convert_fusion.8), channel_id=1, source_target_pairs={{0,48},{1,49},{2,50},{3,51},{64,112},{65,113},{66,114},{67,115},{1... | collective-permute-start | bytes 786440 | tf_op jit(solution)/shard_map/ppermute | solution.py:43
  150.1 6.7 %pair_terms.1 = bf16[8,256,768]{2,1,0:T(8,128)(2,1)S(1)} custom-call(s32[8]{0:T(128)S(1)} %stack.121.order, bf16[256,1024]{1,0:T(8,128)(2,1)S(1)} %copy-done.20, bf16[256,1024]{1,0:T(8,128)(2,1)} %collective-permute-done.10.refs_1_, bf16[256,1792]{1,0:T(8,128)(2,1)S(1)} %collective-permute-done.9.refs_3_.refs_2_, ...), custom_call_target="tpu_custom_call" | custom-call | flops 1 | bytes 1 | tf_op jit(solution)/shard_map/pair_terms/pallas_call | solution.py:68
  157.2 2.2 %collective-permute-start.36 = (bf16[512,768]{1,0:T(8,128)(2,1)S(1)}, bf16[512,768]{1,0:T(8,128)(2,1)S(1)}, u32[]{:S(2)}, u32[]{:S(2)}) collective-permute-start(bf16[512,768]{1,0:T(8,128)(2,1)S(1)} %bitcast.94), channel_id=1, source_target_pairs={{0,12},{1,13},{2,14},{3,15},{64,76},{65,77},{66,78},{67,79},{16,28... | collective-permute-start | bytes 2359304 | tf_op jit(solution)/shard_map/ppermute | solution.py:43
  159.6 1.2 collective-permute-start.30
  160.9 2.5 %collective-permute-done.30 = f32[1,512]{1,0:T(1,128)S(1)} collective-permute-done((f32[1,512]{1,0:T(1,128)S(1)}, f32[1,512]{1,0:T(1,128)S(1)}, u32[]{:S(2)}, u32[]{:S(2)}) %collective-permute-start.30) | collective-permute-done | bytes 2080 | tf_op jit(solution)/shard_map/ppermute | solution.py:43
  163.4 1.1 collective-permute-start.41
  164.7 2.2 %collective-permute-start.28 = (bf16[256,512]{1,0:T(8,128)(2,1)S(1)}, bf16[256,512]{1,0:T(8,128)(2,1)S(1)}, u32[]{:S(2)}, u32[]{:S(2)}) collective-permute-start(bf16[256,512]{1,0:T(8,128)(2,1)S(1)} %select_convert_fusion.2), channel_id=1, source_target_pairs={{0,64},{1,65},{2,66},{3,67},{64,0},{65,1},{66,2},{67,3},{16,80},{1... | collective-permute-start | bytes 786440 | tf_op jit(solution)/shard_map/ppermute | solution.py:43
  167.0 6.3 %collective-permute-done.35 = bf16[512,768]{1,0:T(8,128)(2,1)S(1)} collective-permute-done((bf16[512,768]{1,0:T(8,128)(2,1)S(1)}, bf16[512,768]{1,0:T(8,128)(2,1)S(1)}, u32[]{:S(2)}, u32[]{:S(2)}) %collective-permute-start.35) | collective-permute-done | bytes 786464 | tf_op jit(solution)/shard_map/ppermute | solution.py:43
  173.3 1.2 collective-permute-done.36
  175.1 2.3 %collective-permute-start.39 = (bf16[256,768]{1,0:T(8,128)(2,1)S(1)}, bf16[256,768]{1,0:T(8,128)(2,1)S(1)}, u32[]{:S(2)}, u32[]{:S(2)}) collective-permute-start(bf16[256,768]{1,0:T(8,128)(2,1)S(1)} %add_convert_fusion.2), channel_id=1, source_target_pairs={{0,12},{1,13},{2,14},{3,15},{64,76},{65,77},{66,78},{67,79},{16,28... | collective-permute-start | bytes 1179656 | tf_op jit(solution)/shard_map/ppermute | solution.py:43
  177.4 1.0 collective-permute-start.37
  178.6 3.9 %collective-permute-done.37 = f32[1,512]{1,0:T(1,128)S(1)} collective-permute-done((f32[1,512]{1,0:T(1,128)S(1)}, f32[1,512]{1,0:T(1,128)S(1)}, u32[]{:S(2)}, u32[]{:S(2)}) %collective-permute-start.37) | collective-permute-done | bytes 2080 | tf_op jit(solution)/shard_map/ppermute | solution.py:43
  182.5 2.0 %collective-permute-start.38 = (f32[1,512]{1,0:T(1,128)S(1)}, f32[1,512]{1,0:T(1,128)S(1)}, u32[]{:S(2)}, u32[]{:S(2)}) collective-permute-start(f32[1,512]{1,0:T(1,128)S(1)} %add.220), channel_id=1, source_target_pairs={{0,8},{1,9},{2,10},{3,11},{64,72},{65,73},{66,74},{67,75},{16,24},... | collective-permute-start | bytes 6152 | tf_op jit(solution)/shard_map/ppermute | solution.py:43
  184.5 0.9 add_convert_fusion.7
  185.4 2.2 %collective-permute-done.38 = f32[1,512]{1,0:T(1,128)S(1)} collective-permute-done((f32[1,512]{1,0:T(1,128)S(1)}, f32[1,512]{1,0:T(1,128)S(1)}, u32[]{:S(2)}, u32[]{:S(2)}) %collective-permute-start.38) | collective-permute-done | bytes 2080 | tf_op jit(solution)/shard_map/ppermute | solution.py:43
  188.5 1.1 pad_maximum_fusion.1
  (126 shorter events, 11.6 us)
Async XLA Ops:
  2.3 9.8 %collective-permute-start = (bf16[272,512]{1,0:T(8,128)(2,1)S(1)}, bf16[272,512]{1,0:T(8,128)(2,1)S(1)}, u32[]{:S(2)}, u32[]{:S(2)}) collective-permute-start(bf16[272,512]{1,0:T(8,128)(2,1)S(1)} %pad_maximum_fusion.4.own), channel_id=1, source_target_pairs={{0,16},{1,17},{2,18},{3,19},{64,80},{65,81},{66,82},{67,83},{16,32... | collective-permute-start | bytes 835592 | tf_op jit(solution)/shard_map/ppermute | solution.py:43
  4.0 12.4 %collective-permute-start.1 = (bf16[272,512]{1,0:T(8,128)(2,1)S(1)}, bf16[272,512]{1,0:T(8,128)(2,1)S(1)}, u32[]{:S(2)}, u32[]{:S(2)}) collective-permute-start(bf16[272,512]{1,0:T(8,128)(2,1)S(1)} %pad_maximum_fusion.4.own), channel_id=1, source_target_pairs={{0,48},{1,49},{2,50},{3,51},{64,112},{65,113},{66,114},{67,115},{1... | collective-permute-start | bytes 835592 | tf_op jit(solution)/shard_map/ppermute | solution.py:43
  12.1 7.3 %collective-permute-start.2 = (bf16[128,512]{1,0:T(8,128)(2,1)S(1)}, bf16[128,512]{1,0:T(8,128)(2,1)S(1)}, u32[]{:S(2)}, u32[]{:S(2)}) collective-permute-start(bf16[128,512]{1,0:T(8,128)(2,1)S(1)} %slice.206), channel_id=1, source_target_pairs={{0,16},{1,17},{2,18},{3,19},{64,80},{65,81},{66,82},{67,83},{16,32... | collective-permute-start | bytes 393224 | tf_op jit(solution)/shard_map/ppermute | solution.py:43
  12.5 9.6 %collective-permute-start.4 = (bf16[272,512]{1,0:T(8,128)(2,1)S(1)}, bf16[272,512]{1,0:T(8,128)(2,1)S(1)}, u32[]{:S(2)}, u32[]{:S(2)}) collective-permute-start(bf16[272,512]{1,0:T(8,128)(2,1)S(1)} %pad_maximum_fusion.4.own), channel_id=1, source_target_pairs={{0,64},{1,65},{2,66},{3,67},{64,0},{65,1},{66,2},{67,3},{16,80},{1... | collective-permute-start | bytes 835592 | tf_op jit(solution)/shard_map/ppermute | solution.py:43
  16.4 5.7 %collective-permute-start.3 = (bf16[144,512]{1,0:T(8,128)(2,1)S(1)}, bf16[144,512]{1,0:T(8,128)(2,1)S(1)}, u32[]{:S(2)}, u32[]{:S(2)}) collective-permute-start(bf16[144,512]{1,0:T(8,128)(2,1)S(1)} %slice.207), channel_id=1, source_target_pairs={{0,48},{1,49},{2,50},{3,51},{64,112},{65,113},{66,114},{67,115},{1... | collective-permute-start | bytes 442376 | tf_op jit(solution)/shard_map/ppermute | solution.py:43
  22.1 8.2 %collective-permute-start.8 = (bf16[256,512]{1,0:T(8,128)(2,1)}, bf16[256,512]{1,0:T(8,128)(2,1)S(1)}, u32[]{:S(2)}, u32[]{:S(2)}) collective-permute-start(bf16[256,512]{1,0:T(8,128)(2,1)} %param.7), channel_id=1, source_target_pairs={{0,64},{1,65},{2,66},{3,67},{64,0},{65,1},{66,2},{67,3},{16,80},{1... | collective-permute-start | bytes 786440 | tf_op jit(solution)/shard_map/ppermute | solution.py:43
  25.3 6.9 %collective-permute-start.6 = (bf16[272,512]{1,0:T(8,128)(2,1)S(1)}, bf16[272,512]{1,0:T(8,128)(2,1)S(1)}, u32[]{:S(2)}, u32[]{:S(2)}) collective-permute-start(bf16[272,512]{1,0:T(8,128)(2,1)S(1)} %collective-permute-done.4.other), channel_id=1, source_target_pairs={{0,48},{1,49},{2,50},{3,51},{64,112},{65,113},{66,114},{67,115},{1... | collective-permute-start | bytes 835592 | tf_op jit(solution)/shard_map/ppermute | solution.py:43
  28.1 7.8 %collective-permute-start.5 = (bf16[272,512]{1,0:T(8,128)(2,1)S(1)}, bf16[272,512]{1,0:T(8,128)(2,1)S(1)}, u32[]{:S(2)}, u32[]{:S(2)}) collective-permute-start(bf16[272,512]{1,0:T(8,128)(2,1)S(1)} %collective-permute-done.4.other), channel_id=1, source_target_pairs={{0,16},{1,17},{2,18},{3,19},{64,80},{65,81},{66,82},{67,83},{16,32... | collective-permute-start | bytes 835592 | tf_op jit(solution)/shard_map/ppermute | solution.py:43
  35.9 19.5 %collective-permute-start.13 = (bf16[512,512]{1,0:T(8,128)(2,1)S(1)}, bf16[512,512]{1,0:T(8,128)(2,1)S(1)}, u32[]{:S(2)}, u32[]{:S(2)}) collective-permute-start(bf16[512,512]{1,0:T(8,128)(2,1)S(1)} %pad_maximum_fusion.3.both), channel_id=1, source_target_pairs={{0,48},{1,49},{2,50},{3,51},{64,112},{65,113},{66,114},{67,115},{1... | collective-permute-start | bytes 1572872 | tf_op jit(solution)/shard_map/ppermute | solution.py:43
  35.9 8.2 %collective-permute-start.7 = (bf16[272,512]{1,0:T(8,128)(2,1)S(1)}, bf16[272,512]{1,0:T(8,128)(2,1)}, u32[]{:S(2)}, u32[]{:S(2)}) collective-permute-start(bf16[272,512]{1,0:T(8,128)(2,1)S(1)} %constant_dynamic-update-slice_fusion.far), channel_id=1, source_target_pairs={{0,64},{1,65},{2,66},{3,67},{64,0},{65,1},{66,2},{67,3},{16,80},{1... | collective-permute-start | bytes 835592 | tf_op jit(solution)/shard_map/ppermute | solution.py:43
  37.3 19.4 %collective-permute-start.12 = (bf16[512,512]{1,0:T(8,128)(2,1)S(1)}, bf16[512,512]{1,0:T(8,128)(2,1)S(1)}, u32[]{:S(2)}, u32[]{:S(2)}) collective-permute-start(bf16[512,512]{1,0:T(8,128)(2,1)S(1)} %pad_maximum_fusion.3.both), channel_id=1, source_target_pairs={{0,16},{1,17},{2,18},{3,19},{64,80},{65,81},{66,82},{67,83},{16,32... | collective-permute-start | bytes 1572872 | tf_op jit(solution)/shard_map/ppermute | solution.py:43
  51.3 0.9 copy-start.12
  53.8 2.9 %copy-start.3 = (bf16[256,768]{1,0:T(8,128)(2,1)}, bf16[256,768]{1,0:T(8,128)(2,1)S(1)}, u32[]{:S(2)}) copy-start(bf16[256,768]{1,0:T(8,128)(2,1)S(1)} %get-tuple-element.44.hidden.refs_2_) | copy-start | bytes 1179652
  53.8 2.9 %copy-start.16 = (f32[256,128]{1,0:T(8,128)}, f32[256,128]{1,0:T(8,128)S(1)}, u32[]{:S(2)}) copy-start(f32[256,128]{1,0:T(8,128)S(1)} %get-tuple-element.53.inv) | copy-start | bytes 393220
  53.8 2.9 %copy-start.19 = (bf16[256,1024]{1,0:T(8,128)(2,1)}, bf16[256,1024]{1,0:T(8,128)(2,1)S(1)}, u32[]{:S(2)}) copy-start(bf16[256,1024]{1,0:T(8,128)(2,1)S(1)} %get-tuple-element.71.refs_0_) | copy-start | bytes 1572868
  53.8 11.7 %collective-permute-start.10 = (bf16[256,1024]{1,0:T(8,128)(2,1)}, bf16[256,1024]{1,0:T(8,128)(2,1)}, u32[]{:S(2)}, u32[]{:S(2)}) collective-permute-start(bf16[256,1024]{1,0:T(8,128)(2,1)} %get-tuple-element.48), channel_id=1, source_target_pairs={{0,66},{1,67},{2,64},{3,65},{64,2},{65,3},{66,0},{67,1},{16,82},{1... | collective-permute-start | bytes 1572872 | tf_op jit(solution)/shard_map/ppermute | solution.py:43
  55.3 10.1 %collective-permute-start.11 = (bf16[256,1024]{1,0:T(8,128)(2,1)}, bf16[256,1024]{1,0:T(8,128)(2,1)}, u32[]{:S(2)}, u32[]{:S(2)}) collective-permute-start(bf16[256,1024]{1,0:T(8,128)(2,1)} %get-tuple-element.49), channel_id=1, source_target_pairs={{0,2},{1,3},{2,0},{3,1},{64,66},{65,67},{66,64},{67,65},{16,18},{1... | collective-permute-start | bytes 1572872 | tf_op jit(solution)/shard_map/ppermute | solution.py:43
  55.3 10.1 %collective-permute-start.9 = (bf16[256,1792]{1,0:T(8,128)(2,1)}, bf16[256,1792]{1,0:T(8,128)(2,1)S(1)}, u32[]{:S(2)}, u32[]{:S(2)}) collective-permute-start(bf16[256,1792]{1,0:T(8,128)(2,1)} %get-tuple-element.47), channel_id=1, source_target_pairs={{0,1},{1,0},{2,3},{3,2},{64,65},{65,64},{66,67},{67,66},{16,17},{1... | collective-permute-start | bytes 2752520 | tf_op jit(solution)/shard_map/ppermute | solution.py:43
  55.3 3.9 %copy-start.6 = (bf16[512,512]{1,0:T(8,128)(2,1)}, bf16[512,512]{1,0:T(8,128)(2,1)S(1)}, u32[]{:S(2)}) copy-start(bf16[512,512]{1,0:T(8,128)(2,1)S(1)} %collective-permute-done.13.above) | copy-start | bytes 1572868
  56.2 9.3 %collective-permute-start.15 = (bf16[256,512]{1,0:T(8,128)(2,1)}, bf16[256,512]{1,0:T(8,128)(2,1)}, u32[]{:S(2)}, u32[]{:S(2)}) collective-permute-start(bf16[256,512]{1,0:T(8,128)(2,1)} %pad_maximum_fusion.6), channel_id=1, source_target_pairs={{0,48},{1,49},{2,50},{3,51},{64,112},{65,113},{66,114},{67,115},{1... | collective-permute-start | bytes 786440 | tf_op jit(solution)/shard_map/ppermute | solution.py:43
  56.7 2.5 %copy-start.8 = (bf16[512,512]{1,0:T(8,128)(2,1)}, bf16[512,512]{1,0:T(8,128)(2,1)S(1)}, u32[]{:S(2)}) copy-start(bf16[512,512]{1,0:T(8,128)(2,1)S(1)} %collective-permute-done.12.below) | copy-start | bytes 1572868
  57.5 9.9 %collective-permute-start.14 = (bf16[256,512]{1,0:T(8,128)(2,1)}, bf16[256,512]{1,0:T(8,128)(2,1)}, u32[]{:S(2)}, u32[]{:S(2)}) collective-permute-start(bf16[256,512]{1,0:T(8,128)(2,1)} %pad_maximum_fusion.5), channel_id=1, source_target_pairs={{0,16},{1,17},{2,18},{3,19},{64,80},{65,81},{66,82},{67,83},{16,32... | collective-permute-start | bytes 786440 | tf_op jit(solution)/shard_map/ppermute | solution.py:43
  59.2 1.0 copy-start.4
  60.2 7.3 %copy-start.7 = (bf16[512,512]{1,0:T(8,128)(2,1)S(1)}, bf16[512,512]{1,0:T(8,128)(2,1)}, u32[]{:S(2)}) copy-start(bf16[512,512]{1,0:T(8,128)(2,1)} %copy-done.6) | copy-start | bytes 1572868
  60.2 7.3 %copy-start.9 = (bf16[512,512]{1,0:T(8,128)(2,1)S(1)}, bf16[512,512]{1,0:T(8,128)(2,1)}, u32[]{:S(2)}) copy-start(bf16[512,512]{1,0:T(8,128)(2,1)} %copy-done.8) | copy-start | bytes 1572868
  60.2 7.3 %copy-start.13 = (f32[256,768]{1,0:T(8,128)S(1)}, f32[256,768]{1,0:T(8,128)}, u32[]{:S(2)}) copy-start(f32[256,768]{1,0:T(8,128)} %copy-done.12) | copy-start | bytes 2359300
  60.2 7.3 %copy-start.15 = (f32[256,768]{1,0:T(8,128)S(1)}, f32[256,768]{1,0:T(8,128)}, u32[]{:S(2)}) copy-start(f32[256,768]{1,0:T(8,128)} %copy-done.14) | copy-start | bytes 2359300
  60.2 7.3 %copy-start.17 = (f32[256,128]{1,0:T(8,128)S(1)}, f32[256,128]{1,0:T(8,128)}, u32[]{:S(2)}) copy-start(f32[256,128]{1,0:T(8,128)} %copy-done.16) | copy-start | bytes 393220
  67.5 9.3 %copy-start.25 = (bf16[512]{0:T(512)(128)(2,1)S(1)}, bf16[512]{0:T(512)(128)(2,1)}, u32[]{:S(2)}) copy-start(bf16[512]{0:T(512)(128)(2,1)} %param.5) | copy-start | bytes 3076
  74.3 0.9 copy-start
  75.2 1.0 copy-start.10
  76.8 11.1 %collective-permute-start.18 = (bf16[256,3584]{1,0:T(8,128)(2,1)}, bf16[256,3584]{1,0:T(8,128)(2,1)}, u32[]{:S(2)}, u32[]{:S(2)}) collective-permute-start(bf16[256,3584]{1,0:T(8,128)(2,1)} %get-tuple-element.58), channel_id=1, source_target_pairs={{0,1},{1,0},{2,3},{3,2},{64,65},{65,64},{66,67},{67,66},{16,17},{1... | collective-permute-start | bytes 5505032 | tf_op jit(solution)/shard_map/ppermute | solution.py:43
  76.9 38.7 %collective-permute-start.31 = (bf16[256,1536]{1,0:T(8,128)(2,1)}, bf16[256,1536]{1,0:T(8,128)(2,1)S(1)}, u32[]{:S(2)}, u32[]{:S(2)}) collective-permute-start(bf16[256,1536]{1,0:T(8,128)(2,1)} %copy-done), channel_id=1, source_target_pairs={{0,2},{1,3},{2,0},{3,1},{64,66},{65,67},{66,64},{67,65},{16,18},{1... | collective-permute-start | bytes 2359304 | tf_op jit(solution)/shard_map/ppermute | solution.py:43
  78.9 1.2 copy-start.1
  80.9 7.0 %copy-start.5 = (bf16[256,768]{1,0:T(8,128)(2,1)S(1)}, bf16[256,768]{1,0:T(8,128)(2,1)}, u32[]{:S(2)}) copy-start(bf16[256,768]{1,0:T(8,128)(2,1)} %copy-done.3) | copy-start | bytes 1179652
  80.9 7.0 %copy-start.11 = (bf16[256,2048]{1,0:T(8,128)(2,1)S(1)}, bf16[256,2048]{1,0:T(8,128)(2,1)}, u32[]{:S(2)}) copy-start(bf16[256,2048]{1,0:T(8,128)(2,1)} %copy-done.10) | copy-start | bytes 3145732
  93.4 19.7 %collective-permute-start.19 = (bf16[1024,384]{1,0:T(8,128)(2,1)S(1)}, bf16[1024,384]{1,0:T(8,128)(2,1)S(1)}, u32[]{:S(2)}, u32[]{:S(2)}) collective-permute-start(bf16[1024,384]{1,0:T(8,128)(2,1)S(1)} %bitcast.97), channel_id=1, source_target_pairs={{0,4},{1,5},{2,6},{3,7},{64,68},{65,69},{66,70},{67,71},{16,20},{1... | collective-permute-start | bytes 2359304 | tf_op jit(solution)/shard_map/ppermute | solution.py:43
  95.0 20.6 %collective-permute-start.20 = (bf16[1024,384]{1,0:T(8,128)(2,1)S(1)}, bf16[1024,384]{1,0:T(8,128)(2,1)S(1)}, u32[]{:S(2)}, u32[]{:S(2)}) collective-permute-start(bf16[1024,384]{1,0:T(8,128)(2,1)S(1)} %bitcast.96), channel_id=1, source_target_pairs={{0,12},{1,13},{2,14},{3,15},{64,76},{65,77},{66,78},{67,79},{16,28... | collective-permute-start | bytes 2359304 | tf_op jit(solution)/shard_map/ppermute | solution.py:43
  97.9 17.8 %collective-permute-start.16 = (bf16[512,640]{1,0:T(8,128)(2,1)S(1)}, bf16[512,640]{1,0:T(8,128)(2,1)S(1)}, u32[]{:S(2)}, u32[]{:S(2)}) collective-permute-start(bf16[512,640]{1,0:T(8,128)(2,1)S(1)} %bitcast.99), channel_id=1, source_target_pairs={{0,16},{1,17},{2,18},{3,19},{64,80},{65,81},{66,82},{67,83},{16,0}... | collective-permute-start | bytes 1966088 | tf_op jit(solution)/shard_map/ppermute | solution.py:43
  98.5 17.2 %collective-permute-start.17 = (bf16[512,640]{1,0:T(8,128)(2,1)S(1)}, bf16[512,640]{1,0:T(8,128)(2,1)S(1)}, u32[]{:S(2)}, u32[]{:S(2)}) collective-permute-start(bf16[512,640]{1,0:T(8,128)(2,1)S(1)} %bitcast.98), channel_id=1, source_target_pairs={{0,48},{1,49},{2,50},{3,51},{64,112},{65,113},{66,114},{67,115},{1... | collective-permute-start | bytes 1966088 | tf_op jit(solution)/shard_map/ppermute | solution.py:43
  115.8 8.8 %collective-permute-start.22 = (bf16[256,640]{1,0:T(8,128)(2,1)S(1)}, bf16[256,640]{1,0:T(8,128)(2,1)S(1)}, u32[]{:S(2)}, u32[]{:S(2)}) collective-permute-start(bf16[256,640]{1,0:T(8,128)(2,1)S(1)} %add_convert_fusion.5), channel_id=1, source_target_pairs={{0,16},{1,17},{2,18},{3,19},{64,80},{65,81},{66,82},{67,83},{16,0}... | collective-permute-start | bytes 983048 | tf_op jit(solution)/shard_map/ppermute | solution.py:43
  116.5 9.7 %collective-permute-start.21 = (bf16[256,640]{1,0:T(8,128)(2,1)S(1)}, bf16[256,640]{1,0:T(8,128)(2,1)S(1)}, u32[]{:S(2)}, u32[]{:S(2)}) collective-permute-start(bf16[256,640]{1,0:T(8,128)(2,1)S(1)} %add_convert_fusion.6), channel_id=1, source_target_pairs={{0,48},{1,49},{2,50},{3,51},{64,112},{65,113},{66,114},{67,115},{1... | collective-permute-start | bytes 983048 | tf_op jit(solution)/shard_map/ppermute | solution.py:43
  119.0 37.8 %collective-permute-start.34 = (bf16[512,384]{1,0:T(8,128)(2,1)S(1)}, bf16[512,384]{1,0:T(8,128)(2,1)S(1)}, u32[]{:S(2)}, u32[]{:S(2)}) collective-permute-start(bf16[512,384]{1,0:T(8,128)(2,1)S(1)} %add_convert_fusion.3), channel_id=1, source_target_pairs={{0,4},{1,5},{2,6},{3,7},{64,68},{65,69},{66,70},{67,71},{16,20},{1... | collective-permute-start | bytes 1179656 | tf_op jit(solution)/shard_map/ppermute | solution.py:43
  119.2 37.6 %collective-permute-start.33 = (bf16[512,384]{1,0:T(8,128)(2,1)S(1)}, bf16[512,384]{1,0:T(8,128)(2,1)S(1)}, u32[]{:S(2)}, u32[]{:S(2)}) collective-permute-start(bf16[512,384]{1,0:T(8,128)(2,1)S(1)} %add_convert_fusion.4), channel_id=1, source_target_pairs={{0,12},{1,13},{2,14},{3,15},{64,76},{65,77},{66,78},{67,79},{16,28... | collective-permute-start | bytes 1179656 | tf_op jit(solution)/shard_map/ppermute | solution.py:43
  122.4 27.6 %collective-permute-start.32 = (bf16[256,2560]{1,0:T(8,128)(2,1)S(1)}, bf16[256,2560]{1,0:T(8,128)(2,1)S(1)}, u32[]{:S(2)}, u32[]{:S(2)}) collective-permute-start(bf16[256,2560]{1,0:T(8,128)(2,1)S(1)} %pad_maximum_fusion), channel_id=1, source_target_pairs={{0,1},{1,0},{2,3},{3,2},{64,65},{65,64},{66,67},{67,66},{16,17},{1... | collective-permute-start | bytes 3932168 | tf_op jit(solution)/shard_map/ppermute | solution.py:43
  126.5 9.1 %collective-permute-start.27 = (bf16[256,640]{1,0:T(8,128)(2,1)S(1)}, bf16[256,640]{1,0:T(8,128)(2,1)S(1)}, u32[]{:S(2)}, u32[]{:S(2)}) collective-permute-start(bf16[256,640]{1,0:T(8,128)(2,1)S(1)} %select_convert_fusion.1), channel_id=1, source_target_pairs={{0,64},{1,65},{2,66},{3,67},{64,0},{65,1},{66,2},{67,3},{16,80},{1... | collective-permute-start | bytes 983048 | tf_op jit(solution)/shard_map/ppermute | solution.py:43
  128.3 9.8 %copy-start.18 = (f32[256,128]{1,0:T(8,128)S(1)}, f32[256,128]{1,0:T(8,128)}, u32[]{:S(2)}) copy-start(f32[256,128]{1,0:T(8,128)} %copy-done.16) | copy-start | bytes 393220
  128.3 9.9 %copy-start.24 = (bf16[256,512]{1,0:T(8,128)(2,1)S(1)}, bf16[256,512]{1,0:T(8,128)(2,1)}, u32[]{:S(2)}) copy-start(bf16[256,512]{1,0:T(8,128)(2,1)} %param.4) | copy-start | bytes 786436
  128.3 11.5 %collective-permute-start.23 = (bf16[512,512]{1,0:T(8,128)(2,1)S(1)}, bf16[512,512]{1,0:T(8,128)(2,1)S(1)}, u32[]{:S(2)}, u32[]{:S(2)}) collective-permute-start(bf16[512,512]{1,0:T(8,128)(2,1)S(1)} %bitcast.101), channel_id=1, source_target_pairs={{0,16},{1,17},{2,18},{3,19},{64,80},{65,81},{66,82},{67,83},{16,0}... | collective-permute-start | bytes 1572872 | tf_op jit(solution)/shard_map/ppermute | solution.py:43
  135.5 12.0 %collective-permute-start.24 = (bf16[512,512]{1,0:T(8,128)(2,1)S(1)}, bf16[512,512]{1,0:T(8,128)(2,1)S(1)}, u32[]{:S(2)}, u32[]{:S(2)}) collective-permute-start(bf16[512,512]{1,0:T(8,128)(2,1)S(1)} %bitcast.100), channel_id=1, source_target_pairs={{0,48},{1,49},{2,50},{3,51},{64,112},{65,113},{66,114},{67,115},{1... | collective-permute-start | bytes 1572872 | tf_op jit(solution)/shard_map/ppermute | solution.py:43
  138.1 12.0 %copy-start.2 = (bf16[256,1536]{1,0:T(8,128)(2,1)S(1)}, bf16[256,1536]{1,0:T(8,128)(2,1)}, u32[]{:S(2)}) copy-start(bf16[256,1536]{1,0:T(8,128)(2,1)} %copy-done) | copy-start | bytes 2359300
  138.1 12.0 %copy-start.20 = (bf16[256,1024]{1,0:T(8,128)(2,1)S(1)}, bf16[256,1024]{1,0:T(8,128)(2,1)}, u32[]{:S(2)}) copy-start(bf16[256,1024]{1,0:T(8,128)(2,1)} %copy-done.19) | copy-start | bytes 1572868
  139.8 19.8 %collective-permute-start.29 = (f32[1,512]{1,0:T(1,128)S(1)}, f32[1,512]{1,0:T(1,128)S(1)}, u32[]{:S(2)}, u32[]{:S(2)}) collective-permute-start(f32[1,512]{1,0:T(1,128)S(1)} %bitcast.102), channel_id=1, source_target_pairs={{0,1},{1,0},{2,3},{3,2},{64,65},{65,64},{66,67},{67,66},{16,17},{1... | collective-permute-start | bytes 6152 | tf_op jit(solution)/shard_map/ppermute | solution.py:43
  147.6 16.9 %collective-permute-start.26 = (bf16[256,512]{1,0:T(8,128)(2,1)S(1)}, bf16[256,512]{1,0:T(8,128)(2,1)S(1)}, u32[]{:S(2)}, u32[]{:S(2)}) collective-permute-start(bf16[256,512]{1,0:T(8,128)(2,1)S(1)} %add_convert_fusion.8), channel_id=1, source_target_pairs={{0,48},{1,49},{2,50},{3,51},{64,112},{65,113},{66,114},{67,115},{1... | collective-permute-start | bytes 786440 | tf_op jit(solution)/shard_map/ppermute | solution.py:43
  150.0 14.5 %collective-permute-start.25 = (bf16[256,512]{1,0:T(8,128)(2,1)S(1)}, bf16[256,512]{1,0:T(8,128)(2,1)S(1)}, u32[]{:S(2)}, u32[]{:S(2)}) collective-permute-start(bf16[256,512]{1,0:T(8,128)(2,1)S(1)} %add_convert_fusion.9), channel_id=1, source_target_pairs={{0,16},{1,17},{2,18},{3,19},{64,80},{65,81},{66,82},{67,83},{16,0}... | collective-permute-start | bytes 786440 | tf_op jit(solution)/shard_map/ppermute | solution.py:43
  156.9 16.4 %collective-permute-start.35 = (bf16[512,768]{1,0:T(8,128)(2,1)S(1)}, bf16[512,768]{1,0:T(8,128)(2,1)S(1)}, u32[]{:S(2)}, u32[]{:S(2)}) collective-permute-start(bf16[512,768]{1,0:T(8,128)(2,1)S(1)} %bitcast.95), channel_id=1, source_target_pairs={{0,4},{1,5},{2,6},{3,7},{64,68},{65,69},{66,70},{67,71},{16,20},{1... | collective-permute-start | bytes 2359304 | tf_op jit(solution)/shard_map/ppermute | solution.py:43
  157.2 17.3 %collective-permute-start.36 = (bf16[512,768]{1,0:T(8,128)(2,1)S(1)}, bf16[512,768]{1,0:T(8,128)(2,1)S(1)}, u32[]{:S(2)}, u32[]{:S(2)}) collective-permute-start(bf16[512,768]{1,0:T(8,128)(2,1)S(1)} %bitcast.94), channel_id=1, source_target_pairs={{0,12},{1,13},{2,14},{3,15},{64,76},{65,77},{66,78},{67,79},{16,28... | collective-permute-start | bytes 2359304 | tf_op jit(solution)/shard_map/ppermute | solution.py:43
  159.6 3.7 %collective-permute-start.30 = (f32[1,512]{1,0:T(1,128)S(1)}, f32[1,512]{1,0:T(1,128)S(1)}, u32[]{:S(2)}, u32[]{:S(2)}) collective-permute-start(f32[1,512]{1,0:T(1,128)S(1)} %add.214), channel_id=1, source_target_pairs={{0,2},{1,3},{2,0},{3,1},{64,66},{65,67},{66,64},{67,65},{16,18},{1... | collective-permute-start | bytes 6152 | tf_op jit(solution)/shard_map/ppermute | solution.py:43
  163.4 15.1 %collective-permute-start.41 = (bf16[256,768]{1,0:T(8,128)(2,1)S(1)}, bf16[256,768]{1,0:T(8,128)(2,1)S(1)}, u32[]{:S(2)}, u32[]{:S(2)}) collective-permute-start(bf16[256,768]{1,0:T(8,128)(2,1)S(1)} %select_convert_fusion), channel_id=1, source_target_pairs={{0,2},{1,3},{2,0},{3,1},{64,66},{65,67},{66,64},{67,65},{16,18},{1... | collective-permute-start | bytes 1179656 | tf_op jit(solution)/shard_map/ppermute | solution.py:43
  164.7 19.8 %collective-permute-start.28 = (bf16[256,512]{1,0:T(8,128)(2,1)S(1)}, bf16[256,512]{1,0:T(8,128)(2,1)S(1)}, u32[]{:S(2)}, u32[]{:S(2)}) collective-permute-start(bf16[256,512]{1,0:T(8,128)(2,1)S(1)} %select_convert_fusion.2), channel_id=1, source_target_pairs={{0,64},{1,65},{2,66},{3,67},{64,0},{65,1},{66,2},{67,3},{16,80},{1... | collective-permute-start | bytes 786440 | tf_op jit(solution)/shard_map/ppermute | solution.py:43
  174.6 13.6 %collective-permute-start.40 = (bf16[256,768]{1,0:T(8,128)(2,1)S(1)}, bf16[256,768]{1,0:T(8,128)(2,1)S(1)}, u32[]{:S(2)}, u32[]{:S(2)}) collective-permute-start(bf16[256,768]{1,0:T(8,128)(2,1)S(1)} %add_convert_fusion.1), channel_id=1, source_target_pairs={{0,4},{1,5},{2,6},{3,7},{64,68},{65,69},{66,70},{67,71},{16,20},{1... | collective-permute-start | bytes 1179656 | tf_op jit(solution)/shard_map/ppermute | solution.py:43
  175.1 13.1 %collective-permute-start.39 = (bf16[256,768]{1,0:T(8,128)(2,1)S(1)}, bf16[256,768]{1,0:T(8,128)(2,1)S(1)}, u32[]{:S(2)}, u32[]{:S(2)}) collective-permute-start(bf16[256,768]{1,0:T(8,128)(2,1)S(1)} %add_convert_fusion.2), channel_id=1, source_target_pairs={{0,12},{1,13},{2,14},{3,15},{64,76},{65,77},{66,78},{67,79},{16,28... | collective-permute-start | bytes 1179656 | tf_op jit(solution)/shard_map/ppermute | solution.py:43
  177.4 5.1 %collective-permute-start.37 = (f32[1,512]{1,0:T(1,128)S(1)}, f32[1,512]{1,0:T(1,128)S(1)}, u32[]{:S(2)}, u32[]{:S(2)}) collective-permute-start(f32[1,512]{1,0:T(1,128)S(1)} %add.215), channel_id=1, source_target_pairs={{0,4},{1,5},{2,6},{3,7},{64,68},{65,69},{66,70},{67,71},{16,20},{1... | collective-permute-start | bytes 6152 | tf_op jit(solution)/shard_map/ppermute | solution.py:43
  182.5 5.1 %collective-permute-start.38 = (f32[1,512]{1,0:T(1,128)S(1)}, f32[1,512]{1,0:T(1,128)S(1)}, u32[]{:S(2)}, u32[]{:S(2)}) collective-permute-start(f32[1,512]{1,0:T(1,128)S(1)} %add.220), channel_id=1, source_target_pairs={{0,8},{1,9},{2,10},{3,11},{64,72},{65,73},{66,74},{67,75},{16,24},... | collective-permute-start | bytes 6152 | tf_op jit(solution)/shard_map/ppermute | solution.py:43
  (4 other events, 3.0 us)

commit v3 on v2

--- a/solution.py
+++ b/solution.py
@@ -95,12 +95,12 @@
     return copies
 
 
-def forward_body(spot, own, below, above, far, other, other_below, other_above, other_far, w, gate, up, hidden, inv,
-                 gains, keep, core_out, z_out, cross_out, buf, held, sems):
+def forward_body(spot, own, below, above, other, up2, down2, other_far, w, gate, up, hidden, inv, gains, keep, core_out,
+                 z_out, cross_out, buf, held, sems):
     copies = fetch(w, held, sems, 0, 2, lambda k: k)
     put(buf, spot, [
-        (0, 0, 0, own, 0, 272), (0, 3, 0, below, 0, 272), (0, 1, 0, above, 0, 272), (0, 2, 0, far, 0, 272),
-        (1, 0, 0, other, 0, 272), (1, 3, 0, other_below, 0, 272), (1, 1, 0, other_above, 0, 272),
+        (0, 0, 0, own, 0, 272), (0, 3, 0, below, 0, 272), (0, 1, 0, above, 0, 272), (1, 0, 0, other, 0, 272),
+        (0, 2, 0, up2, 0, 128), (1, 3, 0, up2, 128, 272), (0, 2, 128, down2, 0, 144), (1, 1, 0, down2, 144, 272),
         (1, 2, 0, other_far, 0, 272),
     ])
     z_lo, core = spot[8], spot[9]
@@ -137,13 +137,13 @@
                 (spot, *pieces, w3), hbm=(len(pieces) + 1,))
 
 
-def backward_body(spot, both, below, above, low, high, w, gate, up, inv, pair, products, mine, core_out, buf, acc,
-                  held, sems):
+def backward_body(spot, cot, up, down, other, cot_up, cot_down, far, w, gate, up_val, inv, pair, products, mine,
+                  core_out, buf, acc, held, sems):
     copies = fetch(w, held, sems, 2, 1, lambda k: k)
     put(buf, spot, [
-        (0, 0, 0, both, 0, 256), (1, 0, 0, both, 256, 256), (0, 3, 0, below, 0, 256), (1, 3, 0, below, 256, 256),
-        (0, 1, 0, above, 0, 256), (1, 1, 0, above, 256, 256), (0, 2, 0, low, 0, 128), (1, 2, 0, low, 128, 128),
-        (0, 2, 128, high, 0, 128), (1, 2, 128, high, 128, 128),
+        (0, 0, 0, cot, 0, 256), (0, 3, 0, up, 400, 256), (0, 1, 0, down, 416, 256), (1, 0, 0, other, 0, 256),
+        (0, 2, 0, cot_up, 0, 128), (1, 3, 0, cot_up, 128, 256), (0, 2, 128, cot_down, 0, 128),
+        (1, 1, 0, cot_down, 128, 256), (1, 2, 0, far, 0, 256),
     ])
     core = spot[9]
     for i in range(8):
@@ -154,7 +154,7 @@
         value = dot(buf[:, k * 512:(k + 1) * 512], held[k, 0])
         acc[...] = value if k == 0 else acc[...] + value
     d_hidden = acc[...] * inv[:, 0:1]
-    g, u = gate[...], up[...]
+    g, u = gate[...], up_val[...]
     sigma = jax.nn.sigmoid(g)
     d_gate = (d_hidden * u * sigma * (1.0 + g * (1.0 - sigma))).astype(bf16)
     d_up = (d_hidden * g * sigma).astype(bf16)
@@ -170,8 +170,8 @@
     shapes = [((256, 1536), bf16), ((256, 128), bf16), ((256, 2048), bf16), ((256, 3584), bf16)]
     scratch = [pltpu.VMEM((256, 4096), bf16), pltpu.VMEM((256, 768), f32), pltpu.VMEM((8, 1, 512, 768), bf16),
                pltpu.SemaphoreType.DMA((8,))]
-    return call(backward_body, "backward", shapes, scratch, 15,
-                (spot, *pieces, w3, gate, up, inv), hbm=(len(pieces) + 1,))
+    return call(backward_body, "backward", shapes, scratch, 15, (spot, *pieces, w3, gate, up, inv),
+                hbm=(len(pieces) + 1,))
 
 
 def outer_body(a_from, b_from, rows, cols, order, *refs):
@@ -229,25 +229,25 @@
     two, six, *got = lax.optimization_barrier((terms[2], terms[6], *got, *done))[:4]
     out = [(t.astype(f32) + g[rows:].astype(f32)).astype(bf16) for t, g in zip((two, six), got)]
     last = [send(o, move) for o, move in zip(out, (far, near))]
-    sums = [terms[4 * h + 3].astype(f32) + got[h][:rows].astype(f32) + last[h].astype(f32) for h in (0, 1)]
-    return sums, got, out, last
-
-
-def gather_inputs(own):
+    return got, out, last
+
+
+def finish(terms, got, last, done=()):
+    three, seven = lax.optimization_barrier((terms[3], terms[7], *done))[:2]
+    rows = terms.shape[1]
+    return [t.astype(f32) + g[:rows].astype(f32) + e.astype(f32) for t, g, e in zip((three, seven), got, last)]
+
+
+def gather_both(own, cot):
     below, above, other = send(own, "y+"), send(own, "y-"), send(own, "z+2")
-    far = rows_cat(send(below[:128], "y+"), send(above[128:], "y-"))
-    other = after(other, far)
-    other_below, other_above = send(other, "y+"), send(other, "y-")
-    return (own, below, above, far, other, other_below, other_above, send(far, "z+2"))
-
-
-def gather_cot(own, first, second):
-    other = send(after(own, *first), "z+2")
-    both = after(rows_cat(own, other), *second)
-    below, above = send(both, "y+"), send(both, "y-")
-    low = send(rows_cat(below[:128], below[256:384]), "y+")
-    high = send(rows_cat(above[128:256], above[384:]), "y-")
-    return (both, below, above, low, high)
+    up = send(rows_cat(below[:128], other, cot), "y+")
+    down = send(rows_cat(above[128:], other, cot), "y-")
+    cot_other = send(after(cot, other), "z+2")
+    other_far = send(after(rows_cat(up[:128], down[:144]), cot_other), "z+2")
+    cot_up = send(rows_cat(up[400:528], cot_other), "y+")
+    cot_down = send(rows_cat(down[544:], cot_other), "y-")
+    cot_far = send(rows_cat(cot_up[:128], cot_down[:128]), "z+2")
+    return (own, below, above, other, up, down, other_far), (cot, up, down, cot_other, cot_up, cot_down, cot_far)
 
 
 def local(inputs, gain, weights, d_out):
@@ -263,38 +263,43 @@
     def order(at):
         return jnp.stack([at ^ 1, at ^ 2, at ^ 3, at, at ^ 3, at ^ 2, at ^ 1, at]).astype(jnp.int32)
 
-    x_pieces = gather_inputs(rows_cat(inputs, jnp.broadcast_to(gain.reshape(1, 512), (16, 512))))
-    cot_pieces = gather_cot(d_out, x_pieces[4:5], x_pieces[5:7])
+    own = rows_cat(inputs, jnp.broadcast_to(gain.reshape(1, 512), (16, 512)))
+    x_pieces, cot_pieces = gather_both(own, d_out)
     gate, up_val, hidden, inv, gains, x_keep, core_one, x_same, x_cross = forward(spot, x_pieces, w3)
-    x_same = send(x_same, "z^3")
+    x_same, x_cross = lax.optimization_barrier((x_same, x_cross, *cot_pieces[4:6]))[:2]
+    x_same, x_cross = send(x_same, "z^3"), send(x_cross, "z^1")
     core_one = send(core_one, "c")
     branch_terms = branch_rows(order(y), hidden, w3)
-    x_cross = send(x_cross, "z^1")
     cot_pieces = (after(cot_pieces[0], core_one, x_same, x_cross, branch_terms), *cot_pieces[1:])
     d_pair, products, cot_mine, core_two = backward(spot, cot_pieces, w3, gate, up_val, inv)
     core_two = send(core_two, "c")
-    d_terms = pair_rows(order(y), d_pair, products, w3)
     pair_z = send(d_pair, "z^1")
-    down_terms = outer("down_terms", order(x), [(after(cot_mine, d_terms), 0), (core_two, 0)], [(hidden, 0), (core_one, 1024)], 512, 384)
-    down, down_got, _, down_last = halve(down_terms, "x")
+    down_terms = outer("down_terms", order(x), [(cot_mine, 0), (core_two, 0)], [(hidden, 0), (core_one, 1024)], 512, 384)
+    down_got, _, down_last = halve(down_terms, "x")
+    d_terms = pair_rows(order(y), after(d_pair, down_terms), products, w3)
     core_three = send(jnp.concatenate([x_cross, after(pair_z, *down_got)], axis=1), "c")
+    pair_terms = outer(
+        "pair_terms", order(x), [(x_keep, 0), (x_same, 0), (core_one, 0), (core_three, 0)],
+        [(d_pair, 0), (pair_z, 0), (core_two, 2048), (core_three, 1024)], 256, 768,
+    )
+    down_last = lax.optimization_barrier((*down_last, pair_terms))[:2]
+    pair_got, pair_out, pair_last = halve(after(pair_terms, *down_last), "x")
+    d_w_gate, d_w_up = finish(pair_terms, pair_got, pair_last)
+    down = finish(down_terms, down_got, down_last, (pair_terms,))
     d_w_down = jnp.concatenate(down, axis=1)
     lower = z_lo == 0
     theirs = jnp.where(lower, d_w_down[256:], d_w_down[:256]).astype(bf16)
     d_w_down = jnp.where(lower, d_w_down[:256], d_w_down[256:]) + send(theirs, "z^1").astype(f32)
 
-    pair_terms = outer(
-        "pair_terms", order(x), [(x_keep, 0), (x_same, 0), (core_one, 0), (core_three, 0)],
-        [(d_pair, 0), (pair_z, 0), (core_two, 2048), (core_three, 1024)], 256, 768,
-    )
-    (d_w_gate, d_w_up), _, pair_out, _ = halve(after(pair_terms, *down_last), "x")
-
-    (d_low, d_high), _, _, d_last = halve(d_terms, "y", down_got)
-    (low, high), _, _, _ = halve(after(branch_terms, *d_last), "y")
+    d_got, _, d_last = halve(d_terms, "y", down_got)
+    d_low, d_high = finish(d_terms, d_got, d_last)
+    branch_terms = after(branch_terms, *d_last)
+    branch_got, _, branch_last = halve(branch_terms, "y", (pair_terms,))
+    low, high = finish(branch_terms, branch_got, branch_last)
     upper = z_hi == 1
     mine = jnp.where(upper, d_high, d_low)
     theirs = send(jnp.where(upper, d_low, d_high).astype(bf16), "z+2")
-    mine = mine + theirs.astype(f32)
+    mine = after(mine, pair_terms) + theirs.astype(f32)
     theirs = send(after(jnp.where(upper, low, high).astype(bf16), theirs), "z+2")
     branch = (jnp.where(upper, high, low) + theirs.astype(f32)).astype(bf16)
     d_normed, products = mine[:, :512], mine[:, 512:513] / width

time: 191 us -> 184 us (0.963)
  waiting for transfers between devices: 72.4 us -> 62.5 us
  local copies, waits for them, and re-layouts: 9.73 us -> 15.1 us
    ppermute x42 -> x39, waiting for transfers between devices: 72.4 us -> 62.5 us  [send(): return lax.ppermute(value, AXES, pairs(moves[move]))]
    unnamed x53 -> x62, local copies, waits for them, and re-layouts: 8.05 us -> 13.1 us
    ppermute x42 -> x39, starting transfers between devices: 57 us -> 55.1 us  [send(): return lax.ppermute(value, AXES, pairs(moves[move]))]
  transfers between devices with their start and end apart: 42 -> 39, of which waited for: 19 -> 22; matrix products, arithmetic and copies ran while one was open for 5% -> 5% of each run, Pallas kernels for 17% -> 17%
where the time goes in v3:
time: 184 us
  waiting for transfers between devices  62.5 us (34%)
  starting transfers between devices  55.1 us (30%)
  Pallas kernels  38.6 us (21%)
  local copies, waits for them, and re-layouts  15.1 us (8%)
  other arithmetic  11.2 us (6%)
    ppermute x39, waiting for transfers between devices, send(): return lax.ppermute(value, AXES, pairs(moves[move]))  62.5 us
    ppermute x39, starting transfers between devices, send(): return lax.ppermute(value, AXES, pairs(moves[move]))  55.1 us
    pallas_call x6, Pallas kernels, call(): pl.pallas_call(body, in_specs=[pl.BlockSpec(memory_space=space) for space...  38.6 us
    unnamed x62, local copies, waits for them, and re-layouts  13.1 us
    concatenate x6, other arithmetic, rows_cat(): return jnp.concatenate(parts, axis=0)  3.72 us
  transfers between devices with their start and end apart: 39, of which 22 were waited for; matrix products, arithmetic and copies ran while one was open for 5% of the time, Pallas kernels for 17%

profile of v3, /device:TPU:0, one launch (start us, length us, event | category | flops | bytes accessed | tf_op | source)
XLA Modules:
  0.0 183.6 jit_solution(15137172043899572351)
XLA Ops:
  1.4 1.0 pad_maximum_fusion.7.own
  2.3 1.7 collective-permute-start
  4.1 3.9 %collective-permute-start.2 = (bf16[272,512]{1,0:T(8,128)(2,1)S(1)}, bf16[272,512]{1,0:T(8,128)(2,1)S(1)}, u32[]{:S(2)}, u32[]{:S(2)}) collective-permute-start(bf16[272,512]{1,0:T(8,128)(2,1)S(1)} %pad_maximum_fusion.7.own), channel_id=1, source_target_pairs={{0,64},{1,65},{2,66},{3,67},{64,0},{65,1},{66,2},{67,3},{16,80},{1... | collective-permute-start | bytes 835592 | tf_op jit(solution)/shard_map/ppermute | solution.py:43
  7.9 1.7 collective-permute-start.1
  9.6 2.6 %collective-permute-done.below = bf16[272,512]{1,0:T(8,128)(2,1)S(1)} collective-permute-done((bf16[272,512]{1,0:T(8,128)(2,1)S(1)}, bf16[272,512]{1,0:T(8,128)(2,1)S(1)}, u32[]{:S(2)}, u32[]{:S(2)}) %collective-permute-start) | collective-permute-done | bytes 278560 | tf_op jit(solution)/shard_map/ppermute | solution.py:43
  12.9 1.4 collective-permute-done.2.other
  14.3 1.0 pad_maximum_fusion.4
  15.3 1.6 collective-permute-start.3
  17.7 1.8 %collective-permute-start.4 = (bf16[672,512]{1,0:T(8,128)(2,1)S(1)}, bf16[672,512]{1,0:T(8,128)(2,1)S(1)}, u32[]{:S(2)}, u32[]{:S(2)}) collective-permute-start(bf16[672,512]{1,0:T(8,128)(2,1)S(1)} %pad_maximum_fusion.3), channel_id=1, source_target_pairs={{0,48},{1,49},{2,50},{3,51},{64,112},{65,113},{66,114},{67,115},{1... | collective-permute-start | bytes 2064392 | tf_op jit(solution)/shard_map/ppermute | solution.py:43
  19.5 3.1 %collective-permute-start.5 = (bf16[256,512]{1,0:T(8,128)(2,1)S(1)}, bf16[256,512]{1,0:T(8,128)(2,1)S(1)}, u32[]{:S(2)}, u32[]{:S(2)}) collective-permute-start(bf16[256,512]{1,0:T(8,128)(2,1)S(1)} %copy-done.2), channel_id=1, source_target_pairs={{0,64},{1,65},{2,66},{3,67},{64,0},{65,1},{66,2},{67,3},{16,80},{1... | collective-permute-start | bytes 786440 | tf_op jit(solution)/shard_map/ppermute | solution.py:43
  22.6 10.0 %collective-permute-done.3.up2.up = bf16[656,512]{1,0:T(8,128)(2,1)S(1)} collective-permute-done((bf16[656,512]{1,0:T(8,128)(2,1)S(1)}, bf16[656,512]{1,0:T(8,128)(2,1)S(1)}, u32[]{:S(2)}, u32[]{:S(2)}) %collective-permute-start.3) | collective-permute-done | bytes 671776 | tf_op jit(solution)/shard_map/ppermute | solution.py:43
  32.6 1.1 collective-permute-done.4.down2.down
  33.8 3.0 %collective-permute-start.6 = (bf16[272,512]{1,0:T(8,128)(2,1)S(1)}, bf16[272,512]{1,0:T(8,128)(2,1)}, u32[]{:S(2)}, u32[]{:S(2)}) collective-permute-start(bf16[272,512]{1,0:T(8,128)(2,1)S(1)} %pad_maximum_fusion.8), channel_id=1, source_target_pairs={{0,64},{1,65},{2,66},{3,67},{64,0},{65,1},{66,2},{67,3},{16,80},{1... | collective-permute-start | bytes 835592 | tf_op jit(solution)/shard_map/ppermute | solution.py:43
  36.8 1.0 pad_maximum_fusion.5
  37.8 2.9 %collective-permute-start.9 = (bf16[384,512]{1,0:T(8,128)(2,1)}, bf16[384,512]{1,0:T(8,128)(2,1)S(1)}, u32[]{:S(2)}, u32[]{:S(2)}) collective-permute-start(bf16[384,512]{1,0:T(8,128)(2,1)} %get-tuple-element.136), channel_id=1, source_target_pairs={{0,48},{1,49},{2,50},{3,51},{64,112},{65,113},{66,114},{67,115},{1... | collective-permute-start | bytes 1179656 | tf_op jit(solution)/shard_map/ppermute | solution.py:43
  40.7 1.3 collective-permute-done.6.other_far
  42.0 1.0 copy-done.20
  43.0 1.0 copy-done.22
  43.9 7.2 %forward.1 = (f32[256,768]{1,0:T(8,128)S(1)}, f32[256,768]{1,0:T(8,128)S(1)}, bf16[256,768]{1,0:T(8,128)(2,1)S(1)}, f32[256,128]{1,0:T(8,128)S(1)}, bf16[16,4096...) custom-call(s32[10]{0:T(128)S(1)} %stack.116.spot, ...), custom_call_target="tpu_custom_call" | custom-call | flops 1 | bytes 1 | tf_op jit(solution)/shard_map/forward/pallas_call | solution.py:68
  55.9 3.2 %collective-permute-start.10 = (bf16[256,1024]{1,0:T(8,128)(2,1)}, bf16[256,1024]{1,0:T(8,128)(2,1)}, u32[]{:S(2)}, u32[]{:S(2)}) collective-permute-start(bf16[256,1024]{1,0:T(8,128)(2,1)} %get-tuple-element.61), channel_id=1, source_target_pairs={{0,66},{1,67},{2,64},{3,65},{64,2},{65,3},{66,0},{67,1},{16,82},{1... | collective-permute-start | bytes 1572872 | tf_op jit(solution)/shard_map/ppermute | solution.py:43
  59.9 1.6 collective-permute-start.12
  61.6 1.0 copy-done.5
  62.6 5.3 %branch_rows.1 = bf16[8,256,512]{2,1,0:T(8,128)(2,1)S(1)} custom-call(s32[8]{0:T(128)S(1)} %stack.105.order, bf16[256,768]{1,0:T(8,128)(2,1)S(1)} %copy-done.5, bf16[3,4096,768]{2,1,0:T(8,128)(2,1)} %bitcast.69), custom_call_target="tpu_custom_call" | custom-call | flops 1 | bytes 1 | tf_op jit(solution)/shard_map/branch_rows/pallas_call | solution.py:68
  67.9 4.1 %collective-permute-done.10.refs_1_ = bf16[256,1024]{1,0:T(8,128)(2,1)} collective-permute-done((bf16[256,1024]{1,0:T(8,128)(2,1)}, bf16[256,1024]{1,0:T(8,128)(2,1)}, u32[]{:S(2)}, u32[]{:S(2)}) %collective-permute-start.10) | collective-permute-done | bytes 524320 | tf_op jit(solution)/shard_map/ppermute | solution.py:43
  72.0 2.2 %collective-permute-done.11 = bf16[256,1024]{1,0:T(8,128)(2,1)} collective-permute-done((bf16[256,1024]{1,0:T(8,128)(2,1)}, bf16[256,1024]{1,0:T(8,128)(2,1)}, u32[]{:S(2)}, u32[]{:S(2)}) %collective-permute-start.11) | collective-permute-done | bytes 524320 | tf_op jit(solution)/shard_map/ppermute | solution.py:43
  74.2 4.7 %collective-permute-done.12.far = bf16[256,512]{1,0:T(8,128)(2,1)} collective-permute-done((bf16[256,512]{1,0:T(8,128)(2,1)}, bf16[256,512]{1,0:T(8,128)(2,1)}, u32[]{:S(2)}, u32[]{:S(2)}) %collective-permute-start.12) | collective-permute-done | bytes 262176 | tf_op jit(solution)/shard_map/ppermute | solution.py:43
  79.0 6.7 %backward.1 = (bf16[256,1536]{1,0:T(8,128)(2,1)S(1)}, bf16[256,128]{1,0:T(8,128)(2,1)S(1)}, bf16[256,2048]{1,0:T(8,128)(2,1)S(1)}, bf16[256,3584]{1,0:T(8,128)(2,1)}) custom-call(s32[10]{0:T(128)S(1)} %stack.116.spot, bf16[256,512]{1,0:T(8,128)(2,1)S(1)} %copy-done.3, bf16[656,512]{1,0:T(8,128)(2,1)S(1)} %collective-permute-done.3.up2.up, ...), custom_call_target="tpu_custom_call" | custom-call | flops 1 | bytes 1 | tf_op jit(solution)/shard_map/backward/pallas_call | solution.py:68
  86.5 1.0 copy-done.9
  88.3 3.3 %collective-permute-done.13.refs_1_.refs_6_ = bf16[256,3584]{1,0:T(8,128)(2,1)} collective-permute-done((bf16[256,3584]{1,0:T(8,128)(2,1)}, bf16[256,3584]{1,0:T(8,128)(2,1)}, u32[]{:S(2)}, u32[]{:S(2)}) %collective-permute-start.13) | collective-permute-done | bytes 1835040 | tf_op jit(solution)/shard_map/ppermute | solution.py:43
  91.6 1.0 copy-done.6
  92.6 1.2 copy-done.10
  93.8 5.6 %down_terms.1 = bf16[8,512,384]{2,1,0:T(8,128)(2,1)S(1)} custom-call(s32[8]{0:T(128)S(1)} %stack.121.order, bf16[256,2048]{1,0:T(8,128)(2,1)S(1)} %copy-done.10, bf16[256,3584]{1,0:T(8,128)(2,1)} %collective-permute-done.13.refs_1_.refs_6_, bf16[256,768]{1,0:T(8,128)(2,1)S(1)} %copy-done.6, bf16[256,1792]{1,0:T(8,128)(2,1)} %collective-permute-done.7.refs_3_.refs_2_), custom_call_target="tpu_custom_call" | custom-call | flops 1 | bytes 1 | tf_op jit(solution)/shard_map/down_terms/pallas_call | solution.py:68
  99.6 1.6 collective-permute-start.16
  101.2 2.1 %collective-permute-start.17 = (bf16[1024,384]{1,0:T(8,128)(2,1)S(1)}, bf16[1024,384]{1,0:T(8,128)(2,1)S(1)}, u32[]{:S(2)}, u32[]{:S(2)}) collective-permute-start(bf16[1024,384]{1,0:T(8,128)(2,1)S(1)} %bitcast.74), channel_id=1, source_target_pairs={{0,12},{1,13},{2,14},{3,15},{64,76},{65,77},{66,78},{67,79},{16,28... | collective-permute-start | bytes 2359304 | tf_op jit(solution)/shard_map/ppermute | solution.py:43
  103.3 6.9 %pair_rows.1 = bf16[8,256,640]{2,1,0:T(8,128)(2,1)S(1)} custom-call(s32[8]{0:T(128)S(1)} %stack.105.order, bf16[256,1536]{1,0:T(8,128)(2,1)S(1)} %copy-done.1, bf16[256,128]{1,0:T(8,128)(2,1)S(1)} %get-tuple-element.71.products, bf16[3,4096,768]{2,1,0:T(8,128)(2,1)} %bitcast.71), custom_call_target="tpu_custom_call" | custom-call | flops 1 | bytes 1 | tf_op jit(solution)/shard_map/pair_rows/pallas_call | solution.py:68
  110.4 1.4 collective-permute-start.14
  111.7 1.6 collective-permute-start.15
  113.7 5.6 %collective-permute-done.16 = bf16[1024,384]{1,0:T(8,128)(2,1)S(1)} collective-permute-done((bf16[1024,384]{1,0:T(8,128)(2,1)S(1)}, bf16[1024,384]{1,0:T(8,128)(2,1)S(1)}, u32[]{:S(2)}, u32[]{:S(2)}) %collective-permute-start.16) | collective-permute-done | bytes 786464 | tf_op jit(solution)/shard_map/ppermute | solution.py:43
  119.3 2.4 %collective-permute-done.17 = bf16[1024,384]{1,0:T(8,128)(2,1)S(1)} collective-permute-done((bf16[1024,384]{1,0:T(8,128)(2,1)S(1)}, bf16[1024,384]{1,0:T(8,128)(2,1)S(1)}, u32[]{:S(2)}, u32[]{:S(2)}) %collective-permute-start.17) | collective-permute-done | bytes 786464 | tf_op jit(solution)/shard_map/ppermute | solution.py:43
  121.7 1.1 pad_maximum_fusion
  122.9 3.7 %collective-permute-done.14 = bf16[512,640]{1,0:T(8,128)(2,1)S(1)} collective-permute-done((bf16[512,640]{1,0:T(8,128)(2,1)S(1)}, bf16[512,640]{1,0:T(8,128)(2,1)S(1)}, u32[]{:S(2)}, u32[]{:S(2)}) %collective-permute-start.14) | collective-permute-done | bytes 655392 | tf_op jit(solution)/shard_map/ppermute | solution.py:43
  126.6 2.2 %collective-permute-done.15 = bf16[512,640]{1,0:T(8,128)(2,1)S(1)} collective-permute-done((bf16[512,640]{1,0:T(8,128)(2,1)S(1)}, bf16[512,640]{1,0:T(8,128)(2,1)S(1)}, u32[]{:S(2)}, u32[]{:S(2)}) %collective-permute-start.15) | collective-permute-done | bytes 655392 | tf_op jit(solution)/shard_map/ppermute | solution.py:43
  129.2 2.4 %collective-permute-start.18 = (bf16[256,640]{1,0:T(8,128)(2,1)S(1)}, bf16[256,640]{1,0:T(8,128)(2,1)S(1)}, u32[]{:S(2)}, u32[]{:S(2)}) collective-permute-start(bf16[256,640]{1,0:T(8,128)(2,1)S(1)} %add_convert_fusion.6), channel_id=1, source_target_pairs={{0,48},{1,49},{2,50},{3,51},{64,112},{65,113},{66,114},{67,115},{1... | collective-permute-start | bytes 983048 | tf_op jit(solution)/shard_map/ppermute | solution.py:43
  132.4 1.2 collective-permute-start.30
  133.6 3.4 %collective-permute-done.19 = bf16[256,640]{1,0:T(8,128)(2,1)S(1)} collective-permute-done((bf16[256,640]{1,0:T(8,128)(2,1)S(1)}, bf16[256,640]{1,0:T(8,128)(2,1)S(1)}, u32[]{:S(2)}, u32[]{:S(2)}) %collective-permute-start.19) | collective-permute-done | bytes 327712 | tf_op jit(solution)/shard_map/ppermute | solution.py:43
  137.0 1.5 collective-permute-done.18
  138.8 2.0 %collective-permute-start.26 = (bf16[256,640]{1,0:T(8,128)(2,1)S(1)}, bf16[256,640]{1,0:T(8,128)(2,1)S(1)}, u32[]{:S(2)}, u32[]{:S(2)}) collective-permute-start(bf16[256,640]{1,0:T(8,128)(2,1)S(1)} %get-tuple-element.119), channel_id=1, source_target_pairs={{0,64},{1,65},{2,66},{3,67},{64,0},{65,1},{66,2},{67,3},{16,80},{1... | collective-permute-start | bytes 983048 | tf_op jit(solution)/shard_map/ppermute | solution.py:43
  141.4 2.3 %collective-permute-start.21 = (bf16[512,512]{1,0:T(8,128)(2,1)S(1)}, bf16[512,512]{1,0:T(8,128)(2,1)S(1)}, u32[]{:S(2)}, u32[]{:S(2)}) collective-permute-start(bf16[512,512]{1,0:T(8,128)(2,1)S(1)} %bitcast.78), channel_id=1, source_target_pairs={{0,48},{1,49},{2,50},{3,51},{64,112},{65,113},{66,114},{67,115},{1... | collective-permute-start | bytes 1572872 | tf_op jit(solution)/shard_map/ppermute | solution.py:43
  143.7 6.9 %pair_terms.1 = bf16[8,256,768]{2,1,0:T(8,128)(2,1)S(1)} custom-call(s32[8]{0:T(128)S(1)} %stack.121.order, bf16[256,1024]{1,0:T(8,128)(2,1)S(1)} %copy-done.27, bf16[256,1024]{1,0:T(8,128)(2,1)} %collective-permute-done.10.refs_1_, bf16[256,1792]{1,0:T(8,128)(2,1)} %collective-permute-done.7.refs_3_.refs_2_, ...), custom_call_target="tpu_custom_call" | custom-call | flops 1 | bytes 1 | tf_op jit(solution)/shard_map/pair_terms/pallas_call | solution.py:68
  151.5 1.2 collective-permute-start.33
  153.8 2.0 %collective-permute-start.25 = (bf16[256,512]{1,0:T(8,128)(2,1)S(1)}, bf16[256,512]{1,0:T(8,128)(2,1)S(1)}, u32[]{:S(2)}, u32[]{:S(2)}) collective-permute-start(bf16[256,512]{1,0:T(8,128)(2,1)S(1)} %add_convert_fusion.8), channel_id=1, source_target_pairs={{0,48},{1,49},{2,50},{3,51},{64,112},{65,113},{66,114},{67,115},{1... | collective-permute-start | bytes 786440 | tf_op jit(solution)/shard_map/ppermute | solution.py:43
  156.4 1.8 collective-permute-start.29
  158.3 1.8 collective-permute-done.29
  160.1 1.7 collective-permute-start.38
  161.8 2.0 %collective-permute-done.25 = bf16[256,512]{1,0:T(8,128)(2,1)S(1)} collective-permute-done((bf16[256,512]{1,0:T(8,128)(2,1)S(1)}, bf16[256,512]{1,0:T(8,128)(2,1)S(1)}, u32[]{:S(2)}, u32[]{:S(2)}) %collective-permute-start.25) | collective-permute-done | bytes 262176 | tf_op jit(solution)/shard_map/ppermute | solution.py:43
  164.0 1.6 collective-permute-start.27
  165.7 1.3 collective-permute-done.32
  167.0 1.4 collective-permute-done.33
  169.0 1.3 collective-permute-start.36
  170.3 1.4 collective-permute-start.34
  172.2 4.2 %collective-permute-done.34 = f32[1,512]{1,0:T(1,128)S(1)} collective-permute-done((f32[1,512]{1,0:T(1,128)S(1)}, f32[1,512]{1,0:T(1,128)S(1)}, u32[]{:S(2)}, u32[]{:S(2)}) %collective-permute-start.34) | collective-permute-done | bytes 2080 | tf_op jit(solution)/shard_map/ppermute | solution.py:43
  176.4 2.4 %collective-permute-start.35 = (f32[1,512]{1,0:T(1,128)S(1)}, f32[1,512]{1,0:T(1,128)S(1)}, u32[]{:S(2)}, u32[]{:S(2)}) collective-permute-start(f32[1,512]{1,0:T(1,128)S(1)} %add.220), channel_id=1, source_target_pairs={{0,8},{1,9},{2,10},{3,11},{64,72},{65,73},{66,74},{67,75},{16,24},... | collective-permute-start | bytes 6152 | tf_op jit(solution)/shard_map/ppermute | solution.py:43
  179.8 1.7 collective-permute-done.35
  182.4 1.1 pad_maximum_fusion.1
  (134 shorter events, 17.9 us)
Async XLA Ops:
  0.6 16.4 %copy-start.2 = (bf16[256,512]{1,0:T(8,128)(2,1)S(1)}, bf16[256,512]{1,0:T(8,128)(2,1)}, u32[]{:S(2)}) copy-start(bf16[256,512]{1,0:T(8,128)(2,1)} %cot) | copy-start | bytes 786436
  2.3 9.8 %collective-permute-start = (bf16[272,512]{1,0:T(8,128)(2,1)S(1)}, bf16[272,512]{1,0:T(8,128)(2,1)S(1)}, u32[]{:S(2)}, u32[]{:S(2)}) collective-permute-start(bf16[272,512]{1,0:T(8,128)(2,1)S(1)} %pad_maximum_fusion.7.own), channel_id=1, source_target_pairs={{0,16},{1,17},{2,18},{3,19},{64,80},{65,81},{66,82},{67,83},{16,32... | collective-permute-start | bytes 835592 | tf_op jit(solution)/shard_map/ppermute | solution.py:43
  4.1 10.3 %collective-permute-start.2 = (bf16[272,512]{1,0:T(8,128)(2,1)S(1)}, bf16[272,512]{1,0:T(8,128)(2,1)S(1)}, u32[]{:S(2)}, u32[]{:S(2)}) collective-permute-start(bf16[272,512]{1,0:T(8,128)(2,1)S(1)} %pad_maximum_fusion.7.own), channel_id=1, source_target_pairs={{0,64},{1,65},{2,66},{3,67},{64,0},{65,1},{66,2},{67,3},{16,80},{1... | collective-permute-start | bytes 835592 | tf_op jit(solution)/shard_map/ppermute | solution.py:43
  7.9 9.0 %collective-permute-start.1 = (bf16[272,512]{1,0:T(8,128)(2,1)S(1)}, bf16[272,512]{1,0:T(8,128)(2,1)S(1)}, u32[]{:S(2)}, u32[]{:S(2)}) collective-permute-start(bf16[272,512]{1,0:T(8,128)(2,1)S(1)} %pad_maximum_fusion.7.own), channel_id=1, source_target_pairs={{0,48},{1,49},{2,50},{3,51},{64,112},{65,113},{66,114},{67,115},{1... | collective-permute-start | bytes 835592 | tf_op jit(solution)/shard_map/ppermute | solution.py:43
  15.3 17.2 %collective-permute-start.3 = (bf16[656,512]{1,0:T(8,128)(2,1)S(1)}, bf16[656,512]{1,0:T(8,128)(2,1)S(1)}, u32[]{:S(2)}, u32[]{:S(2)}) collective-permute-start(bf16[656,512]{1,0:T(8,128)(2,1)S(1)} %pad_maximum_fusion.4), channel_id=1, source_target_pairs={{0,16},{1,17},{2,18},{3,19},{64,80},{65,81},{66,82},{67,83},{16,32... | collective-permute-start | bytes 2015240 | tf_op jit(solution)/shard_map/ppermute | solution.py:43
  17.7 16.0 %collective-permute-start.4 = (bf16[672,512]{1,0:T(8,128)(2,1)S(1)}, bf16[672,512]{1,0:T(8,128)(2,1)S(1)}, u32[]{:S(2)}, u32[]{:S(2)}) collective-permute-start(bf16[672,512]{1,0:T(8,128)(2,1)S(1)} %pad_maximum_fusion.3), channel_id=1, source_target_pairs={{0,48},{1,49},{2,50},{3,51},{64,112},{65,113},{66,114},{67,115},{1... | collective-permute-start | bytes 2064392 | tf_op jit(solution)/shard_map/ppermute | solution.py:43
  19.5 14.2 %collective-permute-start.5 = (bf16[256,512]{1,0:T(8,128)(2,1)S(1)}, bf16[256,512]{1,0:T(8,128)(2,1)S(1)}, u32[]{:S(2)}, u32[]{:S(2)}) collective-permute-start(bf16[256,512]{1,0:T(8,128)(2,1)S(1)} %copy-done.2), channel_id=1, source_target_pairs={{0,64},{1,65},{2,66},{3,67},{64,0},{65,1},{66,2},{67,3},{16,80},{1... | collective-permute-start | bytes 786440 | tf_op jit(solution)/shard_map/ppermute | solution.py:43
  33.8 17.4 %copy-start.7 = (bf16[256,512]{1,0:T(8,128)(2,1)}, bf16[256,512]{1,0:T(8,128)(2,1)S(1)}, u32[]{:S(2)}) copy-start(bf16[256,512]{1,0:T(8,128)(2,1)S(1)} %collective-permute-done.5.other) | copy-start | bytes 786436
  33.8 8.2 %collective-permute-start.6 = (bf16[272,512]{1,0:T(8,128)(2,1)S(1)}, bf16[272,512]{1,0:T(8,128)(2,1)}, u32[]{:S(2)}, u32[]{:S(2)}) collective-permute-start(bf16[272,512]{1,0:T(8,128)(2,1)S(1)} %pad_maximum_fusion.8), channel_id=1, source_target_pairs={{0,64},{1,65},{2,66},{3,67},{64,0},{65,1},{66,2},{67,3},{16,80},{1... | collective-permute-start | bytes 835592 | tf_op jit(solution)/shard_map/ppermute | solution.py:43
  37.8 18.2 %collective-permute-start.9 = (bf16[384,512]{1,0:T(8,128)(2,1)}, bf16[384,512]{1,0:T(8,128)(2,1)S(1)}, u32[]{:S(2)}, u32[]{:S(2)}) collective-permute-start(bf16[384,512]{1,0:T(8,128)(2,1)} %get-tuple-element.136), channel_id=1, source_target_pairs={{0,48},{1,49},{2,50},{3,51},{64,112},{65,113},{66,114},{67,115},{1... | collective-permute-start | bytes 1179656 | tf_op jit(solution)/shard_map/ppermute | solution.py:43
  40.6 15.3 %collective-permute-start.8 = (bf16[384,512]{1,0:T(8,128)(2,1)}, bf16[384,512]{1,0:T(8,128)(2,1)S(1)}, u32[]{:S(2)}, u32[]{:S(2)}) collective-permute-start(bf16[384,512]{1,0:T(8,128)(2,1)} %get-tuple-element.137), channel_id=1, source_target_pairs={{0,16},{1,17},{2,18},{3,19},{64,80},{65,81},{66,82},{67,83},{16,32... | collective-permute-start | bytes 1179656 | tf_op jit(solution)/shard_map/ppermute | solution.py:43
  42.0 1.0 copy-start.20
  43.0 1.0 copy-start.22
  52.0 0.9 copy-start.11
  52.9 0.9 copy-start.13
  55.9 18.3 %collective-permute-start.7 = (bf16[256,1792]{1,0:T(8,128)(2,1)}, bf16[256,1792]{1,0:T(8,128)(2,1)}, u32[]{:S(2)}, u32[]{:S(2)}) collective-permute-start(bf16[256,1792]{1,0:T(8,128)(2,1)} %get-tuple-element.58), channel_id=1, source_target_pairs={{0,1},{1,0},{2,3},{3,2},{64,65},{65,64},{66,67},{67,66},{16,17},{1... | collective-permute-start | bytes 2752520 | tf_op jit(solution)/shard_map/ppermute | solution.py:43
  55.9 5.6 %copy-start.15 = (bf16[384,512]{1,0:T(8,128)(2,1)}, bf16[384,512]{1,0:T(8,128)(2,1)S(1)}, u32[]{:S(2)}) copy-start(bf16[384,512]{1,0:T(8,128)(2,1)S(1)} %collective-permute-done.9.cot_down) | copy-start | bytes 1179652
  55.9 5.6 %copy-start.17 = (bf16[384,512]{1,0:T(8,128)(2,1)}, bf16[384,512]{1,0:T(8,128)(2,1)S(1)}, u32[]{:S(2)}) copy-start(bf16[384,512]{1,0:T(8,128)(2,1)S(1)} %collective-permute-done.8.cot_up) | copy-start | bytes 1179652
  55.9 16.1 %collective-permute-start.10 = (bf16[256,1024]{1,0:T(8,128)(2,1)}, bf16[256,1024]{1,0:T(8,128)(2,1)}, u32[]{:S(2)}, u32[]{:S(2)}) collective-permute-start(bf16[256,1024]{1,0:T(8,128)(2,1)} %get-tuple-element.61), channel_id=1, source_target_pairs={{0,66},{1,67},{2,64},{3,65},{64,2},{65,3},{66,0},{67,1},{16,82},{1... | collective-permute-start | bytes 1572872 | tf_op jit(solution)/shard_map/ppermute | solution.py:43
  59.1 15.1 %collective-permute-start.11 = (bf16[256,1024]{1,0:T(8,128)(2,1)}, bf16[256,1024]{1,0:T(8,128)(2,1)}, u32[]{:S(2)}, u32[]{:S(2)}) collective-permute-start(bf16[256,1024]{1,0:T(8,128)(2,1)} %get-tuple-element.62), channel_id=1, source_target_pairs={{0,2},{1,3},{2,0},{3,1},{64,66},{65,67},{66,64},{67,65},{16,18},{1... | collective-permute-start | bytes 1572872 | tf_op jit(solution)/shard_map/ppermute | solution.py:43
  59.9 19.0 %collective-permute-start.12 = (bf16[256,512]{1,0:T(8,128)(2,1)}, bf16[256,512]{1,0:T(8,128)(2,1)}, u32[]{:S(2)}, u32[]{:S(2)}) collective-permute-start(bf16[256,512]{1,0:T(8,128)(2,1)} %pad_maximum_fusion.9), channel_id=1, source_target_pairs={{0,64},{1,65},{2,66},{3,67},{64,0},{65,1},{66,2},{67,3},{16,80},{1... | collective-permute-start | bytes 786440 | tf_op jit(solution)/shard_map/ppermute | solution.py:43
  61.6 1.0 copy-start.5
  62.6 16.3 %copy-start.3 = (bf16[256,512]{1,0:T(8,128)(2,1)S(1)}, bf16[256,512]{1,0:T(8,128)(2,1)}, u32[]{:S(2)}) copy-start(bf16[256,512]{1,0:T(8,128)(2,1)} %cot) | copy-start | bytes 786436
  62.6 16.3 %copy-start.8 = (bf16[256,512]{1,0:T(8,128)(2,1)S(1)}, bf16[256,512]{1,0:T(8,128)(2,1)}, u32[]{:S(2)}) copy-start(bf16[256,512]{1,0:T(8,128)(2,1)} %copy-done.7) | copy-start | bytes 786436
  62.6 16.3 %copy-start.12 = (f32[256,768]{1,0:T(8,128)S(1)}, f32[256,768]{1,0:T(8,128)}, u32[]{:S(2)}) copy-start(f32[256,768]{1,0:T(8,128)} %copy-done.11) | copy-start | bytes 2359300
  62.6 16.3 %copy-start.14 = (f32[256,768]{1,0:T(8,128)S(1)}, f32[256,768]{1,0:T(8,128)}, u32[]{:S(2)}) copy-start(f32[256,768]{1,0:T(8,128)} %copy-done.13) | copy-start | bytes 2359300
  62.6 16.3 %copy-start.16 = (bf16[384,512]{1,0:T(8,128)(2,1)S(1)}, bf16[384,512]{1,0:T(8,128)(2,1)}, u32[]{:S(2)}) copy-start(bf16[384,512]{1,0:T(8,128)(2,1)} %copy-done.15) | copy-start | bytes 1179652
  62.6 16.3 %copy-start.18 = (bf16[384,512]{1,0:T(8,128)(2,1)S(1)}, bf16[384,512]{1,0:T(8,128)(2,1)}, u32[]{:S(2)}) copy-start(bf16[384,512]{1,0:T(8,128)(2,1)} %copy-done.17) | copy-start | bytes 1179652
  62.6 16.3 %copy-start.24 = (f32[256,128]{1,0:T(8,128)S(1)}, f32[256,128]{1,0:T(8,128)}, u32[]{:S(2)}) copy-start(f32[256,128]{1,0:T(8,128)} %copy-done.23) | copy-start | bytes 393220
  78.9 8.5 %copy-start.30 = (bf16[512]{0:T(512)(128)(2,1)S(1)}, bf16[512]{0:T(512)(128)(2,1)}, u32[]{:S(2)}) copy-start(bf16[512]{0:T(512)(128)(2,1)} %param.5) | copy-start | bytes 3076
  85.6 0.9 copy-start
  86.5 1.0 copy-start.9
  87.5 4.1 %collective-permute-start.13 = (bf16[256,3584]{1,0:T(8,128)(2,1)}, bf16[256,3584]{1,0:T(8,128)(2,1)}, u32[]{:S(2)}, u32[]{:S(2)}) collective-permute-start(bf16[256,3584]{1,0:T(8,128)(2,1)} %get-tuple-element.69), channel_id=1, source_target_pairs={{0,1},{1,0},{2,3},{3,2},{64,65},{65,64},{66,67},{67,66},{16,17},{1... | collective-permute-start | bytes 5505032 | tf_op jit(solution)/shard_map/ppermute | solution.py:43
  88.3 33.4 %collective-permute-start.22 = (bf16[256,1536]{1,0:T(8,128)(2,1)}, bf16[256,1536]{1,0:T(8,128)(2,1)S(1)}, u32[]{:S(2)}, u32[]{:S(2)}) collective-permute-start(bf16[256,1536]{1,0:T(8,128)(2,1)} %copy-done), channel_id=1, source_target_pairs={{0,2},{1,3},{2,0},{3,1},{64,66},{65,67},{66,64},{67,65},{16,18},{1... | collective-permute-start | bytes 2359304 | tf_op jit(solution)/shard_map/ppermute | solution.py:43
  91.6 1.0 copy-start.6
  92.6 1.2 copy-start.10
  99.4 3.9 %copy-start.1 = (bf16[256,1536]{1,0:T(8,128)(2,1)S(1)}, bf16[256,1536]{1,0:T(8,128)(2,1)}, u32[]{:S(2)}) copy-start(bf16[256,1536]{1,0:T(8,128)(2,1)} %copy-done) | copy-start | bytes 2359300
  99.6 19.7 %collective-permute-start.16 = (bf16[1024,384]{1,0:T(8,128)(2,1)S(1)}, bf16[1024,384]{1,0:T(8,128)(2,1)S(1)}, u32[]{:S(2)}, u32[]{:S(2)}) collective-permute-start(bf16[1024,384]{1,0:T(8,128)(2,1)S(1)} %bitcast.75), channel_id=1, source_target_pairs={{0,4},{1,5},{2,6},{3,7},{64,68},{65,69},{66,70},{67,71},{16,20},{1... | collective-permute-start | bytes 2359304 | tf_op jit(solution)/shard_map/ppermute | solution.py:43
  101.2 20.5 %collective-permute-start.17 = (bf16[1024,384]{1,0:T(8,128)(2,1)S(1)}, bf16[1024,384]{1,0:T(8,128)(2,1)S(1)}, u32[]{:S(2)}, u32[]{:S(2)}) collective-permute-start(bf16[1024,384]{1,0:T(8,128)(2,1)S(1)} %bitcast.74), channel_id=1, source_target_pairs={{0,12},{1,13},{2,14},{3,15},{64,76},{65,77},{66,78},{67,79},{16,28... | collective-permute-start | bytes 2359304 | tf_op jit(solution)/shard_map/ppermute | solution.py:43
  110.4 16.3 %collective-permute-start.14 = (bf16[512,640]{1,0:T(8,128)(2,1)S(1)}, bf16[512,640]{1,0:T(8,128)(2,1)S(1)}, u32[]{:S(2)}, u32[]{:S(2)}) collective-permute-start(bf16[512,640]{1,0:T(8,128)(2,1)S(1)} %bitcast.77), channel_id=1, source_target_pairs={{0,16},{1,17},{2,18},{3,19},{64,80},{65,81},{66,82},{67,83},{16,0}... | collective-permute-start | bytes 1966088 | tf_op jit(solution)/shard_map/ppermute | solution.py:43
  111.7 17.1 %collective-permute-start.15 = (bf16[512,640]{1,0:T(8,128)(2,1)S(1)}, bf16[512,640]{1,0:T(8,128)(2,1)S(1)}, u32[]{:S(2)}, u32[]{:S(2)}) collective-permute-start(bf16[512,640]{1,0:T(8,128)(2,1)S(1)} %bitcast.76), channel_id=1, source_target_pairs={{0,48},{1,49},{2,50},{3,51},{64,112},{65,113},{66,114},{67,115},{1... | collective-permute-start | bytes 1966088 | tf_op jit(solution)/shard_map/ppermute | solution.py:43
  122.8 18.6 %collective-permute-start.23 = (bf16[256,2560]{1,0:T(8,128)(2,1)S(1)}, bf16[256,2560]{1,0:T(8,128)(2,1)S(1)}, u32[]{:S(2)}, u32[]{:S(2)}) collective-permute-start(bf16[256,2560]{1,0:T(8,128)(2,1)S(1)} %pad_maximum_fusion), channel_id=1, source_target_pairs={{0,1},{1,0},{2,3},{3,2},{64,65},{65,64},{66,67},{67,66},{16,17},{1... | collective-permute-start | bytes 3932168 | tf_op jit(solution)/shard_map/ppermute | solution.py:43
  128.9 8.1 %collective-permute-start.19 = (bf16[256,640]{1,0:T(8,128)(2,1)S(1)}, bf16[256,640]{1,0:T(8,128)(2,1)S(1)}, u32[]{:S(2)}, u32[]{:S(2)}) collective-permute-start(bf16[256,640]{1,0:T(8,128)(2,1)S(1)} %add_convert_fusion.5), channel_id=1, source_target_pairs={{0,16},{1,17},{2,18},{3,19},{64,80},{65,81},{66,82},{67,83},{16,0}... | collective-permute-start | bytes 983048 | tf_op jit(solution)/shard_map/ppermute | solution.py:43
  129.2 9.3 %collective-permute-start.18 = (bf16[256,640]{1,0:T(8,128)(2,1)S(1)}, bf16[256,640]{1,0:T(8,128)(2,1)S(1)}, u32[]{:S(2)}, u32[]{:S(2)}) collective-permute-start(bf16[256,640]{1,0:T(8,128)(2,1)S(1)} %add_convert_fusion.6), channel_id=1, source_target_pairs={{0,48},{1,49},{2,50},{3,51},{64,112},{65,113},{66,114},{67,115},{1... | collective-permute-start | bytes 983048 | tf_op jit(solution)/shard_map/ppermute | solution.py:43
  131.7 19.0 %collective-permute-start.31 = (bf16[512,384]{1,0:T(8,128)(2,1)S(1)}, bf16[512,384]{1,0:T(8,128)(2,1)S(1)}, u32[]{:S(2)}, u32[]{:S(2)}) collective-permute-start(bf16[512,384]{1,0:T(8,128)(2,1)S(1)} %add_convert_fusion.3), channel_id=1, source_target_pairs={{0,4},{1,5},{2,6},{3,7},{64,68},{65,69},{66,70},{67,71},{16,20},{1... | collective-permute-start | bytes 1179656 | tf_op jit(solution)/shard_map/ppermute | solution.py:43
  132.4 18.3 %collective-permute-start.30 = (bf16[512,384]{1,0:T(8,128)(2,1)S(1)}, bf16[512,384]{1,0:T(8,128)(2,1)S(1)}, u32[]{:S(2)}, u32[]{:S(2)}) collective-permute-start(bf16[512,384]{1,0:T(8,128)(2,1)S(1)} %add_convert_fusion.4), channel_id=1, source_target_pairs={{0,12},{1,13},{2,14},{3,15},{64,76},{65,77},{66,78},{67,79},{16,28... | collective-permute-start | bytes 1179656 | tf_op jit(solution)/shard_map/ppermute | solution.py:43
  138.8 13.9 %collective-permute-start.26 = (bf16[256,640]{1,0:T(8,128)(2,1)S(1)}, bf16[256,640]{1,0:T(8,128)(2,1)S(1)}, u32[]{:S(2)}, u32[]{:S(2)}) collective-permute-start(bf16[256,640]{1,0:T(8,128)(2,1)S(1)} %get-tuple-element.119), channel_id=1, source_target_pairs={{0,64},{1,65},{2,66},{3,67},{64,0},{65,1},{66,2},{67,3},{16,80},{1... | collective-permute-start | bytes 983048 | tf_op jit(solution)/shard_map/ppermute | solution.py:43
  140.8 2.9 %copy-start.27 = (bf16[256,1024]{1,0:T(8,128)(2,1)S(1)}, bf16[256,1024]{1,0:T(8,128)(2,1)}, u32[]{:S(2)}) copy-start(bf16[256,1024]{1,0:T(8,128)(2,1)} %copy-done.26) | copy-start | bytes 1572868
  140.9 12.8 %collective-permute-start.20 = (bf16[512,512]{1,0:T(8,128)(2,1)S(1)}, bf16[512,512]{1,0:T(8,128)(2,1)S(1)}, u32[]{:S(2)}, u32[]{:S(2)}) collective-permute-start(bf16[512,512]{1,0:T(8,128)(2,1)S(1)} %bitcast.79), channel_id=1, source_target_pairs={{0,16},{1,17},{2,18},{3,19},{64,80},{65,81},{66,82},{67,83},{16,0}... | collective-permute-start | bytes 1572872 | tf_op jit(solution)/shard_map/ppermute | solution.py:43
  141.4 12.3 %collective-permute-start.21 = (bf16[512,512]{1,0:T(8,128)(2,1)S(1)}, bf16[512,512]{1,0:T(8,128)(2,1)S(1)}, u32[]{:S(2)}, u32[]{:S(2)}) collective-permute-start(bf16[512,512]{1,0:T(8,128)(2,1)S(1)} %bitcast.78), channel_id=1, source_target_pairs={{0,48},{1,49},{2,50},{3,51},{64,112},{65,113},{66,114},{67,115},{1... | collective-permute-start | bytes 1572872 | tf_op jit(solution)/shard_map/ppermute | solution.py:43
  150.8 1.9 %copy-start.25 = (f32[256,128]{1,0:T(8,128)S(1)}, f32[256,128]{1,0:T(8,128)}, u32[]{:S(2)}) copy-start(f32[256,128]{1,0:T(8,128)} %copy-done.23) | copy-start | bytes 393220
  150.8 2.0 %copy-start.29 = (bf16[256,512]{1,0:T(8,128)(2,1)S(1)}, bf16[256,512]{1,0:T(8,128)(2,1)}, u32[]{:S(2)}) copy-start(bf16[256,512]{1,0:T(8,128)(2,1)} %param.4) | copy-start | bytes 786436
  150.8 16.1 %collective-permute-start.32 = (bf16[512,768]{1,0:T(8,128)(2,1)S(1)}, bf16[512,768]{1,0:T(8,128)(2,1)S(1)}, u32[]{:S(2)}, u32[]{:S(2)}) collective-permute-start(bf16[512,768]{1,0:T(8,128)(2,1)S(1)} %bitcast.73), channel_id=1, source_target_pairs={{0,4},{1,5},{2,6},{3,7},{64,68},{65,69},{66,70},{67,71},{16,20},{1... | collective-permute-start | bytes 2359304 | tf_op jit(solution)/shard_map/ppermute | solution.py:43
  151.5 17.0 %collective-permute-start.33 = (bf16[512,768]{1,0:T(8,128)(2,1)S(1)}, bf16[512,768]{1,0:T(8,128)(2,1)S(1)}, u32[]{:S(2)}, u32[]{:S(2)}) collective-permute-start(bf16[512,768]{1,0:T(8,128)(2,1)S(1)} %bitcast.72), channel_id=1, source_target_pairs={{0,12},{1,13},{2,14},{3,15},{64,76},{65,77},{66,78},{67,79},{16,28... | collective-permute-start | bytes 2359304 | tf_op jit(solution)/shard_map/ppermute | solution.py:43
  153.7 2.6 %collective-permute-start.28 = (f32[1,512]{1,0:T(1,128)S(1)}, f32[1,512]{1,0:T(1,128)S(1)}, u32[]{:S(2)}, u32[]{:S(2)}) collective-permute-start(f32[1,512]{1,0:T(1,128)S(1)} %bitcast.80), channel_id=1, source_target_pairs={{0,1},{1,0},{2,3},{3,2},{64,65},{65,64},{66,67},{67,66},{16,17},{1... | collective-permute-start | bytes 6152 | tf_op jit(solution)/shard_map/ppermute | solution.py:43
  153.8 10.0 %collective-permute-start.25 = (bf16[256,512]{1,0:T(8,128)(2,1)S(1)}, bf16[256,512]{1,0:T(8,128)(2,1)S(1)}, u32[]{:S(2)}, u32[]{:S(2)}) collective-permute-start(bf16[256,512]{1,0:T(8,128)(2,1)S(1)} %add_convert_fusion.8), channel_id=1, source_target_pairs={{0,48},{1,49},{2,50},{3,51},{64,112},{65,113},{66,114},{67,115},{1... | collective-permute-start | bytes 786440 | tf_op jit(solution)/shard_map/ppermute | solution.py:43
  155.9 7.9 %collective-permute-start.24 = (bf16[256,512]{1,0:T(8,128)(2,1)S(1)}, bf16[256,512]{1,0:T(8,128)(2,1)S(1)}, u32[]{:S(2)}, u32[]{:S(2)}) collective-permute-start(bf16[256,512]{1,0:T(8,128)(2,1)S(1)} %add_convert_fusion.9), channel_id=1, source_target_pairs={{0,16},{1,17},{2,18},{3,19},{64,80},{65,81},{66,82},{67,83},{16,0}... | collective-permute-start | bytes 786440 | tf_op jit(solution)/shard_map/ppermute | solution.py:43
  156.4 3.7 %collective-permute-start.29 = (f32[1,512]{1,0:T(1,128)S(1)}, f32[1,512]{1,0:T(1,128)S(1)}, u32[]{:S(2)}, u32[]{:S(2)}) collective-permute-start(f32[1,512]{1,0:T(1,128)S(1)} %add.214), channel_id=1, source_target_pairs={{0,2},{1,3},{2,0},{3,1},{64,66},{65,67},{66,64},{67,65},{16,18},{1... | collective-permute-start | bytes 6152 | tf_op jit(solution)/shard_map/ppermute | solution.py:43
  160.1 12.1 %collective-permute-start.38 = (bf16[256,768]{1,0:T(8,128)(2,1)S(1)}, bf16[256,768]{1,0:T(8,128)(2,1)S(1)}, u32[]{:S(2)}, u32[]{:S(2)}) collective-permute-start(bf16[256,768]{1,0:T(8,128)(2,1)S(1)} %select_convert_fusion), channel_id=1, source_target_pairs={{0,2},{1,3},{2,0},{3,1},{64,66},{65,67},{66,64},{67,65},{16,18},{1... | collective-permute-start | bytes 1179656 | tf_op jit(solution)/shard_map/ppermute | solution.py:43
  164.0 14.8 %collective-permute-start.27 = (bf16[256,512]{1,0:T(8,128)(2,1)S(1)}, bf16[256,512]{1,0:T(8,128)(2,1)S(1)}, u32[]{:S(2)}, u32[]{:S(2)}) collective-permute-start(bf16[256,512]{1,0:T(8,128)(2,1)S(1)} %select_convert_fusion.2), channel_id=1, source_target_pairs={{0,64},{1,65},{2,66},{3,67},{64,0},{65,1},{66,2},{67,3},{16,80},{1... | collective-permute-start | bytes 786440 | tf_op jit(solution)/shard_map/ppermute | solution.py:43
  168.5 13.6 %collective-permute-start.37 = (bf16[256,768]{1,0:T(8,128)(2,1)S(1)}, bf16[256,768]{1,0:T(8,128)(2,1)S(1)}, u32[]{:S(2)}, u32[]{:S(2)}) collective-permute-start(bf16[256,768]{1,0:T(8,128)(2,1)S(1)} %add_convert_fusion.1), channel_id=1, source_target_pairs={{0,4},{1,5},{2,6},{3,7},{64,68},{65,69},{66,70},{67,71},{16,20},{1... | collective-permute-start | bytes 1179656 | tf_op jit(solution)/shard_map/ppermute | solution.py:43
  169.0 13.1 %collective-permute-start.36 = (bf16[256,768]{1,0:T(8,128)(2,1)S(1)}, bf16[256,768]{1,0:T(8,128)(2,1)S(1)}, u32[]{:S(2)}, u32[]{:S(2)}) collective-permute-start(bf16[256,768]{1,0:T(8,128)(2,1)S(1)} %add_convert_fusion.2), channel_id=1, source_target_pairs={{0,12},{1,13},{2,14},{3,15},{64,76},{65,77},{66,78},{67,79},{16,28... | collective-permute-start | bytes 1179656 | tf_op jit(solution)/shard_map/ppermute | solution.py:43
  170.3 6.1 %collective-permute-start.34 = (f32[1,512]{1,0:T(1,128)S(1)}, f32[1,512]{1,0:T(1,128)S(1)}, u32[]{:S(2)}, u32[]{:S(2)}) collective-permute-start(f32[1,512]{1,0:T(1,128)S(1)} %add.215), channel_id=1, source_target_pairs={{0,4},{1,5},{2,6},{3,7},{64,68},{65,69},{66,70},{67,71},{16,20},{1... | collective-permute-start | bytes 6152 | tf_op jit(solution)/shard_map/ppermute | solution.py:43
  176.4 5.1 %collective-permute-start.35 = (f32[1,512]{1,0:T(1,128)S(1)}, f32[1,512]{1,0:T(1,128)S(1)}, u32[]{:S(2)}, u32[]{:S(2)}) collective-permute-start(f32[1,512]{1,0:T(1,128)S(1)} %add.220), channel_id=1, source_target_pairs={{0,8},{1,9},{2,10},{3,11},{64,72},{65,73},{66,74},{67,75},{16,24},... | collective-permute-start | bytes 6152 | tf_op jit(solution)/shard_map/ppermute | solution.py:43
  (6 other events, 4.3 us)

commit v4 on v3

--- a/solution.py
+++ b/solution.py
@@ -63,8 +63,8 @@
     return lax.dot_general(a, b, (((0,), (0,)), ((), ())), preferred_element_type=f32)
 
 
-def call(body, name, shapes, scratch, limit, args, hbm=()):
-    spaces = [pltpu.SMEM] + [pltpu.HBM if i in hbm else pltpu.VMEM for i in range(1, len(args))]
+def call(body, name, shapes, scratch, limit, flops, size, args, hbm=(), scalars=1):
+    spaces = [pltpu.SMEM] * scalars + [pltpu.HBM if i in hbm else pltpu.VMEM for i in range(scalars, len(args))]
     return pl.pallas_call(
         body,
         in_specs=[pl.BlockSpec(memory_space=space) for space in spaces],
@@ -72,7 +72,7 @@
         out_shape=[jax.ShapeDtypeStruct(shape, dtype) for shape, dtype in shapes],
         scratch_shapes=scratch,
         compiler_params=pltpu.CompilerParams(vmem_limit_bytes=limit * MiB),
-        cost_estimate=pl.CostEstimate(flops=1, bytes_accessed=1, transcendentals=0),
+        cost_estimate=pl.CostEstimate(flops=flops, bytes_accessed=size, transcendentals=0),
         name=name,
     )(*args)
 
@@ -95,10 +95,8 @@
     return copies
 
 
-def forward_body(spot, own, below, above, other, up2, down2, other_far, w, gate, up, hidden, inv, gains, keep, core_out,
-                 z_out, cross_out, buf, held, sems):
-    copies = fetch(w, held, sems, 0, 2, lambda k: k)
-    put(buf, spot, [
+def assemble_body(spot, own, below, above, other, up2, down2, other_far, full, keep, core_out, z_out, cross_out):
+    put(full, spot, [
         (0, 0, 0, own, 0, 272), (0, 3, 0, below, 0, 272), (0, 1, 0, above, 0, 272), (1, 0, 0, other, 0, 272),
         (0, 2, 0, up2, 0, 128), (1, 3, 0, up2, 128, 272), (0, 2, 128, down2, 0, 144), (1, 1, 0, down2, 144, 272),
         (1, 2, 0, other_far, 0, 272),
@@ -107,15 +105,23 @@
     for i in range(4):
         for ref, zl, c in ((keep, z_lo, core), (core_out, z_lo, 1 - core), (z_out, 1 - z_lo, core),
                            (cross_out, 1 - z_lo, 1 - core)):
-            ref[:, i * 256:(i + 1) * 256] = buf[0:256, lane((2 * i + zl) * 512 + c * 256, 256, 256)]
-    gains[...] = buf[256:272, :]
+            ref[:, i * 256:(i + 1) * 256] = full[0:256, lane((2 * i + zl) * 512 + c * 256, 256, 256)]
+
+
+def assemble(spot, pieces):
+    shapes = [((272, 4096), bf16)] + [((256, 1024), bf16)] * 4
+    return call(assemble_body, "assemble", shapes, [], 4, 0, 8 * MiB, (spot, *pieces))
+
+
+def forward_body(x_ref, x_core, w, gate, up, hidden, inv, core_out, held, sems):
+    copies = fetch(w, held, sems, 0, 2, lambda k: k)
     squares = jnp.zeros((256, 1), f32)
     for k in range(8):
         copies[k].wait()
         cols = slice(k * 512, (k + 1) * 512)
-        x = buf[0:256, cols].astype(f32)
+        x = x_ref[0:256, cols].astype(f32)
         squares = squares + jnp.sum(x * x, axis=1, keepdims=True)
-        scaled = (x * buf[256:272, cols][0:1].astype(f32)).astype(bf16)
+        scaled = (x * x_ref[256:272, cols][0:1].astype(f32)).astype(bf16)
         for ref, j in ((gate, 0), (up, 1)):
             value = dot(scaled, held[k, j])
             ref[...] = value if k == 0 else ref[...] + value
@@ -125,25 +131,25 @@
     gate[...] = g
     up[...] = u
     hidden[...] = (g * jax.nn.sigmoid(g) * u).astype(bf16)
+    core_out[:, 0:1024] = x_core[...]
     core_out[:, 1024:1792] = hidden[...]
     inv[...] = jnp.broadcast_to(inv_rms, (256, 128))
 
 
-def forward(spot, pieces, w3):
-    shapes = [((256, 768), f32), ((256, 768), f32), ((256, 768), bf16), ((256, 128), f32), ((16, 4096), bf16)]
-    shapes += [((256, 1024), bf16), ((256, 1792), bf16), ((256, 1024), bf16), ((256, 1024), bf16)]
-    scratch = [pltpu.VMEM((272, 4096), bf16), pltpu.VMEM((8, 2, 512, 768), bf16), pltpu.SemaphoreType.DMA((8,))]
-    return call(forward_body, "forward", shapes, scratch, 20,
-                (spot, *pieces, w3), hbm=(len(pieces) + 1,))
-
-
-def backward_body(spot, cot, up, down, other, cot_up, cot_down, far, w, gate, up_val, inv, pair, products, mine,
-                  core_out, buf, acc, held, sems):
+def forward(x_full, x_core, w3):
+    shapes = [((256, 768), f32), ((256, 768), f32), ((256, 768), bf16), ((256, 128), f32), ((256, 1792), bf16)]
+    scratch = [pltpu.VMEM((8, 2, 512, 768), bf16), pltpu.SemaphoreType.DMA((8,))]
+    return call(forward_body, "forward", shapes, scratch, 18, 2 * 256 * 4096 * 1536, 16 * MiB,
+                (x_full, x_core, w3), hbm=(2,), scalars=0)
+
+
+def backward_body(spot, both, below, above, low, high, w, gate, up_val, inv, pair, products, mine, core_out, buf, acc,
+                  held, sems):
     copies = fetch(w, held, sems, 2, 1, lambda k: k)
     put(buf, spot, [
-        (0, 0, 0, cot, 0, 256), (0, 3, 0, up, 400, 256), (0, 1, 0, down, 416, 256), (1, 0, 0, other, 0, 256),
-        (0, 2, 0, cot_up, 0, 128), (1, 3, 0, cot_up, 128, 256), (0, 2, 128, cot_down, 0, 128),
-        (1, 1, 0, cot_down, 128, 256), (1, 2, 0, far, 0, 256),
+        (0, 0, 0, both, 0, 256), (1, 0, 0, both, 256, 256), (0, 3, 0, below, 0, 256), (1, 3, 0, below, 256, 256),
+        (0, 1, 0, above, 0, 256), (1, 1, 0, above, 256, 256), (0, 2, 0, low, 0, 128), (1, 2, 0, low, 128, 128),
+        (0, 2, 128, high, 0, 128), (1, 2, 128, high, 128, 128),
     ])
     core = spot[9]
     for i in range(8):
@@ -170,7 +176,7 @@
     shapes = [((256, 1536), bf16), ((256, 128), bf16), ((256, 2048), bf16), ((256, 3584), bf16)]
     scratch = [pltpu.VMEM((256, 4096), bf16), pltpu.VMEM((256, 768), f32), pltpu.VMEM((8, 1, 512, 768), bf16),
                pltpu.SemaphoreType.DMA((8,))]
-    return call(backward_body, "backward", shapes, scratch, 15, (spot, *pieces, w3, gate, up, inv),
+    return call(backward_body, "backward", shapes, scratch, 15, 2 * 256 * 4096 * 768, 8 * MiB, (spot, *pieces, w3, gate, up, inv),
                 hbm=(len(pieces) + 1,))
 
 
@@ -191,7 +197,8 @@
 
 def outer(name, order, a_list, b_list, rows, cols):
     body = functools.partial(outer_body, [f for _, f in a_list], [f for _, f in b_list], rows, cols)
-    return call(body, name, [((8, rows, cols), bf16)], [], 10, (order, *[a for a, _ in a_list], *[b for b, _ in b_list]))[0]
+    flops = 2 * 256 * len(a_list) * rows * 8 * cols
+    return call(body, name, [((8, rows, cols), bf16)], [], 10, flops, 8 * MiB, (order, *[a for a, _ in a_list], *[b for b, _ in b_list]))[0]
 
 
 def branch_rows_body(order, hidden, w, out, held, sems):
@@ -203,7 +210,7 @@
 
 def branch_rows(order, hidden, w3):
     scratch = [pltpu.VMEM((8, 1, 512, 768), bf16), pltpu.SemaphoreType.DMA((8,))]
-    return call(branch_rows_body, "branch_rows", [((8, 256, 512), bf16)], scratch, 8,
+    return call(branch_rows_body, "branch_rows", [((8, 256, 512), bf16)], scratch, 8, 2 * 256 * 768 * 4096, 8 * MiB,
                 (order, hidden, w3), hbm=(2,))[0]
 
 
@@ -218,18 +225,24 @@
 
 def pair_rows(order, pair, products, w3):
     scratch = [pltpu.VMEM((8, 2, 512, 768), bf16), pltpu.SemaphoreType.DMA((8,))]
-    return call(pair_rows_body, "pair_rows", [((8, 256, 640), bf16)], scratch, 15,
+    return call(pair_rows_body, "pair_rows", [((8, 256, 640), bf16)], scratch, 15, 2 * 256 * 1536 * 4096, 16 * MiB,
                 (order, pair, products, w3), hbm=(3,))[0]
 
 
-def halve(terms, axis, done=()):
-    rows, cols = terms.shape[1:]
-    near, far = axis + "^1", axis + "^3"
-    got = [send(terms[4 * h:4 * h + 2].reshape(2 * rows, cols), move) for h, move in ((0, near), (1, far))]
+def first_two(terms):
+    return [terms[4 * h:4 * h + 2].reshape(2 * terms.shape[1], terms.shape[2]) for h in (0, 1)]
+
+
+def second_step(terms, got, axis, done=()):
+    rows = terms.shape[1]
     two, six, *got = lax.optimization_barrier((terms[2], terms[6], *got, *done))[:4]
     out = [(t.astype(f32) + g[rows:].astype(f32)).astype(bf16) for t, g in zip((two, six), got)]
-    last = [send(o, move) for o, move in zip(out, (far, near))]
-    return got, out, last
+    return out, [send(o, axis + move) for o, move in zip(out, ("^3", "^1"))]
+
+
+def halve(terms, axis, done=()):
+    got = [send(value, axis + move) for value, move in zip(first_two(terms), ("^1", "^3"))]
+    return (got, *second_step(terms, got, axis, done))
 
 
 def finish(terms, got, last, done=()):
@@ -240,14 +253,15 @@
 
 def gather_both(own, cot):
     below, above, other = send(own, "y+"), send(own, "y-"), send(own, "z+2")
-    up = send(rows_cat(below[:128], other, cot), "y+")
-    down = send(rows_cat(above[128:], other, cot), "y-")
+    up = send(rows_cat(below[:128], other), "y+")
+    down = send(rows_cat(above[128:], other), "y-")
     cot_other = send(after(cot, other), "z+2")
     other_far = send(after(rows_cat(up[:128], down[:144]), cot_other), "z+2")
-    cot_up = send(rows_cat(up[400:528], cot_other), "y+")
-    cot_down = send(rows_cat(down[544:], cot_other), "y-")
-    cot_far = send(rows_cat(cot_up[:128], cot_down[:128]), "z+2")
-    return (own, below, above, other, up, down, other_far), (cot, up, down, cot_other, cot_up, cot_down, cot_far)
+    both = after(rows_cat(cot, cot_other), up, down)
+    cot_below, cot_above = send(both, "y+"), send(both, "y-")
+    low = send(rows_cat(cot_below[:128], cot_below[256:384]), "y+")
+    high = send(rows_cat(cot_above[128:256], cot_above[384:]), "y-")
+    return (own, below, above, other, up, down, other_far), (both, cot_below, cot_above, low, high)
 
 
 def local(inputs, gain, weights, d_out):
@@ -265,19 +279,21 @@
 
     own = rows_cat(inputs, jnp.broadcast_to(gain.reshape(1, 512), (16, 512)))
     x_pieces, cot_pieces = gather_both(own, d_out)
-    gate, up_val, hidden, inv, gains, x_keep, core_one, x_same, x_cross = forward(spot, x_pieces, w3)
-    x_same, x_cross = lax.optimization_barrier((x_same, x_cross, *cot_pieces[4:6]))[:2]
+    x_full, x_keep, x_core, x_same, x_cross = assemble(spot, x_pieces)
     x_same, x_cross = send(x_same, "z^3"), send(x_cross, "z^1")
+    gate, up_val, hidden, inv, core_one = forward(after(x_full, *cot_pieces[1:3]), x_core, w3)
     core_one = send(core_one, "c")
-    branch_terms = branch_rows(order(y), hidden, w3)
-    cot_pieces = (after(cot_pieces[0], core_one, x_same, x_cross, branch_terms), *cot_pieces[1:])
+    cot_pieces = (after(cot_pieces[0], x_same, x_cross), *cot_pieces[1:])
     d_pair, products, cot_mine, core_two = backward(spot, cot_pieces, w3, gate, up_val, inv)
     core_two = send(core_two, "c")
+    branch_terms = branch_rows(order(y), after(hidden, d_pair), w3)
     pair_z = send(d_pair, "z^1")
-    down_terms = outer("down_terms", order(x), [(cot_mine, 0), (core_two, 0)], [(hidden, 0), (core_one, 1024)], 512, 384)
+    down_terms = outer("down_terms", order(x), [(after(cot_mine, branch_terms), 0), (core_two, 0)], [(hidden, 0), (core_one, 1024)], 512, 384)
+    branch_got = [send(value, move) for value, move in zip(first_two(branch_terms), ("y^1", "y^3"))]
+    d_terms = pair_rows(order(y), after(d_pair, down_terms, *branch_got), products, w3)
     down_got, _, down_last = halve(down_terms, "x")
-    d_terms = pair_rows(order(y), after(d_pair, down_terms), products, w3)
-    core_three = send(jnp.concatenate([x_cross, after(pair_z, *down_got)], axis=1), "c")
+    d_got, _, d_last = halve(d_terms, "y", down_got)
+    core_three = send(jnp.concatenate([x_cross, after(pair_z, *down_got, *d_got)], axis=1), "c")
     pair_terms = outer(
         "pair_terms", order(x), [(x_keep, 0), (x_same, 0), (core_one, 0), (core_three, 0)],
         [(d_pair, 0), (pair_z, 0), (core_two, 2048), (core_three, 1024)], 256, 768,
@@ -291,10 +307,9 @@
     theirs = jnp.where(lower, d_w_down[256:], d_w_down[:256]).astype(bf16)
     d_w_down = jnp.where(lower, d_w_down[:256], d_w_down[256:]) + send(theirs, "z^1").astype(f32)
 
-    d_got, _, d_last = halve(d_terms, "y", down_got)
+    d_last = lax.optimization_barrier((*d_last, pair_terms))[:2]
     d_low, d_high = finish(d_terms, d_got, d_last)
-    branch_terms = after(branch_terms, *d_last)
-    branch_got, _, branch_last = halve(branch_terms, "y", (pair_terms,))
+    _, branch_last = second_step(branch_terms, branch_got, "y", (pair_terms, *d_last))
     low, high = finish(branch_terms, branch_got, branch_last)
     upper = z_hi == 1
     mine = jnp.where(upper, d_high, d_low)
@@ -312,7 +327,7 @@
             d_gain = after(d_gain, *pair_out)
         d_gain = d_gain + send(d_gain, move)
 
-    gain_rows = lax.dynamic_slice(gains, (0, s * 256), (1, 256)).astype(f32).reshape(256, 1)
+    gain_rows = lax.dynamic_slice(x_full, (256, s * 256), (1, 256)).astype(f32).reshape(256, 1)
     d_weights = jnp.stack(
         [(d_w_gate * gain_rows).astype(bf16), (d_w_up * gain_rows).astype(bf16), d_w_down.astype(bf16)], axis=1
     )

time: 184 us -> 181 us (0.984)
  other arithmetic: 11.2 us -> 19.7 us
  starting transfers between devices: 55.1 us -> 46.9 us
  waiting for transfers between devices: 62.5 us -> 56.4 us
  local copies, waits for them, and re-layouts: 15.1 us -> 19.6 us
  Pallas kernels: 38.6 us -> 36.4 us
    ppermute x39 -> x40, starting transfers between devices: 55.1 us -> 46.9 us  [send(): return lax.ppermute(value, AXES, pairs(moves[move]))]
    ppermute x39 -> x40, waiting for transfers between devices: 62.5 us -> 56.4 us  [send(): return lax.ppermute(value, AXES, pairs(moves[move]))]
    convert_element_type x8, other arithmetic: 0.68 us -> 6.7 us  [second_step(): (t.astype(f32) + g[rows:].astype(f32)).astype(bf16)]
    slice x10 -> x8, local copies, waits for them, and re-layouts: 0.51 us -> 3.71 us  [the longest x4 3.65 us: first_two(): terms[4 * h:4 * h + 2].reshape(2 * terms.shape[1], terms.shape[2])]
    pallas_call x6 -> x7, Pallas kernels: 38.6 us -> 36.4 us  [call(): pl.pallas_call(body, in_specs=[pl.BlockSpec(memory_space=space) for space...]
    concatenate x6 -> x7, other arithmetic: 3.72 us -> 1.83 us  [rows_cat(): return jnp.concatenate(parts, axis=0)]
    unnamed x62 -> x56, local copies, waits for them, and re-layouts: 13.1 us -> 13.1 us
  transfers between devices with their start and end apart: 39 -> 40, of which waited for: 22 -> 18; matrix products, arithmetic and copies ran while one was open for 5% -> 11% of each run, Pallas kernels for 17% -> 17%
where the time goes in v4:
time: 181 us; the launch traced here: 180 us
  waiting for transfers between devices  56.4 us (31%)
  starting transfers between devices  46.9 us (26%)
  Pallas kernels  36.4 us (20%)
  other arithmetic  19.7 us (11%)
  local copies, waits for them, and re-layouts  19.6 us (11%)
    ppermute x40, waiting for transfers between devices, send(): return lax.ppermute(value, AXES, pairs(moves[move]))  56.4 us
    ppermute x40, starting transfers between devices, send(): return lax.ppermute(value, AXES, pairs(moves[move]))  46.9 us
    pallas_call x7, Pallas kernels, call(): pl.pallas_call(body, in_specs=[pl.BlockSpec(memory_space=space) for space...  36.4 us
    unnamed x56, local copies, waits for them, and re-layouts  13.1 us
    convert_element_type x8, other arithmetic, second_step(): (t.astype(f32) + g[rows:].astype(f32)).astype(bf16)  6.7 us
    slice x4, local copies, waits for them, and re-layouts, first_two(): terms[4 * h:4 * h + 2].reshape(2 * terms.shape[1], terms.shape[2])  3.65 us
  transfers between devices with their start and end apart: 40, of which 18 were waited for; matrix products, arithmetic and copies ran while one was open for 11% of the time, Pallas kernels for 17%

profile of v4, /device:TPU:0, one launch (start us, length us, event | category | flops | bytes accessed | tf_op | source)
XLA Modules:
  0.0 180.2 jit_solution(4876523514200524453)
XLA Ops:
  2.3 3.2 %collective-permute-start.1 = (bf16[272,512]{1,0:T(8,128)(2,1)S(1)}, bf16[272,512]{1,0:T(8,128)(2,1)S(1)}, u32[]{:S(2)}, u32[]{:S(2)}) collective-permute-start(bf16[272,512]{1,0:T(8,128)(2,1)S(1)} %pad_maximum_fusion.6.own), channel_id=1, source_target_pairs={{0,48},{1,49},{2,50},{3,51},{64,112},{65,113},{66,114},{67,115},{1... | collective-permute-start | bytes 835592 | tf_op jit(solution)/shard_map/ppermute | solution.py:43
  5.5 3.9 %collective-permute-start.2 = (bf16[272,512]{1,0:T(8,128)(2,1)S(1)}, bf16[272,512]{1,0:T(8,128)(2,1)S(1)}, u32[]{:S(2)}, u32[]{:S(2)}) collective-permute-start(bf16[272,512]{1,0:T(8,128)(2,1)S(1)} %pad_maximum_fusion.6.own), channel_id=1, source_target_pairs={{0,64},{1,65},{2,66},{3,67},{64,0},{65,1},{66,2},{67,3},{16,80},{1... | collective-permute-start | bytes 835592 | tf_op jit(solution)/shard_map/ppermute | solution.py:43
  9.4 2.0 %collective-permute-done.1.above = bf16[272,512]{1,0:T(8,128)(2,1)S(1)} collective-permute-done((bf16[272,512]{1,0:T(8,128)(2,1)S(1)}, bf16[272,512]{1,0:T(8,128)(2,1)S(1)}, u32[]{:S(2)}, u32[]{:S(2)}) %collective-permute-start.1) | collective-permute-done | bytes 278560 | tf_op jit(solution)/shard_map/ppermute | solution.py:43
  11.4 4.3 %collective-permute-done.2.other = bf16[272,512]{1,0:T(8,128)(2,1)S(1)} collective-permute-done((bf16[272,512]{1,0:T(8,128)(2,1)S(1)}, bf16[272,512]{1,0:T(8,128)(2,1)S(1)}, u32[]{:S(2)}, u32[]{:S(2)}) %collective-permute-start.2) | collective-permute-done | bytes 278560 | tf_op jit(solution)/shard_map/ppermute | solution.py:43
  16.6 1.8 %collective-permute-done.below = bf16[272,512]{1,0:T(8,128)(2,1)S(1)} collective-permute-done((bf16[272,512]{1,0:T(8,128)(2,1)S(1)}, bf16[272,512]{1,0:T(8,128)(2,1)S(1)}, u32[]{:S(2)}, u32[]{:S(2)}) %collective-permute-start) | collective-permute-done | bytes 278560 | tf_op jit(solution)/shard_map/ppermute | solution.py:43
  18.6 2.7 %collective-permute-start.5 = (bf16[256,512]{1,0:T(8,128)(2,1)S(1)}, bf16[256,512]{1,0:T(8,128)(2,1)S(1)}, u32[]{:S(2)}, u32[]{:S(2)}) collective-permute-start(bf16[256,512]{1,0:T(8,128)(2,1)S(1)} %copy-done.26), channel_id=1, source_target_pairs={{0,64},{1,65},{2,66},{3,67},{64,0},{65,1},{66,2},{67,3},{16,80},{1... | collective-permute-start | bytes 786440 | tf_op jit(solution)/shard_map/ppermute | solution.py:43
  21.3 5.5 %collective-permute-done.5 = bf16[256,512]{1,0:T(8,128)(2,1)S(1)} collective-permute-done((bf16[256,512]{1,0:T(8,128)(2,1)S(1)}, bf16[256,512]{1,0:T(8,128)(2,1)S(1)}, u32[]{:S(2)}, u32[]{:S(2)}) %collective-permute-start.5) | collective-permute-done | bytes 262176 | tf_op jit(solution)/shard_map/ppermute | solution.py:43
  26.8 2.7 %collective-permute-done.3.up2 = bf16[400,512]{1,0:T(8,128)(2,1)S(1)} collective-permute-done((bf16[400,512]{1,0:T(8,128)(2,1)S(1)}, bf16[400,512]{1,0:T(8,128)(2,1)S(1)}, u32[]{:S(2)}, u32[]{:S(2)}) %collective-permute-start.3) | collective-permute-done | bytes 409632 | tf_op jit(solution)/shard_map/ppermute | solution.py:43
  30.6 1.6 collective-permute-start.6
  32.2 1.5 collective-permute-start.7
  33.8 5.1 %collective-permute-done.6.other_far = bf16[272,512]{1,0:T(8,128)(2,1)} collective-permute-done((bf16[272,512]{1,0:T(8,128)(2,1)}, bf16[272,512]{1,0:T(8,128)(2,1)}, u32[]{:S(2)}, u32[]{:S(2)}) %collective-permute-start.6) | collective-permute-done | bytes 278560 | tf_op jit(solution)/shard_map/ppermute | solution.py:43
  38.9 1.4 assemble.1
  41.2 1.8 collective-permute-start.9
  45.3 6.3 %forward.1 = (f32[256,768]{1,0:T(8,128)S(1)}, f32[256,768]{1,0:T(8,128)S(1)}, bf16[256,768]{1,0:T(8,128)(2,1)S(1)}, f32[256,128]{1,0:T(8,128)S(1)}, bf16[256,1792]{1,0:T(8,128)(2,1)}) custom-call(bf16[272,4096]{1,0:T(8,128)(2,1)S(1)} %get-tuple-element.63.x_ref, bf16[256,1024]{1,0:T(8,128)(2,1)S(1)} %get-tuple-element.64.x_core, bf16[3,4096,768]{2,1,0:T(8,128)(2,1)} %bitcast.68), custom_call_target="tpu_custom_call" | custom-call | flops 3221225472 | bytes 16777216 | tf_op jit(solution)/shard_map/forward/pallas_call | solution.py:68
  53.0 6.2 %backward.1 = (bf16[256,1536]{1,0:T(8,128)(2,1)S(1)}, bf16[256,128]{1,0:T(8,128)(2,1)S(1)}, bf16[256,2048]{1,0:T(8,128)(2,1)S(1)}, bf16[256,3584]{1,0:T(8,128)(2,1)}) custom-call(s32[10]{0:T(128)S(1)} %stack.116.spot, bf16[512,512]{1,0:T(8,128)(2,1)S(1)} %pad_maximum_fusion.3.both, bf16[512,512]{1,0:T(8,128)(2,1)S(1)} %collective-permute-done.7.below, ...), custom_call_target="tpu_custom_call" | custom-call | flops 1610612736 | bytes 8388608 | tf_op jit(solution)/shard_map/backward/pallas_call | solution.py:68
  61.9 5.0 %branch_rows.1 = bf16[8,256,512]{2,1,0:T(8,128)(2,1)S(1)} custom-call(s32[8]{0:T(128)S(1)} %stack.105.order, bf16[256,768]{1,0:T(8,128)(2,1)S(1)} %get-tuple-element.73.hidden.refs_2_, bf16[3,4096,768]{2,1,0:T(8,128)(2,1)} %bitcast.70), custom_call_target="tpu_custom_call" | custom-call | flops 1610612736 | bytes 8388608 | tf_op jit(solution)/shard_map/branch_rows/pallas_call | solution.py:68
  66.9 1.3 copy-done.2
  68.2 1.1 fusion.13
  69.3 1.7 collective-permute-start.14
  71.3 1.7 collective-permute-start.16
  74.0 1.3 copy-done.4
  75.3 1.5 copy-done.5
  76.8 1.2 copy-done.8
  78.1 1.2 copy-done.10
  79.2 4.4 %down_terms.1 = bf16[8,512,384]{2,1,0:T(8,128)(2,1)S(1)} custom-call(s32[8]{0:T(128)S(1)} %stack.121.order, bf16[256,2048]{1,0:T(8,128)(2,1)S(1)} %copy-done.8, bf16[256,3584]{1,0:T(8,128)(2,1)S(1)} %copy-done.5, bf16[256,768]{1,0:T(8,128)(2,1)S(1)} %get-tuple-element.73.hidden.refs_2_, bf16[256,1792]{1,0:T(8,128)(2,1)S(1)} %copy-done.10), custom_call_target="tpu_custom_call" | custom-call | flops 1610612736 | bytes 8388608 | tf_op jit(solution)/shard_map/down_terms/pallas_call | solution.py:68
  83.6 1.3 fusion.11
  84.9 1.7 collective-permute-done.13
  86.6 1.5 collective-permute-start.18
  88.1 2.1 %collective-permute-start.19 = (bf16[1024,384]{1,0:T(8,128)(2,1)}, bf16[1024,384]{1,0:T(8,128)(2,1)}, u32[]{:S(2)}, u32[]{:S(2)}) collective-permute-start(bf16[1024,384]{1,0:T(8,128)(2,1)} %bitcast.26), channel_id=1, source_target_pairs={{0,12},{1,13},{2,14},{3,15},{64,76},{65,77},{66,78},{67,79},{16,28... | collective-permute-start | bytes 2359304 | tf_op jit(solution)/shard_map/ppermute | solution.py:43
  90.2 6.9 %pair_rows.1 = bf16[8,256,640]{2,1,0:T(8,128)(2,1)S(1)} custom-call(s32[8]{0:T(128)S(1)} %stack.105.order, bf16[256,1536]{1,0:T(8,128)(2,1)S(1)} %copy-done.13, bf16[256,128]{1,0:T(8,128)(2,1)S(1)} %copy-done.18, bf16[3,4096,768]{2,1,0:T(8,128)(2,1)} %bitcast.71), custom_call_target="tpu_custom_call" | custom-call | flops 3221225472 | bytes 16777216 | tf_op jit(solution)/shard_map/pair_rows/pallas_call | solution.py:68
  97.1 1.5 copy-done
  98.6 1.2 fusion.12
  99.8 1.1 collective-permute-start.21
  101.6 1.4 slice_bitcast_fusion.14
  103.0 12.6 %collective-permute-done.20 = bf16[512,640]{1,0:T(8,128)(2,1)} collective-permute-done((bf16[512,640]{1,0:T(8,128)(2,1)}, bf16[512,640]{1,0:T(8,128)(2,1)}, u32[]{:S(2)}, u32[]{:S(2)}) %collective-permute-start.20) | collective-permute-done | bytes 655392 | tf_op jit(solution)/shard_map/ppermute | solution.py:43
  115.6 1.2 collective-permute-done.21
  116.8 1.2 pad_maximum_fusion
  118.5 1.2 add_convert_fusion.3
  120.4 1.1 add_convert_fusion.4
  122.5 1.1 add_convert_fusion.5
  124.2 1.1 add_convert_fusion.6
  125.2 1.2 collective-permute-start.23
  126.5 6.1 %pair_terms.1 = bf16[8,256,768]{2,1,0:T(8,128)(2,1)S(1)} custom-call(s32[8]{0:T(128)S(1)} %stack.121.order, bf16[256,1024]{1,0:T(8,128)(2,1)S(1)} %copy-done.20, bf16[256,1024]{1,0:T(8,128)(2,1)S(1)} %copy-done.22, bf16[256,1792]{1,0:T(8,128)(2,1)S(1)} %copy-done.11, bf16[256,2560]{1,0:T(8,128)(2,1)S(1)} %collective-permute-done.22.refs_3_.refs_7_, ...), custom_call_target="tpu_custom_call" | custom-call | flops 3221225472 | bytes 8388608 | tf_op jit(solution)/shard_map/pair_terms/pallas_call | solution.py:68
  132.7 1.4 collective-permute-done.31
  134.2 1.6 collective-permute-done.23
  135.8 1.3 fusion.4
  138.1 1.2 collective-permute-start.26
  139.4 2.1 %collective-permute-start.27 = (bf16[256,640]{1,0:T(8,128)(2,1)S(1)}, bf16[256,640]{1,0:T(8,128)(2,1)S(1)}, u32[]{:S(2)}, u32[]{:S(2)}) collective-permute-start(bf16[256,640]{1,0:T(8,128)(2,1)S(1)} %get-tuple-element.127), channel_id=1, source_target_pairs={{0,64},{1,65},{2,66},{3,67},{64,0},{65,1},{66,2},{67,3},{16,80},{1... | collective-permute-start | bytes 983048 | tf_op jit(solution)/shard_map/ppermute | solution.py:43
  142.8 1.1 collective-permute-start.33
  144.0 2.1 %collective-permute-start.34 = (bf16[512,768]{1,0:T(8,128)(2,1)S(1)}, bf16[512,768]{1,0:T(8,128)(2,1)S(1)}, u32[]{:S(2)}, u32[]{:S(2)}) collective-permute-start(bf16[512,768]{1,0:T(8,128)(2,1)S(1)} %bitcast.72), channel_id=1, source_target_pairs={{0,12},{1,13},{2,14},{3,15},{64,76},{65,77},{66,78},{67,79},{16,28... | collective-permute-start | bytes 2359304 | tf_op jit(solution)/shard_map/ppermute | solution.py:43
  146.1 1.4 convert_add_fusion
  147.4 1.5 collective-permute-done.27
  150.1 1.1 collective-permute-done.29
  151.2 1.0 collective-permute-start.39
  152.2 1.1 collective-permute-start.30
  153.3 1.2 select_convert_fusion.2
  154.5 2.2 %collective-permute-start.28 = (bf16[256,512]{1,0:T(8,128)(2,1)S(1)}, bf16[256,512]{1,0:T(8,128)(2,1)S(1)}, u32[]{:S(2)}, u32[]{:S(2)}) collective-permute-start(bf16[256,512]{1,0:T(8,128)(2,1)S(1)} %select_convert_fusion.2), channel_id=1, source_target_pairs={{0,64},{1,65},{2,66},{3,67},{64,0},{65,1},{66,2},{67,3},{16,80},{1... | collective-permute-start | bytes 786440 | tf_op jit(solution)/shard_map/ppermute | solution.py:43
  156.7 6.4 %collective-permute-done.30 = f32[1,512]{1,0:T(1,128)S(1)} collective-permute-done((f32[1,512]{1,0:T(1,128)S(1)}, f32[1,512]{1,0:T(1,128)S(1)}, u32[]{:S(2)}, u32[]{:S(2)}) %collective-permute-start.30) | collective-permute-done | bytes 2080 | tf_op jit(solution)/shard_map/ppermute | solution.py:43
  163.3 1.2 collective-permute-start.38
  164.6 2.2 %collective-permute-start.37 = (bf16[256,768]{1,0:T(8,128)(2,1)S(1)}, bf16[256,768]{1,0:T(8,128)(2,1)S(1)}, u32[]{:S(2)}, u32[]{:S(2)}) collective-permute-start(bf16[256,768]{1,0:T(8,128)(2,1)S(1)} %add_convert_fusion.2), channel_id=1, source_target_pairs={{0,12},{1,13},{2,14},{3,15},{64,76},{65,77},{66,78},{67,79},{16,28... | collective-permute-start | bytes 1179656 | tf_op jit(solution)/shard_map/ppermute | solution.py:43
  167.4 5.6 %collective-permute-done.35 = f32[1,512]{1,0:T(1,128)S(1)} collective-permute-done((f32[1,512]{1,0:T(1,128)S(1)}, f32[1,512]{1,0:T(1,128)S(1)}, u32[]{:S(2)}, u32[]{:S(2)}) %collective-permute-start.35) | collective-permute-done | bytes 2080 | tf_op jit(solution)/shard_map/ppermute | solution.py:43
  173.0 2.6 %collective-permute-start.36 = (f32[1,512]{1,0:T(1,128)S(1)}, f32[1,512]{1,0:T(1,128)S(1)}, u32[]{:S(2)}, u32[]{:S(2)}) collective-permute-start(f32[1,512]{1,0:T(1,128)S(1)} %add.220), channel_id=1, source_target_pairs={{0,8},{1,9},{2,10},{3,11},{64,72},{65,73},{66,74},{67,75},{16,24},... | collective-permute-start | bytes 6152 | tf_op jit(solution)/shard_map/ppermute | solution.py:43
  175.7 2.0 %add_convert_fusion.7 = bf16[256,512]{1,0:T(8,128)(2,1)} fusion(bf16[256,512]{1,0:T(8,128)(2,1)S(1)} %collective-permute-done.28, bf16[256,512]{1,0:T(8,128)(2,1)S(1)} %collective-permute-done.25, bf16[256,512]{1,0:T(8,128)(2,1)S(1)} %get-tuple-element.74, bf16[256,512]{1,0:T(8,128)(2,1)S(1)} %collective-permute-done.26, ...), kind=kLoop, calls=%fused_computation.28 | loop fusion | flops 1835008 | bytes 2097153 | tf_op jit(solution)/shard_map/convert_element_type | solution.py:319
  179.0 1.1 pad_maximum_fusion.1
  (131 shorter events, 21.6 us)
Async XLA Ops:
  0.6 17.9 %copy-start.26 = (bf16[256,512]{1,0:T(8,128)(2,1)S(1)}, bf16[256,512]{1,0:T(8,128)(2,1)}, u32[]{:S(2)}) copy-start(bf16[256,512]{1,0:T(8,128)(2,1)} %param.7) | copy-start | bytes 786436
  2.3 9.1 %collective-permute-start.1 = (bf16[272,512]{1,0:T(8,128)(2,1)S(1)}, bf16[272,512]{1,0:T(8,128)(2,1)S(1)}, u32[]{:S(2)}, u32[]{:S(2)}) collective-permute-start(bf16[272,512]{1,0:T(8,128)(2,1)S(1)} %pad_maximum_fusion.6.own), channel_id=1, source_target_pairs={{0,48},{1,49},{2,50},{3,51},{64,112},{65,113},{66,114},{67,115},{1... | collective-permute-start | bytes 835592 | tf_op jit(solution)/shard_map/ppermute | solution.py:43
  5.5 10.2 %collective-permute-start.2 = (bf16[272,512]{1,0:T(8,128)(2,1)S(1)}, bf16[272,512]{1,0:T(8,128)(2,1)S(1)}, u32[]{:S(2)}, u32[]{:S(2)}) collective-permute-start(bf16[272,512]{1,0:T(8,128)(2,1)S(1)} %pad_maximum_fusion.6.own), channel_id=1, source_target_pairs={{0,64},{1,65},{2,66},{3,67},{64,0},{65,1},{66,2},{67,3},{16,80},{1... | collective-permute-start | bytes 835592 | tf_op jit(solution)/shard_map/ppermute | solution.py:43
  9.4 9.0 %collective-permute-start = (bf16[272,512]{1,0:T(8,128)(2,1)S(1)}, bf16[272,512]{1,0:T(8,128)(2,1)S(1)}, u32[]{:S(2)}, u32[]{:S(2)}) collective-permute-start(bf16[272,512]{1,0:T(8,128)(2,1)S(1)} %pad_maximum_fusion.6.own), channel_id=1, source_target_pairs={{0,16},{1,17},{2,18},{3,19},{64,80},{65,81},{66,82},{67,83},{16,32... | collective-permute-start | bytes 835592 | tf_op jit(solution)/shard_map/ppermute | solution.py:43
  15.8 13.7 %collective-permute-start.4 = (bf16[416,512]{1,0:T(8,128)(2,1)S(1)}, bf16[416,512]{1,0:T(8,128)(2,1)S(1)}, u32[]{:S(2)}, u32[]{:S(2)}) collective-permute-start(bf16[416,512]{1,0:T(8,128)(2,1)S(1)} %pad_maximum_fusion.4), channel_id=1, source_target_pairs={{0,48},{1,49},{2,50},{3,51},{64,112},{65,113},{66,114},{67,115},{1... | collective-permute-start | bytes 1277960 | tf_op jit(solution)/shard_map/ppermute | solution.py:43
  18.5 11.0 %collective-permute-start.3 = (bf16[400,512]{1,0:T(8,128)(2,1)S(1)}, bf16[400,512]{1,0:T(8,128)(2,1)S(1)}, u32[]{:S(2)}, u32[]{:S(2)}) collective-permute-start(bf16[400,512]{1,0:T(8,128)(2,1)S(1)} %pad_maximum_fusion.5), channel_id=1, source_target_pairs={{0,16},{1,17},{2,18},{3,19},{64,80},{65,81},{66,82},{67,83},{16,32... | collective-permute-start | bytes 1228808 | tf_op jit(solution)/shard_map/ppermute | solution.py:43
  18.6 8.1 %collective-permute-start.5 = (bf16[256,512]{1,0:T(8,128)(2,1)S(1)}, bf16[256,512]{1,0:T(8,128)(2,1)S(1)}, u32[]{:S(2)}, u32[]{:S(2)}) collective-permute-start(bf16[256,512]{1,0:T(8,128)(2,1)S(1)} %copy-done.26), channel_id=1, source_target_pairs={{0,64},{1,65},{2,66},{3,67},{64,0},{65,1},{66,2},{67,3},{16,80},{1... | collective-permute-start | bytes 786440 | tf_op jit(solution)/shard_map/ppermute | solution.py:43
  29.5 13.5 %collective-permute-start.8 = (bf16[512,512]{1,0:T(8,128)(2,1)S(1)}, bf16[512,512]{1,0:T(8,128)(2,1)S(1)}, u32[]{:S(2)}, u32[]{:S(2)}) collective-permute-start(bf16[512,512]{1,0:T(8,128)(2,1)S(1)} %pad_maximum_fusion.3.both), channel_id=1, source_target_pairs={{0,48},{1,49},{2,50},{3,51},{64,112},{65,113},{66,114},{67,115},{1... | collective-permute-start | bytes 1572872 | tf_op jit(solution)/shard_map/ppermute | solution.py:43
  30.6 8.4 %collective-permute-start.6 = (bf16[272,512]{1,0:T(8,128)(2,1)}, bf16[272,512]{1,0:T(8,128)(2,1)}, u32[]{:S(2)}, u32[]{:S(2)}) collective-permute-start(bf16[272,512]{1,0:T(8,128)(2,1)} %pad_maximum_fusion.7), channel_id=1, source_target_pairs={{0,64},{1,65},{2,66},{3,67},{64,0},{65,1},{66,2},{67,3},{16,80},{1... | collective-permute-start | bytes 835592 | tf_op jit(solution)/shard_map/ppermute | solution.py:43
  32.2 12.2 %collective-permute-start.7 = (bf16[512,512]{1,0:T(8,128)(2,1)S(1)}, bf16[512,512]{1,0:T(8,128)(2,1)S(1)}, u32[]{:S(2)}, u32[]{:S(2)}) collective-permute-start(bf16[512,512]{1,0:T(8,128)(2,1)S(1)} %pad_maximum_fusion.3.both), channel_id=1, source_target_pairs={{0,16},{1,17},{2,18},{3,19},{64,80},{65,81},{66,82},{67,83},{16,32... | collective-permute-start | bytes 1572872 | tf_op jit(solution)/shard_map/ppermute | solution.py:43
  41.1 10.5 %copy-start.3 = (bf16[272,4096]{1,0:T(8,128)(2,1)}, bf16[272,4096]{1,0:T(8,128)(2,1)S(1)}, u32[]{:S(2)}) copy-start(bf16[272,4096]{1,0:T(8,128)(2,1)S(1)} %get-tuple-element.63.x_ref) | copy-start | bytes 6684676
  41.2 11.0 %collective-permute-start.9 = (bf16[256,1024]{1,0:T(8,128)(2,1)S(1)}, bf16[256,1024]{1,0:T(8,128)(2,1)S(1)}, u32[]{:S(2)}, u32[]{:S(2)}) collective-permute-start(bf16[256,1024]{1,0:T(8,128)(2,1)S(1)} %get-tuple-element.66), channel_id=1, source_target_pairs={{0,66},{1,67},{2,64},{3,65},{64,2},{65,3},{66,0},{67,1},{16,82},{1... | collective-permute-start | bytes 1572872 | tf_op jit(solution)/shard_map/ppermute | solution.py:43
  42.9 10.1 %collective-permute-start.10 = (bf16[256,1024]{1,0:T(8,128)(2,1)S(1)}, bf16[256,1024]{1,0:T(8,128)(2,1)S(1)}, u32[]{:S(2)}, u32[]{:S(2)}) collective-permute-start(bf16[256,1024]{1,0:T(8,128)(2,1)S(1)} %get-tuple-element.67), channel_id=1, source_target_pairs={{0,2},{1,3},{2,0},{3,1},{64,66},{65,67},{66,64},{67,65},{16,18},{1... | collective-permute-start | bytes 1572872 | tf_op jit(solution)/shard_map/ppermute | solution.py:43
  43.0 10.0 %collective-permute-start.12 = (bf16[256,512]{1,0:T(8,128)(2,1)S(1)}, bf16[256,512]{1,0:T(8,128)(2,1)S(1)}, u32[]{:S(2)}, u32[]{:S(2)}) collective-permute-start(bf16[256,512]{1,0:T(8,128)(2,1)S(1)} %pad_maximum_fusion.9), channel_id=1, source_target_pairs={{0,48},{1,49},{2,50},{3,51},{64,112},{65,113},{66,114},{67,115},{1... | collective-permute-start | bytes 786440 | tf_op jit(solution)/shard_map/ppermute | solution.py:43
  44.4 8.6 %collective-permute-start.11 = (bf16[256,512]{1,0:T(8,128)(2,1)S(1)}, bf16[256,512]{1,0:T(8,128)(2,1)S(1)}, u32[]{:S(2)}, u32[]{:S(2)}) collective-permute-start(bf16[256,512]{1,0:T(8,128)(2,1)S(1)} %pad_maximum_fusion.8), channel_id=1, source_target_pairs={{0,16},{1,17},{2,18},{3,19},{64,80},{65,81},{66,82},{67,83},{16,32... | collective-permute-start | bytes 786440 | tf_op jit(solution)/shard_map/ppermute | solution.py:43
  51.6 7.6 %copy-start.15 = (f32[256,128]{1,0:T(8,128)}, f32[256,128]{1,0:T(8,128)S(1)}, u32[]{:S(2)}) copy-start(f32[256,128]{1,0:T(8,128)S(1)} %get-tuple-element.71.inv) | copy-start | bytes 393220
  53.0 6.3 %copy-start.24 = (bf16[256,1024]{1,0:T(8,128)(2,1)}, bf16[256,1024]{1,0:T(8,128)(2,1)S(1)}, u32[]{:S(2)}) copy-start(bf16[256,1024]{1,0:T(8,128)(2,1)S(1)} %collective-permute-done.10) | copy-start | bytes 1572868
  59.3 1.0 copy-start.7
  60.9 13.1 %collective-permute-start.17 = (bf16[256,3584]{1,0:T(8,128)(2,1)}, bf16[256,3584]{1,0:T(8,128)(2,1)S(1)}, u32[]{:S(2)}, u32[]{:S(2)}) collective-permute-start(bf16[256,3584]{1,0:T(8,128)(2,1)} %get-tuple-element.79), channel_id=1, source_target_pairs={{0,1},{1,0},{2,3},{3,2},{64,65},{65,64},{66,67},{67,66},{16,17},{1... | collective-permute-start | bytes 5505032 | tf_op jit(solution)/shard_map/ppermute | solution.py:43
  61.8 11.3 %collective-permute-start.15 = (bf16[256,1792]{1,0:T(8,128)(2,1)}, bf16[256,1792]{1,0:T(8,128)(2,1)S(1)}, u32[]{:S(2)}, u32[]{:S(2)}) collective-permute-start(bf16[256,1792]{1,0:T(8,128)(2,1)} %get-tuple-element.76), channel_id=1, source_target_pairs={{0,1},{1,0},{2,3},{3,2},{64,65},{65,64},{66,67},{67,66},{16,17},{1... | collective-permute-start | bytes 2752520 | tf_op jit(solution)/shard_map/ppermute | solution.py:43
  66.9 1.3 copy-start.2
  69.3 15.7 %collective-permute-start.14 = (bf16[512,512]{1,0:T(8,128)(2,1)}, bf16[512,512]{1,0:T(8,128)(2,1)}, u32[]{:S(2)}, u32[]{:S(2)}) collective-permute-start(bf16[512,512]{1,0:T(8,128)(2,1)} %bitcast.20), channel_id=1, source_target_pairs={{0,16},{1,17},{2,18},{3,19},{64,80},{65,81},{66,82},{67,83},{16,0}... | collective-permute-start | bytes 1572872 | tf_op jit(solution)/shard_map/ppermute | solution.py:43
  71.0 15.6 %collective-permute-start.13 = (bf16[512,512]{1,0:T(8,128)(2,1)}, bf16[512,512]{1,0:T(8,128)(2,1)}, u32[]{:S(2)}, u32[]{:S(2)}) collective-permute-start(bf16[512,512]{1,0:T(8,128)(2,1)} %bitcast.17), channel_id=1, source_target_pairs={{0,48},{1,49},{2,50},{3,51},{64,112},{65,113},{66,114},{67,115},{1... | collective-permute-start | bytes 1572872 | tf_op jit(solution)/shard_map/ppermute | solution.py:43
  71.3 31.7 %collective-permute-start.16 = (bf16[256,1536]{1,0:T(8,128)(2,1)}, bf16[256,1536]{1,0:T(8,128)(2,1)}, u32[]{:S(2)}, u32[]{:S(2)}) collective-permute-start(bf16[256,1536]{1,0:T(8,128)(2,1)} %copy-done.12), channel_id=1, source_target_pairs={{0,2},{1,3},{2,0},{3,1},{64,66},{65,67},{66,64},{67,65},{16,18},{1... | collective-permute-start | bytes 2359304 | tf_op jit(solution)/shard_map/ppermute | solution.py:43
  73.1 1.0 copy-start.9
  74.0 1.3 copy-start.4
  75.3 1.5 copy-start.5
  76.8 1.2 copy-start.8
  78.1 1.2 copy-start.10
  83.6 6.6 %copy-start.13 = (bf16[256,1536]{1,0:T(8,128)(2,1)S(1)}, bf16[256,1536]{1,0:T(8,128)(2,1)}, u32[]{:S(2)}) copy-start(bf16[256,1536]{1,0:T(8,128)(2,1)} %copy-done.12) | copy-start | bytes 2359300
  83.6 6.6 %copy-start.18 = (bf16[256,128]{1,0:T(8,128)(2,1)S(1)}, bf16[256,128]{1,0:T(8,128)(2,1)}, u32[]{:S(2)}) copy-start(bf16[256,128]{1,0:T(8,128)(2,1)} %copy-done.17) | copy-start | bytes 196612
  86.6 30.2 %collective-permute-start.18 = (bf16[1024,384]{1,0:T(8,128)(2,1)}, bf16[1024,384]{1,0:T(8,128)(2,1)}, u32[]{:S(2)}, u32[]{:S(2)}) collective-permute-start(bf16[1024,384]{1,0:T(8,128)(2,1)} %bitcast.25), channel_id=1, source_target_pairs={{0,4},{1,5},{2,6},{3,7},{64,68},{65,69},{66,70},{67,71},{16,20},{1... | collective-permute-start | bytes 2359304 | tf_op jit(solution)/shard_map/ppermute | solution.py:43
  88.1 28.7 %collective-permute-start.19 = (bf16[1024,384]{1,0:T(8,128)(2,1)}, bf16[1024,384]{1,0:T(8,128)(2,1)}, u32[]{:S(2)}, u32[]{:S(2)}) collective-permute-start(bf16[1024,384]{1,0:T(8,128)(2,1)} %bitcast.26), channel_id=1, source_target_pairs={{0,12},{1,13},{2,14},{3,15},{64,76},{65,77},{66,78},{67,79},{16,28... | collective-permute-start | bytes 2359304 | tf_op jit(solution)/shard_map/ppermute | solution.py:43
  97.1 1.5 copy-start
  98.6 2.2 %copy-start.27 = (bf16[512]{0:T(512)(128)(2,1)S(1)}, bf16[512]{0:T(512)(128)(2,1)}, u32[]{:S(2)}) copy-start(bf16[512]{0:T(512)(128)(2,1)} %param.5) | copy-start | bytes 3076
  99.8 15.8 %collective-permute-start.20 = (bf16[512,640]{1,0:T(8,128)(2,1)}, bf16[512,640]{1,0:T(8,128)(2,1)}, u32[]{:S(2)}, u32[]{:S(2)}) collective-permute-start(bf16[512,640]{1,0:T(8,128)(2,1)} %bitcast.27), channel_id=1, source_target_pairs={{0,16},{1,17},{2,18},{3,19},{64,80},{65,81},{66,82},{67,83},{16,0}... | collective-permute-start | bytes 1966088 | tf_op jit(solution)/shard_map/ppermute | solution.py:43
  99.8 17.0 %collective-permute-start.21 = (bf16[512,640]{1,0:T(8,128)(2,1)}, bf16[512,640]{1,0:T(8,128)(2,1)}, u32[]{:S(2)}, u32[]{:S(2)}) collective-permute-start(bf16[512,640]{1,0:T(8,128)(2,1)} %bitcast.28), channel_id=1, source_target_pairs={{0,48},{1,49},{2,50},{3,51},{64,112},{65,113},{66,114},{67,115},{1... | collective-permute-start | bytes 1966088 | tf_op jit(solution)/shard_map/ppermute | solution.py:43
  100.9 15.9 %copy-start.25 = (bf16[256,1024]{1,0:T(8,128)(2,1)S(1)}, bf16[256,1024]{1,0:T(8,128)(2,1)}, u32[]{:S(2)}) copy-start(bf16[256,1024]{1,0:T(8,128)(2,1)} %copy-done.24) | copy-start | bytes 1572868
  101.6 16.5 %copy-start.1 = (bf16[8,256,640]{2,1,0:T(8,128)(2,1)S(1)}, bf16[8,256,640]{2,1,0:T(8,128)(2,1)}, u32[]{:S(2)}) copy-start(bf16[8,256,640]{2,1,0:T(8,128)(2,1)} %copy-done) | copy-start | bytes 7864324
  118.0 8.4 %collective-permute-start.22 = (bf16[256,2560]{1,0:T(8,128)(2,1)S(1)}, bf16[256,2560]{1,0:T(8,128)(2,1)S(1)}, u32[]{:S(2)}, u32[]{:S(2)}) collective-permute-start(bf16[256,2560]{1,0:T(8,128)(2,1)S(1)} %pad_maximum_fusion), channel_id=1, source_target_pairs={{0,1},{1,0},{2,3},{3,2},{64,65},{65,64},{66,67},{67,66},{16,17},{1... | collective-permute-start | bytes 3932168 | tf_op jit(solution)/shard_map/ppermute | solution.py:43
  118.3 8.2 %copy-start.22 = (bf16[256,1024]{1,0:T(8,128)(2,1)S(1)}, bf16[256,1024]{1,0:T(8,128)(2,1)}, u32[]{:S(2)}) copy-start(bf16[256,1024]{1,0:T(8,128)(2,1)} %copy-done.21) | copy-start | bytes 1572868
  118.4 8.0 %copy-start.6 = (bf16[256,3584]{1,0:T(8,128)(2,1)S(1)}, bf16[256,3584]{1,0:T(8,128)(2,1)}, u32[]{:S(2)}) copy-start(bf16[256,3584]{1,0:T(8,128)(2,1)} %copy-done.4) | copy-start | bytes 5505028
  118.4 8.0 %copy-start.11 = (bf16[256,1792]{1,0:T(8,128)(2,1)S(1)}, bf16[256,1792]{1,0:T(8,128)(2,1)}, u32[]{:S(2)}) copy-start(bf16[256,1792]{1,0:T(8,128)(2,1)} %copy-done.9) | copy-start | bytes 2752516
  118.5 8.0 %copy-start.14 = (bf16[256,1536]{1,0:T(8,128)(2,1)S(1)}, bf16[256,1536]{1,0:T(8,128)(2,1)}, u32[]{:S(2)}) copy-start(bf16[256,1536]{1,0:T(8,128)(2,1)} %copy-done.12) | copy-start | bytes 2359300
  118.5 8.0 %copy-start.20 = (bf16[256,1024]{1,0:T(8,128)(2,1)S(1)}, bf16[256,1024]{1,0:T(8,128)(2,1)}, u32[]{:S(2)}) copy-start(bf16[256,1024]{1,0:T(8,128)(2,1)} %copy-done.19) | copy-start | bytes 1572868
  119.7 12.9 %collective-permute-start.32 = (bf16[512,384]{1,0:T(8,128)(2,1)S(1)}, bf16[512,384]{1,0:T(8,128)(2,1)S(1)}, u32[]{:S(2)}, u32[]{:S(2)}) collective-permute-start(bf16[512,384]{1,0:T(8,128)(2,1)S(1)} %add_convert_fusion.3), channel_id=1, source_target_pairs={{0,4},{1,5},{2,6},{3,7},{64,68},{65,69},{66,70},{67,71},{16,20},{1... | collective-permute-start | bytes 1179656 | tf_op jit(solution)/shard_map/ppermute | solution.py:43
  121.5 12.5 %collective-permute-start.31 = (bf16[512,384]{1,0:T(8,128)(2,1)S(1)}, bf16[512,384]{1,0:T(8,128)(2,1)S(1)}, u32[]{:S(2)}, u32[]{:S(2)}) collective-permute-start(bf16[512,384]{1,0:T(8,128)(2,1)S(1)} %add_convert_fusion.4), channel_id=1, source_target_pairs={{0,12},{1,13},{2,14},{3,15},{64,76},{65,77},{66,78},{67,79},{16,28... | collective-permute-start | bytes 1179656 | tf_op jit(solution)/shard_map/ppermute | solution.py:43
  123.5 10.6 %collective-permute-start.24 = (bf16[256,640]{1,0:T(8,128)(2,1)S(1)}, bf16[256,640]{1,0:T(8,128)(2,1)S(1)}, u32[]{:S(2)}, u32[]{:S(2)}) collective-permute-start(bf16[256,640]{1,0:T(8,128)(2,1)S(1)} %add_convert_fusion.5), channel_id=1, source_target_pairs={{0,16},{1,17},{2,18},{3,19},{64,80},{65,81},{66,82},{67,83},{16,0}... | collective-permute-start | bytes 983048 | tf_op jit(solution)/shard_map/ppermute | solution.py:43
  125.2 10.6 %collective-permute-start.23 = (bf16[256,640]{1,0:T(8,128)(2,1)S(1)}, bf16[256,640]{1,0:T(8,128)(2,1)S(1)}, u32[]{:S(2)}, u32[]{:S(2)}) collective-permute-start(bf16[256,640]{1,0:T(8,128)(2,1)S(1)} %add_convert_fusion.6), channel_id=1, source_target_pairs={{0,48},{1,49},{2,50},{3,51},{64,112},{65,113},{66,114},{67,115},{1... | collective-permute-start | bytes 983048 | tf_op jit(solution)/shard_map/ppermute | solution.py:43
  138.1 14.1 %collective-permute-start.26 = (bf16[256,512]{1,0:T(8,128)(2,1)S(1)}, bf16[256,512]{1,0:T(8,128)(2,1)S(1)}, u32[]{:S(2)}, u32[]{:S(2)}) collective-permute-start(bf16[256,512]{1,0:T(8,128)(2,1)S(1)} %add_convert_fusion.8), channel_id=1, source_target_pairs={{0,48},{1,49},{2,50},{3,51},{64,112},{65,113},{66,114},{67,115},{1... | collective-permute-start | bytes 786440 | tf_op jit(solution)/shard_map/ppermute | solution.py:43
  139.4 9.6 %collective-permute-start.27 = (bf16[256,640]{1,0:T(8,128)(2,1)S(1)}, bf16[256,640]{1,0:T(8,128)(2,1)S(1)}, u32[]{:S(2)}, u32[]{:S(2)}) collective-permute-start(bf16[256,640]{1,0:T(8,128)(2,1)S(1)} %get-tuple-element.127), channel_id=1, source_target_pairs={{0,64},{1,65},{2,66},{3,67},{64,0},{65,1},{66,2},{67,3},{16,80},{1... | collective-permute-start | bytes 983048 | tf_op jit(solution)/shard_map/ppermute | solution.py:43
  142.5 10.8 %collective-permute-start.25 = (bf16[256,512]{1,0:T(8,128)(2,1)S(1)}, bf16[256,512]{1,0:T(8,128)(2,1)S(1)}, u32[]{:S(2)}, u32[]{:S(2)}) collective-permute-start(bf16[256,512]{1,0:T(8,128)(2,1)S(1)} %add_convert_fusion.9), channel_id=1, source_target_pairs={{0,16},{1,17},{2,18},{3,19},{64,80},{65,81},{66,82},{67,83},{16,0}... | collective-permute-start | bytes 786440 | tf_op jit(solution)/shard_map/ppermute | solution.py:43
  142.8 20.4 %collective-permute-start.33 = (bf16[512,768]{1,0:T(8,128)(2,1)S(1)}, bf16[512,768]{1,0:T(8,128)(2,1)S(1)}, u32[]{:S(2)}, u32[]{:S(2)}) collective-permute-start(bf16[512,768]{1,0:T(8,128)(2,1)S(1)} %bitcast.73), channel_id=1, source_target_pairs={{0,4},{1,5},{2,6},{3,7},{64,68},{65,69},{66,70},{67,71},{16,20},{1... | collective-permute-start | bytes 2359304 | tf_op jit(solution)/shard_map/ppermute | solution.py:43
  143.9 5.0 %copy-start.16 = (f32[256,128]{1,0:T(8,128)S(1)}, f32[256,128]{1,0:T(8,128)}, u32[]{:S(2)}) copy-start(f32[256,128]{1,0:T(8,128)} %copy-done.15) | copy-start | bytes 393220
  143.9 5.2 %copy-start.23 = (bf16[256,512]{1,0:T(8,128)(2,1)S(1)}, bf16[256,512]{1,0:T(8,128)(2,1)}, u32[]{:S(2)}) copy-start(bf16[256,512]{1,0:T(8,128)(2,1)} %param.4) | copy-start | bytes 786436
  144.0 19.2 %collective-permute-start.34 = (bf16[512,768]{1,0:T(8,128)(2,1)S(1)}, bf16[512,768]{1,0:T(8,128)(2,1)S(1)}, u32[]{:S(2)}, u32[]{:S(2)}) collective-permute-start(bf16[512,768]{1,0:T(8,128)(2,1)S(1)} %bitcast.72), channel_id=1, source_target_pairs={{0,12},{1,13},{2,14},{3,15},{64,76},{65,77},{66,78},{67,79},{16,28... | collective-permute-start | bytes 2359304 | tf_op jit(solution)/shard_map/ppermute | solution.py:43
  150.0 1.2 collective-permute-start.29
  151.2 16.2 %collective-permute-start.39 = (bf16[256,768]{1,0:T(8,128)(2,1)S(1)}, bf16[256,768]{1,0:T(8,128)(2,1)S(1)}, u32[]{:S(2)}, u32[]{:S(2)}) collective-permute-start(bf16[256,768]{1,0:T(8,128)(2,1)S(1)} %select_convert_fusion), channel_id=1, source_target_pairs={{0,2},{1,3},{2,0},{3,1},{64,66},{65,67},{66,64},{67,65},{16,18},{1... | collective-permute-start | bytes 1179656 | tf_op jit(solution)/shard_map/ppermute | solution.py:43
  152.2 11.0 %collective-permute-start.30 = (f32[1,512]{1,0:T(1,128)S(1)}, f32[1,512]{1,0:T(1,128)S(1)}, u32[]{:S(2)}, u32[]{:S(2)}) collective-permute-start(f32[1,512]{1,0:T(1,128)S(1)} %add.214), channel_id=1, source_target_pairs={{0,2},{1,3},{2,0},{3,1},{64,66},{65,67},{66,64},{67,65},{16,18},{1... | collective-permute-start | bytes 6152 | tf_op jit(solution)/shard_map/ppermute | solution.py:43
  154.5 21.2 %collective-permute-start.28 = (bf16[256,512]{1,0:T(8,128)(2,1)S(1)}, bf16[256,512]{1,0:T(8,128)(2,1)S(1)}, u32[]{:S(2)}, u32[]{:S(2)}) collective-permute-start(bf16[256,512]{1,0:T(8,128)(2,1)S(1)} %select_convert_fusion.2), channel_id=1, source_target_pairs={{0,64},{1,65},{2,66},{3,67},{64,0},{65,1},{66,2},{67,3},{16,80},{1... | collective-permute-start | bytes 786440 | tf_op jit(solution)/shard_map/ppermute | solution.py:43
  163.3 15.4 %collective-permute-start.38 = (bf16[256,768]{1,0:T(8,128)(2,1)S(1)}, bf16[256,768]{1,0:T(8,128)(2,1)S(1)}, u32[]{:S(2)}, u32[]{:S(2)}) collective-permute-start(bf16[256,768]{1,0:T(8,128)(2,1)S(1)} %add_convert_fusion.1), channel_id=1, source_target_pairs={{0,4},{1,5},{2,6},{3,7},{64,68},{65,69},{66,70},{67,71},{16,20},{1... | collective-permute-start | bytes 1179656 | tf_op jit(solution)/shard_map/ppermute | solution.py:43
  164.6 14.1 %collective-permute-start.37 = (bf16[256,768]{1,0:T(8,128)(2,1)S(1)}, bf16[256,768]{1,0:T(8,128)(2,1)S(1)}, u32[]{:S(2)}, u32[]{:S(2)}) collective-permute-start(bf16[256,768]{1,0:T(8,128)(2,1)S(1)} %add_convert_fusion.2), channel_id=1, source_target_pairs={{0,12},{1,13},{2,14},{3,15},{64,76},{65,77},{66,78},{67,79},{16,28... | collective-permute-start | bytes 1179656 | tf_op jit(solution)/shard_map/ppermute | solution.py:43
  166.7 6.3 %collective-permute-start.35 = (f32[1,512]{1,0:T(1,128)S(1)}, f32[1,512]{1,0:T(1,128)S(1)}, u32[]{:S(2)}, u32[]{:S(2)}) collective-permute-start(f32[1,512]{1,0:T(1,128)S(1)} %add.215), channel_id=1, source_target_pairs={{0,4},{1,5},{2,6},{3,7},{64,68},{65,69},{66,70},{67,71},{16,20},{1... | collective-permute-start | bytes 6152 | tf_op jit(solution)/shard_map/ppermute | solution.py:43
  173.0 5.1 %collective-permute-start.36 = (f32[1,512]{1,0:T(1,128)S(1)}, f32[1,512]{1,0:T(1,128)S(1)}, u32[]{:S(2)}, u32[]{:S(2)}) collective-permute-start(f32[1,512]{1,0:T(1,128)S(1)} %add.220), channel_id=1, source_target_pairs={{0,8},{1,9},{2,10},{3,11},{64,72},{65,73},{66,74},{67,75},{16,24},... | collective-permute-start | bytes 6152 | tf_op jit(solution)/shard_map/ppermute | solution.py:43
  (4 other events, 3.2 us)

commit v5 on v4

--- a/solution.py
+++ b/solution.py
@@ -63,14 +63,35 @@
     return lax.dot_general(a, b, (((0,), (0,)), ((), ())), preferred_element_type=f32)
 
 
-def call(body, name, shapes, scratch, limit, flops, size, args, hbm=(), scalars=1):
-    spaces = [pltpu.SMEM] * scalars + [pltpu.HBM if i in hbm else pltpu.VMEM for i in range(scalars, len(args))]
+def call(body, name, shapes, scratch, limit, flops, size, args, hbm=(), scalars=1, direct=()):
+    loads = [i for i in range(scalars, len(args)) if i not in hbm and i not in direct]
+    spaces = [pltpu.SMEM] * scalars + [
+        pltpu.HBM if i in hbm else pltpu.VMEM if i in direct else pl.ANY for i in range(scalars, len(args))
+    ]
+
+    def whole(*refs):
+        ins, rest = list(refs[:len(args)]), refs[len(args):]
+        outs, rest = rest[:len(shapes)], rest[len(shapes):]
+        own, rest = rest[:len(scratch)], rest[len(scratch):]
+        copies = []
+        for n, i in enumerate(loads):
+            copies.append(pltpu.make_async_copy(ins[i], rest[n], rest[-1].at[n]))
+            copies[-1].start()
+            ins[i] = rest[n]
+
+        def ready():
+            for copy in copies:
+                copy.wait()
+
+        body(ready, *ins, *outs, *own)
+
+    held = [pltpu.VMEM(args[i].shape, args[i].dtype) for i in loads] + [pltpu.SemaphoreType.DMA((max(len(loads), 1),))]
     return pl.pallas_call(
-        body,
+        whole,
         in_specs=[pl.BlockSpec(memory_space=space) for space in spaces],
         out_specs=[pl.BlockSpec(memory_space=pltpu.VMEM) for _ in shapes],
         out_shape=[jax.ShapeDtypeStruct(shape, dtype) for shape, dtype in shapes],
-        scratch_shapes=scratch,
+        scratch_shapes=list(scratch) + held,
         compiler_params=pltpu.CompilerParams(vmem_limit_bytes=limit * MiB),
         cost_estimate=pl.CostEstimate(flops=flops, bytes_accessed=size, transcendentals=0),
         name=name,
@@ -95,12 +116,14 @@
     return copies
 
 
-def assemble_body(spot, own, below, above, other, up2, down2, other_far, full, keep, core_out, z_out, cross_out):
+def assemble_body(ready, spot, own, below, above, other, up2, down2, other_far, full, gains, keep, core_out, z_out,
+                  cross_out):
     put(full, spot, [
         (0, 0, 0, own, 0, 272), (0, 3, 0, below, 0, 272), (0, 1, 0, above, 0, 272), (1, 0, 0, other, 0, 272),
         (0, 2, 0, up2, 0, 128), (1, 3, 0, up2, 128, 272), (0, 2, 128, down2, 0, 144), (1, 1, 0, down2, 144, 272),
         (1, 2, 0, other_far, 0, 272),
     ])
+    gains[...] = full[256:272, :]
     z_lo, core = spot[8], spot[9]
     for i in range(4):
         for ref, zl, c in ((keep, z_lo, core), (core_out, z_lo, 1 - core), (z_out, 1 - z_lo, core),
@@ -109,13 +132,14 @@
 
 
 def assemble(spot, pieces):
-    shapes = [((272, 4096), bf16)] + [((256, 1024), bf16)] * 4
-    return call(assemble_body, "assemble", shapes, [], 4, 0, 8 * MiB, (spot, *pieces))
-
-
-def forward_body(x_ref, x_core, w, gate, up, hidden, inv, core_out, held, sems):
+    shapes = [((272, 4096), bf16), ((16, 4096), bf16)] + [((256, 1024), bf16)] * 4
+    return call(assemble_body, "assemble", shapes, [], 4, 0, 8 * MiB, (spot, *pieces), direct=range(1, 8))
+
+
+def forward_body(ready, x_ref, x_core, w, gate, up, hidden, inv, core_out, held, sems):
     copies = fetch(w, held, sems, 0, 2, lambda k: k)
     squares = jnp.zeros((256, 1), f32)
+    ready()
     for k in range(8):
         copies[k].wait()
         cols = slice(k * 512, (k + 1) * 512)
@@ -140,10 +164,10 @@
     shapes = [((256, 768), f32), ((256, 768), f32), ((256, 768), bf16), ((256, 128), f32), ((256, 1792), bf16)]
     scratch = [pltpu.VMEM((8, 2, 512, 768), bf16), pltpu.SemaphoreType.DMA((8,))]
     return call(forward_body, "forward", shapes, scratch, 18, 2 * 256 * 4096 * 1536, 16 * MiB,
-                (x_full, x_core, w3), hbm=(2,), scalars=0)
-
-
-def backward_body(spot, both, below, above, low, high, w, gate, up_val, inv, pair, products, mine, core_out, buf, acc,
+                (x_full, x_core, w3), hbm=(2,), scalars=0, direct=(0,))
+
+
+def backward_body(ready, spot, both, below, above, low, high, w, gate, up_val, inv, pair, products, mine, core_out, buf, acc,
                   held, sems):
     copies = fetch(w, held, sems, 2, 1, lambda k: k)
     put(buf, spot, [
@@ -159,6 +183,7 @@
         copies[k].wait()
         value = dot(buf[:, k * 512:(k + 1) * 512], held[k, 0])
         acc[...] = value if k == 0 else acc[...] + value
+    ready()
     d_hidden = acc[...] * inv[:, 0:1]
     g, u = gate[...], up_val[...]
     sigma = jax.nn.sigmoid(g)
@@ -176,79 +201,90 @@
     shapes = [((256, 1536), bf16), ((256, 128), bf16), ((256, 2048), bf16), ((256, 3584), bf16)]
     scratch = [pltpu.VMEM((256, 4096), bf16), pltpu.VMEM((256, 768), f32), pltpu.VMEM((8, 1, 512, 768), bf16),
                pltpu.SemaphoreType.DMA((8,))]
-    return call(backward_body, "backward", shapes, scratch, 15, 2 * 256 * 4096 * 768, 8 * MiB, (spot, *pieces, w3, gate, up, inv),
-                hbm=(len(pieces) + 1,))
-
-
-def outer_body(a_from, b_from, rows, cols, order, *refs):
+    return call(backward_body, "backward", shapes, scratch, 16, 2 * 256 * 4096 * 768, 8 * MiB, (spot, *pieces, w3, gate, up, inv),
+                hbm=(6,), direct=range(1, 6))
+
+
+def store(outs, k, value):
+    half, i = k // 4, k % 4
+    if i < 2:
+        rows = value.shape[0]
+        outs[half][i * rows:(i + 1) * rows, :] = value
+    else:
+        outs[2 * i - 2 + half][...] = value
+
+
+def halving_shapes(rows, cols):
+    return [((2 * rows, cols), bf16)] * 2 + [((rows, cols), bf16)] * 4
+
+
+def outer_body(a_from, b_from, rows, cols, ready, order, *refs):
     n = len(a_from)
-    a_refs, b_refs, out = refs[:n], refs[n:2 * n], refs[2 * n]
-
-    def step(i, carry):
+    a_refs, b_refs, outs = refs[:n], refs[n:2 * n], refs[2 * n:]
+    ready()
+    for k in range(8):
         total = None
         for a, a0, b, b0 in zip(a_refs, a_from, b_refs, b_from):
-            value = dot_tn(a[:, lane(order[i] * rows + a0, rows, 256)], b[:, lane(i // 4 * cols + b0, cols, 128)])
+            b0 = k // 4 * cols + b0
+            value = dot_tn(a[:, lane(order[k] * rows + a0, rows, 256)], b[:, b0:b0 + cols])
             total = value if total is None else total + value
-        out[i] = total.astype(bf16)
-        return carry
-
-    lax.fori_loop(0, 8, step, 0)
+        store(outs, k, total.astype(bf16))
 
 
 def outer(name, order, a_list, b_list, rows, cols):
     body = functools.partial(outer_body, [f for _, f in a_list], [f for _, f in b_list], rows, cols)
     flops = 2 * 256 * len(a_list) * rows * 8 * cols
-    return call(body, name, [((8, rows, cols), bf16)], [], 10, flops, 8 * MiB, (order, *[a for a, _ in a_list], *[b for b, _ in b_list]))[0]
-
-
-def branch_rows_body(order, hidden, w, out, held, sems):
+    return call(body, name, halving_shapes(rows, cols), [], 16, flops, 8 * MiB,
+                (order, *[a for a, _ in a_list], *[b for b, _ in b_list]))
+
+
+def branch_rows_body(ready, order, hidden, w, *refs):
+    outs, held, sems = refs[:6], refs[6], refs[7]
     copies = fetch(w, held, sems, 2, 1, lambda k: k // 4 * 4 + order[k])
+    ready()
     for k in range(8):
         copies[k].wait()
-        out[k] = dot_nt(hidden[...], held[k, 0]).astype(bf16)
+        store(outs, k, dot_nt(hidden[...], held[k, 0]).astype(bf16))
 
 
 def branch_rows(order, hidden, w3):
     scratch = [pltpu.VMEM((8, 1, 512, 768), bf16), pltpu.SemaphoreType.DMA((8,))]
-    return call(branch_rows_body, "branch_rows", [((8, 256, 512), bf16)], scratch, 8, 2 * 256 * 768 * 4096, 8 * MiB,
-                (order, hidden, w3), hbm=(2,))[0]
-
-
-def pair_rows_body(order, pair, products, w, out, held, sems):
+    return call(branch_rows_body, "branch_rows", halving_shapes(256, 512), scratch, 10, 2 * 256 * 768 * 4096, 8 * MiB,
+                (order, hidden, w3), hbm=(2,))
+
+
+def pair_rows_body(ready, order, pair, products, w, *refs):
+    outs, held, sems = refs[:6], refs[6], refs[7]
     copies = fetch(w, held, sems, 0, 2, lambda k: k // 4 * 4 + order[k])
+    ready()
     for k in range(8):
         copies[k].wait()
         value = dot_nt(pair[:, 0:768], held[k, 0]) + dot_nt(pair[:, 768:1536], held[k, 1])
-        out[k, :, 0:512] = value.astype(bf16)
-        out[k, :, 512:640] = products[...]
+        store(outs, k, jnp.concatenate([value.astype(bf16), products[...]], axis=1))
 
 
 def pair_rows(order, pair, products, w3):
     scratch = [pltpu.VMEM((8, 2, 512, 768), bf16), pltpu.SemaphoreType.DMA((8,))]
-    return call(pair_rows_body, "pair_rows", [((8, 256, 640), bf16)], scratch, 15, 2 * 256 * 1536 * 4096, 16 * MiB,
-                (order, pair, products, w3), hbm=(3,))[0]
-
-
-def first_two(terms):
-    return [terms[4 * h:4 * h + 2].reshape(2 * terms.shape[1], terms.shape[2]) for h in (0, 1)]
+    return call(pair_rows_body, "pair_rows", halving_shapes(256, 640), scratch, 16, 2 * 256 * 1536 * 4096, 16 * MiB,
+                (order, pair, products, w3), hbm=(3,))
 
 
 def second_step(terms, got, axis, done=()):
-    rows = terms.shape[1]
-    two, six, *got = lax.optimization_barrier((terms[2], terms[6], *got, *done))[:4]
+    rows = terms[2].shape[0]
+    two, six, *got = lax.optimization_barrier((terms[2], terms[3], *got, *done))[:4]
     out = [(t.astype(f32) + g[rows:].astype(f32)).astype(bf16) for t, g in zip((two, six), got)]
     return out, [send(o, axis + move) for o, move in zip(out, ("^3", "^1"))]
 
 
 def halve(terms, axis, done=()):
-    got = [send(value, axis + move) for value, move in zip(first_two(terms), ("^1", "^3"))]
+    got = [send(value, axis + move) for value, move in zip(terms[0:2], ("^1", "^3"))]
     return (got, *second_step(terms, got, axis, done))
 
 
 def finish(terms, got, last, done=()):
-    three, seven = lax.optimization_barrier((terms[3], terms[7], *done))[:2]
-    rows = terms.shape[1]
-    return [t.astype(f32) + g[:rows].astype(f32) + e.astype(f32) for t, g, e in zip((three, seven), got, last)]
+    low, high = lax.optimization_barrier((terms[4], terms[5], *done))[:2]
+    rows = terms[4].shape[0]
+    return [t.astype(f32) + g[:rows].astype(f32) + e.astype(f32) for t, g, e in zip((low, high), got, last)]
 
 
 def gather_both(own, cot):
@@ -279,7 +315,7 @@
 
     own = rows_cat(inputs, jnp.broadcast_to(gain.reshape(1, 512), (16, 512)))
     x_pieces, cot_pieces = gather_both(own, d_out)
-    x_full, x_keep, x_core, x_same, x_cross = assemble(spot, x_pieces)
+    x_full, gains, x_keep, x_core, x_same, x_cross = assemble(spot, x_pieces)
     x_same, x_cross = send(x_same, "z^3"), send(x_cross, "z^1")
     gate, up_val, hidden, inv, core_one = forward(after(x_full, *cot_pieces[1:3]), x_core, w3)
     core_one = send(core_one, "c")
@@ -288,33 +324,35 @@
     core_two = send(core_two, "c")
     branch_terms = branch_rows(order(y), after(hidden, d_pair), w3)
     pair_z = send(d_pair, "z^1")
-    down_terms = outer("down_terms", order(x), [(after(cot_mine, branch_terms), 0), (core_two, 0)], [(hidden, 0), (core_one, 1024)], 512, 384)
-    branch_got = [send(value, move) for value, move in zip(first_two(branch_terms), ("y^1", "y^3"))]
-    d_terms = pair_rows(order(y), after(d_pair, down_terms, *branch_got), products, w3)
+    down_terms = outer("down_terms", order(x), [(after(cot_mine, branch_terms[0]), 0), (core_two, 0)], [(hidden, 0), (core_one, 1024)], 512, 384)
+    branch_got = [send(value, move) for value, move in zip(branch_terms[0:2], ("y^1", "y^3"))]
+    d_terms = pair_rows(order(y), after(d_pair, down_terms[0]), products, w3)
     down_got, _, down_last = halve(down_terms, "x")
-    d_got, _, d_last = halve(d_terms, "y", down_got)
-    core_three = send(jnp.concatenate([x_cross, after(pair_z, *down_got, *d_got)], axis=1), "c")
+    d_terms = lax.optimization_barrier((*d_terms, *branch_got))[:6]
+    d_got = [send(value, move) for value, move in zip(d_terms[0:2], ("y^1", "y^3"))]
+    core_three = send(jnp.concatenate([x_cross, after(pair_z, d_terms[0], *down_got)], axis=1), "c")
     pair_terms = outer(
         "pair_terms", order(x), [(x_keep, 0), (x_same, 0), (core_one, 0), (core_three, 0)],
         [(d_pair, 0), (pair_z, 0), (core_two, 2048), (core_three, 1024)], 256, 768,
     )
-    down_last = lax.optimization_barrier((*down_last, pair_terms))[:2]
-    pair_got, pair_out, pair_last = halve(after(pair_terms, *down_last), "x")
+    down_last = lax.optimization_barrier((*down_last, pair_terms[0]))[:2]
+    pair_terms = lax.optimization_barrier((*pair_terms, *down_last))[:6]
+    pair_got, pair_out, pair_last = halve(pair_terms, "x")
     d_w_gate, d_w_up = finish(pair_terms, pair_got, pair_last)
-    down = finish(down_terms, down_got, down_last, (pair_terms,))
+    down = finish(down_terms, down_got, down_last, (pair_terms[0],))
     d_w_down = jnp.concatenate(down, axis=1)
     lower = z_lo == 0
     theirs = jnp.where(lower, d_w_down[256:], d_w_down[:256]).astype(bf16)
     d_w_down = jnp.where(lower, d_w_down[:256], d_w_down[256:]) + send(theirs, "z^1").astype(f32)
 
-    d_last = lax.optimization_barrier((*d_last, pair_terms))[:2]
+    _, d_last = second_step(d_terms, d_got, "y", (pair_terms[0],))
     d_low, d_high = finish(d_terms, d_got, d_last)
-    _, branch_last = second_step(branch_terms, branch_got, "y", (pair_terms, *d_last))
+    _, branch_last = second_step(branch_terms, branch_got, "y", (pair_terms[0], *d_last))
     low, high = finish(branch_terms, branch_got, branch_last)
     upper = z_hi == 1
     mine = jnp.where(upper, d_high, d_low)
     theirs = send(jnp.where(upper, d_low, d_high).astype(bf16), "z+2")
-    mine = after(mine, pair_terms) + theirs.astype(f32)
+    mine = mine + theirs.astype(f32)
     theirs = send(after(jnp.where(upper, low, high).astype(bf16), theirs), "z+2")
     branch = (jnp.where(upper, high, low) + theirs.astype(f32)).astype(bf16)
     d_normed, products = mine[:, :512], mine[:, 512:513] / width
@@ -327,7 +365,7 @@
             d_gain = after(d_gain, *pair_out)
         d_gain = d_gain + send(d_gain, move)
 
-    gain_rows = lax.dynamic_slice(x_full, (256, s * 256), (1, 256)).astype(f32).reshape(256, 1)
+    gain_rows = lax.dynamic_slice(gains, (0, s * 256), (1, 256)).astype(f32).reshape(256, 1)
     d_weights = jnp.stack(
         [(d_w_gate * gain_rows).astype(bf16), (d_w_up * gain_rows).astype(bf16), d_w_down.astype(bf16)], axis=1
     )

time: 181 us -> 171 us (0.945)
  local copies, waits for them, and re-layouts: 19.6 us -> 6.48 us
  waiting for transfers between devices: 56.4 us -> 68.3 us
  other arithmetic: 19.7 us -> 13.7 us
  starting transfers between devices: 46.9 us -> 43 us
    ppermute x40, waiting for transfers between devices: 56.4 us -> 68.3 us  [send(): return lax.ppermute(value, AXES, pairs(moves[move]))]
    unnamed x56 -> x72, local copies, waits for them, and re-layouts: 13.1 us -> 5.46 us
    convert_element_type x8, other arithmetic: 6.7 us -> 2.3 us  [second_step(): (t.astype(f32) + g[rows:].astype(f32)).astype(bf16)]
    ppermute x40, starting transfers between devices: 46.9 us -> 43 us  [send(): return lax.ppermute(value, AXES, pairs(moves[move]))]
    slice x4 -> x0, local copies, waits for them, and re-layouts: 3.65 us -> none  [first_two(): terms[4 * h:4 * h + 2].reshape(2 * terms.shape[1], terms.shape[2])]
  transfers between devices with their start and end apart: 40 -> 40, of which waited for: 18 -> 21; matrix products, arithmetic and copies ran while one was open for 11% -> 6% of each run, Pallas kernels for 17% -> 18%
where the time goes in v5:
time: 171 us; the launch traced here: 170 us
  waiting for transfers between devices  68.3 us (40%)
  starting transfers between devices  43 us (25%)
  Pallas kernels  37.8 us (22%)
  other arithmetic  13.7 us (8%)
  local copies, waits for them, and re-layouts  6.48 us (4%)
    ppermute x40, waiting for transfers between devices, send(): return lax.ppermute(value, AXES, pairs(moves[move]))  68.3 us
    ppermute x40, starting transfers between devices, send(): return lax.ppermute(value, AXES, pairs(moves[move]))  43 us
    pallas_call x7, Pallas kernels, call(): pl.pallas_call(whole, in_specs=[pl.BlockSpec(memory_space=space) for spac...  37.8 us
    unnamed x72, local copies, waits for them, and re-layouts  5.46 us
  transfers between devices with their start and end apart: 40, of which 21 were waited for; matrix products, arithmetic and copies ran while one was open for 6% of the time, Pallas kernels for 18%

profile of v5, /device:TPU:0, one launch (start us, length us, event | category | flops | bytes accessed | tf_op | source)
XLA Modules:
  0.0 170.3 jit_solution(17578153076383690525)
XLA Ops:
  1.3 1.0 pad_maximum_fusion.6.refs_1_
  2.3 3.2 %collective-permute-start.1 = (bf16[272,512]{1,0:T(8,128)(2,1)S(1)}, bf16[272,512]{1,0:T(8,128)(2,1)S(1)}, u32[]{:S(2)}, u32[]{:S(2)}) collective-permute-start(bf16[272,512]{1,0:T(8,128)(2,1)S(1)} %pad_maximum_fusion.6.refs_1_), channel_id=1, source_target_pairs={{0,48},{1,49},{2,50},{3,51},{64,112},{65,113},{66,114},{67,115},{1... | collective-permute-start | bytes 835592 | tf_op jit(solution)/shard_map/ppermute | solution.py:43
  5.5 3.9 %collective-permute-start.2 = (bf16[272,512]{1,0:T(8,128)(2,1)S(1)}, bf16[272,512]{1,0:T(8,128)(2,1)S(1)}, u32[]{:S(2)}, u32[]{:S(2)}) collective-permute-start(bf16[272,512]{1,0:T(8,128)(2,1)S(1)} %pad_maximum_fusion.6.refs_1_), channel_id=1, source_target_pairs={{0,64},{1,65},{2,66},{3,67},{64,0},{65,1},{66,2},{67,3},{16,80},{1... | collective-permute-start | bytes 835592 | tf_op jit(solution)/shard_map/ppermute | solution.py:43
  9.4 2.0 %collective-permute-done.1.refs_3_ = bf16[272,512]{1,0:T(8,128)(2,1)S(1)} collective-permute-done((bf16[272,512]{1,0:T(8,128)(2,1)S(1)}, bf16[272,512]{1,0:T(8,128)(2,1)S(1)}, u32[]{:S(2)}, u32[]{:S(2)}) %collective-permute-start.1) | collective-permute-done | bytes 278560 | tf_op jit(solution)/shard_map/ppermute | solution.py:43
  11.4 4.3 %collective-permute-done.2.refs_4_ = bf16[272,512]{1,0:T(8,128)(2,1)S(1)} collective-permute-done((bf16[272,512]{1,0:T(8,128)(2,1)S(1)}, bf16[272,512]{1,0:T(8,128)(2,1)S(1)}, u32[]{:S(2)}, u32[]{:S(2)}) %collective-permute-start.2) | collective-permute-done | bytes 278560 | tf_op jit(solution)/shard_map/ppermute | solution.py:43
  15.8 0.8 collective-permute-start.4
  16.6 1.8 %collective-permute-done.refs_2_ = bf16[272,512]{1,0:T(8,128)(2,1)S(1)} collective-permute-done((bf16[272,512]{1,0:T(8,128)(2,1)S(1)}, bf16[272,512]{1,0:T(8,128)(2,1)S(1)}, u32[]{:S(2)}, u32[]{:S(2)}) %collective-permute-start) | collective-permute-done | bytes 278560 | tf_op jit(solution)/shard_map/ppermute | solution.py:43
  18.6 2.7 %collective-permute-start.5 = (bf16[256,512]{1,0:T(8,128)(2,1)S(1)}, bf16[256,512]{1,0:T(8,128)(2,1)S(1)}, u32[]{:S(2)}, u32[]{:S(2)}) collective-permute-start(bf16[256,512]{1,0:T(8,128)(2,1)S(1)} %copy-done.34), channel_id=1, source_target_pairs={{0,64},{1,65},{2,66},{3,67},{64,0},{65,1},{66,2},{67,3},{16,80},{1... | collective-permute-start | bytes 786440 | tf_op jit(solution)/shard_map/ppermute | solution.py:43
  21.3 5.5 %collective-permute-done.5 = bf16[256,512]{1,0:T(8,128)(2,1)S(1)} collective-permute-done((bf16[256,512]{1,0:T(8,128)(2,1)S(1)}, bf16[256,512]{1,0:T(8,128)(2,1)S(1)}, u32[]{:S(2)}, u32[]{:S(2)}) %collective-permute-start.5) | collective-permute-done | bytes 262176 | tf_op jit(solution)/shard_map/ppermute | solution.py:43
  26.7 2.7 %collective-permute-done.3.refs_5_ = bf16[400,512]{1,0:T(8,128)(2,1)S(1)} collective-permute-done((bf16[400,512]{1,0:T(8,128)(2,1)S(1)}, bf16[400,512]{1,0:T(8,128)(2,1)S(1)}, u32[]{:S(2)}, u32[]{:S(2)}) %collective-permute-start.3) | collective-permute-done | bytes 409632 | tf_op jit(solution)/shard_map/ppermute | solution.py:43
  29.8 0.7 pad_maximum_fusion.7
  30.5 1.6 collective-permute-start.6
  32.2 1.5 collective-permute-start.7
  33.8 5.1 %collective-permute-done.6.refs_7_ = bf16[272,512]{1,0:T(8,128)(2,1)} collective-permute-done((bf16[272,512]{1,0:T(8,128)(2,1)}, bf16[272,512]{1,0:T(8,128)(2,1)}, u32[]{:S(2)}, u32[]{:S(2)}) %collective-permute-start.6) | collective-permute-done | bytes 278560 | tf_op jit(solution)/shard_map/ppermute | solution.py:43
  38.9 1.4 assemble.1
  41.0 0.8 copy-done.15
  41.8 1.8 %collective-permute-start.9 = (bf16[256,1024]{1,0:T(8,128)(2,1)S(1)}, bf16[256,1024]{1,0:T(8,128)(2,1)S(1)}, u32[]{:S(2)}, u32[]{:S(2)}) collective-permute-start(bf16[256,1024]{1,0:T(8,128)(2,1)S(1)} %get-tuple-element.99), channel_id=1, source_target_pairs={{0,66},{1,67},{2,64},{3,65},{64,2},{65,3},{66,0},{67,1},{16,82},{1... | collective-permute-start | bytes 1572872 | tf_op jit(solution)/shard_map/ppermute | solution.py:43
  44.4 1.5 collective-permute-start.11
  45.9 6.3 %forward.1 = (f32[256,768]{1,0:T(8,128)S(1)}, f32[256,768]{1,0:T(8,128)S(1)}, bf16[256,768]{1,0:T(8,128)(2,1)S(1)}, f32[256,128]{1,0:T(8,128)S(1)}, bf16[256,1792]{1,0:T(8,128)(2,1)}) custom-call(bf16[272,4096]{1,0:T(8,128)(2,1)S(1)} %get-tuple-element.96.refs_0_, bf16[256,1024]{1,0:T(8,128)(2,1)S(1)} %get-tuple-element.97.refs_1_, ...), custom_call_target="tpu_custom_call" | custom-call | flops 3221225472 | bytes 16777216 | tf_op jit(solution)/shard_map/forward/pallas_call | solution.py:89
  52.9 0.8 copy-done.17
  53.7 6.9 %backward.1 = (bf16[256,1536]{1,0:T(8,128)(2,1)S(1)}, bf16[256,128]{1,0:T(8,128)(2,1)S(1)}, bf16[256,2048]{1,0:T(8,128)(2,1)S(1)}, bf16[256,3584]{1,0:T(8,128)(2,1)}) custom-call(s32[10]{0:T(128)S(1)} %stack.116.refs_0_, bf16[512,512]{1,0:T(8,128)(2,1)S(1)} %pad_maximum_fusion.3.refs_1_, bf16[512,512]{1,0:T(8,128)(2,1)S(1)} %collective-permute-done.7.refs_2_, ...), custom_call_target="tpu_custom_call" | custom-call | flops 1610612736 | bytes 8388608 | tf_op jit(solution)/shard_map/backward/pallas_call | solution.py:89
  60.6 1.0 copy-done.11
  62.2 1.5 collective-permute-start.16
  63.7 5.2 %branch_rows.1 = (bf16[512,512]{1,0:T(8,128)(2,1)S(1)}, bf16[512,512]{1,0:T(8,128)(2,1)S(1)}, bf16[256,512]{1,0:T(8,128)(2,1)S(1)}, bf16[256,512]{1,0:T(8,128)(2...) custom-call(s32[8]{0:T(128)S(1)} %stack.105.refs_0_, ...), custom_call_target="tpu_custom_call" | custom-call | flops 1610612736 | bytes 8388608 | tf_op jit(solution)/shard_map/branch_rows/pallas_call | solution.py:89
  68.9 0.7 copy-done.6
  69.6 0.7 copy-done.8
  70.3 4.8 %down_terms.1 = (bf16[1024,384]{1,0:T(8,128)(2,1)S(1)}, bf16[1024,384]{1,0:T(8,128)(2,1)S(1)}, bf16[512,384]{1,0:T(8,128)(2,1)S(1)}, bf16[512,384]{1,0:T(8,128)(...) custom-call(s32[8]{0:T(128)S(1)} %stack.121.refs_0_, bf16[256,2048]{1,0:T(8,128)(2,1)S(1)} %copy-done.12, ...), custom_call_target="tpu_custom_call" | custom-call | flops 1610612736 | bytes 8388608 | tf_op jit(solution)/shard_map/down_terms/pallas_call | solution.py:89
  75.1 2.8 %collective-permute-start.19 = (bf16[1024,384]{1,0:T(8,128)(2,1)S(1)}, bf16[1024,384]{1,0:T(8,128)(2,1)S(1)}, u32[]{:S(2)}, u32[]{:S(2)}) collective-permute-start(bf16[1024,384]{1,0:T(8,128)(2,1)S(1)} %get-tuple-element.129), channel_id=1, source_target_pairs={{0,12},{1,13},{2,14},{3,15},{64,76},{65,77},{66,78},{67,79},{16,28... | collective-permute-start | bytes 2359304 | tf_op jit(solution)/shard_map/ppermute | solution.py:43
  78.2 1.7 collective-permute-start.13
  79.8 7.1 %pair_rows.1 = (bf16[512,640]{1,0:T(8,128)(2,1)S(1)}, bf16[512,640]{1,0:T(8,128)(2,1)S(1)}, bf16[256,640]{1,0:T(8,128)(2,1)S(1)}, bf16[256,640]{1,0:T(8,128)(2,1...) custom-call(s32[8]{0:T(128)S(1)} %stack.105.refs_0_, ...), custom_call_target="tpu_custom_call" | custom-call | flops 3221225472 | bytes 16777216 | tf_op jit(solution)/shard_map/pair_rows/pallas_call | solution.py:89
  87.0 5.5 %collective-permute-done.13 = bf16[512,512]{1,0:T(8,128)(2,1)S(1)} collective-permute-done((bf16[512,512]{1,0:T(8,128)(2,1)S(1)}, bf16[512,512]{1,0:T(8,128)(2,1)S(1)}, u32[]{:S(2)}, u32[]{:S(2)}) %collective-permute-start.13) | collective-permute-done | bytes 524320 | tf_op jit(solution)/shard_map/ppermute | solution.py:43
  92.6 3.0 %collective-permute-done.19 = bf16[1024,384]{1,0:T(8,128)(2,1)S(1)} collective-permute-done((bf16[1024,384]{1,0:T(8,128)(2,1)S(1)}, bf16[1024,384]{1,0:T(8,128)(2,1)S(1)}, u32[]{:S(2)}, u32[]{:S(2)}) %collective-permute-start.19) | collective-permute-done | bytes 786464 | tf_op jit(solution)/shard_map/ppermute | solution.py:43
  95.6 1.3 collective-permute-done.18
  97.0 1.6 collective-permute-start.23
  99.9 1.6 collective-permute-start.21
  101.5 6.0 %pair_terms.1 = (bf16[512,768]{1,0:T(8,128)(2,1)S(1)}, bf16[512,768]{1,0:T(8,128)(2,1)S(1)}, bf16[256,768]{1,0:T(8,128)(2,1)S(1)}, bf16[256,768]{1,0:T(8,128)(2,...) custom-call(s32[8]{0:T(128)S(1)} %stack.121.refs_0_, bf16[256,1024]{1,0:T(8,128)(2,1)S(1)} %copy-done.16, ...), custom_call_target="tpu_custom_call" | custom-call | flops 3221225472 | bytes 8388608 | tf_op jit(solution)/shard_map/pair_terms/pallas_call | solution.py:89
  107.5 0.7 copy-done
  108.3 2.1 %collective-permute-done.22 = bf16[512,384]{1,0:T(8,128)(2,1)S(1)} collective-permute-done((bf16[512,384]{1,0:T(8,128)(2,1)S(1)}, bf16[512,384]{1,0:T(8,128)(2,1)S(1)}, u32[]{:S(2)}, u32[]{:S(2)}) %collective-permute-start.22) | collective-permute-done | bytes 393248 | tf_op jit(solution)/shard_map/ppermute | solution.py:43
  110.4 1.6 collective-permute-done.21
  112.0 4.6 %collective-permute-done.24 = bf16[512,640]{1,0:T(8,128)(2,1)S(1)} collective-permute-done((bf16[512,640]{1,0:T(8,128)(2,1)S(1)}, bf16[512,640]{1,0:T(8,128)(2,1)S(1)}, u32[]{:S(2)}, u32[]{:S(2)}) %collective-permute-start.24) | collective-permute-done | bytes 655392 | tf_op jit(solution)/shard_map/ppermute | solution.py:43
  116.7 0.9 add_convert_fusion.5
  117.6 0.8 add_convert_fusion.6
  118.5 1.0 collective-permute-start.25
  119.8 1.3 collective-permute-start.34
  121.1 1.6 convert_add_fusion
  122.8 4.1 %collective-permute-done.26 = bf16[256,640]{1,0:T(8,128)(2,1)} collective-permute-done((bf16[256,640]{1,0:T(8,128)(2,1)}, bf16[256,640]{1,0:T(8,128)(2,1)}, u32[]{:S(2)}, u32[]{:S(2)}) %collective-permute-start.26) | collective-permute-done | bytes 327712 | tf_op jit(solution)/shard_map/ppermute | solution.py:43
  126.8 2.1 %collective-permute-done.25 = bf16[256,640]{1,0:T(8,128)(2,1)} collective-permute-done((bf16[256,640]{1,0:T(8,128)(2,1)}, bf16[256,640]{1,0:T(8,128)(2,1)}, u32[]{:S(2)}, u32[]{:S(2)}) %collective-permute-start.25) | collective-permute-done | bytes 327712 | tf_op jit(solution)/shard_map/ppermute | solution.py:43
  129.0 1.4 select_convert_fusion.1
  130.4 1.9 %collective-permute-start.29 = (bf16[256,640]{1,0:T(8,128)(2,1)S(1)}, bf16[256,640]{1,0:T(8,128)(2,1)S(1)}, u32[]{:S(2)}, u32[]{:S(2)}) collective-permute-start(bf16[256,640]{1,0:T(8,128)(2,1)S(1)} %select_convert_fusion.1), channel_id=1, source_target_pairs={{0,64},{1,65},{2,66},{3,67},{64,0},{65,1},{66,2},{67,3},{16,80},{1... | collective-permute-start | bytes 983048 | tf_op jit(solution)/shard_map/ppermute | solution.py:43
  132.4 0.8 collective-permute-start.28
  133.5 6.5 %collective-permute-done.29 = bf16[256,640]{1,0:T(8,128)(2,1)S(1)} collective-permute-done((bf16[256,640]{1,0:T(8,128)(2,1)S(1)}, bf16[256,640]{1,0:T(8,128)(2,1)S(1)}, u32[]{:S(2)}, u32[]{:S(2)}) %collective-permute-start.29) | collective-permute-done | bytes 327712 | tf_op jit(solution)/shard_map/ppermute | solution.py:43
  140.0 1.4 convert_add_fusion.2
  141.5 0.9 fusion.3
  142.4 1.1 collective-permute-done.31
  143.5 0.8 collective-permute-start.39
  144.3 1.3 collective-permute-start.32
  145.8 1.9 %collective-permute-start.30 = (bf16[256,512]{1,0:T(8,128)(2,1)S(1)}, bf16[256,512]{1,0:T(8,128)(2,1)S(1)}, u32[]{:S(2)}, u32[]{:S(2)}) collective-permute-start(bf16[256,512]{1,0:T(8,128)(2,1)S(1)} %select_convert_fusion.2), channel_id=1, source_target_pairs={{0,64},{1,65},{2,66},{3,67},{64,0},{65,1},{66,2},{67,3},{16,80},{1... | collective-permute-start | bytes 786440 | tf_op jit(solution)/shard_map/ppermute | solution.py:43
  147.8 7.8 %collective-permute-done.32 = f32[1,512]{1,0:T(1,128)S(1)} collective-permute-done((f32[1,512]{1,0:T(1,128)S(1)}, f32[1,512]{1,0:T(1,128)S(1)}, u32[]{:S(2)}, u32[]{:S(2)}) %collective-permute-start.32) | collective-permute-done | bytes 2080 | tf_op jit(solution)/shard_map/ppermute | solution.py:43
  156.8 1.7 %collective-permute-start.38 = (bf16[256,768]{1,0:T(8,128)(2,1)S(1)}, bf16[256,768]{1,0:T(8,128)(2,1)S(1)}, u32[]{:S(2)}, u32[]{:S(2)}) collective-permute-start(bf16[256,768]{1,0:T(8,128)(2,1)S(1)} %add_convert_fusion.1), channel_id=1, source_target_pairs={{0,4},{1,5},{2,6},{3,7},{64,68},{65,69},{66,70},{67,71},{16,20},{1... | collective-permute-start | bytes 1179656 | tf_op jit(solution)/shard_map/ppermute | solution.py:43
  158.5 1.5 collective-permute-start.37
  160.1 0.9 collective-permute-start.36
  161.1 6.2 %collective-permute-done.36 = f32[1,512]{1,0:T(1,128)S(1)} collective-permute-done((f32[1,512]{1,0:T(1,128)S(1)}, f32[1,512]{1,0:T(1,128)S(1)}, u32[]{:S(2)}, u32[]{:S(2)}) %collective-permute-start.36) | collective-permute-done | bytes 2080 | tf_op jit(solution)/shard_map/ppermute | solution.py:43
  167.9 0.9 add_convert_fusion.7
  169.2 1.1 pad_maximum_fusion.1
  (138 shorter events, 9.3 us)
Async XLA Ops:
  1.3 17.2 %copy-start.34 = (bf16[256,512]{1,0:T(8,128)(2,1)S(1)}, bf16[256,512]{1,0:T(8,128)(2,1)}, u32[]{:S(2)}) copy-start(bf16[256,512]{1,0:T(8,128)(2,1)} %param.7) | copy-start | bytes 786436
  2.3 9.1 %collective-permute-start.1 = (bf16[272,512]{1,0:T(8,128)(2,1)S(1)}, bf16[272,512]{1,0:T(8,128)(2,1)S(1)}, u32[]{:S(2)}, u32[]{:S(2)}) collective-permute-start(bf16[272,512]{1,0:T(8,128)(2,1)S(1)} %pad_maximum_fusion.6.refs_1_), channel_id=1, source_target_pairs={{0,48},{1,49},{2,50},{3,51},{64,112},{65,113},{66,114},{67,115},{1... | collective-permute-start | bytes 835592 | tf_op jit(solution)/shard_map/ppermute | solution.py:43
  5.5 10.2 %collective-permute-start.2 = (bf16[272,512]{1,0:T(8,128)(2,1)S(1)}, bf16[272,512]{1,0:T(8,128)(2,1)S(1)}, u32[]{:S(2)}, u32[]{:S(2)}) collective-permute-start(bf16[272,512]{1,0:T(8,128)(2,1)S(1)} %pad_maximum_fusion.6.refs_1_), channel_id=1, source_target_pairs={{0,64},{1,65},{2,66},{3,67},{64,0},{65,1},{66,2},{67,3},{16,80},{1... | collective-permute-start | bytes 835592 | tf_op jit(solution)/shard_map/ppermute | solution.py:43
  9.4 9.0 %collective-permute-start = (bf16[272,512]{1,0:T(8,128)(2,1)S(1)}, bf16[272,512]{1,0:T(8,128)(2,1)S(1)}, u32[]{:S(2)}, u32[]{:S(2)}) collective-permute-start(bf16[272,512]{1,0:T(8,128)(2,1)S(1)} %pad_maximum_fusion.6.refs_1_), channel_id=1, source_target_pairs={{0,16},{1,17},{2,18},{3,19},{64,80},{65,81},{66,82},{67,83},{16,32... | collective-permute-start | bytes 835592 | tf_op jit(solution)/shard_map/ppermute | solution.py:43
  15.8 13.7 %collective-permute-start.4 = (bf16[416,512]{1,0:T(8,128)(2,1)S(1)}, bf16[416,512]{1,0:T(8,128)(2,1)S(1)}, u32[]{:S(2)}, u32[]{:S(2)}) collective-permute-start(bf16[416,512]{1,0:T(8,128)(2,1)S(1)} %pad_maximum_fusion.4), channel_id=1, source_target_pairs={{0,48},{1,49},{2,50},{3,51},{64,112},{65,113},{66,114},{67,115},{1... | collective-permute-start | bytes 1277960 | tf_op jit(solution)/shard_map/ppermute | solution.py:43
  18.5 11.0 %collective-permute-start.3 = (bf16[400,512]{1,0:T(8,128)(2,1)S(1)}, bf16[400,512]{1,0:T(8,128)(2,1)S(1)}, u32[]{:S(2)}, u32[]{:S(2)}) collective-permute-start(bf16[400,512]{1,0:T(8,128)(2,1)S(1)} %pad_maximum_fusion.5), channel_id=1, source_target_pairs={{0,16},{1,17},{2,18},{3,19},{64,80},{65,81},{66,82},{67,83},{16,32... | collective-permute-start | bytes 1228808 | tf_op jit(solution)/shard_map/ppermute | solution.py:43
  18.6 8.1 %collective-permute-start.5 = (bf16[256,512]{1,0:T(8,128)(2,1)S(1)}, bf16[256,512]{1,0:T(8,128)(2,1)S(1)}, u32[]{:S(2)}, u32[]{:S(2)}) collective-permute-start(bf16[256,512]{1,0:T(8,128)(2,1)S(1)} %copy-done.34), channel_id=1, source_target_pairs={{0,64},{1,65},{2,66},{3,67},{64,0},{65,1},{66,2},{67,3},{16,80},{1... | collective-permute-start | bytes 786440 | tf_op jit(solution)/shard_map/ppermute | solution.py:43
  29.5 14.2 %collective-permute-start.8 = (bf16[512,512]{1,0:T(8,128)(2,1)S(1)}, bf16[512,512]{1,0:T(8,128)(2,1)S(1)}, u32[]{:S(2)}, u32[]{:S(2)}) collective-permute-start(bf16[512,512]{1,0:T(8,128)(2,1)S(1)} %pad_maximum_fusion.3.refs_1_), channel_id=1, source_target_pairs={{0,48},{1,49},{2,50},{3,51},{64,112},{65,113},{66,114},{67,115},{1... | collective-permute-start | bytes 1572872 | tf_op jit(solution)/shard_map/ppermute | solution.py:43
  30.5 8.4 %collective-permute-start.6 = (bf16[272,512]{1,0:T(8,128)(2,1)}, bf16[272,512]{1,0:T(8,128)(2,1)}, u32[]{:S(2)}, u32[]{:S(2)}) collective-permute-start(bf16[272,512]{1,0:T(8,128)(2,1)} %pad_maximum_fusion.7), channel_id=1, source_target_pairs={{0,64},{1,65},{2,66},{3,67},{64,0},{65,1},{66,2},{67,3},{16,80},{1... | collective-permute-start | bytes 835592 | tf_op jit(solution)/shard_map/ppermute | solution.py:43
  32.2 12.2 %collective-permute-start.7 = (bf16[512,512]{1,0:T(8,128)(2,1)S(1)}, bf16[512,512]{1,0:T(8,128)(2,1)S(1)}, u32[]{:S(2)}, u32[]{:S(2)}) collective-permute-start(bf16[512,512]{1,0:T(8,128)(2,1)S(1)} %pad_maximum_fusion.3.refs_1_), channel_id=1, source_target_pairs={{0,16},{1,17},{2,18},{3,19},{64,80},{65,81},{66,82},{67,83},{16,32... | collective-permute-start | bytes 1572872 | tf_op jit(solution)/shard_map/ppermute | solution.py:43
  41.8 11.0 %collective-permute-start.9 = (bf16[256,1024]{1,0:T(8,128)(2,1)S(1)}, bf16[256,1024]{1,0:T(8,128)(2,1)S(1)}, u32[]{:S(2)}, u32[]{:S(2)}) collective-permute-start(bf16[256,1024]{1,0:T(8,128)(2,1)S(1)} %get-tuple-element.99), channel_id=1, source_target_pairs={{0,66},{1,67},{2,64},{3,65},{64,2},{65,3},{66,0},{67,1},{16,82},{1... | collective-permute-start | bytes 1572872 | tf_op jit(solution)/shard_map/ppermute | solution.py:43
  43.6 10.0 %collective-permute-start.10 = (bf16[256,1024]{1,0:T(8,128)(2,1)S(1)}, bf16[256,1024]{1,0:T(8,128)(2,1)S(1)}, u32[]{:S(2)}, u32[]{:S(2)}) collective-permute-start(bf16[256,1024]{1,0:T(8,128)(2,1)S(1)} %get-tuple-element.100), channel_id=1, source_target_pairs={{0,2},{1,3},{2,0},{3,1},{64,66},{65,67},{66,64},{67,65},{16,18},{1... | collective-permute-start | bytes 1572872 | tf_op jit(solution)/shard_map/ppermute | solution.py:43
  43.7 10.0 %collective-permute-start.12 = (bf16[256,512]{1,0:T(8,128)(2,1)S(1)}, bf16[256,512]{1,0:T(8,128)(2,1)S(1)}, u32[]{:S(2)}, u32[]{:S(2)}) collective-permute-start(bf16[256,512]{1,0:T(8,128)(2,1)S(1)} %pad_maximum_fusion.9), channel_id=1, source_target_pairs={{0,48},{1,49},{2,50},{3,51},{64,112},{65,113},{66,114},{67,115},{1... | collective-permute-start | bytes 786440 | tf_op jit(solution)/shard_map/ppermute | solution.py:43
  44.4 9.2 %collective-permute-start.11 = (bf16[256,512]{1,0:T(8,128)(2,1)S(1)}, bf16[256,512]{1,0:T(8,128)(2,1)S(1)}, u32[]{:S(2)}, u32[]{:S(2)}) collective-permute-start(bf16[256,512]{1,0:T(8,128)(2,1)S(1)} %pad_maximum_fusion.8), channel_id=1, source_target_pairs={{0,16},{1,17},{2,18},{3,19},{64,80},{65,81},{66,82},{67,83},{16,32... | collective-permute-start | bytes 786440 | tf_op jit(solution)/shard_map/ppermute | solution.py:43
  53.6 6.9 %copy-start.30 = (bf16[256,1024]{1,0:T(8,128)(2,1)}, bf16[256,1024]{1,0:T(8,128)(2,1)S(1)}, u32[]{:S(2)}) copy-start(bf16[256,1024]{1,0:T(8,128)(2,1)S(1)} %collective-permute-done.10) | copy-start | bytes 1572868
  61.5 8.7 %collective-permute-start.17 = (bf16[256,3584]{1,0:T(8,128)(2,1)}, bf16[256,3584]{1,0:T(8,128)(2,1)}, u32[]{:S(2)}, u32[]{:S(2)}) collective-permute-start(bf16[256,3584]{1,0:T(8,128)(2,1)} %get-tuple-element.118), channel_id=1, source_target_pairs={{0,1},{1,0},{2,3},{3,2},{64,65},{65,64},{66,67},{67,66},{16,17},{1... | collective-permute-start | bytes 5505032 | tf_op jit(solution)/shard_map/ppermute | solution.py:43
  61.5 8.7 %collective-permute-start.15 = (bf16[256,1792]{1,0:T(8,128)(2,1)}, bf16[256,1792]{1,0:T(8,128)(2,1)}, u32[]{:S(2)}, u32[]{:S(2)}) collective-permute-start(bf16[256,1792]{1,0:T(8,128)(2,1)} %get-tuple-element.115), channel_id=1, source_target_pairs={{0,1},{1,0},{2,3},{3,2},{64,65},{65,64},{66,67},{67,66},{16,17},{1... | collective-permute-start | bytes 2752520 | tf_op jit(solution)/shard_map/ppermute | solution.py:43
  62.2 30.4 %collective-permute-start.16 = (bf16[256,1536]{1,0:T(8,128)(2,1)S(1)}, bf16[256,1536]{1,0:T(8,128)(2,1)S(1)}, u32[]{:S(2)}, u32[]{:S(2)}) collective-permute-start(bf16[256,1536]{1,0:T(8,128)(2,1)S(1)} %get-tuple-element.120.refs_1_.refs_5_), channel_id=1, source_target_pairs={{0,2},{1,3},{2,0},{3,1},{64,66},{65,67},{66,64},{67,65},{16,18},{1... | collective-permute-start | bytes 2359304 | tf_op jit(solution)/shard_map/ppermute | solution.py:43
  63.7 6.6 %copy-start.12 = (bf16[256,2048]{1,0:T(8,128)(2,1)S(1)}, bf16[256,2048]{1,0:T(8,128)(2,1)}, u32[]{:S(2)}) copy-start(bf16[256,2048]{1,0:T(8,128)(2,1)} %copy-done.11) | copy-start | bytes 3145732
  75.1 11.9 %copy-start.2 = (bf16[512,384]{1,0:T(8,128)(2,1)}, bf16[512,384]{1,0:T(8,128)(2,1)S(1)}, u32[]{:S(2)}) copy-start(bf16[512,384]{1,0:T(8,128)(2,1)S(1)} %get-tuple-element.178) | copy-start | bytes 1179652
  75.1 11.9 %copy-start.4 = (bf16[512,384]{1,0:T(8,128)(2,1)}, bf16[512,384]{1,0:T(8,128)(2,1)S(1)}, u32[]{:S(2)}) copy-start(bf16[512,384]{1,0:T(8,128)(2,1)S(1)} %get-tuple-element.179) | copy-start | bytes 1179652
  75.1 20.5 %collective-permute-start.19 = (bf16[1024,384]{1,0:T(8,128)(2,1)S(1)}, bf16[1024,384]{1,0:T(8,128)(2,1)S(1)}, u32[]{:S(2)}, u32[]{:S(2)}) collective-permute-start(bf16[1024,384]{1,0:T(8,128)(2,1)S(1)} %get-tuple-element.129), channel_id=1, source_target_pairs={{0,12},{1,13},{2,14},{3,15},{64,76},{65,77},{66,78},{67,79},{16,28... | collective-permute-start | bytes 2359304 | tf_op jit(solution)/shard_map/ppermute | solution.py:43
  77.9 18.9 %collective-permute-start.18 = (bf16[1024,384]{1,0:T(8,128)(2,1)S(1)}, bf16[1024,384]{1,0:T(8,128)(2,1)S(1)}, u32[]{:S(2)}, u32[]{:S(2)}) collective-permute-start(bf16[1024,384]{1,0:T(8,128)(2,1)S(1)} %get-tuple-element.119), channel_id=1, source_target_pairs={{0,4},{1,5},{2,6},{3,7},{64,68},{65,69},{66,70},{67,71},{16,20},{1... | collective-permute-start | bytes 2359304 | tf_op jit(solution)/shard_map/ppermute | solution.py:43
  78.2 14.3 %collective-permute-start.13 = (bf16[512,512]{1,0:T(8,128)(2,1)S(1)}, bf16[512,512]{1,0:T(8,128)(2,1)S(1)}, u32[]{:S(2)}, u32[]{:S(2)}) collective-permute-start(bf16[512,512]{1,0:T(8,128)(2,1)S(1)} %get-tuple-element.110), channel_id=1, source_target_pairs={{0,48},{1,49},{2,50},{3,51},{64,112},{65,113},{66,114},{67,115},{1... | collective-permute-start | bytes 1572872 | tf_op jit(solution)/shard_map/ppermute | solution.py:43
  79.8 12.8 %collective-permute-start.14 = (bf16[512,512]{1,0:T(8,128)(2,1)S(1)}, bf16[512,512]{1,0:T(8,128)(2,1)S(1)}, u32[]{:S(2)}, u32[]{:S(2)}) collective-permute-start(bf16[512,512]{1,0:T(8,128)(2,1)S(1)} %get-tuple-element.113), channel_id=1, source_target_pairs={{0,16},{1,17},{2,18},{3,19},{64,80},{65,81},{66,82},{67,83},{16,0}... | collective-permute-start | bytes 1572872 | tf_op jit(solution)/shard_map/ppermute | solution.py:43
  79.8 17.0 %copy-start.31 = (bf16[256,1024]{1,0:T(8,128)(2,1)S(1)}, bf16[256,1024]{1,0:T(8,128)(2,1)}, u32[]{:S(2)}) copy-start(bf16[256,1024]{1,0:T(8,128)(2,1)} %copy-done.30) | copy-start | bytes 1572868
  95.6 5.9 %copy-start.28 = (bf16[1024,384]{1,0:T(8,128)(2,1)}, bf16[1024,384]{1,0:T(8,128)(2,1)S(1)}, u32[]{:S(2)}) copy-start(bf16[1024,384]{1,0:T(8,128)(2,1)S(1)} %collective-permute-done.19) | copy-start | bytes 2359300
  96.8 10.7 %copy-start.29 = (bf16[1024,384]{1,0:T(8,128)(2,1)}, bf16[1024,384]{1,0:T(8,128)(2,1)S(1)}, u32[]{:S(2)}) copy-start(bf16[1024,384]{1,0:T(8,128)(2,1)S(1)} %collective-permute-done.18) | copy-start | bytes 2359300
  96.9 4.5 %copy-start.16 = (bf16[256,1024]{1,0:T(8,128)(2,1)S(1)}, bf16[256,1024]{1,0:T(8,128)(2,1)}, u32[]{:S(2)}) copy-start(bf16[256,1024]{1,0:T(8,128)(2,1)} %copy-done.15) | copy-start | bytes 1572868
  96.9 4.5 %copy-start.18 = (bf16[256,1024]{1,0:T(8,128)(2,1)S(1)}, bf16[256,1024]{1,0:T(8,128)(2,1)}, u32[]{:S(2)}) copy-start(bf16[256,1024]{1,0:T(8,128)(2,1)} %copy-done.17) | copy-start | bytes 1572868
  96.9 4.5 %collective-permute-start.20 = (bf16[256,2560]{1,0:T(8,128)(2,1)S(1)}, bf16[256,2560]{1,0:T(8,128)(2,1)S(1)}, u32[]{:S(2)}, u32[]{:S(2)}) collective-permute-start(bf16[256,2560]{1,0:T(8,128)(2,1)S(1)} %pad_maximum_fusion), channel_id=1, source_target_pairs={{0,1},{1,0},{2,3},{3,2},{64,65},{65,64},{66,67},{67,66},{16,17},{1... | collective-permute-start | bytes 3932168 | tf_op jit(solution)/shard_map/ppermute | solution.py:43
  97.0 19.6 %collective-permute-start.23 = (bf16[512,640]{1,0:T(8,128)(2,1)S(1)}, bf16[512,640]{1,0:T(8,128)(2,1)S(1)}, u32[]{:S(2)}, u32[]{:S(2)}) collective-permute-start(bf16[512,640]{1,0:T(8,128)(2,1)S(1)} %get-tuple-element.128), channel_id=1, source_target_pairs={{0,16},{1,17},{2,18},{3,19},{64,80},{65,81},{66,82},{67,83},{16,0}... | collective-permute-start | bytes 1966088 | tf_op jit(solution)/shard_map/ppermute | solution.py:43
  98.7 18.0 %collective-permute-start.24 = (bf16[512,640]{1,0:T(8,128)(2,1)S(1)}, bf16[512,640]{1,0:T(8,128)(2,1)S(1)}, u32[]{:S(2)}, u32[]{:S(2)}) collective-permute-start(bf16[512,640]{1,0:T(8,128)(2,1)S(1)} %get-tuple-element.148), channel_id=1, source_target_pairs={{0,48},{1,49},{2,50},{3,51},{64,112},{65,113},{66,114},{67,115},{1... | collective-permute-start | bytes 1966088 | tf_op jit(solution)/shard_map/ppermute | solution.py:43
  99.4 11.0 %collective-permute-start.22 = (bf16[512,384]{1,0:T(8,128)(2,1)S(1)}, bf16[512,384]{1,0:T(8,128)(2,1)S(1)}, u32[]{:S(2)}, u32[]{:S(2)}) collective-permute-start(bf16[512,384]{1,0:T(8,128)(2,1)S(1)} %add_convert_fusion.3), channel_id=1, source_target_pairs={{0,4},{1,5},{2,6},{3,7},{64,68},{65,69},{66,70},{67,71},{16,20},{1... | collective-permute-start | bytes 1179656 | tf_op jit(solution)/shard_map/ppermute | solution.py:43
  99.9 12.1 %collective-permute-start.21 = (bf16[512,384]{1,0:T(8,128)(2,1)S(1)}, bf16[512,384]{1,0:T(8,128)(2,1)S(1)}, u32[]{:S(2)}, u32[]{:S(2)}) collective-permute-start(bf16[512,384]{1,0:T(8,128)(2,1)S(1)} %add_convert_fusion.4), channel_id=1, source_target_pairs={{0,12},{1,13},{2,14},{3,15},{64,76},{65,77},{66,78},{67,79},{16,28... | collective-permute-start | bytes 1179656 | tf_op jit(solution)/shard_map/ppermute | solution.py:43
  108.3 10.2 %copy-start.13 = (bf16[512,768]{1,0:T(8,128)(2,1)}, bf16[512,768]{1,0:T(8,128)(2,1)S(1)}, u32[]{:S(2)}) copy-start(bf16[512,768]{1,0:T(8,128)(2,1)S(1)} %get-tuple-element.145) | copy-start | bytes 2359300
  108.3 10.2 %copy-start.14 = (bf16[512,768]{1,0:T(8,128)(2,1)}, bf16[512,768]{1,0:T(8,128)(2,1)S(1)}, u32[]{:S(2)}) copy-start(bf16[512,768]{1,0:T(8,128)(2,1)S(1)} %get-tuple-element.165) | copy-start | bytes 2359300
  108.3 11.2 %copy-start.35 = (bf16[512]{0:T(512)(128)(2,1)S(1)}, bf16[512]{0:T(512)(128)(2,1)}, u32[]{:S(2)}) copy-start(bf16[512]{0:T(512)(128)(2,1)} %param.5) | copy-start | bytes 3076
  108.3 12.9 %copy-start.3 = (bf16[512,384]{1,0:T(8,128)(2,1)S(1)}, bf16[512,384]{1,0:T(8,128)(2,1)}, u32[]{:S(2)}) copy-start(bf16[512,384]{1,0:T(8,128)(2,1)} %copy-done.2) | copy-start | bytes 1179652
  108.3 12.9 %copy-start.5 = (bf16[512,384]{1,0:T(8,128)(2,1)S(1)}, bf16[512,384]{1,0:T(8,128)(2,1)}, u32[]{:S(2)}) copy-start(bf16[512,384]{1,0:T(8,128)(2,1)} %copy-done.4) | copy-start | bytes 1179652
  110.4 8.0 %copy-start.32 = (bf16[512,384]{1,0:T(8,128)(2,1)}, bf16[512,384]{1,0:T(8,128)(2,1)S(1)}, u32[]{:S(2)}) copy-start(bf16[512,384]{1,0:T(8,128)(2,1)S(1)} %collective-permute-done.22) | copy-start | bytes 1179652
  112.0 6.4 %copy-start.33 = (bf16[512,384]{1,0:T(8,128)(2,1)}, bf16[512,384]{1,0:T(8,128)(2,1)S(1)}, u32[]{:S(2)}) copy-start(bf16[512,384]{1,0:T(8,128)(2,1)S(1)} %collective-permute-done.21) | copy-start | bytes 1179652
  117.6 9.3 %collective-permute-start.26 = (bf16[256,640]{1,0:T(8,128)(2,1)}, bf16[256,640]{1,0:T(8,128)(2,1)}, u32[]{:S(2)}, u32[]{:S(2)}) collective-permute-start(bf16[256,640]{1,0:T(8,128)(2,1)} %add_convert_fusion.5), channel_id=1, source_target_pairs={{0,16},{1,17},{2,18},{3,19},{64,80},{65,81},{66,82},{67,83},{16,0}... | collective-permute-start | bytes 983048 | tf_op jit(solution)/shard_map/ppermute | solution.py:43
  118.5 10.5 %collective-permute-start.25 = (bf16[256,640]{1,0:T(8,128)(2,1)}, bf16[256,640]{1,0:T(8,128)(2,1)}, u32[]{:S(2)}, u32[]{:S(2)}) collective-permute-start(bf16[256,640]{1,0:T(8,128)(2,1)} %add_convert_fusion.6), channel_id=1, source_target_pairs={{0,48},{1,49},{2,50},{3,51},{64,112},{65,113},{66,114},{67,115},{1... | collective-permute-start | bytes 983048 | tf_op jit(solution)/shard_map/ppermute | solution.py:43
  119.5 36.0 %collective-permute-start.33 = (bf16[512,768]{1,0:T(8,128)(2,1)}, bf16[512,768]{1,0:T(8,128)(2,1)S(1)}, u32[]{:S(2)}, u32[]{:S(2)}) collective-permute-start(bf16[512,768]{1,0:T(8,128)(2,1)} %copy-done.13), channel_id=1, source_target_pairs={{0,4},{1,5},{2,6},{3,7},{64,68},{65,69},{66,70},{67,71},{16,20},{1... | collective-permute-start | bytes 2359304 | tf_op jit(solution)/shard_map/ppermute | solution.py:43
  119.8 9.2 %copy-start.20 = (bf16[512,640]{1,0:T(8,128)(2,1)S(1)}, bf16[512,640]{1,0:T(8,128)(2,1)}, u32[]{:S(2)}) copy-start(bf16[512,640]{1,0:T(8,128)(2,1)} %copy-done.19) | copy-start | bytes 1966084
  119.8 9.2 %copy-start.22 = (bf16[512,640]{1,0:T(8,128)(2,1)S(1)}, bf16[512,640]{1,0:T(8,128)(2,1)}, u32[]{:S(2)}) copy-start(bf16[512,640]{1,0:T(8,128)(2,1)} %copy-done.21) | copy-start | bytes 1966084
  119.8 35.8 %collective-permute-start.34 = (bf16[512,768]{1,0:T(8,128)(2,1)}, bf16[512,768]{1,0:T(8,128)(2,1)S(1)}, u32[]{:S(2)}, u32[]{:S(2)}) collective-permute-start(bf16[512,768]{1,0:T(8,128)(2,1)} %copy-done.14), channel_id=1, source_target_pairs={{0,12},{1,13},{2,14},{3,15},{64,76},{65,77},{66,78},{67,79},{16,28... | collective-permute-start | bytes 2359304 | tf_op jit(solution)/shard_map/ppermute | solution.py:43
  122.7 9.6 %copy-start.9 = (bf16[256,512]{1,0:T(8,128)(2,1)S(1)}, bf16[256,512]{1,0:T(8,128)(2,1)}, u32[]{:S(2)}) copy-start(bf16[256,512]{1,0:T(8,128)(2,1)} %copy-done.8) | copy-start | bytes 786436
  122.7 9.6 %copy-start.26 = (bf16[512,512]{1,0:T(8,128)(2,1)S(1)}, bf16[512,512]{1,0:T(8,128)(2,1)}, u32[]{:S(2)}) copy-start(bf16[512,512]{1,0:T(8,128)(2,1)} %copy-done.25) | copy-start | bytes 1572868
  129.0 4.2 %copy-start.24 = (bf16[512,512]{1,0:T(8,128)(2,1)S(1)}, bf16[512,512]{1,0:T(8,128)(2,1)}, u32[]{:S(2)}) copy-start(bf16[512,512]{1,0:T(8,128)(2,1)} %copy-done.23) | copy-start | bytes 1572868
  130.4 9.6 %collective-permute-start.29 = (bf16[256,640]{1,0:T(8,128)(2,1)S(1)}, bf16[256,640]{1,0:T(8,128)(2,1)S(1)}, u32[]{:S(2)}, u32[]{:S(2)}) collective-permute-start(bf16[256,640]{1,0:T(8,128)(2,1)S(1)} %select_convert_fusion.1), channel_id=1, source_target_pairs={{0,64},{1,65},{2,66},{3,67},{64,0},{65,1},{66,2},{67,3},{16,80},{1... | collective-permute-start | bytes 983048 | tf_op jit(solution)/shard_map/ppermute | solution.py:43
  132.4 11.9 %collective-permute-start.28 = (bf16[256,512]{1,0:T(8,128)(2,1)S(1)}, bf16[256,512]{1,0:T(8,128)(2,1)S(1)}, u32[]{:S(2)}, u32[]{:S(2)}) collective-permute-start(bf16[256,512]{1,0:T(8,128)(2,1)S(1)} %add_convert_fusion.8), channel_id=1, source_target_pairs={{0,48},{1,49},{2,50},{3,51},{64,112},{65,113},{66,114},{67,115},{1... | collective-permute-start | bytes 786440 | tf_op jit(solution)/shard_map/ppermute | solution.py:43
  133.2 8.2 %copy-start.27 = (bf16[256,512]{1,0:T(8,128)(2,1)S(1)}, bf16[256,512]{1,0:T(8,128)(2,1)}, u32[]{:S(2)}) copy-start(bf16[256,512]{1,0:T(8,128)(2,1)} %param.4) | copy-start | bytes 786436
  133.3 12.4 %collective-permute-start.27 = (bf16[256,512]{1,0:T(8,128)(2,1)S(1)}, bf16[256,512]{1,0:T(8,128)(2,1)S(1)}, u32[]{:S(2)}, u32[]{:S(2)}) collective-permute-start(bf16[256,512]{1,0:T(8,128)(2,1)S(1)} %add_convert_fusion.9), channel_id=1, source_target_pairs={{0,16},{1,17},{2,18},{3,19},{64,80},{65,81},{66,82},{67,83},{16,0}... | collective-permute-start | bytes 786440 | tf_op jit(solution)/shard_map/ppermute | solution.py:43
  142.4 1.2 collective-permute-start.31
  143.5 17.5 %collective-permute-start.39 = (bf16[256,768]{1,0:T(8,128)(2,1)S(1)}, bf16[256,768]{1,0:T(8,128)(2,1)S(1)}, u32[]{:S(2)}, u32[]{:S(2)}) collective-permute-start(bf16[256,768]{1,0:T(8,128)(2,1)S(1)} %select_convert_fusion), channel_id=1, source_target_pairs={{0,2},{1,3},{2,0},{3,1},{64,66},{65,67},{66,64},{67,65},{16,18},{1... | collective-permute-start | bytes 1179656 | tf_op jit(solution)/shard_map/ppermute | solution.py:43
  144.3 11.2 %collective-permute-start.32 = (f32[1,512]{1,0:T(1,128)S(1)}, f32[1,512]{1,0:T(1,128)S(1)}, u32[]{:S(2)}, u32[]{:S(2)}) collective-permute-start(f32[1,512]{1,0:T(1,128)S(1)} %add.216), channel_id=1, source_target_pairs={{0,2},{1,3},{2,0},{3,1},{64,66},{65,67},{66,64},{67,65},{16,18},{1... | collective-permute-start | bytes 6152 | tf_op jit(solution)/shard_map/ppermute | solution.py:43
  145.8 22.0 %collective-permute-start.30 = (bf16[256,512]{1,0:T(8,128)(2,1)S(1)}, bf16[256,512]{1,0:T(8,128)(2,1)S(1)}, u32[]{:S(2)}, u32[]{:S(2)}) collective-permute-start(bf16[256,512]{1,0:T(8,128)(2,1)S(1)} %select_convert_fusion.2), channel_id=1, source_target_pairs={{0,64},{1,65},{2,66},{3,67},{64,0},{65,1},{66,2},{67,3},{16,80},{1... | collective-permute-start | bytes 786440 | tf_op jit(solution)/shard_map/ppermute | solution.py:43
  155.8 4.3 %collective-permute-start.35 = (f32[1,512]{1,0:T(1,128)S(1)}, f32[1,512]{1,0:T(1,128)S(1)}, u32[]{:S(2)}, u32[]{:S(2)}) collective-permute-start(f32[1,512]{1,0:T(1,128)S(1)} %add.217), channel_id=1, source_target_pairs={{0,4},{1,5},{2,6},{3,7},{64,68},{65,69},{66,70},{67,71},{16,20},{1... | collective-permute-start | bytes 6152 | tf_op jit(solution)/shard_map/ppermute | solution.py:43
  156.8 12.0 %collective-permute-start.38 = (bf16[256,768]{1,0:T(8,128)(2,1)S(1)}, bf16[256,768]{1,0:T(8,128)(2,1)S(1)}, u32[]{:S(2)}, u32[]{:S(2)}) collective-permute-start(bf16[256,768]{1,0:T(8,128)(2,1)S(1)} %add_convert_fusion.1), channel_id=1, source_target_pairs={{0,4},{1,5},{2,6},{3,7},{64,68},{65,69},{66,70},{67,71},{16,20},{1... | collective-permute-start | bytes 1179656 | tf_op jit(solution)/shard_map/ppermute | solution.py:43
  158.5 10.3 %collective-permute-start.37 = (bf16[256,768]{1,0:T(8,128)(2,1)S(1)}, bf16[256,768]{1,0:T(8,128)(2,1)S(1)}, u32[]{:S(2)}, u32[]{:S(2)}) collective-permute-start(bf16[256,768]{1,0:T(8,128)(2,1)S(1)} %add_convert_fusion.2), channel_id=1, source_target_pairs={{0,12},{1,13},{2,14},{3,15},{64,76},{65,77},{66,78},{67,79},{16,28... | collective-permute-start | bytes 1179656 | tf_op jit(solution)/shard_map/ppermute | solution.py:43
  160.1 7.2 %collective-permute-start.36 = (f32[1,512]{1,0:T(1,128)S(1)}, f32[1,512]{1,0:T(1,128)S(1)}, u32[]{:S(2)}, u32[]{:S(2)}) collective-permute-start(f32[1,512]{1,0:T(1,128)S(1)} %add.220), channel_id=1, source_target_pairs={{0,8},{1,9},{2,10},{3,11},{64,72},{65,73},{66,74},{67,75},{16,24},... | collective-permute-start | bytes 6152 | tf_op jit(solution)/shard_map/ppermute | solution.py:43
  161.1 7.7 %copy-start.1 = (bf16[256,768]{1,0:T(8,128)(2,1)S(1)}, bf16[256,768]{1,0:T(8,128)(2,1)}, u32[]{:S(2)}) copy-start(bf16[256,768]{1,0:T(8,128)(2,1)} %copy-done) | copy-start | bytes 1179652
  (12 other events, 19.2 us)

commit v6 on v5

--- a/solution.py
+++ b/solution.py
@@ -319,18 +319,19 @@
     x_same, x_cross = send(x_same, "z^3"), send(x_cross, "z^1")
     gate, up_val, hidden, inv, core_one = forward(after(x_full, *cot_pieces[1:3]), x_core, w3)
     core_one = send(core_one, "c")
-    cot_pieces = (after(cot_pieces[0], x_same, x_cross), *cot_pieces[1:])
+    branch_terms = branch_rows(order(y), hidden, w3)
+    cot_pieces = (after(cot_pieces[0], x_same, x_cross, branch_terms[0]), *cot_pieces[1:])
     d_pair, products, cot_mine, core_two = backward(spot, cot_pieces, w3, gate, up_val, inv)
     core_two = send(core_two, "c")
-    branch_terms = branch_rows(order(y), after(hidden, d_pair), w3)
     pair_z = send(d_pair, "z^1")
-    down_terms = outer("down_terms", order(x), [(after(cot_mine, branch_terms[0]), 0), (core_two, 0)], [(hidden, 0), (core_one, 1024)], 512, 384)
-    branch_got = [send(value, move) for value, move in zip(branch_terms[0:2], ("y^1", "y^3"))]
+    down_terms = outer("down_terms", order(x), [(cot_mine, 0), (core_two, 0)], [(hidden, 0), (core_one, 1024)], 512, 384)
+    branch_got, _, branch_last = halve(branch_terms, "y", (down_terms[0],))
+    low, high = finish(branch_terms, branch_got, branch_last)
     d_terms = pair_rows(order(y), after(d_pair, down_terms[0]), products, w3)
     down_got, _, down_last = halve(down_terms, "x")
-    d_terms = lax.optimization_barrier((*d_terms, *branch_got))[:6]
+    d_terms = lax.optimization_barrier((*d_terms, *branch_last))[:6]
     d_got = [send(value, move) for value, move in zip(d_terms[0:2], ("y^1", "y^3"))]
-    core_three = send(jnp.concatenate([x_cross, after(pair_z, d_terms[0], *down_got)], axis=1), "c")
+    core_three = send(jnp.concatenate([x_cross, after(pair_z, d_terms[0], *branch_last, *down_got)], axis=1), "c")
     pair_terms = outer(
         "pair_terms", order(x), [(x_keep, 0), (x_same, 0), (core_one, 0), (core_three, 0)],
         [(d_pair, 0), (pair_z, 0), (core_two, 2048), (core_three, 1024)], 256, 768,
@@ -347,8 +348,6 @@
 
     _, d_last = second_step(d_terms, d_got, "y", (pair_terms[0],))
     d_low, d_high = finish(d_terms, d_got, d_last)
-    _, branch_last = second_step(branch_terms, branch_got, "y", (pair_terms[0], *d_last))
-    low, high = finish(branch_terms, branch_got, branch_last)
     upper = z_hi == 1
     mine = jnp.where(upper, d_high, d_low)
     theirs = send(jnp.where(upper, d_low, d_high).astype(bf16), "z+2")
@@ -361,8 +360,8 @@
     d_input = (d_normed * gain.astype(f32) - inv[:, :1] * products * x_own).astype(bf16)
     d_gain = jnp.sum(d_normed * x_own, axis=0, keepdims=True)
     for move in ("c", "z^1", "x^1", "x+2"):
-        if move == "x^1":
-            d_gain = after(d_gain, *pair_out)
+        if move in ("c", "x+2"):
+            d_gain = after(d_gain, *(pair_out if move == "c" else pair_last))
         d_gain = d_gain + send(d_gain, move)
 
     gain_rows = lax.dynamic_slice(gains, (0, s * 256), (1, 256)).astype(f32).reshape(256, 1)

time: 171 us -> 176 us (1.029)
  local copies, waits for them, and re-layouts: 6.48 us -> 9.72 us
  starting transfers between devices: 43 us -> 46.1 us
  waiting for transfers between devices: 68.3 us -> 65.2 us
    ppermute x40, starting transfers between devices: 43 us -> 46.1 us  [send(): return lax.ppermute(value, AXES, pairs(moves[move]))]
    ppermute x40, waiting for transfers between devices: 68.3 us -> 65.2 us  [send(): return lax.ppermute(value, AXES, pairs(moves[move]))]
    unnamed x72 -> x90, local copies, waits for them, and re-layouts: 5.46 us -> 8.16 us
  transfers between devices with their start and end apart: 40 -> 40, of which waited for: 21 -> 19; matrix products, arithmetic and copies ran while one was open for 6% -> 8% of each run, Pallas kernels for 18% -> 18%
where the time goes in v6:
time: 176 us
  waiting for transfers between devices  65.2 us (37%)
  starting transfers between devices  46.1 us (26%)
  Pallas kernels  38.3 us (22%)
  other arithmetic  15.1 us (9%)
  local copies, waits for them, and re-layouts  9.72 us (6%)
    ppermute x40, waiting for transfers between devices, send(): return lax.ppermute(value, AXES, pairs(moves[move]))  65.2 us
    ppermute x40, starting transfers between devices, send(): return lax.ppermute(value, AXES, pairs(moves[move]))  46.1 us
    pallas_call x7, Pallas kernels, call(): pl.pallas_call(whole, in_specs=[pl.BlockSpec(memory_space=space) for spac...  38.3 us
    unnamed x90, local copies, waits for them, and re-layouts  8.16 us
  transfers between devices with their start and end apart: 40, of which 19 were waited for; matrix products, arithmetic and copies ran while one was open for 8% of the time, Pallas kernels for 18%

profile of v6, /device:TPU:0, one launch (start us, length us, event | category | flops | bytes accessed | tf_op | source)
XLA Modules:
  0.0 175.8 jit_solution(7863210457719271310)
XLA Ops:
  1.3 1.0 pad_maximum_fusion.6.refs_1_
  2.3 3.2 %collective-permute-start.1 = (bf16[272,512]{1,0:T(8,128)(2,1)S(1)}, bf16[272,512]{1,0:T(8,128)(2,1)S(1)}, u32[]{:S(2)}, u32[]{:S(2)}) collective-permute-start(bf16[272,512]{1,0:T(8,128)(2,1)S(1)} %pad_maximum_fusion.6.refs_1_), channel_id=1, source_target_pairs={{0,48},{1,49},{2,50},{3,51},{64,112},{65,113},{66,114},{67,115},{1... | collective-permute-start | bytes 835592 | tf_op jit(solution)/shard_map/ppermute | solution.py:43
  5.5 3.9 %collective-permute-start.2 = (bf16[272,512]{1,0:T(8,128)(2,1)S(1)}, bf16[272,512]{1,0:T(8,128)(2,1)S(1)}, u32[]{:S(2)}, u32[]{:S(2)}) collective-permute-start(bf16[272,512]{1,0:T(8,128)(2,1)S(1)} %pad_maximum_fusion.6.refs_1_), channel_id=1, source_target_pairs={{0,64},{1,65},{2,66},{3,67},{64,0},{65,1},{66,2},{67,3},{16,80},{1... | collective-permute-start | bytes 835592 | tf_op jit(solution)/shard_map/ppermute | solution.py:43
  9.4 2.0 %collective-permute-done.1.refs_3_ = bf16[272,512]{1,0:T(8,128)(2,1)S(1)} collective-permute-done((bf16[272,512]{1,0:T(8,128)(2,1)S(1)}, bf16[272,512]{1,0:T(8,128)(2,1)S(1)}, u32[]{:S(2)}, u32[]{:S(2)}) %collective-permute-start.1) | collective-permute-done | bytes 278560 | tf_op jit(solution)/shard_map/ppermute | solution.py:43
  11.4 4.3 %collective-permute-done.2.refs_4_ = bf16[272,512]{1,0:T(8,128)(2,1)S(1)} collective-permute-done((bf16[272,512]{1,0:T(8,128)(2,1)S(1)}, bf16[272,512]{1,0:T(8,128)(2,1)S(1)}, u32[]{:S(2)}, u32[]{:S(2)}) %collective-permute-start.2) | collective-permute-done | bytes 278560 | tf_op jit(solution)/shard_map/ppermute | solution.py:43
  15.8 0.8 collective-permute-start.4
  16.6 1.8 %collective-permute-done.refs_2_ = bf16[272,512]{1,0:T(8,128)(2,1)S(1)} collective-permute-done((bf16[272,512]{1,0:T(8,128)(2,1)S(1)}, bf16[272,512]{1,0:T(8,128)(2,1)S(1)}, u32[]{:S(2)}, u32[]{:S(2)}) %collective-permute-start) | collective-permute-done | bytes 278560 | tf_op jit(solution)/shard_map/ppermute | solution.py:43
  18.6 2.7 %collective-permute-start.5 = (bf16[256,512]{1,0:T(8,128)(2,1)S(1)}, bf16[256,512]{1,0:T(8,128)(2,1)S(1)}, u32[]{:S(2)}, u32[]{:S(2)}) collective-permute-start(bf16[256,512]{1,0:T(8,128)(2,1)S(1)} %copy-done.43), channel_id=1, source_target_pairs={{0,64},{1,65},{2,66},{3,67},{64,0},{65,1},{66,2},{67,3},{16,80},{1... | collective-permute-start | bytes 786440 | tf_op jit(solution)/shard_map/ppermute | solution.py:43
  21.3 5.5 %collective-permute-done.5 = bf16[256,512]{1,0:T(8,128)(2,1)S(1)} collective-permute-done((bf16[256,512]{1,0:T(8,128)(2,1)S(1)}, bf16[256,512]{1,0:T(8,128)(2,1)S(1)}, u32[]{:S(2)}, u32[]{:S(2)}) %collective-permute-start.5) | collective-permute-done | bytes 262176 | tf_op jit(solution)/shard_map/ppermute | solution.py:43
  26.7 2.7 %collective-permute-done.3.refs_5_ = bf16[400,512]{1,0:T(8,128)(2,1)S(1)} collective-permute-done((bf16[400,512]{1,0:T(8,128)(2,1)S(1)}, bf16[400,512]{1,0:T(8,128)(2,1)S(1)}, u32[]{:S(2)}, u32[]{:S(2)}) %collective-permute-start.3) | collective-permute-done | bytes 409632 | tf_op jit(solution)/shard_map/ppermute | solution.py:43
  29.5 3.2 %collective-permute-start.8 = (bf16[512,512]{1,0:T(8,128)(2,1)S(1)}, bf16[512,512]{1,0:T(8,128)(2,1)S(1)}, u32[]{:S(2)}, u32[]{:S(2)}) collective-permute-start(bf16[512,512]{1,0:T(8,128)(2,1)S(1)} %pad_maximum_fusion.3.refs_1_), channel_id=1, source_target_pairs={{0,48},{1,49},{2,50},{3,51},{64,112},{65,113},{66,114},{67,115},{1... | collective-permute-start | bytes 1572872 | tf_op jit(solution)/shard_map/ppermute | solution.py:43
  32.7 0.7 pad_maximum_fusion.7
  33.5 1.4 collective-permute-start.6
  35.6 6.2 %collective-permute-done.6.refs_7_ = bf16[272,512]{1,0:T(8,128)(2,1)} collective-permute-done((bf16[272,512]{1,0:T(8,128)(2,1)}, bf16[272,512]{1,0:T(8,128)(2,1)}, u32[]{:S(2)}, u32[]{:S(2)}) %collective-permute-start.6) | collective-permute-done | bytes 278560 | tf_op jit(solution)/shard_map/ppermute | solution.py:43
  41.8 1.4 assemble.1
  44.0 0.8 copy-done.23
  44.7 1.6 collective-permute-start.11
  46.6 3.5 %collective-permute-start.14 = (bf16[256,512]{1,0:T(8,128)(2,1)S(1)}, bf16[256,512]{1,0:T(8,128)(2,1)S(1)}, u32[]{:S(2)}, u32[]{:S(2)}) collective-permute-start(bf16[256,512]{1,0:T(8,128)(2,1)S(1)} %pad_maximum_fusion.9), channel_id=1, source_target_pairs={{0,48},{1,49},{2,50},{3,51},{64,112},{65,113},{66,114},{67,115},{1... | collective-permute-start | bytes 786440 | tf_op jit(solution)/shard_map/ppermute | solution.py:43
  50.0 6.4 %forward.1 = (f32[256,768]{1,0:T(8,128)S(1)}, f32[256,768]{1,0:T(8,128)S(1)}, bf16[256,768]{1,0:T(8,128)(2,1)S(1)}, f32[256,128]{1,0:T(8,128)S(1)}, bf16[256,1792]{1,0:T(8,128)(2,1)}) custom-call(bf16[272,4096]{1,0:T(8,128)(2,1)S(1)} %get-tuple-element.95.refs_0_, bf16[256,1024]{1,0:T(8,128)(2,1)S(1)} %get-tuple-element.96.refs_1_, ...), custom_call_target="tpu_custom_call" | custom-call | flops 3221225472 | bytes 16777216 | tf_op jit(solution)/shard_map/forward/pallas_call | solution.py:89
  56.4 5.8 %branch_rows.1 = (bf16[512,512]{1,0:T(8,128)(2,1)}, bf16[512,512]{1,0:T(8,128)(2,1)}, bf16[256,512]{1,0:T(8,128)(2,1)S(1)}, bf16[256,512]{1,0:T(8,128)(2,1)S(1)}...) custom-call(s32[8]{0:T(128)S(1)} %copy-done.16, bf16[256,768]{1,0:T(8,128)(2,1)S(1)} %get-tuple-element.97.refs_1_.refs_3_, ...), custom_call_target="tpu_custom_call" | custom-call | flops 1610612736 | bytes 8388608 | tf_op jit(solution)/shard_map/branch_rows/pallas_call | solution.py:89
  62.3 6.8 %backward.1 = (bf16[256,1536]{1,0:T(8,128)(2,1)S(1)}, bf16[256,128]{1,0:T(8,128)(2,1)S(1)}, bf16[256,2048]{1,0:T(8,128)(2,1)S(1)}, bf16[256,3584]{1,0:T(8,128)(2,1)}) custom-call(s32[10]{0:T(128)S(1)} %copy-done.15, bf16[512,512]{1,0:T(8,128)(2,1)S(1)} %pad_maximum_fusion.3.refs_1_, bf16[512,512]{1,0:T(8,128)(2,1)S(1)} %collective-permute-done.7.refs_2_, ...), custom_call_target="tpu_custom_call" | custom-call | flops 1610612736 | bytes 8388608 | tf_op jit(solution)/shard_map/backward/pallas_call | solution.py:89
  69.8 1.0 copy-done.19
  71.4 2.0 %collective-permute-start.21 = (bf16[256,1536]{1,0:T(8,128)(2,1)S(1)}, bf16[256,1536]{1,0:T(8,128)(2,1)S(1)}, u32[]{:S(2)}, u32[]{:S(2)}) collective-permute-start(bf16[256,1536]{1,0:T(8,128)(2,1)S(1)} %get-tuple-element.121.refs_1_.refs_5_), channel_id=1, source_target_pairs={{0,2},{1,3},{2,0},{3,1},{64,66},{65,67},{66,64},{67,65},{16,18},{1... | collective-permute-start | bytes 2359304 | tf_op jit(solution)/shard_map/ppermute | solution.py:43
  73.4 2.8 %collective-permute-done.16.refs_4_.refs_3_ = bf16[256,1792]{1,0:T(8,128)(2,1)} collective-permute-done((bf16[256,1792]{1,0:T(8,128)(2,1)}, bf16[256,1792]{1,0:T(8,128)(2,1)}, u32[]{:S(2)}, u32[]{:S(2)}) %collective-permute-start.16) | collective-permute-done | bytes 917536 | tf_op jit(solution)/shard_map/ppermute | solution.py:43
  76.2 1.0 copy-done.11
  77.2 1.2 copy-done.20
  78.4 4.8 %down_terms.1 = (bf16[1024,384]{1,0:T(8,128)(2,1)S(1)}, bf16[1024,384]{1,0:T(8,128)(2,1)S(1)}, bf16[512,384]{1,0:T(8,128)(2,1)S(1)}, bf16[512,384]{1,0:T(8,128)(...) custom-call(s32[8]{0:T(128)S(1)} %stack.121.refs_0_, bf16[256,2048]{1,0:T(8,128)(2,1)S(1)} %copy-done.20, ...), custom_call_target="tpu_custom_call" | custom-call | flops 1610612736 | bytes 8388608 | tf_op jit(solution)/shard_map/down_terms/pallas_call | solution.py:89
  83.3 1.6 collective-permute-start.22
  84.8 2.1 %collective-permute-start.23 = (bf16[1024,384]{1,0:T(8,128)(2,1)S(1)}, bf16[1024,384]{1,0:T(8,128)(2,1)S(1)}, u32[]{:S(2)}, u32[]{:S(2)}) collective-permute-start(bf16[1024,384]{1,0:T(8,128)(2,1)S(1)} %get-tuple-element.137), channel_id=1, source_target_pairs={{0,12},{1,13},{2,14},{3,15},{64,76},{65,77},{66,78},{67,79},{16,28... | collective-permute-start | bytes 2359304 | tf_op jit(solution)/shard_map/ppermute | solution.py:43
  87.0 0.7 collective-permute-start.18
  87.7 1.0 add_convert_fusion.9
  88.8 0.9 collective-permute-start.17
  89.7 7.1 %pair_rows.1 = (bf16[512,640]{1,0:T(8,128)(2,1)S(1)}, bf16[512,640]{1,0:T(8,128)(2,1)S(1)}, bf16[256,640]{1,0:T(8,128)(2,1)S(1)}, bf16[256,640]{1,0:T(8,128)(2,1...) custom-call(s32[8]{0:T(128)S(1)} %copy-done.17, ...), custom_call_target="tpu_custom_call" | custom-call | flops 3221225472 | bytes 16777216 | tf_op jit(solution)/shard_map/pair_rows/pallas_call | solution.py:89
  96.8 6.1 %collective-permute-done.22 = bf16[1024,384]{1,0:T(8,128)(2,1)S(1)} collective-permute-done((bf16[1024,384]{1,0:T(8,128)(2,1)S(1)}, bf16[1024,384]{1,0:T(8,128)(2,1)S(1)}, u32[]{:S(2)}, u32[]{:S(2)}) %collective-permute-start.22) | collective-permute-done | bytes 786464 | tf_op jit(solution)/shard_map/ppermute | solution.py:43
  102.9 2.4 %collective-permute-done.23 = bf16[1024,384]{1,0:T(8,128)(2,1)S(1)} collective-permute-done((bf16[1024,384]{1,0:T(8,128)(2,1)S(1)}, bf16[1024,384]{1,0:T(8,128)(2,1)S(1)}, u32[]{:S(2)}, u32[]{:S(2)}) %collective-permute-start.23) | collective-permute-done | bytes 786464 | tf_op jit(solution)/shard_map/ppermute | solution.py:43
  105.7 0.9 collective-permute-start.20
  106.8 2.2 %collective-permute-start.25 = (bf16[512,384]{1,0:T(8,128)(2,1)S(1)}, bf16[512,384]{1,0:T(8,128)(2,1)}, u32[]{:S(2)}, u32[]{:S(2)}) collective-permute-start(bf16[512,384]{1,0:T(8,128)(2,1)S(1)} %add_convert_fusion.4), channel_id=1, source_target_pairs={{0,12},{1,13},{2,14},{3,15},{64,76},{65,77},{66,78},{67,79},{16,28... | collective-permute-start | bytes 1179656 | tf_op jit(solution)/shard_map/ppermute | solution.py:43
  109.0 6.0 %pair_terms.1 = (bf16[512,768]{1,0:T(8,128)(2,1)S(1)}, bf16[512,768]{1,0:T(8,128)(2,1)S(1)}, bf16[256,768]{1,0:T(8,128)(2,1)S(1)}, bf16[256,768]{1,0:T(8,128)(2,...) custom-call(s32[8]{0:T(128)S(1)} %stack.121.refs_0_, bf16[256,1024]{1,0:T(8,128)(2,1)S(1)} %copy-done.24, ...), custom_call_target="tpu_custom_call" | custom-call | flops 3221225472 | bytes 8388608 | tf_op jit(solution)/shard_map/pair_terms/pallas_call | solution.py:89
  115.1 0.7 copy-done
  115.8 0.8 copy-done.2
  116.6 0.7 copy-done.4
  117.6 1.5 collective-permute-done.25
  119.1 3.6 %collective-permute-done.19 = bf16[512,640]{1,0:T(8,128)(2,1)S(1)} collective-permute-done((bf16[512,640]{1,0:T(8,128)(2,1)S(1)}, bf16[512,640]{1,0:T(8,128)(2,1)S(1)}, u32[]{:S(2)}, u32[]{:S(2)}) %collective-permute-start.19) | collective-permute-done | bytes 655392 | tf_op jit(solution)/shard_map/ppermute | solution.py:43
  122.7 1.2 collective-permute-done.20
  123.9 0.9 add_convert_fusion.5
  125.4 0.8 add_convert_fusion.6
  126.2 1.0 collective-permute-start.27
  127.3 2.2 %collective-permute-start.32 = (bf16[512,768]{1,0:T(8,128)(2,1)}, bf16[512,768]{1,0:T(8,128)(2,1)S(1)}, u32[]{:S(2)}, u32[]{:S(2)}) collective-permute-start(bf16[512,768]{1,0:T(8,128)(2,1)} %copy-done.21), channel_id=1, source_target_pairs={{0,12},{1,13},{2,14},{3,15},{64,76},{65,77},{66,78},{67,79},{16,28... | collective-permute-start | bytes 2359304 | tf_op jit(solution)/shard_map/ppermute | solution.py:43
  129.5 4.7 %collective-permute-done.28 = bf16[256,640]{1,0:T(8,128)(2,1)S(1)} collective-permute-done((bf16[256,640]{1,0:T(8,128)(2,1)}, bf16[256,640]{1,0:T(8,128)(2,1)S(1)}, u32[]{:S(2)}, u32[]{:S(2)}) %collective-permute-start.28) | collective-permute-done | bytes 327712 | tf_op jit(solution)/shard_map/ppermute | solution.py:43
  134.2 2.2 %collective-permute-done.27 = bf16[256,640]{1,0:T(8,128)(2,1)S(1)} collective-permute-done((bf16[256,640]{1,0:T(8,128)(2,1)}, bf16[256,640]{1,0:T(8,128)(2,1)S(1)}, u32[]{:S(2)}, u32[]{:S(2)}) %collective-permute-start.27) | collective-permute-done | bytes 327712 | tf_op jit(solution)/shard_map/ppermute | solution.py:43
  136.4 1.3 select_convert_fusion.1
  137.7 3.2 %collective-permute-start.29 = (bf16[256,640]{1,0:T(8,128)(2,1)S(1)}, bf16[256,640]{1,0:T(8,128)(2,1)S(1)}, u32[]{:S(2)}, u32[]{:S(2)}) collective-permute-start(bf16[256,640]{1,0:T(8,128)(2,1)S(1)} %select_convert_fusion.1), channel_id=1, source_target_pairs={{0,64},{1,65},{2,66},{3,67},{64,0},{65,1},{66,2},{67,3},{16,80},{1... | collective-permute-start | bytes 983048 | tf_op jit(solution)/shard_map/ppermute | solution.py:43
  140.9 1.4 convert_add_fusion
  142.5 7.4 %collective-permute-done.29 = bf16[256,640]{1,0:T(8,128)(2,1)S(1)} collective-permute-done((bf16[256,640]{1,0:T(8,128)(2,1)S(1)}, bf16[256,640]{1,0:T(8,128)(2,1)S(1)}, u32[]{:S(2)}, u32[]{:S(2)}) %collective-permute-start.29) | collective-permute-done | bytes 327712 | tf_op jit(solution)/shard_map/ppermute | solution.py:43
  150.4 0.9 fusion.3
  152.3 1.2 select_convert_fusion.2
  153.5 3.2 %collective-permute-start.30 = (bf16[256,512]{1,0:T(8,128)(2,1)S(1)}, bf16[256,512]{1,0:T(8,128)(2,1)S(1)}, u32[]{:S(2)}, u32[]{:S(2)}) collective-permute-start(bf16[256,512]{1,0:T(8,128)(2,1)S(1)} %select_convert_fusion.2), channel_id=1, source_target_pairs={{0,64},{1,65},{2,66},{3,67},{64,0},{65,1},{66,2},{67,3},{16,80},{1... | collective-permute-start | bytes 786440 | tf_op jit(solution)/shard_map/ppermute | solution.py:43
  157.5 2.1 %collective-permute-start.36 = (bf16[256,768]{1,0:T(8,128)(2,1)S(1)}, bf16[256,768]{1,0:T(8,128)(2,1)S(1)}, u32[]{:S(2)}, u32[]{:S(2)}) collective-permute-start(bf16[256,768]{1,0:T(8,128)(2,1)S(1)} %add_convert_fusion.2), channel_id=1, source_target_pairs={{0,12},{1,13},{2,14},{3,15},{64,76},{65,77},{66,78},{67,79},{16,28... | collective-permute-start | bytes 1179656 | tf_op jit(solution)/shard_map/ppermute | solution.py:43
  159.5 3.1 %collective-permute-done.34 = f32[1,512]{1,0:T(1,128)S(1)} collective-permute-done((f32[1,512]{1,0:T(1,128)S(1)}, f32[1,512]{1,0:T(1,128)S(1)}, u32[]{:S(2)}, u32[]{:S(2)}) %collective-permute-start.34) | collective-permute-done | bytes 2080 | tf_op jit(solution)/shard_map/ppermute | solution.py:43
  162.8 5.4 %collective-permute-done.35 = f32[1,512]{1,0:T(1,128)S(1)} collective-permute-done((f32[1,512]{1,0:T(1,128)S(1)}, f32[1,512]{1,0:T(1,128)S(1)}, u32[]{:S(2)}, u32[]{:S(2)}) %collective-permute-start.35) | collective-permute-done | bytes 2080 | tf_op jit(solution)/shard_map/ppermute | solution.py:43
  168.3 1.9 %add_convert_fusion.7 = bf16[256,512]{1,0:T(8,128)(2,1)} fusion(bf16[256,512]{1,0:T(8,128)(2,1)S(1)} %collective-permute-done.30, bf16[256,512]{1,0:T(8,128)(2,1)S(1)} %copy-done.35, bf16[256,512]{1,0:T(8,128)(2,1)S(1)} %get-tuple-element.100, bf16[256,512]{1,0:T(8,128)(2,1)S(1)} %collective-permute-done.18, bf16[256,512]{1,0:T(8,128)(2,1)S(1)} %get-tuple-element.117, ...), kind=kLoop, calls=%fused_computation.28 | loop fusion | flops 1835008 | bytes 2097153 | tf_op jit(solution)/shard_map/convert_element_type | solution.py:356
  170.2 1.8 %collective-permute-start.38 = (f32[1,512]{1,0:T(1,128)S(1)}, f32[1,512]{1,0:T(1,128)S(1)}, u32[]{:S(2)}, u32[]{:S(2)}) collective-permute-start(f32[1,512]{1,0:T(1,128)S(1)} %add.220), channel_id=1, source_target_pairs={{0,8},{1,9},{2,10},{3,11},{64,72},{65,73},{66,74},{67,75},{16,24},... | collective-permute-start | bytes 6152 | tf_op jit(solution)/shard_map/ppermute | solution.py:43
  172.3 1.1 pad_maximum_fusion.1
  173.5 1.8 %collective-permute-done.38 = f32[1,512]{1,0:T(1,128)S(1)} collective-permute-done((f32[1,512]{1,0:T(1,128)S(1)}, f32[1,512]{1,0:T(1,128)S(1)}, u32[]{:S(2)}, u32[]{:S(2)}) %collective-permute-start.38) | collective-permute-done | bytes 2080 | tf_op jit(solution)/shard_map/ppermute | solution.py:43
  (156 shorter events, 8.8 us)
Async XLA Ops:
  1.3 17.2 %copy-start.43 = (bf16[256,512]{1,0:T(8,128)(2,1)S(1)}, bf16[256,512]{1,0:T(8,128)(2,1)}, u32[]{:S(2)}) copy-start(bf16[256,512]{1,0:T(8,128)(2,1)} %param.7) | copy-start | bytes 786436
  2.3 9.1 %collective-permute-start.1 = (bf16[272,512]{1,0:T(8,128)(2,1)S(1)}, bf16[272,512]{1,0:T(8,128)(2,1)S(1)}, u32[]{:S(2)}, u32[]{:S(2)}) collective-permute-start(bf16[272,512]{1,0:T(8,128)(2,1)S(1)} %pad_maximum_fusion.6.refs_1_), channel_id=1, source_target_pairs={{0,48},{1,49},{2,50},{3,51},{64,112},{65,113},{66,114},{67,115},{1... | collective-permute-start | bytes 835592 | tf_op jit(solution)/shard_map/ppermute | solution.py:43
  5.5 10.2 %collective-permute-start.2 = (bf16[272,512]{1,0:T(8,128)(2,1)S(1)}, bf16[272,512]{1,0:T(8,128)(2,1)S(1)}, u32[]{:S(2)}, u32[]{:S(2)}) collective-permute-start(bf16[272,512]{1,0:T(8,128)(2,1)S(1)} %pad_maximum_fusion.6.refs_1_), channel_id=1, source_target_pairs={{0,64},{1,65},{2,66},{3,67},{64,0},{65,1},{66,2},{67,3},{16,80},{1... | collective-permute-start | bytes 835592 | tf_op jit(solution)/shard_map/ppermute | solution.py:43
  9.4 9.0 %collective-permute-start = (bf16[272,512]{1,0:T(8,128)(2,1)S(1)}, bf16[272,512]{1,0:T(8,128)(2,1)S(1)}, u32[]{:S(2)}, u32[]{:S(2)}) collective-permute-start(bf16[272,512]{1,0:T(8,128)(2,1)S(1)} %pad_maximum_fusion.6.refs_1_), channel_id=1, source_target_pairs={{0,16},{1,17},{2,18},{3,19},{64,80},{65,81},{66,82},{67,83},{16,32... | collective-permute-start | bytes 835592 | tf_op jit(solution)/shard_map/ppermute | solution.py:43
  15.8 13.7 %collective-permute-start.4 = (bf16[416,512]{1,0:T(8,128)(2,1)S(1)}, bf16[416,512]{1,0:T(8,128)(2,1)S(1)}, u32[]{:S(2)}, u32[]{:S(2)}) collective-permute-start(bf16[416,512]{1,0:T(8,128)(2,1)S(1)} %pad_maximum_fusion.4), channel_id=1, source_target_pairs={{0,48},{1,49},{2,50},{3,51},{64,112},{65,113},{66,114},{67,115},{1... | collective-permute-start | bytes 1277960 | tf_op jit(solution)/shard_map/ppermute | solution.py:43
  18.5 11.0 %collective-permute-start.3 = (bf16[400,512]{1,0:T(8,128)(2,1)S(1)}, bf16[400,512]{1,0:T(8,128)(2,1)S(1)}, u32[]{:S(2)}, u32[]{:S(2)}) collective-permute-start(bf16[400,512]{1,0:T(8,128)(2,1)S(1)} %pad_maximum_fusion.5), channel_id=1, source_target_pairs={{0,16},{1,17},{2,18},{3,19},{64,80},{65,81},{66,82},{67,83},{16,32... | collective-permute-start | bytes 1228808 | tf_op jit(solution)/shard_map/ppermute | solution.py:43
  18.6 8.1 %collective-permute-start.5 = (bf16[256,512]{1,0:T(8,128)(2,1)S(1)}, bf16[256,512]{1,0:T(8,128)(2,1)S(1)}, u32[]{:S(2)}, u32[]{:S(2)}) collective-permute-start(bf16[256,512]{1,0:T(8,128)(2,1)S(1)} %copy-done.43), channel_id=1, source_target_pairs={{0,64},{1,65},{2,66},{3,67},{64,0},{65,1},{66,2},{67,3},{16,80},{1... | collective-permute-start | bytes 786440 | tf_op jit(solution)/shard_map/ppermute | solution.py:43
  29.5 16.9 %collective-permute-start.7 = (bf16[512,512]{1,0:T(8,128)(2,1)S(1)}, bf16[512,512]{1,0:T(8,128)(2,1)S(1)}, u32[]{:S(2)}, u32[]{:S(2)}) collective-permute-start(bf16[512,512]{1,0:T(8,128)(2,1)S(1)} %pad_maximum_fusion.3.refs_1_), channel_id=1, source_target_pairs={{0,16},{1,17},{2,18},{3,19},{64,80},{65,81},{66,82},{67,83},{16,32... | collective-permute-start | bytes 1572872 | tf_op jit(solution)/shard_map/ppermute | solution.py:43
  29.5 16.9 %collective-permute-start.8 = (bf16[512,512]{1,0:T(8,128)(2,1)S(1)}, bf16[512,512]{1,0:T(8,128)(2,1)S(1)}, u32[]{:S(2)}, u32[]{:S(2)}) collective-permute-start(bf16[512,512]{1,0:T(8,128)(2,1)S(1)} %pad_maximum_fusion.3.refs_1_), channel_id=1, source_target_pairs={{0,48},{1,49},{2,50},{3,51},{64,112},{65,113},{66,114},{67,115},{1... | collective-permute-start | bytes 1572872 | tf_op jit(solution)/shard_map/ppermute | solution.py:43
  33.5 8.4 %collective-permute-start.6 = (bf16[272,512]{1,0:T(8,128)(2,1)}, bf16[272,512]{1,0:T(8,128)(2,1)}, u32[]{:S(2)}, u32[]{:S(2)}) collective-permute-start(bf16[272,512]{1,0:T(8,128)(2,1)} %pad_maximum_fusion.7), channel_id=1, source_target_pairs={{0,64},{1,65},{2,66},{3,67},{64,0},{65,1},{66,2},{67,3},{16,80},{1... | collective-permute-start | bytes 835592 | tf_op jit(solution)/shard_map/ppermute | solution.py:43
  35.6 10.8 %copy-start.14 = (s32[10]{0:T(128)}, s32[10]{0:T(128)S(1)}, u32[]{:S(2)}) copy-start(s32[10]{0:T(128)S(1)} %stack.116.refs_0_) | copy-start | bytes 124
  44.7 17.5 %collective-permute-start.11 = (bf16[256,1024]{1,0:T(8,128)(2,1)S(1)}, bf16[256,1024]{1,0:T(8,128)(2,1)S(1)}, u32[]{:S(2)}, u32[]{:S(2)}) collective-permute-start(bf16[256,1024]{1,0:T(8,128)(2,1)S(1)} %get-tuple-element.105), channel_id=1, source_target_pairs={{0,66},{1,67},{2,64},{3,65},{64,2},{65,3},{66,0},{67,1},{16,82},{1... | collective-permute-start | bytes 1572872 | tf_op jit(solution)/shard_map/ppermute | solution.py:43
  46.3 15.9 %collective-permute-start.12 = (bf16[256,1024]{1,0:T(8,128)(2,1)S(1)}, bf16[256,1024]{1,0:T(8,128)(2,1)S(1)}, u32[]{:S(2)}, u32[]{:S(2)}) collective-permute-start(bf16[256,1024]{1,0:T(8,128)(2,1)S(1)} %get-tuple-element.106), channel_id=1, source_target_pairs={{0,2},{1,3},{2,0},{3,1},{64,66},{65,67},{66,64},{67,65},{16,18},{1... | collective-permute-start | bytes 1572872 | tf_op jit(solution)/shard_map/ppermute | solution.py:43
  46.4 15.8 %collective-permute-start.13 = (bf16[256,512]{1,0:T(8,128)(2,1)S(1)}, bf16[256,512]{1,0:T(8,128)(2,1)S(1)}, u32[]{:S(2)}, u32[]{:S(2)}) collective-permute-start(bf16[256,512]{1,0:T(8,128)(2,1)S(1)} %pad_maximum_fusion.8), channel_id=1, source_target_pairs={{0,16},{1,17},{2,18},{3,19},{64,80},{65,81},{66,82},{67,83},{16,32... | collective-permute-start | bytes 786440 | tf_op jit(solution)/shard_map/ppermute | solution.py:43
  46.6 15.7 %collective-permute-start.14 = (bf16[256,512]{1,0:T(8,128)(2,1)S(1)}, bf16[256,512]{1,0:T(8,128)(2,1)S(1)}, u32[]{:S(2)}, u32[]{:S(2)}) collective-permute-start(bf16[256,512]{1,0:T(8,128)(2,1)S(1)} %pad_maximum_fusion.9), channel_id=1, source_target_pairs={{0,48},{1,49},{2,50},{3,51},{64,112},{65,113},{66,114},{67,115},{1... | collective-permute-start | bytes 786440 | tf_op jit(solution)/shard_map/ppermute | solution.py:43
  50.0 6.4 %copy-start.16 = (s32[8]{0:T(128)S(1)}, s32[8]{0:T(128)}, u32[]{:S(2)}) copy-start(s32[8]{0:T(128)} %stack.105.refs_0_) | copy-start | bytes 100
  62.2 6.9 %copy-start.25 = (bf16[256,1024]{1,0:T(8,128)(2,1)}, bf16[256,1024]{1,0:T(8,128)(2,1)S(1)}, u32[]{:S(2)}) copy-start(bf16[256,1024]{1,0:T(8,128)(2,1)S(1)} %collective-permute-done.11.refs_2_) | copy-start | bytes 1572868
  62.2 6.9 %copy-start.39 = (bf16[256,1024]{1,0:T(8,128)(2,1)}, bf16[256,1024]{1,0:T(8,128)(2,1)S(1)}, u32[]{:S(2)}) copy-start(bf16[256,1024]{1,0:T(8,128)(2,1)S(1)} %collective-permute-done.12) | copy-start | bytes 1572868
  70.8 5.4 %collective-permute-start.15 = (bf16[256,3584]{1,0:T(8,128)(2,1)}, bf16[256,3584]{1,0:T(8,128)(2,1)}, u32[]{:S(2)}, u32[]{:S(2)}) collective-permute-start(bf16[256,3584]{1,0:T(8,128)(2,1)} %get-tuple-element.112), channel_id=1, source_target_pairs={{0,1},{1,0},{2,3},{3,2},{64,65},{65,64},{66,67},{67,66},{16,17},{1... | collective-permute-start | bytes 5505032 | tf_op jit(solution)/shard_map/ppermute | solution.py:43
  70.8 5.4 %collective-permute-start.16 = (bf16[256,1792]{1,0:T(8,128)(2,1)}, bf16[256,1792]{1,0:T(8,128)(2,1)}, u32[]{:S(2)}, u32[]{:S(2)}) collective-permute-start(bf16[256,1792]{1,0:T(8,128)(2,1)} %get-tuple-element.113), channel_id=1, source_target_pairs={{0,1},{1,0},{2,3},{3,2},{64,65},{65,64},{66,67},{67,66},{16,17},{1... | collective-permute-start | bytes 2752520 | tf_op jit(solution)/shard_map/ppermute | solution.py:43
  71.3 15.7 %collective-permute-start.10 = (bf16[512,512]{1,0:T(8,128)(2,1)}, bf16[512,512]{1,0:T(8,128)(2,1)S(1)}, u32[]{:S(2)}, u32[]{:S(2)}) collective-permute-start(bf16[512,512]{1,0:T(8,128)(2,1)} %get-tuple-element.104), channel_id=1, source_target_pairs={{0,16},{1,17},{2,18},{3,19},{64,80},{65,81},{66,82},{67,83},{16,0}... | collective-permute-start | bytes 1572872 | tf_op jit(solution)/shard_map/ppermute | solution.py:43
  71.3 15.7 %collective-permute-start.9 = (bf16[512,512]{1,0:T(8,128)(2,1)}, bf16[512,512]{1,0:T(8,128)(2,1)}, u32[]{:S(2)}, u32[]{:S(2)}) collective-permute-start(bf16[512,512]{1,0:T(8,128)(2,1)} %get-tuple-element.101), channel_id=1, source_target_pairs={{0,48},{1,49},{2,50},{3,51},{64,112},{65,113},{66,114},{67,115},{1... | collective-permute-start | bytes 1572872 | tf_op jit(solution)/shard_map/ppermute | solution.py:43
  71.4 25.4 %collective-permute-start.21 = (bf16[256,1536]{1,0:T(8,128)(2,1)S(1)}, bf16[256,1536]{1,0:T(8,128)(2,1)S(1)}, u32[]{:S(2)}, u32[]{:S(2)}) collective-permute-start(bf16[256,1536]{1,0:T(8,128)(2,1)S(1)} %get-tuple-element.121.refs_1_.refs_5_), channel_id=1, source_target_pairs={{0,2},{1,3},{2,0},{3,1},{64,66},{65,67},{66,64},{67,65},{16,18},{1... | collective-permute-start | bytes 2359304 | tf_op jit(solution)/shard_map/ppermute | solution.py:43
  83.2 13.6 %copy-start.6 = (bf16[512,384]{1,0:T(8,128)(2,1)}, bf16[512,384]{1,0:T(8,128)(2,1)S(1)}, u32[]{:S(2)}) copy-start(bf16[512,384]{1,0:T(8,128)(2,1)S(1)} %get-tuple-element.176) | copy-start | bytes 1179652
  83.2 13.6 %copy-start.8 = (bf16[512,384]{1,0:T(8,128)(2,1)}, bf16[512,384]{1,0:T(8,128)(2,1)S(1)}, u32[]{:S(2)}) copy-start(bf16[512,384]{1,0:T(8,128)(2,1)S(1)} %get-tuple-element.177) | copy-start | bytes 1179652
  83.2 6.4 %copy-start.13 = (bf16[256,128]{1,0:T(8,128)(2,1)S(1)}, bf16[256,128]{1,0:T(8,128)(2,1)}, u32[]{:S(2)}) copy-start(bf16[256,128]{1,0:T(8,128)(2,1)} %copy-done.12) | copy-start | bytes 196612
  83.3 6.4 %copy-start.17 = (s32[8]{0:T(128)S(1)}, s32[8]{0:T(128)}, u32[]{:S(2)}) copy-start(s32[8]{0:T(128)} %stack.105.refs_0_) | copy-start | bytes 100
  83.3 19.7 %collective-permute-start.22 = (bf16[1024,384]{1,0:T(8,128)(2,1)S(1)}, bf16[1024,384]{1,0:T(8,128)(2,1)S(1)}, u32[]{:S(2)}, u32[]{:S(2)}) collective-permute-start(bf16[1024,384]{1,0:T(8,128)(2,1)S(1)} %get-tuple-element.114), channel_id=1, source_target_pairs={{0,4},{1,5},{2,6},{3,7},{64,68},{65,69},{66,70},{67,71},{16,20},{1... | collective-permute-start | bytes 2359304 | tf_op jit(solution)/shard_map/ppermute | solution.py:43
  84.8 20.5 %collective-permute-start.23 = (bf16[1024,384]{1,0:T(8,128)(2,1)S(1)}, bf16[1024,384]{1,0:T(8,128)(2,1)S(1)}, u32[]{:S(2)}, u32[]{:S(2)}) collective-permute-start(bf16[1024,384]{1,0:T(8,128)(2,1)S(1)} %get-tuple-element.137), channel_id=1, source_target_pairs={{0,12},{1,13},{2,14},{3,15},{64,76},{65,77},{66,78},{67,79},{16,28... | collective-permute-start | bytes 2359304 | tf_op jit(solution)/shard_map/ppermute | solution.py:43
  87.0 9.8 %collective-permute-start.18 = (bf16[256,512]{1,0:T(8,128)(2,1)S(1)}, bf16[256,512]{1,0:T(8,128)(2,1)S(1)}, u32[]{:S(2)}, u32[]{:S(2)}) collective-permute-start(bf16[256,512]{1,0:T(8,128)(2,1)S(1)} %add_convert_fusion.8), channel_id=1, source_target_pairs={{0,48},{1,49},{2,50},{3,51},{64,112},{65,113},{66,114},{67,115},{1... | collective-permute-start | bytes 786440 | tf_op jit(solution)/shard_map/ppermute | solution.py:43
  88.8 8.0 %collective-permute-start.17 = (bf16[256,512]{1,0:T(8,128)(2,1)S(1)}, bf16[256,512]{1,0:T(8,128)(2,1)S(1)}, u32[]{:S(2)}, u32[]{:S(2)}) collective-permute-start(bf16[256,512]{1,0:T(8,128)(2,1)S(1)} %add_convert_fusion.9), channel_id=1, source_target_pairs={{0,16},{1,17},{2,18},{3,19},{64,80},{65,81},{66,82},{67,83},{16,0}... | collective-permute-start | bytes 786440 | tf_op jit(solution)/shard_map/ppermute | solution.py:43
  89.7 15.7 %copy-start.40 = (bf16[256,1024]{1,0:T(8,128)(2,1)S(1)}, bf16[256,1024]{1,0:T(8,128)(2,1)}, u32[]{:S(2)}) copy-start(bf16[256,1024]{1,0:T(8,128)(2,1)} %copy-done.39) | copy-start | bytes 1572868
  96.8 8.6 %copy-start.34 = (bf16[256,512]{1,0:T(8,128)(2,1)}, bf16[256,512]{1,0:T(8,128)(2,1)S(1)}, u32[]{:S(2)}) copy-start(bf16[256,512]{1,0:T(8,128)(2,1)S(1)} %collective-permute-done.17) | copy-start | bytes 786436
  105.5 3.5 %collective-permute-start.24 = (bf16[256,2560]{1,0:T(8,128)(2,1)S(1)}, bf16[256,2560]{1,0:T(8,128)(2,1)S(1)}, u32[]{:S(2)}, u32[]{:S(2)}) collective-permute-start(bf16[256,2560]{1,0:T(8,128)(2,1)S(1)} %pad_maximum_fusion), channel_id=1, source_target_pairs={{0,1},{1,0},{2,3},{3,2},{64,65},{65,64},{66,67},{67,66},{16,17},{1... | collective-permute-start | bytes 3932168 | tf_op jit(solution)/shard_map/ppermute | solution.py:43
  105.6 17.1 %collective-permute-start.19 = (bf16[512,640]{1,0:T(8,128)(2,1)S(1)}, bf16[512,640]{1,0:T(8,128)(2,1)S(1)}, u32[]{:S(2)}, u32[]{:S(2)}) collective-permute-start(bf16[512,640]{1,0:T(8,128)(2,1)S(1)} %get-tuple-element.132), channel_id=1, source_target_pairs={{0,16},{1,17},{2,18},{3,19},{64,80},{65,81},{66,82},{67,83},{16,0}... | collective-permute-start | bytes 1966088 | tf_op jit(solution)/shard_map/ppermute | solution.py:43
  105.7 18.3 %collective-permute-start.20 = (bf16[512,640]{1,0:T(8,128)(2,1)S(1)}, bf16[512,640]{1,0:T(8,128)(2,1)S(1)}, u32[]{:S(2)}, u32[]{:S(2)}) collective-permute-start(bf16[512,640]{1,0:T(8,128)(2,1)S(1)} %get-tuple-element.135), channel_id=1, source_target_pairs={{0,48},{1,49},{2,50},{3,51},{64,112},{65,113},{66,114},{67,115},{1... | collective-permute-start | bytes 1966088 | tf_op jit(solution)/shard_map/ppermute | solution.py:43
  106.6 11.0 %collective-permute-start.26 = (bf16[512,384]{1,0:T(8,128)(2,1)S(1)}, bf16[512,384]{1,0:T(8,128)(2,1)S(1)}, u32[]{:S(2)}, u32[]{:S(2)}) collective-permute-start(bf16[512,384]{1,0:T(8,128)(2,1)S(1)} %add_convert_fusion.3), channel_id=1, source_target_pairs={{0,4},{1,5},{2,6},{3,7},{64,68},{65,69},{66,70},{67,71},{16,20},{1... | collective-permute-start | bytes 1179656 | tf_op jit(solution)/shard_map/ppermute | solution.py:43
  106.8 12.3 %collective-permute-start.25 = (bf16[512,384]{1,0:T(8,128)(2,1)S(1)}, bf16[512,384]{1,0:T(8,128)(2,1)}, u32[]{:S(2)}, u32[]{:S(2)}) collective-permute-start(bf16[512,384]{1,0:T(8,128)(2,1)S(1)} %add_convert_fusion.4), channel_id=1, source_target_pairs={{0,12},{1,13},{2,14},{3,15},{64,76},{65,77},{66,78},{67,79},{16,28... | collective-permute-start | bytes 1179656 | tf_op jit(solution)/shard_map/ppermute | solution.py:43
  117.3 8.8 %copy-start.21 = (bf16[512,768]{1,0:T(8,128)(2,1)}, bf16[512,768]{1,0:T(8,128)(2,1)S(1)}, u32[]{:S(2)}) copy-start(bf16[512,768]{1,0:T(8,128)(2,1)S(1)} %get-tuple-element.162) | copy-start | bytes 2359300
  117.3 8.8 %copy-start.22 = (bf16[512,768]{1,0:T(8,128)(2,1)}, bf16[512,768]{1,0:T(8,128)(2,1)S(1)}, u32[]{:S(2)}) copy-start(bf16[512,768]{1,0:T(8,128)(2,1)S(1)} %get-tuple-element.153) | copy-start | bytes 2359300
  117.3 9.8 %copy-start.44 = (bf16[512]{0:T(512)(128)(2,1)S(1)}, bf16[512]{0:T(512)(128)(2,1)}, u32[]{:S(2)}) copy-start(bf16[512]{0:T(512)(128)(2,1)} %param.5) | copy-start | bytes 3076
  117.6 8.6 %copy-start.41 = (bf16[512,384]{1,0:T(8,128)(2,1)}, bf16[512,384]{1,0:T(8,128)(2,1)S(1)}, u32[]{:S(2)}) copy-start(bf16[512,384]{1,0:T(8,128)(2,1)S(1)} %collective-permute-done.26) | copy-start | bytes 1179652
  124.8 9.3 %collective-permute-start.28 = (bf16[256,640]{1,0:T(8,128)(2,1)}, bf16[256,640]{1,0:T(8,128)(2,1)S(1)}, u32[]{:S(2)}, u32[]{:S(2)}) collective-permute-start(bf16[256,640]{1,0:T(8,128)(2,1)} %add_convert_fusion.5), channel_id=1, source_target_pairs={{0,16},{1,17},{2,18},{3,19},{64,80},{65,81},{66,82},{67,83},{16,0}... | collective-permute-start | bytes 983048 | tf_op jit(solution)/shard_map/ppermute | solution.py:43
  126.2 14.7 %copy-start.7 = (bf16[512,384]{1,0:T(8,128)(2,1)S(1)}, bf16[512,384]{1,0:T(8,128)(2,1)}, u32[]{:S(2)}) copy-start(bf16[512,384]{1,0:T(8,128)(2,1)} %copy-done.6) | copy-start | bytes 1179652
  126.2 14.7 %copy-start.9 = (bf16[512,384]{1,0:T(8,128)(2,1)S(1)}, bf16[512,384]{1,0:T(8,128)(2,1)}, u32[]{:S(2)}) copy-start(bf16[512,384]{1,0:T(8,128)(2,1)} %copy-done.8) | copy-start | bytes 1179652
  126.2 10.2 %collective-permute-start.27 = (bf16[256,640]{1,0:T(8,128)(2,1)}, bf16[256,640]{1,0:T(8,128)(2,1)S(1)}, u32[]{:S(2)}, u32[]{:S(2)}) collective-permute-start(bf16[256,640]{1,0:T(8,128)(2,1)} %add_convert_fusion.6), channel_id=1, source_target_pairs={{0,48},{1,49},{2,50},{3,51},{64,112},{65,113},{66,114},{67,115},{1... | collective-permute-start | bytes 983048 | tf_op jit(solution)/shard_map/ppermute | solution.py:43
  127.2 13.7 %copy-start.37 = (bf16[1024,384]{1,0:T(8,128)(2,1)S(1)}, bf16[1024,384]{1,0:T(8,128)(2,1)}, u32[]{:S(2)}) copy-start(bf16[1024,384]{1,0:T(8,128)(2,1)} %copy-done.36) | copy-start | bytes 2359300
  127.2 13.7 %copy-start.42 = (bf16[512,384]{1,0:T(8,128)(2,1)S(1)}, bf16[512,384]{1,0:T(8,128)(2,1)}, u32[]{:S(2)}) copy-start(bf16[512,384]{1,0:T(8,128)(2,1)} %copy-done.41) | copy-start | bytes 1179652
  127.2 24.0 %collective-permute-start.31 = (bf16[512,768]{1,0:T(8,128)(2,1)}, bf16[512,768]{1,0:T(8,128)(2,1)S(1)}, u32[]{:S(2)}, u32[]{:S(2)}) collective-permute-start(bf16[512,768]{1,0:T(8,128)(2,1)} %copy-done.22), channel_id=1, source_target_pairs={{0,4},{1,5},{2,6},{3,7},{64,68},{65,69},{66,70},{67,71},{16,20},{1... | collective-permute-start | bytes 2359304 | tf_op jit(solution)/shard_map/ppermute | solution.py:43
  127.3 23.9 %collective-permute-start.32 = (bf16[512,768]{1,0:T(8,128)(2,1)}, bf16[512,768]{1,0:T(8,128)(2,1)S(1)}, u32[]{:S(2)}, u32[]{:S(2)}) collective-permute-start(bf16[512,768]{1,0:T(8,128)(2,1)} %copy-done.21), channel_id=1, source_target_pairs={{0,12},{1,13},{2,14},{3,15},{64,76},{65,77},{66,78},{67,79},{16,28... | collective-permute-start | bytes 2359304 | tf_op jit(solution)/shard_map/ppermute | solution.py:43
  137.7 12.2 %collective-permute-start.29 = (bf16[256,640]{1,0:T(8,128)(2,1)S(1)}, bf16[256,640]{1,0:T(8,128)(2,1)S(1)}, u32[]{:S(2)}, u32[]{:S(2)}) collective-permute-start(bf16[256,640]{1,0:T(8,128)(2,1)S(1)} %select_convert_fusion.1), channel_id=1, source_target_pairs={{0,64},{1,65},{2,66},{3,67},{64,0},{65,1},{66,2},{67,3},{16,80},{1... | collective-permute-start | bytes 983048 | tf_op jit(solution)/shard_map/ppermute | solution.py:43
  142.3 7.7 %copy-start.28 = (bf16[512,640]{1,0:T(8,128)(2,1)S(1)}, bf16[512,640]{1,0:T(8,128)(2,1)}, u32[]{:S(2)}) copy-start(bf16[512,640]{1,0:T(8,128)(2,1)} %copy-done.27) | copy-start | bytes 1966084
  142.3 7.6 %copy-start.30 = (bf16[512,640]{1,0:T(8,128)(2,1)S(1)}, bf16[512,640]{1,0:T(8,128)(2,1)}, u32[]{:S(2)}) copy-start(bf16[512,640]{1,0:T(8,128)(2,1)} %copy-done.29) | copy-start | bytes 1966084
  142.4 8.0 %copy-start.33 = (bf16[256,512]{1,0:T(8,128)(2,1)S(1)}, bf16[256,512]{1,0:T(8,128)(2,1)}, u32[]{:S(2)}) copy-start(bf16[256,512]{1,0:T(8,128)(2,1)} %param.4) | copy-start | bytes 786436
  142.4 20.3 %collective-permute-start.39 = (bf16[256,768]{1,0:T(8,128)(2,1)S(1)}, bf16[256,768]{1,0:T(8,128)(2,1)S(1)}, u32[]{:S(2)}, u32[]{:S(2)}) collective-permute-start(bf16[256,768]{1,0:T(8,128)(2,1)S(1)} %select_convert_fusion), channel_id=1, source_target_pairs={{0,2},{1,3},{2,0},{3,1},{64,66},{65,67},{66,64},{67,65},{16,18},{1... | collective-permute-start | bytes 1179656 | tf_op jit(solution)/shard_map/ppermute | solution.py:43
  151.5 5.2 %collective-permute-start.33 = (f32[1,512]{1,0:T(1,128)S(1)}, f32[1,512]{1,0:T(1,128)S(1)}, u32[]{:S(2)}, u32[]{:S(2)}) collective-permute-start(f32[1,512]{1,0:T(1,128)S(1)} %bitcast.32), channel_id=1, source_target_pairs={{0,1},{1,0},{2,3},{3,2},{64,65},{65,64},{66,67},{67,66},{16,17},{1... | collective-permute-start | bytes 6152 | tf_op jit(solution)/shard_map/ppermute | solution.py:43
  153.5 14.8 %collective-permute-start.30 = (bf16[256,512]{1,0:T(8,128)(2,1)S(1)}, bf16[256,512]{1,0:T(8,128)(2,1)S(1)}, u32[]{:S(2)}, u32[]{:S(2)}) collective-permute-start(bf16[256,512]{1,0:T(8,128)(2,1)S(1)} %select_convert_fusion.2), channel_id=1, source_target_pairs={{0,64},{1,65},{2,66},{3,67},{64,0},{65,1},{66,2},{67,3},{16,80},{1... | collective-permute-start | bytes 786440 | tf_op jit(solution)/shard_map/ppermute | solution.py:43
  156.7 6.0 %collective-permute-start.34 = (f32[1,512]{1,0:T(1,128)S(1)}, f32[1,512]{1,0:T(1,128)S(1)}, u32[]{:S(2)}, u32[]{:S(2)}) collective-permute-start(f32[1,512]{1,0:T(1,128)S(1)} %add.218), channel_id=1, source_target_pairs={{0,2},{1,3},{2,0},{3,1},{64,66},{65,67},{66,64},{67,65},{16,18},{1... | collective-permute-start | bytes 6152 | tf_op jit(solution)/shard_map/ppermute | solution.py:43
  157.4 12.7 %collective-permute-start.37 = (bf16[256,768]{1,0:T(8,128)(2,1)S(1)}, bf16[256,768]{1,0:T(8,128)(2,1)S(1)}, u32[]{:S(2)}, u32[]{:S(2)}) collective-permute-start(bf16[256,768]{1,0:T(8,128)(2,1)S(1)} %add_convert_fusion.1), channel_id=1, source_target_pairs={{0,4},{1,5},{2,6},{3,7},{64,68},{65,69},{66,70},{67,71},{16,20},{1... | collective-permute-start | bytes 1179656 | tf_op jit(solution)/shard_map/ppermute | solution.py:43
  157.5 12.7 %collective-permute-start.36 = (bf16[256,768]{1,0:T(8,128)(2,1)S(1)}, bf16[256,768]{1,0:T(8,128)(2,1)S(1)}, u32[]{:S(2)}, u32[]{:S(2)}) collective-permute-start(bf16[256,768]{1,0:T(8,128)(2,1)S(1)} %add_convert_fusion.2), channel_id=1, source_target_pairs={{0,12},{1,13},{2,14},{3,15},{64,76},{65,77},{66,78},{67,79},{16,28... | collective-permute-start | bytes 1179656 | tf_op jit(solution)/shard_map/ppermute | solution.py:43
  162.7 5.6 %collective-permute-start.35 = (f32[1,512]{1,0:T(1,128)S(1)}, f32[1,512]{1,0:T(1,128)S(1)}, u32[]{:S(2)}, u32[]{:S(2)}) collective-permute-start(f32[1,512]{1,0:T(1,128)S(1)} %add.219), channel_id=1, source_target_pairs={{0,4},{1,5},{2,6},{3,7},{64,68},{65,69},{66,70},{67,71},{16,20},{1... | collective-permute-start | bytes 6152 | tf_op jit(solution)/shard_map/ppermute | solution.py:43
  162.8 9.1 %copy-start.3 = (bf16[256,768]{1,0:T(8,128)(2,1)S(1)}, bf16[256,768]{1,0:T(8,128)(2,1)}, u32[]{:S(2)}) copy-start(bf16[256,768]{1,0:T(8,128)(2,1)} %copy-done.2) | copy-start | bytes 1179652
  162.8 9.1 %copy-start.5 = (bf16[256,768]{1,0:T(8,128)(2,1)S(1)}, bf16[256,768]{1,0:T(8,128)(2,1)}, u32[]{:S(2)}) copy-start(bf16[256,768]{1,0:T(8,128)(2,1)} %copy-done.4) | copy-start | bytes 1179652
  170.2 5.1 %collective-permute-start.38 = (f32[1,512]{1,0:T(1,128)S(1)}, f32[1,512]{1,0:T(1,128)S(1)}, u32[]{:S(2)}, u32[]{:S(2)}) collective-permute-start(f32[1,512]{1,0:T(1,128)S(1)} %add.220), channel_id=1, source_target_pairs={{0,8},{1,9},{2,10},{3,11},{64,72},{65,73},{66,74},{67,75},{16,24},... | collective-permute-start | bytes 6152 | tf_op jit(solution)/shard_map/ppermute | solution.py:43
  (21 other events, 45.4 us)

commit v7 on v5

--- a/solution.py
+++ b/solution.py
@@ -342,7 +342,7 @@
     down = finish(down_terms, down_got, down_last, (pair_terms[0],))
     d_w_down = jnp.concatenate(down, axis=1)
     lower = z_lo == 0
-    theirs = jnp.where(lower, d_w_down[256:], d_w_down[:256]).astype(bf16)
+    theirs = after(jnp.where(lower, d_w_down[256:], d_w_down[:256]).astype(bf16), *pair_got)
     d_w_down = jnp.where(lower, d_w_down[:256], d_w_down[256:]) + send(theirs, "z^1").astype(f32)
 
     _, d_last = second_step(d_terms, d_got, "y", (pair_terms[0],))
@@ -352,7 +352,7 @@
     upper = z_hi == 1
     mine = jnp.where(upper, d_high, d_low)
     theirs = send(jnp.where(upper, d_low, d_high).astype(bf16), "z+2")
-    mine = mine + theirs.astype(f32)
+    mine = after(mine, *pair_got) + theirs.astype(f32)
     theirs = send(after(jnp.where(upper, low, high).astype(bf16), theirs), "z+2")
     branch = (jnp.where(upper, high, low) + theirs.astype(f32)).astype(bf16)
     d_normed, products = mine[:, :512], mine[:, 512:513] / width
@@ -361,8 +361,8 @@
     d_input = (d_normed * gain.astype(f32) - inv[:, :1] * products * x_own).astype(bf16)
     d_gain = jnp.sum(d_normed * x_own, axis=0, keepdims=True)
     for move in ("c", "z^1", "x^1", "x+2"):
-        if move == "x^1":
-            d_gain = after(d_gain, *pair_out)
+        if move in ("c", "x+2"):
+            d_gain = after(d_gain, *(pair_out if move == "c" else pair_last))
         d_gain = d_gain + send(d_gain, move)
 
     gain_rows = lax.dynamic_slice(gains, (0, s * 256), (1, 256)).astype(f32).reshape(256, 1)

time: 171 us -> 176 us (1.029)
  other arithmetic: 13.7 us -> 19.2 us
  waiting for transfers between devices: 68.3 us -> 64.8 us
    ppermute x40, waiting for transfers between devices: 68.3 us -> 64.8 us  [send(): return lax.ppermute(value, AXES, pairs(moves[move]))]
    convert_element_type x8, other arithmetic: 2.3 us -> 5.74 us  [second_step(): (t.astype(f32) + g[rows:].astype(f32)).astype(bf16)]
    another operation x3, other arithmetic: 1.59 us -> 3.71 us  [local(): jnp.stack([(d_w_gate * gain_rows).astype(bf16), (d_w_up * gain_rows).asty...]
    unnamed x72 -> x106, local copies, waits for them, and re-layouts: 5.46 us -> 7.06 us
  transfers between devices with their start and end apart: 40 -> 40, of which waited for: 21 -> 22; matrix products, arithmetic and copies ran while one was open for 6% -> 10% of each run, Pallas kernels for 18% -> 18%
where the time goes in v7:
time: 176 us; the launch traced here: 175 us
  waiting for transfers between devices  64.8 us (37%)
  starting transfers between devices  44.2 us (25%)
  Pallas kernels  37.7 us (21%)
  other arithmetic  19.2 us (11%)
  local copies, waits for them, and re-layouts  8.07 us (5%)
    ppermute x40, waiting for transfers between devices, send(): return lax.ppermute(value, AXES, pairs(moves[move]))  64.8 us
    ppermute x40, starting transfers between devices, send(): return lax.ppermute(value, AXES, pairs(moves[move]))  44.2 us
    pallas_call x7, Pallas kernels, call(): pl.pallas_call(whole, in_specs=[pl.BlockSpec(memory_space=space) for spac...  37.7 us
    unnamed x106, local copies, waits for them, and re-layouts  7.06 us
    convert_element_type x8, other arithmetic, second_step(): (t.astype(f32) + g[rows:].astype(f32)).astype(bf16)  5.74 us
    another operation x3, other arithmetic, local(): jnp.stack([(d_w_gate * gain_rows).astype(bf16), (d_w_up * gain_rows).asty...  3.71 us
  transfers between devices with their start and end apart: 40, of which 22 were waited for; matrix products, arithmetic and copies ran while one was open for 10% of the time, Pallas kernels for 18%

profile of v7, /device:TPU:0, one launch (start us, length us, event | category | flops | bytes accessed | tf_op | source)
XLA Modules:
  0.0 175.0 jit_solution(13998701517968333559)
XLA Ops:
  1.3 1.0 pad_maximum_fusion.6.refs_1_
  2.3 3.2 %collective-permute-start.1 = (bf16[272,512]{1,0:T(8,128)(2,1)S(1)}, bf16[272,512]{1,0:T(8,128)(2,1)S(1)}, u32[]{:S(2)}, u32[]{:S(2)}) collective-permute-start(bf16[272,512]{1,0:T(8,128)(2,1)S(1)} %pad_maximum_fusion.6.refs_1_), channel_id=1, source_target_pairs={{0,48},{1,49},{2,50},{3,51},{64,112},{65,113},{66,114},{67,115},{1... | collective-permute-start | bytes 835592 | tf_op jit(solution)/shard_map/ppermute | solution.py:43
  5.5 3.9 %collective-permute-start.2 = (bf16[272,512]{1,0:T(8,128)(2,1)S(1)}, bf16[272,512]{1,0:T(8,128)(2,1)S(1)}, u32[]{:S(2)}, u32[]{:S(2)}) collective-permute-start(bf16[272,512]{1,0:T(8,128)(2,1)S(1)} %pad_maximum_fusion.6.refs_1_), channel_id=1, source_target_pairs={{0,64},{1,65},{2,66},{3,67},{64,0},{65,1},{66,2},{67,3},{16,80},{1... | collective-permute-start | bytes 835592 | tf_op jit(solution)/shard_map/ppermute | solution.py:43
  9.4 2.0 %collective-permute-done.1.refs_3_ = bf16[272,512]{1,0:T(8,128)(2,1)S(1)} collective-permute-done((bf16[272,512]{1,0:T(8,128)(2,1)S(1)}, bf16[272,512]{1,0:T(8,128)(2,1)S(1)}, u32[]{:S(2)}, u32[]{:S(2)}) %collective-permute-start.1) | collective-permute-done | bytes 278560 | tf_op jit(solution)/shard_map/ppermute | solution.py:43
  11.4 4.3 %collective-permute-done.2.refs_4_ = bf16[272,512]{1,0:T(8,128)(2,1)S(1)} collective-permute-done((bf16[272,512]{1,0:T(8,128)(2,1)S(1)}, bf16[272,512]{1,0:T(8,128)(2,1)S(1)}, u32[]{:S(2)}, u32[]{:S(2)}) %collective-permute-start.2) | collective-permute-done | bytes 278560 | tf_op jit(solution)/shard_map/ppermute | solution.py:43
  15.8 0.8 collective-permute-start.4
  16.6 1.8 %collective-permute-done.refs_2_ = bf16[272,512]{1,0:T(8,128)(2,1)S(1)} collective-permute-done((bf16[272,512]{1,0:T(8,128)(2,1)S(1)}, bf16[272,512]{1,0:T(8,128)(2,1)S(1)}, u32[]{:S(2)}, u32[]{:S(2)}) %collective-permute-start) | collective-permute-done | bytes 278560 | tf_op jit(solution)/shard_map/ppermute | solution.py:43
  18.6 2.7 %collective-permute-start.5 = (bf16[256,512]{1,0:T(8,128)(2,1)S(1)}, bf16[256,512]{1,0:T(8,128)(2,1)S(1)}, u32[]{:S(2)}, u32[]{:S(2)}) collective-permute-start(bf16[256,512]{1,0:T(8,128)(2,1)S(1)} %copy-done.51), channel_id=1, source_target_pairs={{0,64},{1,65},{2,66},{3,67},{64,0},{65,1},{66,2},{67,3},{16,80},{1... | collective-permute-start | bytes 786440 | tf_op jit(solution)/shard_map/ppermute | solution.py:43
  21.3 5.5 %collective-permute-done.5 = bf16[256,512]{1,0:T(8,128)(2,1)S(1)} collective-permute-done((bf16[256,512]{1,0:T(8,128)(2,1)S(1)}, bf16[256,512]{1,0:T(8,128)(2,1)S(1)}, u32[]{:S(2)}, u32[]{:S(2)}) %collective-permute-start.5) | collective-permute-done | bytes 262176 | tf_op jit(solution)/shard_map/ppermute | solution.py:43
  26.7 2.7 %collective-permute-done.3.refs_5_ = bf16[400,512]{1,0:T(8,128)(2,1)S(1)} collective-permute-done((bf16[400,512]{1,0:T(8,128)(2,1)S(1)}, bf16[400,512]{1,0:T(8,128)(2,1)S(1)}, u32[]{:S(2)}, u32[]{:S(2)}) %collective-permute-start.3) | collective-permute-done | bytes 409632 | tf_op jit(solution)/shard_map/ppermute | solution.py:43
  30.5 1.6 collective-permute-start.6
  32.2 1.5 collective-permute-start.7
  33.8 5.1 %collective-permute-done.6.refs_7_ = bf16[272,512]{1,0:T(8,128)(2,1)} collective-permute-done((bf16[272,512]{1,0:T(8,128)(2,1)}, bf16[272,512]{1,0:T(8,128)(2,1)}, u32[]{:S(2)}, u32[]{:S(2)}) %collective-permute-start.6) | collective-permute-done | bytes 278560 | tf_op jit(solution)/shard_map/ppermute | solution.py:43
  38.9 1.4 assemble.1
  41.0 0.8 copy-done.19
  41.8 1.8 %collective-permute-start.9 = (bf16[256,1024]{1,0:T(8,128)(2,1)S(1)}, bf16[256,1024]{1,0:T(8,128)(2,1)S(1)}, u32[]{:S(2)}, u32[]{:S(2)}) collective-permute-start(bf16[256,1024]{1,0:T(8,128)(2,1)S(1)} %get-tuple-element.102), channel_id=1, source_target_pairs={{0,66},{1,67},{2,64},{3,65},{64,2},{65,3},{66,0},{67,1},{16,82},{1... | collective-permute-start | bytes 1572872 | tf_op jit(solution)/shard_map/ppermute | solution.py:43
  44.4 1.4 collective-permute-start.11
  45.9 6.3 %forward.1 = (f32[256,768]{1,0:T(8,128)S(1)}, f32[256,768]{1,0:T(8,128)S(1)}, bf16[256,768]{1,0:T(8,128)(2,1)S(1)}, f32[256,128]{1,0:T(8,128)S(1)}, bf16[256,1792]{1,0:T(8,128)(2,1)}) custom-call(bf16[272,4096]{1,0:T(8,128)(2,1)S(1)} %get-tuple-element.99.refs_0_, bf16[256,1024]{1,0:T(8,128)(2,1)S(1)} %get-tuple-element.100.refs_1_, ...), custom_call_target="tpu_custom_call" | custom-call | flops 3221225472 | bytes 16777216 | tf_op jit(solution)/shard_map/forward/pallas_call | solution.py:89
  52.8 0.8 copy-done.21
  54.4 6.8 %backward.1 = (bf16[256,1536]{1,0:T(8,128)(2,1)S(1)}, bf16[256,128]{1,0:T(8,128)(2,1)S(1)}, bf16[256,2048]{1,0:T(8,128)(2,1)S(1)}, bf16[256,3584]{1,0:T(8,128)(2,1)}) custom-call(s32[10]{0:T(128)S(1)} %stack.116.refs_0_, bf16[512,512]{1,0:T(8,128)(2,1)S(1)} %pad_maximum_fusion.3.refs_1_, bf16[512,512]{1,0:T(8,128)(2,1)S(1)} %collective-permute-done.7.refs_2_, ...), custom_call_target="tpu_custom_call" | custom-call | flops 1610612736 | bytes 8388608 | tf_op jit(solution)/shard_map/backward/pallas_call | solution.py:89
  61.3 1.0 copy-done.15
  62.9 1.4 collective-permute-start.16
  64.4 5.2 %branch_rows.1 = (bf16[512,512]{1,0:T(8,128)(2,1)S(1)}, bf16[512,512]{1,0:T(8,128)(2,1)S(1)}, bf16[256,512]{1,0:T(8,128)(2,1)S(1)}, bf16[256,512]{1,0:T(8,128)(2...) custom-call(s32[8]{0:T(128)S(1)} %stack.105.refs_0_, ...), custom_call_target="tpu_custom_call" | custom-call | flops 1610612736 | bytes 8388608 | tf_op jit(solution)/shard_map/branch_rows/pallas_call | solution.py:89
  71.0 4.8 %down_terms.1 = (bf16[1024,384]{1,0:T(8,128)(2,1)S(1)}, bf16[1024,384]{1,0:T(8,128)(2,1)S(1)}, bf16[512,384]{1,0:T(8,128)(2,1)S(1)}, bf16[512,384]{1,0:T(8,128)(...) custom-call(s32[8]{0:T(128)S(1)} %stack.121.refs_0_, bf16[256,2048]{1,0:T(8,128)(2,1)S(1)} %copy-done.16, ...), custom_call_target="tpu_custom_call" | custom-call | flops 1610612736 | bytes 8388608 | tf_op jit(solution)/shard_map/down_terms/pallas_call | solution.py:89
  75.8 2.8 %collective-permute-start.19 = (bf16[1024,384]{1,0:T(8,128)(2,1)S(1)}, bf16[1024,384]{1,0:T(8,128)(2,1)S(1)}, u32[]{:S(2)}, u32[]{:S(2)}) collective-permute-start(bf16[1024,384]{1,0:T(8,128)(2,1)S(1)} %get-tuple-element.132), channel_id=1, source_target_pairs={{0,12},{1,13},{2,14},{3,15},{64,76},{65,77},{66,78},{67,79},{16,28... | collective-permute-start | bytes 2359304 | tf_op jit(solution)/shard_map/ppermute | solution.py:43
  78.9 1.7 collective-permute-start.13
  80.5 7.1 %pair_rows.1 = (bf16[512,640]{1,0:T(8,128)(2,1)S(1)}, bf16[512,640]{1,0:T(8,128)(2,1)S(1)}, bf16[256,640]{1,0:T(8,128)(2,1)S(1)}, bf16[256,640]{1,0:T(8,128)(2,1...) custom-call(s32[8]{0:T(128)S(1)} %stack.105.refs_0_, ...), custom_call_target="tpu_custom_call" | custom-call | flops 3221225472 | bytes 16777216 | tf_op jit(solution)/shard_map/pair_rows/pallas_call | solution.py:89
  88.4 4.7 %collective-permute-done.13 = bf16[512,512]{1,0:T(8,128)(2,1)S(1)} collective-permute-done((bf16[512,512]{1,0:T(8,128)(2,1)S(1)}, bf16[512,512]{1,0:T(8,128)(2,1)S(1)}, u32[]{:S(2)}, u32[]{:S(2)}) %collective-permute-start.13) | collective-permute-done | bytes 524320 | tf_op jit(solution)/shard_map/ppermute | solution.py:43
  93.3 2.9 %collective-permute-done.19 = bf16[1024,384]{1,0:T(8,128)(2,1)S(1)} collective-permute-done((bf16[1024,384]{1,0:T(8,128)(2,1)S(1)}, bf16[1024,384]{1,0:T(8,128)(2,1)S(1)}, u32[]{:S(2)}, u32[]{:S(2)}) %collective-permute-start.19) | collective-permute-done | bytes 786464 | tf_op jit(solution)/shard_map/ppermute | solution.py:43
  96.3 1.3 collective-permute-done.18
  97.7 1.6 collective-permute-start.23
  100.6 1.6 collective-permute-start.21
  102.2 6.0 %pair_terms.1 = (bf16[512,768]{1,0:T(8,128)(2,1)S(1)}, bf16[512,768]{1,0:T(8,128)(2,1)S(1)}, bf16[256,768]{1,0:T(8,128)(2,1)S(1)}, bf16[256,768]{1,0:T(8,128)(2,...) custom-call(s32[8]{0:T(128)S(1)} %stack.121.refs_0_, bf16[256,1024]{1,0:T(8,128)(2,1)S(1)} %copy-done.20, ...), custom_call_target="tpu_custom_call" | custom-call | flops 3221225472 | bytes 8388608 | tf_op jit(solution)/shard_map/pair_terms/pallas_call | solution.py:89
  109.0 2.1 %collective-permute-done.22 = bf16[512,384]{1,0:T(8,128)(2,1)S(1)} collective-permute-done((bf16[512,384]{1,0:T(8,128)(2,1)S(1)}, bf16[512,384]{1,0:T(8,128)(2,1)S(1)}, u32[]{:S(2)}, u32[]{:S(2)}) %collective-permute-start.22) | collective-permute-done | bytes 393248 | tf_op jit(solution)/shard_map/ppermute | solution.py:43
  111.1 1.6 collective-permute-done.21
  112.8 4.6 %collective-permute-done.24 = bf16[512,640]{1,0:T(8,128)(2,1)S(1)} collective-permute-done((bf16[512,640]{1,0:T(8,128)(2,1)S(1)}, bf16[512,640]{1,0:T(8,128)(2,1)S(1)}, u32[]{:S(2)}, u32[]{:S(2)}) %collective-permute-start.24) | collective-permute-done | bytes 655392 | tf_op jit(solution)/shard_map/ppermute | solution.py:43
  117.4 0.9 add_convert_fusion.5
  118.3 0.8 add_convert_fusion.6
  119.1 1.0 collective-permute-start.25
  120.6 1.3 collective-permute-start.32
  121.9 5.6 %collective-permute-done.26 = bf16[256,640]{1,0:T(8,128)(2,1)S(1)} collective-permute-done((bf16[256,640]{1,0:T(8,128)(2,1)}, bf16[256,640]{1,0:T(8,128)(2,1)S(1)}, u32[]{:S(2)}, u32[]{:S(2)}) %collective-permute-start.26) | collective-permute-done | bytes 327712 | tf_op jit(solution)/shard_map/ppermute | solution.py:43
  127.5 2.2 %collective-permute-done.25 = bf16[256,640]{1,0:T(8,128)(2,1)} collective-permute-done((bf16[256,640]{1,0:T(8,128)(2,1)}, bf16[256,640]{1,0:T(8,128)(2,1)}, u32[]{:S(2)}, u32[]{:S(2)}) %collective-permute-start.25) | collective-permute-done | bytes 327712 | tf_op jit(solution)/shard_map/ppermute | solution.py:43
  129.7 1.0 add_convert_fusion.8
  131.5 1.1 add_convert_fusion.9
  132.8 1.4 fusion.4
  134.2 2.0 %collective-permute-start.29 = (bf16[256,640]{1,0:T(8,128)(2,1)S(1)}, bf16[256,640]{1,0:T(8,128)(2,1)S(1)}, u32[]{:S(2)}, u32[]{:S(2)}) collective-permute-start(bf16[256,640]{1,0:T(8,128)(2,1)S(1)} %get-tuple-element.187), channel_id=1, source_target_pairs={{0,64},{1,65},{2,66},{3,67},{64,0},{65,1},{66,2},{67,3},{16,80},{1... | collective-permute-start | bytes 983048 | tf_op jit(solution)/shard_map/ppermute | solution.py:43
  136.5 2.1 %collective-permute-done.28 = bf16[256,512]{1,0:T(8,128)(2,1)S(1)} collective-permute-done((bf16[256,512]{1,0:T(8,128)(2,1)S(1)}, bf16[256,512]{1,0:T(8,128)(2,1)S(1)}, u32[]{:S(2)}, u32[]{:S(2)}) %collective-permute-start.28) | collective-permute-done | bytes 262176 | tf_op jit(solution)/shard_map/ppermute | solution.py:43
  139.1 0.9 select_convert_fusion.2
  140.0 3.2 %collective-permute-done.29 = bf16[256,640]{1,0:T(8,128)(2,1)S(1)} collective-permute-done((bf16[256,640]{1,0:T(8,128)(2,1)S(1)}, bf16[256,640]{1,0:T(8,128)(2,1)S(1)}, u32[]{:S(2)}, u32[]{:S(2)}) %collective-permute-start.29) | collective-permute-done | bytes 327712 | tf_op jit(solution)/shard_map/ppermute | solution.py:43
  143.2 2.1 %collective-permute-start.30 = (bf16[256,512]{1,0:T(8,128)(2,1)}, bf16[256,512]{1,0:T(8,128)(2,1)}, u32[]{:S(2)}, u32[]{:S(2)}) collective-permute-start(bf16[256,512]{1,0:T(8,128)(2,1)} %select_convert_fusion.2), channel_id=1, source_target_pairs={{0,64},{1,65},{2,66},{3,67},{64,0},{65,1},{66,2},{67,3},{16,80},{1... | collective-permute-start | bytes 786440 | tf_op jit(solution)/shard_map/ppermute | solution.py:43
  145.6 0.9 add_convert_fusion.1
  146.7 0.8 add_convert_fusion.2
  147.6 1.4 collective-permute-start.36
  149.0 0.9 fusion.3
  149.9 0.8 select_convert_fusion
  151.3 1.5 collective-permute-start.34
  152.8 9.8 %collective-permute-done.34 = f32[1,512]{1,0:T(1,128)S(1)} collective-permute-done((f32[1,512]{1,0:T(1,128)S(1)}, f32[1,512]{1,0:T(1,128)S(1)}, u32[]{:S(2)}, u32[]{:S(2)}) %collective-permute-start.34) | collective-permute-done | bytes 2080 | tf_op jit(solution)/shard_map/ppermute | solution.py:43
  162.6 1.2 collective-permute-start.35
  164.5 1.7 collective-permute-done.35
  166.2 2.1 %add_convert_fusion.7 = bf16[256,512]{1,0:T(8,128)(2,1)} fusion(bf16[256,512]{1,0:T(8,128)(2,1)} %collective-permute-done.30, bf16[256,512]{1,0:T(8,128)(2,1)} %copy-done.32, bf16[256,512]{1,0:T(8,128)(2,1)S(1)} %get-tuple-element.112, bf16[256,512]{1,0:T(8,128)(2,1)S(1)} %copy-done.31, bf16[256,512]{1,0:T(8,128)(2,1)S(1)} %get-tuple-element.158, ...), kind=kLoop, calls=%fused_computation.28 | loop fusion | flops 1835008 | bytes 2097153 | tf_op jit(solution)/shard_map/convert_element_type | solution.py:357
  168.2 2.5 %collective-permute-start.38 = (f32[1,512]{1,0:T(1,128)S(1)}, f32[1,512]{1,0:T(1,128)S(1)}, u32[]{:S(2)}, u32[]{:S(2)}) collective-permute-start(f32[1,512]{1,0:T(1,128)S(1)} %add.220), channel_id=1, source_target_pairs={{0,8},{1,9},{2,10},{3,11},{64,72},{65,73},{66,74},{67,75},{16,24},... | collective-permute-start | bytes 6152 | tf_op jit(solution)/shard_map/ppermute | solution.py:43
  170.7 1.1 fusion.7
  171.8 1.5 fusion.5
  173.3 1.1 pad_maximum_fusion.1
  (172 shorter events, 14.8 us)
Async XLA Ops:
  1.3 17.2 %copy-start.51 = (bf16[256,512]{1,0:T(8,128)(2,1)S(1)}, bf16[256,512]{1,0:T(8,128)(2,1)}, u32[]{:S(2)}) copy-start(bf16[256,512]{1,0:T(8,128)(2,1)} %param.7) | copy-start | bytes 786436
  2.3 9.1 %collective-permute-start.1 = (bf16[272,512]{1,0:T(8,128)(2,1)S(1)}, bf16[272,512]{1,0:T(8,128)(2,1)S(1)}, u32[]{:S(2)}, u32[]{:S(2)}) collective-permute-start(bf16[272,512]{1,0:T(8,128)(2,1)S(1)} %pad_maximum_fusion.6.refs_1_), channel_id=1, source_target_pairs={{0,48},{1,49},{2,50},{3,51},{64,112},{65,113},{66,114},{67,115},{1... | collective-permute-start | bytes 835592 | tf_op jit(solution)/shard_map/ppermute | solution.py:43
  5.5 10.2 %collective-permute-start.2 = (bf16[272,512]{1,0:T(8,128)(2,1)S(1)}, bf16[272,512]{1,0:T(8,128)(2,1)S(1)}, u32[]{:S(2)}, u32[]{:S(2)}) collective-permute-start(bf16[272,512]{1,0:T(8,128)(2,1)S(1)} %pad_maximum_fusion.6.refs_1_), channel_id=1, source_target_pairs={{0,64},{1,65},{2,66},{3,67},{64,0},{65,1},{66,2},{67,3},{16,80},{1... | collective-permute-start | bytes 835592 | tf_op jit(solution)/shard_map/ppermute | solution.py:43
  9.4 9.0 %collective-permute-start = (bf16[272,512]{1,0:T(8,128)(2,1)S(1)}, bf16[272,512]{1,0:T(8,128)(2,1)S(1)}, u32[]{:S(2)}, u32[]{:S(2)}) collective-permute-start(bf16[272,512]{1,0:T(8,128)(2,1)S(1)} %pad_maximum_fusion.6.refs_1_), channel_id=1, source_target_pairs={{0,16},{1,17},{2,18},{3,19},{64,80},{65,81},{66,82},{67,83},{16,32... | collective-permute-start | bytes 835592 | tf_op jit(solution)/shard_map/ppermute | solution.py:43
  15.8 13.7 %collective-permute-start.4 = (bf16[416,512]{1,0:T(8,128)(2,1)S(1)}, bf16[416,512]{1,0:T(8,128)(2,1)S(1)}, u32[]{:S(2)}, u32[]{:S(2)}) collective-permute-start(bf16[416,512]{1,0:T(8,128)(2,1)S(1)} %pad_maximum_fusion.4), channel_id=1, source_target_pairs={{0,48},{1,49},{2,50},{3,51},{64,112},{65,113},{66,114},{67,115},{1... | collective-permute-start | bytes 1277960 | tf_op jit(solution)/shard_map/ppermute | solution.py:43
  18.5 11.0 %collective-permute-start.3 = (bf16[400,512]{1,0:T(8,128)(2,1)S(1)}, bf16[400,512]{1,0:T(8,128)(2,1)S(1)}, u32[]{:S(2)}, u32[]{:S(2)}) collective-permute-start(bf16[400,512]{1,0:T(8,128)(2,1)S(1)} %pad_maximum_fusion.5), channel_id=1, source_target_pairs={{0,16},{1,17},{2,18},{3,19},{64,80},{65,81},{66,82},{67,83},{16,32... | collective-permute-start | bytes 1228808 | tf_op jit(solution)/shard_map/ppermute | solution.py:43
  18.6 8.1 %collective-permute-start.5 = (bf16[256,512]{1,0:T(8,128)(2,1)S(1)}, bf16[256,512]{1,0:T(8,128)(2,1)S(1)}, u32[]{:S(2)}, u32[]{:S(2)}) collective-permute-start(bf16[256,512]{1,0:T(8,128)(2,1)S(1)} %copy-done.51), channel_id=1, source_target_pairs={{0,64},{1,65},{2,66},{3,67},{64,0},{65,1},{66,2},{67,3},{16,80},{1... | collective-permute-start | bytes 786440 | tf_op jit(solution)/shard_map/ppermute | solution.py:43
  29.5 14.1 %collective-permute-start.8 = (bf16[512,512]{1,0:T(8,128)(2,1)S(1)}, bf16[512,512]{1,0:T(8,128)(2,1)S(1)}, u32[]{:S(2)}, u32[]{:S(2)}) collective-permute-start(bf16[512,512]{1,0:T(8,128)(2,1)S(1)} %pad_maximum_fusion.3.refs_1_), channel_id=1, source_target_pairs={{0,48},{1,49},{2,50},{3,51},{64,112},{65,113},{66,114},{67,115},{1... | collective-permute-start | bytes 1572872 | tf_op jit(solution)/shard_map/ppermute | solution.py:43
  30.5 8.4 %collective-permute-start.6 = (bf16[272,512]{1,0:T(8,128)(2,1)}, bf16[272,512]{1,0:T(8,128)(2,1)}, u32[]{:S(2)}, u32[]{:S(2)}) collective-permute-start(bf16[272,512]{1,0:T(8,128)(2,1)} %pad_maximum_fusion.7), channel_id=1, source_target_pairs={{0,64},{1,65},{2,66},{3,67},{64,0},{65,1},{66,2},{67,3},{16,80},{1... | collective-permute-start | bytes 835592 | tf_op jit(solution)/shard_map/ppermute | solution.py:43
  32.2 12.2 %collective-permute-start.7 = (bf16[512,512]{1,0:T(8,128)(2,1)S(1)}, bf16[512,512]{1,0:T(8,128)(2,1)S(1)}, u32[]{:S(2)}, u32[]{:S(2)}) collective-permute-start(bf16[512,512]{1,0:T(8,128)(2,1)S(1)} %pad_maximum_fusion.3.refs_1_), channel_id=1, source_target_pairs={{0,16},{1,17},{2,18},{3,19},{64,80},{65,81},{66,82},{67,83},{16,32... | collective-permute-start | bytes 1572872 | tf_op jit(solution)/shard_map/ppermute | solution.py:43
  41.8 11.0 %collective-permute-start.9 = (bf16[256,1024]{1,0:T(8,128)(2,1)S(1)}, bf16[256,1024]{1,0:T(8,128)(2,1)S(1)}, u32[]{:S(2)}, u32[]{:S(2)}) collective-permute-start(bf16[256,1024]{1,0:T(8,128)(2,1)S(1)} %get-tuple-element.102), channel_id=1, source_target_pairs={{0,66},{1,67},{2,64},{3,65},{64,2},{65,3},{66,0},{67,1},{16,82},{1... | collective-permute-start | bytes 1572872 | tf_op jit(solution)/shard_map/ppermute | solution.py:43
  43.6 10.0 %collective-permute-start.10 = (bf16[256,1024]{1,0:T(8,128)(2,1)S(1)}, bf16[256,1024]{1,0:T(8,128)(2,1)S(1)}, u32[]{:S(2)}, u32[]{:S(2)}) collective-permute-start(bf16[256,1024]{1,0:T(8,128)(2,1)S(1)} %get-tuple-element.103), channel_id=1, source_target_pairs={{0,2},{1,3},{2,0},{3,1},{64,66},{65,67},{66,64},{67,65},{16,18},{1... | collective-permute-start | bytes 1572872 | tf_op jit(solution)/shard_map/ppermute | solution.py:43
  43.7 10.0 %collective-permute-start.12 = (bf16[256,512]{1,0:T(8,128)(2,1)S(1)}, bf16[256,512]{1,0:T(8,128)(2,1)S(1)}, u32[]{:S(2)}, u32[]{:S(2)}) collective-permute-start(bf16[256,512]{1,0:T(8,128)(2,1)S(1)} %pad_maximum_fusion.9), channel_id=1, source_target_pairs={{0,48},{1,49},{2,50},{3,51},{64,112},{65,113},{66,114},{67,115},{1... | collective-permute-start | bytes 786440 | tf_op jit(solution)/shard_map/ppermute | solution.py:43
  44.4 9.2 %collective-permute-start.11 = (bf16[256,512]{1,0:T(8,128)(2,1)S(1)}, bf16[256,512]{1,0:T(8,128)(2,1)S(1)}, u32[]{:S(2)}, u32[]{:S(2)}) collective-permute-start(bf16[256,512]{1,0:T(8,128)(2,1)S(1)} %pad_maximum_fusion.8), channel_id=1, source_target_pairs={{0,16},{1,17},{2,18},{3,19},{64,80},{65,81},{66,82},{67,83},{16,32... | collective-permute-start | bytes 786440 | tf_op jit(solution)/shard_map/ppermute | solution.py:43
  62.3 8.7 %collective-permute-start.17 = (bf16[256,3584]{1,0:T(8,128)(2,1)}, bf16[256,3584]{1,0:T(8,128)(2,1)}, u32[]{:S(2)}, u32[]{:S(2)}) collective-permute-start(bf16[256,3584]{1,0:T(8,128)(2,1)} %get-tuple-element.121), channel_id=1, source_target_pairs={{0,1},{1,0},{2,3},{3,2},{64,65},{65,64},{66,67},{67,66},{16,17},{1... | collective-permute-start | bytes 5505032 | tf_op jit(solution)/shard_map/ppermute | solution.py:43
  62.3 8.7 %collective-permute-start.15 = (bf16[256,1792]{1,0:T(8,128)(2,1)}, bf16[256,1792]{1,0:T(8,128)(2,1)}, u32[]{:S(2)}, u32[]{:S(2)}) collective-permute-start(bf16[256,1792]{1,0:T(8,128)(2,1)} %get-tuple-element.118), channel_id=1, source_target_pairs={{0,1},{1,0},{2,3},{3,2},{64,65},{65,64},{66,67},{67,66},{16,17},{1... | collective-permute-start | bytes 2752520 | tf_op jit(solution)/shard_map/ppermute | solution.py:43
  62.9 30.4 %collective-permute-start.16 = (bf16[256,1536]{1,0:T(8,128)(2,1)S(1)}, bf16[256,1536]{1,0:T(8,128)(2,1)S(1)}, u32[]{:S(2)}, u32[]{:S(2)}) collective-permute-start(bf16[256,1536]{1,0:T(8,128)(2,1)S(1)} %get-tuple-element.123.refs_1_.refs_5_), channel_id=1, source_target_pairs={{0,2},{1,3},{2,0},{3,1},{64,66},{65,67},{66,64},{67,65},{16,18},{1... | collective-permute-start | bytes 2359304 | tf_op jit(solution)/shard_map/ppermute | solution.py:43
  64.4 6.6 %copy-start.16 = (bf16[256,2048]{1,0:T(8,128)(2,1)S(1)}, bf16[256,2048]{1,0:T(8,128)(2,1)}, u32[]{:S(2)}) copy-start(bf16[256,2048]{1,0:T(8,128)(2,1)} %copy-done.15) | copy-start | bytes 3145732
  75.8 11.9 %copy-start.2 = (bf16[512,384]{1,0:T(8,128)(2,1)}, bf16[512,384]{1,0:T(8,128)(2,1)S(1)}, u32[]{:S(2)}) copy-start(bf16[512,384]{1,0:T(8,128)(2,1)S(1)} %get-tuple-element.183) | copy-start | bytes 1179652
  75.8 11.9 %copy-start.4 = (bf16[512,384]{1,0:T(8,128)(2,1)}, bf16[512,384]{1,0:T(8,128)(2,1)S(1)}, u32[]{:S(2)}) copy-start(bf16[512,384]{1,0:T(8,128)(2,1)S(1)} %get-tuple-element.184) | copy-start | bytes 1179652
  75.8 20.5 %collective-permute-start.19 = (bf16[1024,384]{1,0:T(8,128)(2,1)S(1)}, bf16[1024,384]{1,0:T(8,128)(2,1)S(1)}, u32[]{:S(2)}, u32[]{:S(2)}) collective-permute-start(bf16[1024,384]{1,0:T(8,128)(2,1)S(1)} %get-tuple-element.132), channel_id=1, source_target_pairs={{0,12},{1,13},{2,14},{3,15},{64,76},{65,77},{66,78},{67,79},{16,28... | collective-permute-start | bytes 2359304 | tf_op jit(solution)/shard_map/ppermute | solution.py:43
  78.6 18.9 %collective-permute-start.18 = (bf16[1024,384]{1,0:T(8,128)(2,1)S(1)}, bf16[1024,384]{1,0:T(8,128)(2,1)S(1)}, u32[]{:S(2)}, u32[]{:S(2)}) collective-permute-start(bf16[1024,384]{1,0:T(8,128)(2,1)S(1)} %get-tuple-element.122), channel_id=1, source_target_pairs={{0,4},{1,5},{2,6},{3,7},{64,68},{65,69},{66,70},{67,71},{16,20},{1... | collective-permute-start | bytes 2359304 | tf_op jit(solution)/shard_map/ppermute | solution.py:43
  78.9 14.3 %collective-permute-start.13 = (bf16[512,512]{1,0:T(8,128)(2,1)S(1)}, bf16[512,512]{1,0:T(8,128)(2,1)S(1)}, u32[]{:S(2)}, u32[]{:S(2)}) collective-permute-start(bf16[512,512]{1,0:T(8,128)(2,1)S(1)} %get-tuple-element.113), channel_id=1, source_target_pairs={{0,48},{1,49},{2,50},{3,51},{64,112},{65,113},{66,114},{67,115},{1... | collective-permute-start | bytes 1572872 | tf_op jit(solution)/shard_map/ppermute | solution.py:43
  80.5 12.8 %collective-permute-start.14 = (bf16[512,512]{1,0:T(8,128)(2,1)S(1)}, bf16[512,512]{1,0:T(8,128)(2,1)S(1)}, u32[]{:S(2)}, u32[]{:S(2)}) collective-permute-start(bf16[512,512]{1,0:T(8,128)(2,1)S(1)} %get-tuple-element.116), channel_id=1, source_target_pairs={{0,16},{1,17},{2,18},{3,19},{64,80},{65,81},{66,82},{67,83},{16,0}... | collective-permute-start | bytes 1572872 | tf_op jit(solution)/shard_map/ppermute | solution.py:43
  80.5 17.0 %copy-start.46 = (bf16[256,1024]{1,0:T(8,128)(2,1)S(1)}, bf16[256,1024]{1,0:T(8,128)(2,1)}, u32[]{:S(2)}) copy-start(bf16[256,1024]{1,0:T(8,128)(2,1)} %copy-done.45) | copy-start | bytes 1572868
  88.4 9.2 %copy-start.6 = (bf16[256,640]{1,0:T(8,128)(2,1)}, bf16[256,640]{1,0:T(8,128)(2,1)S(1)}, u32[]{:S(2)}) copy-start(bf16[256,640]{1,0:T(8,128)(2,1)S(1)} %get-tuple-element.163) | copy-start | bytes 983044
  97.7 4.5 %collective-permute-start.20 = (bf16[256,2560]{1,0:T(8,128)(2,1)S(1)}, bf16[256,2560]{1,0:T(8,128)(2,1)S(1)}, u32[]{:S(2)}, u32[]{:S(2)}) collective-permute-start(bf16[256,2560]{1,0:T(8,128)(2,1)S(1)} %pad_maximum_fusion), channel_id=1, source_target_pairs={{0,1},{1,0},{2,3},{3,2},{64,65},{65,64},{66,67},{67,66},{16,17},{1... | collective-permute-start | bytes 3932168 | tf_op jit(solution)/shard_map/ppermute | solution.py:43
  97.7 19.6 %collective-permute-start.23 = (bf16[512,640]{1,0:T(8,128)(2,1)S(1)}, bf16[512,640]{1,0:T(8,128)(2,1)S(1)}, u32[]{:S(2)}, u32[]{:S(2)}) collective-permute-start(bf16[512,640]{1,0:T(8,128)(2,1)S(1)} %get-tuple-element.131), channel_id=1, source_target_pairs={{0,16},{1,17},{2,18},{3,19},{64,80},{65,81},{66,82},{67,83},{16,0}... | collective-permute-start | bytes 1966088 | tf_op jit(solution)/shard_map/ppermute | solution.py:43
  99.4 18.0 %collective-permute-start.24 = (bf16[512,640]{1,0:T(8,128)(2,1)S(1)}, bf16[512,640]{1,0:T(8,128)(2,1)S(1)}, u32[]{:S(2)}, u32[]{:S(2)}) collective-permute-start(bf16[512,640]{1,0:T(8,128)(2,1)S(1)} %get-tuple-element.151), channel_id=1, source_target_pairs={{0,48},{1,49},{2,50},{3,51},{64,112},{65,113},{66,114},{67,115},{1... | collective-permute-start | bytes 1966088 | tf_op jit(solution)/shard_map/ppermute | solution.py:43
  100.1 11.0 %collective-permute-start.22 = (bf16[512,384]{1,0:T(8,128)(2,1)S(1)}, bf16[512,384]{1,0:T(8,128)(2,1)S(1)}, u32[]{:S(2)}, u32[]{:S(2)}) collective-permute-start(bf16[512,384]{1,0:T(8,128)(2,1)S(1)} %add_convert_fusion.3), channel_id=1, source_target_pairs={{0,4},{1,5},{2,6},{3,7},{64,68},{65,69},{66,70},{67,71},{16,20},{1... | collective-permute-start | bytes 1179656 | tf_op jit(solution)/shard_map/ppermute | solution.py:43
  100.6 12.1 %collective-permute-start.21 = (bf16[512,384]{1,0:T(8,128)(2,1)S(1)}, bf16[512,384]{1,0:T(8,128)(2,1)S(1)}, u32[]{:S(2)}, u32[]{:S(2)}) collective-permute-start(bf16[512,384]{1,0:T(8,128)(2,1)S(1)} %add_convert_fusion.4), channel_id=1, source_target_pairs={{0,12},{1,13},{2,14},{3,15},{64,76},{65,77},{66,78},{67,79},{16,28... | collective-permute-start | bytes 1179656 | tf_op jit(solution)/shard_map/ppermute | solution.py:43
  109.0 10.1 %copy-start.17 = (bf16[512,768]{1,0:T(8,128)(2,1)}, bf16[512,768]{1,0:T(8,128)(2,1)S(1)}, u32[]{:S(2)}) copy-start(bf16[512,768]{1,0:T(8,128)(2,1)S(1)} %get-tuple-element.148) | copy-start | bytes 2359300
  109.0 10.1 %copy-start.18 = (bf16[512,768]{1,0:T(8,128)(2,1)}, bf16[512,768]{1,0:T(8,128)(2,1)S(1)}, u32[]{:S(2)}) copy-start(bf16[512,768]{1,0:T(8,128)(2,1)S(1)} %get-tuple-element.166) | copy-start | bytes 2359300
  109.0 11.2 %copy-start.52 = (bf16[512]{0:T(512)(128)(2,1)S(1)}, bf16[512]{0:T(512)(128)(2,1)}, u32[]{:S(2)}) copy-start(bf16[512]{0:T(512)(128)(2,1)} %param.5) | copy-start | bytes 3076
  109.0 20.7 %copy-start.13 = (bf16[256,512]{1,0:T(8,128)(2,1)S(1)}, bf16[256,512]{1,0:T(8,128)(2,1)}, u32[]{:S(2)}) copy-start(bf16[256,512]{1,0:T(8,128)(2,1)} %copy-done.12) | copy-start | bytes 786436
  111.1 8.0 %copy-start.47 = (bf16[512,384]{1,0:T(8,128)(2,1)}, bf16[512,384]{1,0:T(8,128)(2,1)S(1)}, u32[]{:S(2)}) copy-start(bf16[512,384]{1,0:T(8,128)(2,1)S(1)} %collective-permute-done.22) | copy-start | bytes 1179652
  112.8 6.4 %copy-start.49 = (bf16[512,384]{1,0:T(8,128)(2,1)}, bf16[512,384]{1,0:T(8,128)(2,1)S(1)}, u32[]{:S(2)}) copy-start(bf16[512,384]{1,0:T(8,128)(2,1)S(1)} %collective-permute-done.21) | copy-start | bytes 1179652
  112.8 18.7 %copy-start.11 = (bf16[256,512]{1,0:T(8,128)(2,1)S(1)}, bf16[256,512]{1,0:T(8,128)(2,1)}, u32[]{:S(2)}) copy-start(bf16[256,512]{1,0:T(8,128)(2,1)} %copy-done.10) | copy-start | bytes 786436
  118.3 14.5 %copy-start.7 = (bf16[256,640]{1,0:T(8,128)(2,1)S(1)}, bf16[256,640]{1,0:T(8,128)(2,1)}, u32[]{:S(2)}) copy-start(bf16[256,640]{1,0:T(8,128)(2,1)} %copy-done.6) | copy-start | bytes 983044
  118.3 14.5 %copy-start.9 = (bf16[256,640]{1,0:T(8,128)(2,1)S(1)}, bf16[256,640]{1,0:T(8,128)(2,1)}, u32[]{:S(2)}) copy-start(bf16[256,640]{1,0:T(8,128)(2,1)} %copy-done.8) | copy-start | bytes 983044
  118.3 9.1 %collective-permute-start.26 = (bf16[256,640]{1,0:T(8,128)(2,1)}, bf16[256,640]{1,0:T(8,128)(2,1)S(1)}, u32[]{:S(2)}, u32[]{:S(2)}) collective-permute-start(bf16[256,640]{1,0:T(8,128)(2,1)} %add_convert_fusion.5), channel_id=1, source_target_pairs={{0,16},{1,17},{2,18},{3,19},{64,80},{65,81},{66,82},{67,83},{16,0}... | collective-permute-start | bytes 983048 | tf_op jit(solution)/shard_map/ppermute | solution.py:43
  119.1 10.5 %collective-permute-start.25 = (bf16[256,640]{1,0:T(8,128)(2,1)}, bf16[256,640]{1,0:T(8,128)(2,1)}, u32[]{:S(2)}, u32[]{:S(2)}) collective-permute-start(bf16[256,640]{1,0:T(8,128)(2,1)} %add_convert_fusion.6), channel_id=1, source_target_pairs={{0,48},{1,49},{2,50},{3,51},{64,112},{65,113},{66,114},{67,115},{1... | collective-permute-start | bytes 983048 | tf_op jit(solution)/shard_map/ppermute | solution.py:43
  120.2 12.6 %copy-start.42 = (bf16[512,640]{1,0:T(8,128)(2,1)S(1)}, bf16[512,640]{1,0:T(8,128)(2,1)}, u32[]{:S(2)}) copy-start(bf16[512,640]{1,0:T(8,128)(2,1)} %copy-done.41) | copy-start | bytes 1966084
  120.2 12.6 %copy-start.44 = (bf16[512,640]{1,0:T(8,128)(2,1)S(1)}, bf16[512,640]{1,0:T(8,128)(2,1)}, u32[]{:S(2)}) copy-start(bf16[512,640]{1,0:T(8,128)(2,1)} %copy-done.43) | copy-start | bytes 1966084
  120.2 25.1 %collective-permute-start.31 = (bf16[512,768]{1,0:T(8,128)(2,1)}, bf16[512,768]{1,0:T(8,128)(2,1)S(1)}, u32[]{:S(2)}, u32[]{:S(2)}) collective-permute-start(bf16[512,768]{1,0:T(8,128)(2,1)} %copy-done.17), channel_id=1, source_target_pairs={{0,4},{1,5},{2,6},{3,7},{64,68},{65,69},{66,70},{67,71},{16,20},{1... | collective-permute-start | bytes 2359304 | tf_op jit(solution)/shard_map/ppermute | solution.py:43
  120.6 24.8 %collective-permute-start.32 = (bf16[512,768]{1,0:T(8,128)(2,1)}, bf16[512,768]{1,0:T(8,128)(2,1)S(1)}, u32[]{:S(2)}, u32[]{:S(2)}) collective-permute-start(bf16[512,768]{1,0:T(8,128)(2,1)} %copy-done.18), channel_id=1, source_target_pairs={{0,12},{1,13},{2,14},{3,15},{64,76},{65,77},{66,78},{67,79},{16,28... | collective-permute-start | bytes 2359304 | tf_op jit(solution)/shard_map/ppermute | solution.py:43
  130.7 7.9 %collective-permute-start.28 = (bf16[256,512]{1,0:T(8,128)(2,1)S(1)}, bf16[256,512]{1,0:T(8,128)(2,1)S(1)}, u32[]{:S(2)}, u32[]{:S(2)}) collective-permute-start(bf16[256,512]{1,0:T(8,128)(2,1)S(1)} %add_convert_fusion.8), channel_id=1, source_target_pairs={{0,48},{1,49},{2,50},{3,51},{64,112},{65,113},{66,114},{67,115},{1... | collective-permute-start | bytes 786440 | tf_op jit(solution)/shard_map/ppermute | solution.py:43
  132.6 6.5 %collective-permute-start.27 = (bf16[256,512]{1,0:T(8,128)(2,1)S(1)}, bf16[256,512]{1,0:T(8,128)(2,1)S(1)}, u32[]{:S(2)}, u32[]{:S(2)}) collective-permute-start(bf16[256,512]{1,0:T(8,128)(2,1)S(1)} %add_convert_fusion.9), channel_id=1, source_target_pairs={{0,16},{1,17},{2,18},{3,19},{64,80},{65,81},{66,82},{67,83},{16,0}... | collective-permute-start | bytes 786440 | tf_op jit(solution)/shard_map/ppermute | solution.py:43
  134.2 4.8 %copy-start.26 = (bf16[512,512]{1,0:T(8,128)(2,1)S(1)}, bf16[512,512]{1,0:T(8,128)(2,1)}, u32[]{:S(2)}) copy-start(bf16[512,512]{1,0:T(8,128)(2,1)} %copy-done.25) | copy-start | bytes 1572868
  134.2 4.8 %copy-start.28 = (bf16[512,512]{1,0:T(8,128)(2,1)S(1)}, bf16[512,512]{1,0:T(8,128)(2,1)}, u32[]{:S(2)}) copy-start(bf16[512,512]{1,0:T(8,128)(2,1)} %copy-done.27) | copy-start | bytes 1572868
  134.2 9.0 %collective-permute-start.29 = (bf16[256,640]{1,0:T(8,128)(2,1)S(1)}, bf16[256,640]{1,0:T(8,128)(2,1)S(1)}, u32[]{:S(2)}, u32[]{:S(2)}) collective-permute-start(bf16[256,640]{1,0:T(8,128)(2,1)S(1)} %get-tuple-element.187), channel_id=1, source_target_pairs={{0,64},{1,65},{2,66},{3,67},{64,0},{65,1},{66,2},{67,3},{16,80},{1... | collective-permute-start | bytes 983048 | tf_op jit(solution)/shard_map/ppermute | solution.py:43
  136.5 13.4 %copy-start.23 = (f32[512,384]{1,0:T(8,128)}, f32[512,384]{1,0:T(8,128)S(1)}, u32[]{:S(2)}) copy-start(f32[512,384]{1,0:T(8,128)S(1)} %get-tuple-element.197) | copy-start | bytes 2359300
  138.6 6.8 %copy-start.30 = (bf16[256,512]{1,0:T(8,128)(2,1)}, bf16[256,512]{1,0:T(8,128)(2,1)S(1)}, u32[]{:S(2)}) copy-start(bf16[256,512]{1,0:T(8,128)(2,1)S(1)} %collective-permute-done.28) | copy-start | bytes 786436
  139.1 6.4 %copy-start.32 = (bf16[256,512]{1,0:T(8,128)(2,1)}, bf16[256,512]{1,0:T(8,128)(2,1)S(1)}, u32[]{:S(2)}) copy-start(bf16[256,512]{1,0:T(8,128)(2,1)S(1)} %collective-permute-done.27) | copy-start | bytes 786436
  143.2 22.9 %collective-permute-start.30 = (bf16[256,512]{1,0:T(8,128)(2,1)}, bf16[256,512]{1,0:T(8,128)(2,1)}, u32[]{:S(2)}, u32[]{:S(2)}) collective-permute-start(bf16[256,512]{1,0:T(8,128)(2,1)} %select_convert_fusion.2), channel_id=1, source_target_pairs={{0,64},{1,65},{2,66},{3,67},{64,0},{65,1},{66,2},{67,3},{16,80},{1... | collective-permute-start | bytes 786440 | tf_op jit(solution)/shard_map/ppermute | solution.py:43
  146.4 21.8 %collective-permute-start.37 = (bf16[256,768]{1,0:T(8,128)(2,1)}, bf16[256,768]{1,0:T(8,128)(2,1)}, u32[]{:S(2)}, u32[]{:S(2)}) collective-permute-start(bf16[256,768]{1,0:T(8,128)(2,1)} %add_convert_fusion.1), channel_id=1, source_target_pairs={{0,4},{1,5},{2,6},{3,7},{64,68},{65,69},{66,70},{67,71},{16,20},{1... | collective-permute-start | bytes 1179656 | tf_op jit(solution)/shard_map/ppermute | solution.py:43
  147.6 18.6 %copy-start.31 = (bf16[256,512]{1,0:T(8,128)(2,1)S(1)}, bf16[256,512]{1,0:T(8,128)(2,1)}, u32[]{:S(2)}) copy-start(bf16[256,512]{1,0:T(8,128)(2,1)} %copy-done.30) | copy-start | bytes 786436
  147.6 20.7 %collective-permute-start.36 = (bf16[256,768]{1,0:T(8,128)(2,1)}, bf16[256,768]{1,0:T(8,128)(2,1)}, u32[]{:S(2)}, u32[]{:S(2)}) collective-permute-start(bf16[256,768]{1,0:T(8,128)(2,1)} %add_convert_fusion.2), channel_id=1, source_target_pairs={{0,12},{1,13},{2,14},{3,15},{64,76},{65,77},{66,78},{67,79},{16,28... | collective-permute-start | bytes 1179656 | tf_op jit(solution)/shard_map/ppermute | solution.py:43
  149.8 1.4 collective-permute-start.33
  150.7 20.0 %copy-start.24 = (f32[512,384]{1,0:T(8,128)S(1)}, f32[512,384]{1,0:T(8,128)}, u32[]{:S(2)}) copy-start(f32[512,384]{1,0:T(8,128)} %copy-done.23) | copy-start | bytes 2359300
  150.7 20.0 %collective-permute-start.39 = (bf16[256,768]{1,0:T(8,128)(2,1)}, bf16[256,768]{1,0:T(8,128)(2,1)}, u32[]{:S(2)}, u32[]{:S(2)}) collective-permute-start(bf16[256,768]{1,0:T(8,128)(2,1)} %select_convert_fusion), channel_id=1, source_target_pairs={{0,2},{1,3},{2,0},{3,1},{64,66},{65,67},{66,64},{67,65},{16,18},{1... | collective-permute-start | bytes 1179656 | tf_op jit(solution)/shard_map/ppermute | solution.py:43
  151.3 11.3 %collective-permute-start.34 = (f32[1,512]{1,0:T(1,128)S(1)}, f32[1,512]{1,0:T(1,128)S(1)}, u32[]{:S(2)}, u32[]{:S(2)}) collective-permute-start(f32[1,512]{1,0:T(1,128)S(1)} %add.218), channel_id=1, source_target_pairs={{0,2},{1,3},{2,0},{3,1},{64,66},{65,67},{66,64},{67,65},{16,18},{1... | collective-permute-start | bytes 6152 | tf_op jit(solution)/shard_map/ppermute | solution.py:43
  162.6 3.6 %collective-permute-start.35 = (f32[1,512]{1,0:T(1,128)S(1)}, f32[1,512]{1,0:T(1,128)S(1)}, u32[]{:S(2)}, u32[]{:S(2)}) collective-permute-start(f32[1,512]{1,0:T(1,128)S(1)} %add.219), channel_id=1, source_target_pairs={{0,4},{1,5},{2,6},{3,7},{64,68},{65,69},{66,70},{67,71},{16,20},{1... | collective-permute-start | bytes 6152 | tf_op jit(solution)/shard_map/ppermute | solution.py:43
  168.2 6.2 %collective-permute-start.38 = (f32[1,512]{1,0:T(1,128)S(1)}, f32[1,512]{1,0:T(1,128)S(1)}, u32[]{:S(2)}, u32[]{:S(2)}) collective-permute-start(f32[1,512]{1,0:T(1,128)S(1)} %add.220), channel_id=1, source_target_pairs={{0,8},{1,9},{2,10},{3,11},{64,72},{65,73},{66,74},{67,75},{16,24},... | collective-permute-start | bytes 6152 | tf_op jit(solution)/shard_map/ppermute | solution.py:43
  (29 other events, 72.2 us)

commit v8 on v5

--- a/solution.py
+++ b/solution.py
@@ -322,15 +322,13 @@
     cot_pieces = (after(cot_pieces[0], x_same, x_cross), *cot_pieces[1:])
     d_pair, products, cot_mine, core_two = backward(spot, cot_pieces, w3, gate, up_val, inv)
     core_two = send(core_two, "c")
-    branch_terms = branch_rows(order(y), after(hidden, d_pair), w3)
+    d_terms = pair_rows(order(y), d_pair, products, w3)
     pair_z = send(d_pair, "z^1")
-    down_terms = outer("down_terms", order(x), [(after(cot_mine, branch_terms[0]), 0), (core_two, 0)], [(hidden, 0), (core_one, 1024)], 512, 384)
-    branch_got = [send(value, move) for value, move in zip(branch_terms[0:2], ("y^1", "y^3"))]
-    d_terms = pair_rows(order(y), after(d_pair, down_terms[0]), products, w3)
+    down_terms = outer("down_terms", order(x), [(after(cot_mine, d_terms[0]), 0), (core_two, 0)], [(hidden, 0), (core_one, 1024)], 512, 384)
+    branch_terms = branch_rows(order(y), after(hidden, down_terms[0]), w3)
     down_got, _, down_last = halve(down_terms, "x")
-    d_terms = lax.optimization_barrier((*d_terms, *branch_got))[:6]
-    d_got = [send(value, move) for value, move in zip(d_terms[0:2], ("y^1", "y^3"))]
-    core_three = send(jnp.concatenate([x_cross, after(pair_z, d_terms[0], *down_got)], axis=1), "c")
+    d_got, _, d_last = halve(d_terms, "y", down_got)
+    core_three = send(jnp.concatenate([x_cross, after(pair_z, branch_terms[0], *down_got, *d_got)], axis=1), "c")
     pair_terms = outer(
         "pair_terms", order(x), [(x_keep, 0), (x_same, 0), (core_one, 0), (core_three, 0)],
         [(d_pair, 0), (pair_z, 0), (core_two, 2048), (core_three, 1024)], 256, 768,
@@ -345,13 +343,14 @@
     theirs = jnp.where(lower, d_w_down[256:], d_w_down[:256]).astype(bf16)
     d_w_down = jnp.where(lower, d_w_down[:256], d_w_down[256:]) + send(theirs, "z^1").astype(f32)
 
-    _, d_last = second_step(d_terms, d_got, "y", (pair_terms[0],))
+    d_last = lax.optimization_barrier((*d_last, pair_terms[0]))[:2]
     d_low, d_high = finish(d_terms, d_got, d_last)
-    _, branch_last = second_step(branch_terms, branch_got, "y", (pair_terms[0], *d_last))
-    low, high = finish(branch_terms, branch_got, branch_last)
     upper = z_hi == 1
     mine = jnp.where(upper, d_high, d_low)
     theirs = send(jnp.where(upper, d_low, d_high).astype(bf16), "z+2")
+    branch_terms = lax.optimization_barrier((*branch_terms, theirs))[:6]
+    branch_got, _, branch_last = halve(branch_terms, "y")
+    low, high = finish(branch_terms, branch_got, branch_last)
     mine = mine + theirs.astype(f32)
     theirs = send(after(jnp.where(upper, low, high).astype(bf16), theirs), "z+2")
     branch = (jnp.where(upper, high, low) + theirs.astype(f32)).astype(bf16)
@@ -362,7 +361,7 @@
     d_gain = jnp.sum(d_normed * x_own, axis=0, keepdims=True)
     for move in ("c", "z^1", "x^1", "x+2"):
         if move == "x^1":
-            d_gain = after(d_gain, *pair_out)
+            d_gain = after(d_gain, *pair_last)
         d_gain = d_gain + send(d_gain, move)
 
     gain_rows = lax.dynamic_slice(gains, (0, s * 256), (1, 256)).astype(f32).reshape(256, 1)

time: 171 us -> 178 us (1.041)
  local copies, waits for them, and re-layouts: 6.48 us -> 15 us
  waiting for transfers between devices: 68.3 us -> 63.1 us
  other arithmetic: 13.7 us -> 17.1 us
    unnamed x72 -> x94, local copies, waits for them, and re-layouts: 5.46 us -> 14 us
    ppermute x40, waiting for transfers between devices: 68.3 us -> 63.1 us  [send(): return lax.ppermute(value, AXES, pairs(moves[move]))]
  transfers between devices with their start and end apart: 40 -> 40, of which waited for: 21 -> 22; matrix products, arithmetic and copies ran while one was open for 6% -> 7% of each run, Pallas kernels for 18% -> 18%
where the time goes in v8:
time: 178 us; the launch traced here: 177 us
  waiting for transfers between devices  63.1 us (35%)
  starting transfers between devices  42.4 us (24%)
  Pallas kernels  38.6 us (22%)
  other arithmetic  17.1 us (10%)
  local copies, waits for them, and re-layouts  15 us (8%)
    ppermute x40, waiting for transfers between devices, send(): return lax.ppermute(value, AXES, pairs(moves[move]))  63.1 us
    ppermute x40, starting transfers between devices, send(): return lax.ppermute(value, AXES, pairs(moves[move]))  42.4 us
    pallas_call x7, Pallas kernels, call(): pl.pallas_call(whole, in_specs=[pl.BlockSpec(memory_space=space) for spac...  38.6 us
    unnamed x94, local copies, waits for them, and re-layouts  14 us
    convert_element_type x8, other arithmetic, second_step(): (t.astype(f32) + g[rows:].astype(f32)).astype(bf16)  3.71 us
  transfers between devices with their start and end apart: 40, of which 22 were waited for; matrix products, arithmetic and copies ran while one was open for 7% of the time, Pallas kernels for 18%

profile of v8, /device:TPU:0, one launch (start us, length us, event | category | flops | bytes accessed | tf_op | source)
XLA Modules:
  0.0 177.3 jit_solution(3706845476232615988)
XLA Ops:
  1.3 1.0 pad_maximum_fusion.6.refs_1_
  2.3 3.2 %collective-permute-start.1 = (bf16[272,512]{1,0:T(8,128)(2,1)S(1)}, bf16[272,512]{1,0:T(8,128)(2,1)S(1)}, u32[]{:S(2)}, u32[]{:S(2)}) collective-permute-start(bf16[272,512]{1,0:T(8,128)(2,1)S(1)} %pad_maximum_fusion.6.refs_1_), channel_id=1, source_target_pairs={{0,48},{1,49},{2,50},{3,51},{64,112},{65,113},{66,114},{67,115},{1... | collective-permute-start | bytes 835592 | tf_op jit(solution)/shard_map/ppermute | solution.py:43
  5.5 3.9 %collective-permute-start.2 = (bf16[272,512]{1,0:T(8,128)(2,1)S(1)}, bf16[272,512]{1,0:T(8,128)(2,1)S(1)}, u32[]{:S(2)}, u32[]{:S(2)}) collective-permute-start(bf16[272,512]{1,0:T(8,128)(2,1)S(1)} %pad_maximum_fusion.6.refs_1_), channel_id=1, source_target_pairs={{0,64},{1,65},{2,66},{3,67},{64,0},{65,1},{66,2},{67,3},{16,80},{1... | collective-permute-start | bytes 835592 | tf_op jit(solution)/shard_map/ppermute | solution.py:43
  9.4 2.0 %collective-permute-done.1.refs_3_ = bf16[272,512]{1,0:T(8,128)(2,1)S(1)} collective-permute-done((bf16[272,512]{1,0:T(8,128)(2,1)S(1)}, bf16[272,512]{1,0:T(8,128)(2,1)S(1)}, u32[]{:S(2)}, u32[]{:S(2)}) %collective-permute-start.1) | collective-permute-done | bytes 278560 | tf_op jit(solution)/shard_map/ppermute | solution.py:43
  11.4 4.3 %collective-permute-done.2.refs_4_ = bf16[272,512]{1,0:T(8,128)(2,1)S(1)} collective-permute-done((bf16[272,512]{1,0:T(8,128)(2,1)S(1)}, bf16[272,512]{1,0:T(8,128)(2,1)S(1)}, u32[]{:S(2)}, u32[]{:S(2)}) %collective-permute-start.2) | collective-permute-done | bytes 278560 | tf_op jit(solution)/shard_map/ppermute | solution.py:43
  15.8 0.8 collective-permute-start.4
  16.6 1.8 %collective-permute-done.refs_2_ = bf16[272,512]{1,0:T(8,128)(2,1)S(1)} collective-permute-done((bf16[272,512]{1,0:T(8,128)(2,1)S(1)}, bf16[272,512]{1,0:T(8,128)(2,1)S(1)}, u32[]{:S(2)}, u32[]{:S(2)}) %collective-permute-start) | collective-permute-done | bytes 278560 | tf_op jit(solution)/shard_map/ppermute | solution.py:43
  18.6 2.7 %collective-permute-start.5 = (bf16[256,512]{1,0:T(8,128)(2,1)S(1)}, bf16[256,512]{1,0:T(8,128)(2,1)S(1)}, u32[]{:S(2)}, u32[]{:S(2)}) collective-permute-start(bf16[256,512]{1,0:T(8,128)(2,1)S(1)} %copy-done.45), channel_id=1, source_target_pairs={{0,64},{1,65},{2,66},{3,67},{64,0},{65,1},{66,2},{67,3},{16,80},{1... | collective-permute-start | bytes 786440 | tf_op jit(solution)/shard_map/ppermute | solution.py:43
  21.3 5.5 %collective-permute-done.5 = bf16[256,512]{1,0:T(8,128)(2,1)S(1)} collective-permute-done((bf16[256,512]{1,0:T(8,128)(2,1)S(1)}, bf16[256,512]{1,0:T(8,128)(2,1)S(1)}, u32[]{:S(2)}, u32[]{:S(2)}) %collective-permute-start.5) | collective-permute-done | bytes 262176 | tf_op jit(solution)/shard_map/ppermute | solution.py:43
  26.7 2.7 %collective-permute-done.3.refs_5_ = bf16[400,512]{1,0:T(8,128)(2,1)S(1)} collective-permute-done((bf16[400,512]{1,0:T(8,128)(2,1)S(1)}, bf16[400,512]{1,0:T(8,128)(2,1)S(1)}, u32[]{:S(2)}, u32[]{:S(2)}) %collective-permute-start.3) | collective-permute-done | bytes 409632 | tf_op jit(solution)/shard_map/ppermute | solution.py:43
  30.5 1.6 collective-permute-start.6
  32.2 1.5 collective-permute-start.7
  33.8 5.1 %collective-permute-done.6.refs_7_ = bf16[272,512]{1,0:T(8,128)(2,1)} collective-permute-done((bf16[272,512]{1,0:T(8,128)(2,1)}, bf16[272,512]{1,0:T(8,128)(2,1)}, u32[]{:S(2)}, u32[]{:S(2)}) %collective-permute-start.6) | collective-permute-done | bytes 278560 | tf_op jit(solution)/shard_map/ppermute | solution.py:43
  38.9 1.4 assemble.1
  41.0 0.8 copy-done.25
  41.9 1.8 %collective-permute-start.9 = (bf16[256,1024]{1,0:T(8,128)(2,1)S(1)}, bf16[256,1024]{1,0:T(8,128)(2,1)S(1)}, u32[]{:S(2)}, u32[]{:S(2)}) collective-permute-start(bf16[256,1024]{1,0:T(8,128)(2,1)S(1)} %get-tuple-element.100), channel_id=1, source_target_pairs={{0,66},{1,67},{2,64},{3,65},{64,2},{65,3},{66,0},{67,1},{16,82},{1... | collective-permute-start | bytes 1572872 | tf_op jit(solution)/shard_map/ppermute | solution.py:43
  44.4 1.5 collective-permute-start.11
  45.9 6.3 %forward.1 = (f32[256,768]{1,0:T(8,128)S(1)}, f32[256,768]{1,0:T(8,128)S(1)}, bf16[256,768]{1,0:T(8,128)(2,1)S(1)}, f32[256,128]{1,0:T(8,128)S(1)}, bf16[256,1792]{1,0:T(8,128)(2,1)}) custom-call(bf16[272,4096]{1,0:T(8,128)(2,1)S(1)} %get-tuple-element.97.refs_0_, bf16[256,1024]{1,0:T(8,128)(2,1)S(1)} %get-tuple-element.98.refs_1_, ...), custom_call_target="tpu_custom_call" | custom-call | flops 3221225472 | bytes 16777216 | tf_op jit(solution)/shard_map/forward/pallas_call | solution.py:89
  54.3 6.9 %backward.1 = (bf16[256,1536]{1,0:T(8,128)(2,1)S(1)}, bf16[256,128]{1,0:T(8,128)(2,1)S(1)}, bf16[256,2048]{1,0:T(8,128)(2,1)S(1)}, bf16[256,3584]{1,0:T(8,128)(2,1)}) custom-call(s32[10]{0:T(128)S(1)} %copy-done.19, bf16[512,512]{1,0:T(8,128)(2,1)S(1)} %pad_maximum_fusion.3.refs_1_, bf16[512,512]{1,0:T(8,128)(2,1)S(1)} %collective-permute-done.7.refs_2_, ...), custom_call_target="tpu_custom_call" | custom-call | flops 1610612736 | bytes 8388608 | tf_op jit(solution)/shard_map/backward/pallas_call | solution.py:89
  61.8 1.0 copy-done.21
  63.5 1.6 collective-permute-start.21
  65.1 0.8 copy-done.17
  65.9 7.1 %pair_rows.1 = (bf16[512,640]{1,0:T(8,128)(2,1)S(1)}, bf16[512,640]{1,0:T(8,128)(2,1)S(1)}, bf16[256,640]{1,0:T(8,128)(2,1)S(1)}, bf16[256,640]{1,0:T(8,128)(2,1...) custom-call(s32[8]{0:T(128)S(1)} %stack.105.refs_0_, ...), custom_call_target="tpu_custom_call" | custom-call | flops 3221225472 | bytes 16777216 | tf_op jit(solution)/shard_map/pair_rows/pallas_call | solution.py:89
  73.1 4.8 %down_terms.1 = (bf16[1024,384]{1,0:T(8,128)(2,1)S(1)}, bf16[1024,384]{1,0:T(8,128)(2,1)S(1)}, bf16[512,384]{1,0:T(8,128)(2,1)S(1)}, bf16[512,384]{1,0:T(8,128)(...) custom-call(s32[8]{0:T(128)S(1)} %stack.121.refs_0_, bf16[256,2048]{1,0:T(8,128)(2,1)S(1)} %copy-done.22, ...), custom_call_target="tpu_custom_call" | custom-call | flops 1610612736 | bytes 8388608 | tf_op jit(solution)/shard_map/down_terms/pallas_call | solution.py:89
  78.6 2.8 %collective-permute-start.18 = (bf16[1024,384]{1,0:T(8,128)(2,1)S(1)}, bf16[1024,384]{1,0:T(8,128)(2,1)S(1)}, u32[]{:S(2)}, u32[]{:S(2)}) collective-permute-start(bf16[1024,384]{1,0:T(8,128)(2,1)S(1)} %get-tuple-element.127), channel_id=1, source_target_pairs={{0,12},{1,13},{2,14},{3,15},{64,76},{65,77},{66,78},{67,79},{16,28... | collective-permute-start | bytes 2359304 | tf_op jit(solution)/shard_map/ppermute | solution.py:43
  81.6 1.7 collective-permute-start.16
  83.3 5.2 %branch_rows.1 = (bf16[512,512]{1,0:T(8,128)(2,1)S(1)}, bf16[512,512]{1,0:T(8,128)(2,1)S(1)}, bf16[256,512]{1,0:T(8,128)(2,1)S(1)}, bf16[256,512]{1,0:T(8,128)(2...) custom-call(s32[8]{0:T(128)S(1)} %stack.105.refs_0_, bf16[256,768]{1,0:T(8,128)(2,1)S(1)} %copy-done.11, ...), custom_call_target="tpu_custom_call" | custom-call | flops 1610612736 | bytes 8388608 | tf_op jit(solution)/shard_map/branch_rows/pallas_call | solution.py:89
  90.0 0.8 copy-done.31
  90.8 7.9 %collective-permute-done.16 = bf16[512,640]{1,0:T(8,128)(2,1)S(1)} collective-permute-done((bf16[512,640]{1,0:T(8,128)(2,1)S(1)}, bf16[512,640]{1,0:T(8,128)(2,1)S(1)}, u32[]{:S(2)}, u32[]{:S(2)}) %collective-permute-start.16) | collective-permute-done | bytes 655392 | tf_op jit(solution)/shard_map/ppermute | solution.py:43
  99.0 1.3 collective-permute-done.17
  100.3 1.3 pad_maximum_fusion
  101.6 0.8 add_convert_fusion.5
  102.4 1.5 collective-permute-start.20
  103.9 0.9 add_convert_fusion.3
  105.1 0.9 add_convert_fusion.4
  105.9 1.3 collective-permute-start.23
  107.2 0.8 add_convert_fusion.6
  108.7 1.0 copy-done.26
  109.7 1.0 copy-done.28
  110.8 6.9 %pair_terms.1 = (bf16[512,768]{1,0:T(8,128)(2,1)S(1)}, bf16[512,768]{1,0:T(8,128)(2,1)}, bf16[256,768]{1,0:T(8,128)(2,1)S(1)}, bf16[256,768]{1,0:T(8,128)(2,1)S(...) custom-call(s32[8]{0:T(128)S(1)} %stack.121.refs_0_, bf16[256,1024]{1,0:T(8,128)(2,1)S(1)} %copy-done.26, ...), custom_call_target="tpu_custom_call" | custom-call | flops 3221225472 | bytes 8388608 | tf_op jit(solution)/shard_map/pair_terms/pallas_call | solution.py:89
  120.0 0.9 copy-done.23
  121.0 2.2 %select_convert_fusion.1 = bf16[256,640]{1,0:T(8,128)(2,1)} fusion(bf16[256,640]{1,0:T(8,128)(2,1)} %collective-permute-done.19, bf16[256,640]{1,0:T(8,128)(2,1)S(1)} %get-tuple-element.123, bf16[256,640]{1,0:T(8,128)(2,1)} %collective-permute-done.20, bf16[256,640]{1,0:T(8,128)(2,1)S(1)} %get-tuple-element.150, pred[]{:T(512)S(6)} %eq.26, ...), kind=kLoop, calls=%fused_computation.19 | loop fusion | flops 1966080 | bytes 2293761 | tf_op jit(solution)/shard_map/convert_element_type | solution.py:350
  123.2 1.4 collective-permute-start.25
  125.3 1.4 collective-permute-start.33
  126.7 1.7 collective-permute-start.34
  128.4 5.7 %collective-permute-done.25 = bf16[256,640]{1,0:T(8,128)(2,1)S(1)} collective-permute-done((bf16[256,640]{1,0:T(8,128)(2,1)}, bf16[256,640]{1,0:T(8,128)(2,1)S(1)}, u32[]{:S(2)}, u32[]{:S(2)}) %collective-permute-start.25) | collective-permute-done | bytes 327712 | tf_op jit(solution)/shard_map/ppermute | solution.py:43
  134.2 1.6 convert_add_fusion.2
  136.0 0.9 fusion.3
  136.8 2.6 %collective-permute-start.26 = (bf16[512,512]{1,0:T(8,128)(2,1)S(1)}, bf16[512,512]{1,0:T(8,128)(2,1)S(1)}, u32[]{:S(2)}, u32[]{:S(2)}) collective-permute-start(bf16[512,512]{1,0:T(8,128)(2,1)S(1)} %copy-done.32), channel_id=1, source_target_pairs={{0,48},{1,49},{2,50},{3,51},{64,112},{65,113},{66,114},{67,115},{1... | collective-permute-start | bytes 1572872 | tf_op jit(solution)/shard_map/ppermute | solution.py:43
  139.4 1.4 convert_add_fusion
  141.3 3.2 %collective-permute-done.32 = f32[1,512]{1,0:T(1,128)S(1)} collective-permute-done((f32[1,512]{1,0:T(1,128)S(1)}, f32[1,512]{1,0:T(1,128)S(1)}, u32[]{:S(2)}, u32[]{:S(2)}) %collective-permute-start.32) | collective-permute-done | bytes 2080 | tf_op jit(solution)/shard_map/ppermute | solution.py:43
  144.8 1.6 collective-permute-done.34
  146.6 5.7 %collective-permute-done.26 = bf16[512,512]{1,0:T(8,128)(2,1)S(1)} collective-permute-done((bf16[512,512]{1,0:T(8,128)(2,1)S(1)}, bf16[512,512]{1,0:T(8,128)(2,1)S(1)}, u32[]{:S(2)}, u32[]{:S(2)}) %collective-permute-start.26) | collective-permute-done | bytes 524320 | tf_op jit(solution)/shard_map/ppermute | solution.py:43
  152.4 1.1 collective-permute-done.27
  153.5 1.6 collective-permute-start.29
  155.4 1.8 %collective-permute-start.35 = (bf16[256,768]{1,0:T(8,128)(2,1)S(1)}, bf16[256,768]{1,0:T(8,128)(2,1)S(1)}, u32[]{:S(2)}, u32[]{:S(2)}) collective-permute-start(bf16[256,768]{1,0:T(8,128)(2,1)S(1)} %add_convert_fusion.2), channel_id=1, source_target_pairs={{0,12},{1,13},{2,14},{3,15},{64,76},{65,77},{66,78},{67,79},{16,28... | collective-permute-start | bytes 1179656 | tf_op jit(solution)/shard_map/ppermute | solution.py:43
  157.3 5.2 %collective-permute-done.29 = bf16[256,512]{1,0:T(8,128)(2,1)S(1)} collective-permute-done((bf16[256,512]{1,0:T(8,128)(2,1)S(1)}, bf16[256,512]{1,0:T(8,128)(2,1)S(1)}, u32[]{:S(2)}, u32[]{:S(2)}) %collective-permute-start.29) | collective-permute-done | bytes 262176 | tf_op jit(solution)/shard_map/ppermute | solution.py:43
  163.1 1.6 collective-permute-start.30
  164.7 2.5 %collective-permute-done.35 = bf16[256,768]{1,0:T(8,128)(2,1)S(1)} collective-permute-done((bf16[256,768]{1,0:T(8,128)(2,1)S(1)}, bf16[256,768]{1,0:T(8,128)(2,1)S(1)}, u32[]{:S(2)}, u32[]{:S(2)}) %collective-permute-start.35) | collective-permute-done | bytes 393248 | tf_op jit(solution)/shard_map/ppermute | solution.py:43
  167.5 3.2 %collective-permute-done.37 = f32[1,512]{1,0:T(1,128)S(1)} collective-permute-done((f32[1,512]{1,0:T(1,128)S(1)}, f32[1,512]{1,0:T(1,128)S(1)}, u32[]{:S(2)}, u32[]{:S(2)}) %collective-permute-start.37) | collective-permute-done | bytes 2080 | tf_op jit(solution)/shard_map/ppermute | solution.py:43
  170.7 1.1 collective-permute-start.38
  171.9 1.1 pad_maximum_fusion.1
  173.0 2.8 %collective-permute-done.38 = f32[1,512]{1,0:T(1,128)S(1)} collective-permute-done((f32[1,512]{1,0:T(1,128)S(1)}, f32[1,512]{1,0:T(1,128)S(1)}, u32[]{:S(2)}, u32[]{:S(2)}) %collective-permute-start.38) | collective-permute-done | bytes 2080 | tf_op jit(solution)/shard_map/ppermute | solution.py:43
  176.4 0.9 add_convert_fusion.7
  (160 shorter events, 16.7 us)
Async XLA Ops:
  1.3 17.2 %copy-start.45 = (bf16[256,512]{1,0:T(8,128)(2,1)S(1)}, bf16[256,512]{1,0:T(8,128)(2,1)}, u32[]{:S(2)}) copy-start(bf16[256,512]{1,0:T(8,128)(2,1)} %param.7) | copy-start | bytes 786436
  2.3 9.1 %collective-permute-start.1 = (bf16[272,512]{1,0:T(8,128)(2,1)S(1)}, bf16[272,512]{1,0:T(8,128)(2,1)S(1)}, u32[]{:S(2)}, u32[]{:S(2)}) collective-permute-start(bf16[272,512]{1,0:T(8,128)(2,1)S(1)} %pad_maximum_fusion.6.refs_1_), channel_id=1, source_target_pairs={{0,48},{1,49},{2,50},{3,51},{64,112},{65,113},{66,114},{67,115},{1... | collective-permute-start | bytes 835592 | tf_op jit(solution)/shard_map/ppermute | solution.py:43
  5.5 10.2 %collective-permute-start.2 = (bf16[272,512]{1,0:T(8,128)(2,1)S(1)}, bf16[272,512]{1,0:T(8,128)(2,1)S(1)}, u32[]{:S(2)}, u32[]{:S(2)}) collective-permute-start(bf16[272,512]{1,0:T(8,128)(2,1)S(1)} %pad_maximum_fusion.6.refs_1_), channel_id=1, source_target_pairs={{0,64},{1,65},{2,66},{3,67},{64,0},{65,1},{66,2},{67,3},{16,80},{1... | collective-permute-start | bytes 835592 | tf_op jit(solution)/shard_map/ppermute | solution.py:43
  9.4 9.0 %collective-permute-start = (bf16[272,512]{1,0:T(8,128)(2,1)S(1)}, bf16[272,512]{1,0:T(8,128)(2,1)S(1)}, u32[]{:S(2)}, u32[]{:S(2)}) collective-permute-start(bf16[272,512]{1,0:T(8,128)(2,1)S(1)} %pad_maximum_fusion.6.refs_1_), channel_id=1, source_target_pairs={{0,16},{1,17},{2,18},{3,19},{64,80},{65,81},{66,82},{67,83},{16,32... | collective-permute-start | bytes 835592 | tf_op jit(solution)/shard_map/ppermute | solution.py:43
  15.8 13.7 %collective-permute-start.4 = (bf16[416,512]{1,0:T(8,128)(2,1)S(1)}, bf16[416,512]{1,0:T(8,128)(2,1)S(1)}, u32[]{:S(2)}, u32[]{:S(2)}) collective-permute-start(bf16[416,512]{1,0:T(8,128)(2,1)S(1)} %pad_maximum_fusion.4), channel_id=1, source_target_pairs={{0,48},{1,49},{2,50},{3,51},{64,112},{65,113},{66,114},{67,115},{1... | collective-permute-start | bytes 1277960 | tf_op jit(solution)/shard_map/ppermute | solution.py:43
  18.5 11.0 %collective-permute-start.3 = (bf16[400,512]{1,0:T(8,128)(2,1)S(1)}, bf16[400,512]{1,0:T(8,128)(2,1)S(1)}, u32[]{:S(2)}, u32[]{:S(2)}) collective-permute-start(bf16[400,512]{1,0:T(8,128)(2,1)S(1)} %pad_maximum_fusion.5), channel_id=1, source_target_pairs={{0,16},{1,17},{2,18},{3,19},{64,80},{65,81},{66,82},{67,83},{16,32... | collective-permute-start | bytes 1228808 | tf_op jit(solution)/shard_map/ppermute | solution.py:43
  18.6 8.1 %collective-permute-start.5 = (bf16[256,512]{1,0:T(8,128)(2,1)S(1)}, bf16[256,512]{1,0:T(8,128)(2,1)S(1)}, u32[]{:S(2)}, u32[]{:S(2)}) collective-permute-start(bf16[256,512]{1,0:T(8,128)(2,1)S(1)} %copy-done.45), channel_id=1, source_target_pairs={{0,64},{1,65},{2,66},{3,67},{64,0},{65,1},{66,2},{67,3},{16,80},{1... | collective-permute-start | bytes 786440 | tf_op jit(solution)/shard_map/ppermute | solution.py:43
  29.5 14.2 %collective-permute-start.8 = (bf16[512,512]{1,0:T(8,128)(2,1)S(1)}, bf16[512,512]{1,0:T(8,128)(2,1)S(1)}, u32[]{:S(2)}, u32[]{:S(2)}) collective-permute-start(bf16[512,512]{1,0:T(8,128)(2,1)S(1)} %pad_maximum_fusion.3.refs_1_), channel_id=1, source_target_pairs={{0,48},{1,49},{2,50},{3,51},{64,112},{65,113},{66,114},{67,115},{1... | collective-permute-start | bytes 1572872 | tf_op jit(solution)/shard_map/ppermute | solution.py:43
  30.5 8.4 %collective-permute-start.6 = (bf16[272,512]{1,0:T(8,128)(2,1)}, bf16[272,512]{1,0:T(8,128)(2,1)}, u32[]{:S(2)}, u32[]{:S(2)}) collective-permute-start(bf16[272,512]{1,0:T(8,128)(2,1)} %pad_maximum_fusion.7), channel_id=1, source_target_pairs={{0,64},{1,65},{2,66},{3,67},{64,0},{65,1},{66,2},{67,3},{16,80},{1... | collective-permute-start | bytes 835592 | tf_op jit(solution)/shard_map/ppermute | solution.py:43
  32.2 12.2 %collective-permute-start.7 = (bf16[512,512]{1,0:T(8,128)(2,1)S(1)}, bf16[512,512]{1,0:T(8,128)(2,1)S(1)}, u32[]{:S(2)}, u32[]{:S(2)}) collective-permute-start(bf16[512,512]{1,0:T(8,128)(2,1)S(1)} %pad_maximum_fusion.3.refs_1_), channel_id=1, source_target_pairs={{0,16},{1,17},{2,18},{3,19},{64,80},{65,81},{66,82},{67,83},{16,32... | collective-permute-start | bytes 1572872 | tf_op jit(solution)/shard_map/ppermute | solution.py:43
  33.8 9.9 %copy-start.18 = (s32[10]{0:T(128)}, s32[10]{0:T(128)S(1)}, u32[]{:S(2)}) copy-start(s32[10]{0:T(128)S(1)} %stack.116.refs_0_) | copy-start | bytes 124
  41.9 11.2 %collective-permute-start.9 = (bf16[256,1024]{1,0:T(8,128)(2,1)S(1)}, bf16[256,1024]{1,0:T(8,128)(2,1)S(1)}, u32[]{:S(2)}, u32[]{:S(2)}) collective-permute-start(bf16[256,1024]{1,0:T(8,128)(2,1)S(1)} %get-tuple-element.100), channel_id=1, source_target_pairs={{0,66},{1,67},{2,64},{3,65},{64,2},{65,3},{66,0},{67,1},{16,82},{1... | collective-permute-start | bytes 1572872 | tf_op jit(solution)/shard_map/ppermute | solution.py:43
  43.7 9.8 %collective-permute-start.10 = (bf16[256,1024]{1,0:T(8,128)(2,1)S(1)}, bf16[256,1024]{1,0:T(8,128)(2,1)S(1)}, u32[]{:S(2)}, u32[]{:S(2)}) collective-permute-start(bf16[256,1024]{1,0:T(8,128)(2,1)S(1)} %get-tuple-element.101), channel_id=1, source_target_pairs={{0,2},{1,3},{2,0},{3,1},{64,66},{65,67},{66,64},{67,65},{16,18},{1... | collective-permute-start | bytes 1572872 | tf_op jit(solution)/shard_map/ppermute | solution.py:43
  43.7 9.8 %collective-permute-start.12 = (bf16[256,512]{1,0:T(8,128)(2,1)S(1)}, bf16[256,512]{1,0:T(8,128)(2,1)S(1)}, u32[]{:S(2)}, u32[]{:S(2)}) collective-permute-start(bf16[256,512]{1,0:T(8,128)(2,1)S(1)} %pad_maximum_fusion.9), channel_id=1, source_target_pairs={{0,48},{1,49},{2,50},{3,51},{64,112},{65,113},{66,114},{67,115},{1... | collective-permute-start | bytes 786440 | tf_op jit(solution)/shard_map/ppermute | solution.py:43
  44.4 9.1 %collective-permute-start.11 = (bf16[256,512]{1,0:T(8,128)(2,1)S(1)}, bf16[256,512]{1,0:T(8,128)(2,1)S(1)}, u32[]{:S(2)}, u32[]{:S(2)}) collective-permute-start(bf16[256,512]{1,0:T(8,128)(2,1)S(1)} %pad_maximum_fusion.8), channel_id=1, source_target_pairs={{0,16},{1,17},{2,18},{3,19},{64,80},{65,81},{66,82},{67,83},{16,32... | collective-permute-start | bytes 786440 | tf_op jit(solution)/shard_map/ppermute | solution.py:43
  45.9 8.4 %copy-start.19 = (s32[10]{0:T(128)S(1)}, s32[10]{0:T(128)}, u32[]{:S(2)}) copy-start(s32[10]{0:T(128)} %copy-done.18) | copy-start | bytes 124
  53.0 8.1 %copy-start.27 = (bf16[256,1024]{1,0:T(8,128)(2,1)}, bf16[256,1024]{1,0:T(8,128)(2,1)S(1)}, u32[]{:S(2)}) copy-start(bf16[256,1024]{1,0:T(8,128)(2,1)S(1)} %collective-permute-done.9.refs_2_) | copy-start | bytes 1572868
  62.8 10.3 %collective-permute-start.13 = (bf16[256,3584]{1,0:T(8,128)(2,1)}, bf16[256,3584]{1,0:T(8,128)(2,1)}, u32[]{:S(2)}, u32[]{:S(2)}) collective-permute-start(bf16[256,3584]{1,0:T(8,128)(2,1)} %get-tuple-element.111), channel_id=1, source_target_pairs={{0,1},{1,0},{2,3},{3,2},{64,65},{65,64},{66,67},{67,66},{16,17},{1... | collective-permute-start | bytes 5505032 | tf_op jit(solution)/shard_map/ppermute | solution.py:43
  62.8 10.2 %collective-permute-start.14 = (bf16[256,1792]{1,0:T(8,128)(2,1)}, bf16[256,1792]{1,0:T(8,128)(2,1)}, u32[]{:S(2)}, u32[]{:S(2)}) collective-permute-start(bf16[256,1792]{1,0:T(8,128)(2,1)} %get-tuple-element.112), channel_id=1, source_target_pairs={{0,1},{1,0},{2,3},{3,2},{64,65},{65,64},{66,67},{67,66},{16,17},{1... | collective-permute-start | bytes 2752520 | tf_op jit(solution)/shard_map/ppermute | solution.py:43
  63.5 35.4 %collective-permute-start.21 = (bf16[256,1536]{1,0:T(8,128)(2,1)S(1)}, bf16[256,1536]{1,0:T(8,128)(2,1)S(1)}, u32[]{:S(2)}, u32[]{:S(2)}) collective-permute-start(bf16[256,1536]{1,0:T(8,128)(2,1)S(1)} %get-tuple-element.107.refs_1_.refs_5_), channel_id=1, source_target_pairs={{0,2},{1,3},{2,0},{3,1},{64,66},{65,67},{66,64},{67,65},{16,18},{1... | collective-permute-start | bytes 2359304 | tf_op jit(solution)/shard_map/ppermute | solution.py:43
  65.9 7.1 %copy-start.11 = (bf16[256,768]{1,0:T(8,128)(2,1)S(1)}, bf16[256,768]{1,0:T(8,128)(2,1)}, u32[]{:S(2)}) copy-start(bf16[256,768]{1,0:T(8,128)(2,1)} %copy-done.10) | copy-start | bytes 1179652
  65.9 7.1 %copy-start.22 = (bf16[256,2048]{1,0:T(8,128)(2,1)S(1)}, bf16[256,2048]{1,0:T(8,128)(2,1)}, u32[]{:S(2)}) copy-start(bf16[256,2048]{1,0:T(8,128)(2,1)} %copy-done.21) | copy-start | bytes 3145732
  78.6 9.8 %copy-start.6 = (bf16[512,384]{1,0:T(8,128)(2,1)}, bf16[512,384]{1,0:T(8,128)(2,1)S(1)}, u32[]{:S(2)}) copy-start(bf16[512,384]{1,0:T(8,128)(2,1)S(1)} %get-tuple-element.180) | copy-start | bytes 1179652
  78.6 20.4 %collective-permute-start.18 = (bf16[1024,384]{1,0:T(8,128)(2,1)S(1)}, bf16[1024,384]{1,0:T(8,128)(2,1)S(1)}, u32[]{:S(2)}, u32[]{:S(2)}) collective-permute-start(bf16[1024,384]{1,0:T(8,128)(2,1)S(1)} %get-tuple-element.127), channel_id=1, source_target_pairs={{0,12},{1,13},{2,14},{3,15},{64,76},{65,77},{66,78},{67,79},{16,28... | collective-permute-start | bytes 2359304 | tf_op jit(solution)/shard_map/ppermute | solution.py:43
  81.4 18.9 %collective-permute-start.17 = (bf16[1024,384]{1,0:T(8,128)(2,1)S(1)}, bf16[1024,384]{1,0:T(8,128)(2,1)S(1)}, u32[]{:S(2)}, u32[]{:S(2)}) collective-permute-start(bf16[1024,384]{1,0:T(8,128)(2,1)S(1)} %get-tuple-element.113), channel_id=1, source_target_pairs={{0,4},{1,5},{2,6},{3,7},{64,68},{65,69},{66,70},{67,71},{16,20},{1... | collective-permute-start | bytes 2359304 | tf_op jit(solution)/shard_map/ppermute | solution.py:43
  81.6 18.7 %copy-start.44 = (bf16[256,1024]{1,0:T(8,128)(2,1)S(1)}, bf16[256,1024]{1,0:T(8,128)(2,1)}, u32[]{:S(2)}) copy-start(bf16[256,1024]{1,0:T(8,128)(2,1)} %copy-done.43) | copy-start | bytes 1572868
  81.6 17.1 %collective-permute-start.16 = (bf16[512,640]{1,0:T(8,128)(2,1)S(1)}, bf16[512,640]{1,0:T(8,128)(2,1)S(1)}, u32[]{:S(2)}, u32[]{:S(2)}) collective-permute-start(bf16[512,640]{1,0:T(8,128)(2,1)S(1)} %get-tuple-element.126), channel_id=1, source_target_pairs={{0,48},{1,49},{2,50},{3,51},{64,112},{65,113},{66,114},{67,115},{1... | collective-permute-start | bytes 1966088 | tf_op jit(solution)/shard_map/ppermute | solution.py:43
  83.3 15.6 %collective-permute-start.15 = (bf16[512,640]{1,0:T(8,128)(2,1)S(1)}, bf16[512,640]{1,0:T(8,128)(2,1)S(1)}, u32[]{:S(2)}, u32[]{:S(2)}) collective-permute-start(bf16[512,640]{1,0:T(8,128)(2,1)S(1)} %get-tuple-element.109), channel_id=1, source_target_pairs={{0,16},{1,17},{2,18},{3,19},{64,80},{65,81},{66,82},{67,83},{16,0}... | collective-permute-start | bytes 1966088 | tf_op jit(solution)/shard_map/ppermute | solution.py:43
  90.8 10.7 %copy-start.12 = (bf16[256,512]{1,0:T(8,128)(2,1)}, bf16[256,512]{1,0:T(8,128)(2,1)S(1)}, u32[]{:S(2)}) copy-start(bf16[256,512]{1,0:T(8,128)(2,1)S(1)} %get-tuple-element.159) | copy-start | bytes 786436
  98.9 8.3 %copy-start.36 = (bf16[512,640]{1,0:T(8,128)(2,1)}, bf16[512,640]{1,0:T(8,128)(2,1)S(1)}, u32[]{:S(2)}) copy-start(bf16[512,640]{1,0:T(8,128)(2,1)S(1)} %collective-permute-done.15) | copy-start | bytes 1966084
  99.0 4.9 %copy-start.39 = (bf16[1024,384]{1,0:T(8,128)(2,1)}, bf16[1024,384]{1,0:T(8,128)(2,1)S(1)}, u32[]{:S(2)}) copy-start(bf16[1024,384]{1,0:T(8,128)(2,1)S(1)} %collective-permute-done.18) | copy-start | bytes 2359300
  100.3 4.8 %copy-start.41 = (bf16[1024,384]{1,0:T(8,128)(2,1)}, bf16[1024,384]{1,0:T(8,128)(2,1)S(1)}, u32[]{:S(2)}) copy-start(bf16[1024,384]{1,0:T(8,128)(2,1)S(1)} %collective-permute-done.17) | copy-start | bytes 2359300
  101.5 7.1 %collective-permute-start.22 = (bf16[256,2560]{1,0:T(8,128)(2,1)}, bf16[256,2560]{1,0:T(8,128)(2,1)}, u32[]{:S(2)}, u32[]{:S(2)}) collective-permute-start(bf16[256,2560]{1,0:T(8,128)(2,1)} %pad_maximum_fusion), channel_id=1, source_target_pairs={{0,1},{1,0},{2,3},{3,2},{64,65},{65,64},{66,67},{67,66},{16,17},{1... | collective-permute-start | bytes 3932168 | tf_op jit(solution)/shard_map/ppermute | solution.py:43
  102.4 18.6 %collective-permute-start.20 = (bf16[256,640]{1,0:T(8,128)(2,1)}, bf16[256,640]{1,0:T(8,128)(2,1)}, u32[]{:S(2)}, u32[]{:S(2)}) collective-permute-start(bf16[256,640]{1,0:T(8,128)(2,1)} %add_convert_fusion.5), channel_id=1, source_target_pairs={{0,16},{1,17},{2,18},{3,19},{64,80},{65,81},{66,82},{67,83},{16,0}... | collective-permute-start | bytes 983048 | tf_op jit(solution)/shard_map/ppermute | solution.py:43
  104.8 16.2 %collective-permute-start.24 = (bf16[512,384]{1,0:T(8,128)(2,1)}, bf16[512,384]{1,0:T(8,128)(2,1)}, u32[]{:S(2)}, u32[]{:S(2)}) collective-permute-start(bf16[512,384]{1,0:T(8,128)(2,1)} %add_convert_fusion.3), channel_id=1, source_target_pairs={{0,4},{1,5},{2,6},{3,7},{64,68},{65,69},{66,70},{67,71},{16,20},{1... | collective-permute-start | bytes 1179656 | tf_op jit(solution)/shard_map/ppermute | solution.py:43
  105.9 15.0 %collective-permute-start.23 = (bf16[512,384]{1,0:T(8,128)(2,1)}, bf16[512,384]{1,0:T(8,128)(2,1)}, u32[]{:S(2)}, u32[]{:S(2)}) collective-permute-start(bf16[512,384]{1,0:T(8,128)(2,1)} %add_convert_fusion.4), channel_id=1, source_target_pairs={{0,12},{1,13},{2,14},{3,15},{64,76},{65,77},{66,78},{67,79},{16,28... | collective-permute-start | bytes 1179656 | tf_op jit(solution)/shard_map/ppermute | solution.py:43
  108.0 12.9 %collective-permute-start.19 = (bf16[256,640]{1,0:T(8,128)(2,1)}, bf16[256,640]{1,0:T(8,128)(2,1)}, u32[]{:S(2)}, u32[]{:S(2)}) collective-permute-start(bf16[256,640]{1,0:T(8,128)(2,1)} %add_convert_fusion.6), channel_id=1, source_target_pairs={{0,48},{1,49},{2,50},{3,51},{64,112},{65,113},{66,114},{67,115},{1... | collective-permute-start | bytes 983048 | tf_op jit(solution)/shard_map/ppermute | solution.py:43
  110.8 10.2 %copy-start.34 = (bf16[512,640]{1,0:T(8,128)(2,1)S(1)}, bf16[512,640]{1,0:T(8,128)(2,1)}, u32[]{:S(2)}) copy-start(bf16[512,640]{1,0:T(8,128)(2,1)} %copy-done.33) | copy-start | bytes 1966084
  110.8 10.2 %copy-start.37 = (bf16[512,640]{1,0:T(8,128)(2,1)S(1)}, bf16[512,640]{1,0:T(8,128)(2,1)}, u32[]{:S(2)}) copy-start(bf16[512,640]{1,0:T(8,128)(2,1)} %copy-done.36) | copy-start | bytes 1966084
  120.9 3.7 %copy-start.46 = (bf16[512]{0:T(512)(128)(2,1)S(1)}, bf16[512]{0:T(512)(128)(2,1)}, u32[]{:S(2)}) copy-start(bf16[512]{0:T(512)(128)(2,1)} %param.5) | copy-start | bytes 3076
  120.9 13.3 %copy-start.35 = (bf16[512,640]{1,0:T(8,128)(2,1)S(1)}, bf16[512,640]{1,0:T(8,128)(2,1)}, u32[]{:S(2)}) copy-start(bf16[512,640]{1,0:T(8,128)(2,1)} %copy-done.33) | copy-start | bytes 1966084
  120.9 4.4 %copy-start.24 = (bf16[512,768]{1,0:T(8,128)(2,1)S(1)}, bf16[512,768]{1,0:T(8,128)(2,1)}, u32[]{:S(2)}) copy-start(bf16[512,768]{1,0:T(8,128)(2,1)} %copy-done.23) | copy-start | bytes 2359300
  123.2 11.0 %collective-permute-start.25 = (bf16[256,640]{1,0:T(8,128)(2,1)}, bf16[256,640]{1,0:T(8,128)(2,1)S(1)}, u32[]{:S(2)}, u32[]{:S(2)}) collective-permute-start(bf16[256,640]{1,0:T(8,128)(2,1)} %select_convert_fusion.1), channel_id=1, source_target_pairs={{0,64},{1,65},{2,66},{3,67},{64,0},{65,1},{66,2},{67,3},{16,80},{1... | collective-permute-start | bytes 983048 | tf_op jit(solution)/shard_map/ppermute | solution.py:43
  125.3 21.1 %collective-permute-start.33 = (bf16[512,768]{1,0:T(8,128)(2,1)S(1)}, bf16[512,768]{1,0:T(8,128)(2,1)S(1)}, u32[]{:S(2)}, u32[]{:S(2)}) collective-permute-start(bf16[512,768]{1,0:T(8,128)(2,1)S(1)} %copy-done.24), channel_id=1, source_target_pairs={{0,4},{1,5},{2,6},{3,7},{64,68},{65,69},{66,70},{67,71},{16,20},{1... | collective-permute-start | bytes 2359304 | tf_op jit(solution)/shard_map/ppermute | solution.py:43
  126.7 19.7 %collective-permute-start.34 = (bf16[512,768]{1,0:T(8,128)(2,1)}, bf16[512,768]{1,0:T(8,128)(2,1)S(1)}, u32[]{:S(2)}, u32[]{:S(2)}) collective-permute-start(bf16[512,768]{1,0:T(8,128)(2,1)} %get-tuple-element.167), channel_id=1, source_target_pairs={{0,12},{1,13},{2,14},{3,15},{64,76},{65,77},{66,78},{67,79},{16,28... | collective-permute-start | bytes 2359304 | tf_op jit(solution)/shard_map/ppermute | solution.py:43
  134.2 5.2 %copy-start.40 = (bf16[1024,384]{1,0:T(8,128)(2,1)S(1)}, bf16[1024,384]{1,0:T(8,128)(2,1)}, u32[]{:S(2)}) copy-start(bf16[1024,384]{1,0:T(8,128)(2,1)} %copy-done.39) | copy-start | bytes 2359300
  134.2 5.2 %copy-start.42 = (bf16[1024,384]{1,0:T(8,128)(2,1)S(1)}, bf16[1024,384]{1,0:T(8,128)(2,1)}, u32[]{:S(2)}) copy-start(bf16[1024,384]{1,0:T(8,128)(2,1)} %copy-done.41) | copy-start | bytes 2359300
  136.8 4.0 %collective-permute-start.31 = (f32[1,512]{1,0:T(1,128)S(1)}, f32[1,512]{1,0:T(1,128)S(1)}, u32[]{:S(2)}, u32[]{:S(2)}) collective-permute-start(f32[1,512]{1,0:T(1,128)S(1)} %bitcast.32), channel_id=1, source_target_pairs={{0,1},{1,0},{2,3},{3,2},{64,65},{65,64},{66,67},{67,66},{16,17},{1... | collective-permute-start | bytes 6152 | tf_op jit(solution)/shard_map/ppermute | solution.py:43
  136.8 15.5 %collective-permute-start.26 = (bf16[512,512]{1,0:T(8,128)(2,1)S(1)}, bf16[512,512]{1,0:T(8,128)(2,1)S(1)}, u32[]{:S(2)}, u32[]{:S(2)}) collective-permute-start(bf16[512,512]{1,0:T(8,128)(2,1)S(1)} %copy-done.32), channel_id=1, source_target_pairs={{0,48},{1,49},{2,50},{3,51},{64,112},{65,113},{66,114},{67,115},{1... | collective-permute-start | bytes 1572872 | tf_op jit(solution)/shard_map/ppermute | solution.py:43
  139.4 14.1 %collective-permute-start.27 = (bf16[512,512]{1,0:T(8,128)(2,1)S(1)}, bf16[512,512]{1,0:T(8,128)(2,1)S(1)}, u32[]{:S(2)}, u32[]{:S(2)}) collective-permute-start(bf16[512,512]{1,0:T(8,128)(2,1)S(1)} %copy-done.30), channel_id=1, source_target_pairs={{0,16},{1,17},{2,18},{3,19},{64,80},{65,81},{66,82},{67,83},{16,0}... | collective-permute-start | bytes 1572872 | tf_op jit(solution)/shard_map/ppermute | solution.py:43
  140.8 5.6 %copy-start.1 = (bf16[256,768]{1,0:T(8,128)(2,1)S(1)}, bf16[256,768]{1,0:T(8,128)(2,1)}, u32[]{:S(2)}) copy-start(bf16[256,768]{1,0:T(8,128)(2,1)} %copy-done) | copy-start | bytes 1179652
  140.9 3.7 %collective-permute-start.32 = (f32[1,512]{1,0:T(1,128)S(1)}, f32[1,512]{1,0:T(1,128)S(1)}, u32[]{:S(2)}, u32[]{:S(2)}) collective-permute-start(f32[1,512]{1,0:T(1,128)S(1)} %add.216), channel_id=1, source_target_pairs={{0,2},{1,3},{2,0},{3,1},{64,66},{65,67},{66,64},{67,65},{16,18},{1... | collective-permute-start | bytes 6152 | tf_op jit(solution)/shard_map/ppermute | solution.py:43
  141.2 12.2 %copy-start.15 = (bf16[256,512]{1,0:T(8,128)(2,1)S(1)}, bf16[256,512]{1,0:T(8,128)(2,1)}, u32[]{:S(2)}) copy-start(bf16[256,512]{1,0:T(8,128)(2,1)} %copy-done.14) | copy-start | bytes 786436
  141.3 13.8 %copy-start.13 = (bf16[256,512]{1,0:T(8,128)(2,1)S(1)}, bf16[256,512]{1,0:T(8,128)(2,1)}, u32[]{:S(2)}) copy-start(bf16[256,512]{1,0:T(8,128)(2,1)} %copy-done.12) | copy-start | bytes 786436
  144.5 12.6 %collective-permute-start.39 = (bf16[256,768]{1,0:T(8,128)(2,1)S(1)}, bf16[256,768]{1,0:T(8,128)(2,1)S(1)}, u32[]{:S(2)}, u32[]{:S(2)}) collective-permute-start(bf16[256,768]{1,0:T(8,128)(2,1)S(1)} %select_convert_fusion), channel_id=1, source_target_pairs={{0,2},{1,3},{2,0},{3,1},{64,66},{65,67},{66,64},{67,65},{16,18},{1... | collective-permute-start | bytes 1179656 | tf_op jit(solution)/shard_map/ppermute | solution.py:43
  146.6 18.1 %collective-permute-start.36 = (bf16[256,768]{1,0:T(8,128)(2,1)S(1)}, bf16[256,768]{1,0:T(8,128)(2,1)S(1)}, u32[]{:S(2)}, u32[]{:S(2)}) collective-permute-start(bf16[256,768]{1,0:T(8,128)(2,1)S(1)} %add_convert_fusion.1), channel_id=1, source_target_pairs={{0,4},{1,5},{2,6},{3,7},{64,68},{65,69},{66,70},{67,71},{16,20},{1... | collective-permute-start | bytes 1179656 | tf_op jit(solution)/shard_map/ppermute | solution.py:43
  153.5 8.9 %collective-permute-start.29 = (bf16[256,512]{1,0:T(8,128)(2,1)S(1)}, bf16[256,512]{1,0:T(8,128)(2,1)S(1)}, u32[]{:S(2)}, u32[]{:S(2)}) collective-permute-start(bf16[256,512]{1,0:T(8,128)(2,1)S(1)} %add_convert_fusion.8), channel_id=1, source_target_pairs={{0,48},{1,49},{2,50},{3,51},{64,112},{65,113},{66,114},{67,115},{1... | collective-permute-start | bytes 786440 | tf_op jit(solution)/shard_map/ppermute | solution.py:43
  155.2 7.7 %collective-permute-start.28 = (bf16[256,512]{1,0:T(8,128)(2,1)S(1)}, bf16[256,512]{1,0:T(8,128)(2,1)S(1)}, u32[]{:S(2)}, u32[]{:S(2)}) collective-permute-start(bf16[256,512]{1,0:T(8,128)(2,1)S(1)} %add_convert_fusion.9), channel_id=1, source_target_pairs={{0,16},{1,17},{2,18},{3,19},{64,80},{65,81},{66,82},{67,83},{16,0}... | collective-permute-start | bytes 786440 | tf_op jit(solution)/shard_map/ppermute | solution.py:43
  155.4 11.8 %collective-permute-start.35 = (bf16[256,768]{1,0:T(8,128)(2,1)S(1)}, bf16[256,768]{1,0:T(8,128)(2,1)S(1)}, u32[]{:S(2)}, u32[]{:S(2)}) collective-permute-start(bf16[256,768]{1,0:T(8,128)(2,1)S(1)} %add_convert_fusion.2), channel_id=1, source_target_pairs={{0,12},{1,13},{2,14},{3,15},{64,76},{65,77},{66,78},{67,79},{16,28... | collective-permute-start | bytes 1179656 | tf_op jit(solution)/shard_map/ppermute | solution.py:43
  157.3 9.9 %copy-start.3 = (bf16[256,768]{1,0:T(8,128)(2,1)S(1)}, bf16[256,768]{1,0:T(8,128)(2,1)}, u32[]{:S(2)}) copy-start(bf16[256,768]{1,0:T(8,128)(2,1)} %copy-done.2) | copy-start | bytes 1179652
  157.3 9.9 %copy-start.5 = (bf16[256,768]{1,0:T(8,128)(2,1)S(1)}, bf16[256,768]{1,0:T(8,128)(2,1)}, u32[]{:S(2)}) copy-start(bf16[256,768]{1,0:T(8,128)(2,1)} %copy-done.4) | copy-start | bytes 1179652
  163.1 13.3 %collective-permute-start.30 = (bf16[256,512]{1,0:T(8,128)(2,1)S(1)}, bf16[256,512]{1,0:T(8,128)(2,1)S(1)}, u32[]{:S(2)}, u32[]{:S(2)}) collective-permute-start(bf16[256,512]{1,0:T(8,128)(2,1)S(1)} %select_convert_fusion.2), channel_id=1, source_target_pairs={{0,64},{1,65},{2,66},{3,67},{64,0},{65,1},{66,2},{67,3},{16,80},{1... | collective-permute-start | bytes 786440 | tf_op jit(solution)/shard_map/ppermute | solution.py:43
  167.1 3.6 %collective-permute-start.37 = (f32[1,512]{1,0:T(1,128)S(1)}, f32[1,512]{1,0:T(1,128)S(1)}, u32[]{:S(2)}, u32[]{:S(2)}) collective-permute-start(f32[1,512]{1,0:T(1,128)S(1)} %add.217), channel_id=1, source_target_pairs={{0,4},{1,5},{2,6},{3,7},{64,68},{65,69},{66,70},{67,71},{16,20},{1... | collective-permute-start | bytes 6152 | tf_op jit(solution)/shard_map/ppermute | solution.py:43
  170.7 5.1 %collective-permute-start.38 = (f32[1,512]{1,0:T(1,128)S(1)}, f32[1,512]{1,0:T(1,128)S(1)}, u32[]{:S(2)}, u32[]{:S(2)}) collective-permute-start(f32[1,512]{1,0:T(1,128)S(1)} %add.220), channel_id=1, source_target_pairs={{0,8},{1,9},{2,10},{3,11},{64,72},{65,73},{66,74},{67,75},{16,24},... | collective-permute-start | bytes 6152 | tf_op jit(solution)/shard_map/ppermute | solution.py:43
  (23 other events, 32.0 us)

commit v9 on v5

--- a/solution.py
+++ b/solution.py
@@ -337,13 +337,14 @@
     )
     down_last = lax.optimization_barrier((*down_last, pair_terms[0]))[:2]
     pair_terms = lax.optimization_barrier((*pair_terms, *down_last))[:6]
-    pair_got, pair_out, pair_last = halve(pair_terms, "x")
-    d_w_gate, d_w_up = finish(pair_terms, pair_got, pair_last)
     down = finish(down_terms, down_got, down_last, (pair_terms[0],))
     d_w_down = jnp.concatenate(down, axis=1)
     lower = z_lo == 0
     theirs = jnp.where(lower, d_w_down[256:], d_w_down[:256]).astype(bf16)
-    d_w_down = jnp.where(lower, d_w_down[:256], d_w_down[256:]) + send(theirs, "z^1").astype(f32)
+    down_z = send(theirs, "z^1")
+    pair_got, pair_out, pair_last = halve(pair_terms, "x", (down_z,))
+    d_w_gate, d_w_up = finish(pair_terms, pair_got, pair_last)
+    d_w_down = jnp.where(lower, d_w_down[:256], d_w_down[256:]) + down_z.astype(f32)
 
     _, d_last = second_step(d_terms, d_got, "y", (pair_terms[0],))
     d_low, d_high = finish(d_terms, d_got, d_last)
@@ -351,8 +352,8 @@
     low, high = finish(branch_terms, branch_got, branch_last)
     upper = z_hi == 1
     mine = jnp.where(upper, d_high, d_low)
-    theirs = send(jnp.where(upper, d_low, d_high).astype(bf16), "z+2")
-    mine = mine + theirs.astype(f32)
+    theirs = send(after(jnp.where(upper, d_low, d_high).astype(bf16), *pair_got), "z+2")
+    mine = after(mine, *pair_got) + theirs.astype(f32)
     theirs = send(after(jnp.where(upper, low, high).astype(bf16), theirs), "z+2")
     branch = (jnp.where(upper, high, low) + theirs.astype(f32)).astype(bf16)
     d_normed, products = mine[:, :512], mine[:, 512:513] / width
@@ -362,7 +363,7 @@
     d_gain = jnp.sum(d_normed * x_own, axis=0, keepdims=True)
     for move in ("c", "z^1", "x^1", "x+2"):
         if move == "x^1":
-            d_gain = after(d_gain, *pair_out)
+            d_gain = after(d_gain, *pair_last)
         d_gain = d_gain + send(d_gain, move)
 
     gain_rows = lax.dynamic_slice(gains, (0, s * 256), (1, 256)).astype(f32).reshape(256, 1)

time: 171 us -> 167 us (0.977)
  waiting for transfers between devices: 68.3 us -> 64.1 us
  local copies, waits for them, and re-layouts: 6.48 us -> 9.1 us
    ppermute x40, waiting for transfers between devices: 68.3 us -> 64.1 us  [send(): return lax.ppermute(value, AXES, pairs(moves[move]))]
    unnamed x72 -> x82, local copies, waits for them, and re-layouts: 5.46 us -> 8.08 us
  transfers between devices with their start and end apart: 40 -> 40, of which waited for: 21 -> 23; matrix products, arithmetic and copies ran while one was open for 6% -> 6% of each run, Pallas kernels for 18% -> 19%
where the time goes in v9:
time: 167 us
  waiting for transfers between devices  64.1 us (38%)
  starting transfers between devices  42.2 us (25%)
  Pallas kernels  38.4 us (23%)
  other arithmetic  12.1 us (7%)
  local copies, waits for them, and re-layouts  9.1 us (5%)
    ppermute x40, waiting for transfers between devices, send(): return lax.ppermute(value, AXES, pairs(moves[move]))  64.1 us
    ppermute x40, starting transfers between devices, send(): return lax.ppermute(value, AXES, pairs(moves[move]))  42.2 us
    pallas_call x7, Pallas kernels, call(): pl.pallas_call(whole, in_specs=[pl.BlockSpec(memory_space=space) for spac...  38.4 us
    unnamed x82, local copies, waits for them, and re-layouts  8.08 us
  transfers between devices with their start and end apart: 40, of which 23 were waited for; matrix products, arithmetic and copies ran while one was open for 6% of the time, Pallas kernels for 19%

profile of v9, /device:TPU:0, one launch (start us, length us, event | category | flops | bytes accessed | tf_op | source)
XLA Modules:
  0.0 167.1 jit_solution(13688230914726682422)
XLA Ops:
  1.3 1.0 pad_maximum_fusion.6.refs_1_
  2.3 3.2 %collective-permute-start.1 = (bf16[272,512]{1,0:T(8,128)(2,1)S(1)}, bf16[272,512]{1,0:T(8,128)(2,1)S(1)}, u32[]{:S(2)}, u32[]{:S(2)}) collective-permute-start(bf16[272,512]{1,0:T(8,128)(2,1)S(1)} %pad_maximum_fusion.6.refs_1_), channel_id=1, source_target_pairs={{0,48},{1,49},{2,50},{3,51},{64,112},{65,113},{66,114},{67,115},{1... | collective-permute-start | bytes 835592 | tf_op jit(solution)/shard_map/ppermute | solution.py:43
  5.5 3.9 %collective-permute-start.2 = (bf16[272,512]{1,0:T(8,128)(2,1)S(1)}, bf16[272,512]{1,0:T(8,128)(2,1)S(1)}, u32[]{:S(2)}, u32[]{:S(2)}) collective-permute-start(bf16[272,512]{1,0:T(8,128)(2,1)S(1)} %pad_maximum_fusion.6.refs_1_), channel_id=1, source_target_pairs={{0,64},{1,65},{2,66},{3,67},{64,0},{65,1},{66,2},{67,3},{16,80},{1... | collective-permute-start | bytes 835592 | tf_op jit(solution)/shard_map/ppermute | solution.py:43
  9.4 2.0 %collective-permute-done.1.refs_3_ = bf16[272,512]{1,0:T(8,128)(2,1)S(1)} collective-permute-done((bf16[272,512]{1,0:T(8,128)(2,1)S(1)}, bf16[272,512]{1,0:T(8,128)(2,1)S(1)}, u32[]{:S(2)}, u32[]{:S(2)}) %collective-permute-start.1) | collective-permute-done | bytes 278560 | tf_op jit(solution)/shard_map/ppermute | solution.py:43
  11.4 4.3 %collective-permute-done.2.refs_4_ = bf16[272,512]{1,0:T(8,128)(2,1)S(1)} collective-permute-done((bf16[272,512]{1,0:T(8,128)(2,1)S(1)}, bf16[272,512]{1,0:T(8,128)(2,1)S(1)}, u32[]{:S(2)}, u32[]{:S(2)}) %collective-permute-start.2) | collective-permute-done | bytes 278560 | tf_op jit(solution)/shard_map/ppermute | solution.py:43
  15.8 0.8 collective-permute-start.4
  16.6 1.8 %collective-permute-done.refs_2_ = bf16[272,512]{1,0:T(8,128)(2,1)S(1)} collective-permute-done((bf16[272,512]{1,0:T(8,128)(2,1)S(1)}, bf16[272,512]{1,0:T(8,128)(2,1)S(1)}, u32[]{:S(2)}, u32[]{:S(2)}) %collective-permute-start) | collective-permute-done | bytes 278560 | tf_op jit(solution)/shard_map/ppermute | solution.py:43
  18.6 2.7 %collective-permute-start.5 = (bf16[256,512]{1,0:T(8,128)(2,1)S(1)}, bf16[256,512]{1,0:T(8,128)(2,1)S(1)}, u32[]{:S(2)}, u32[]{:S(2)}) collective-permute-start(bf16[256,512]{1,0:T(8,128)(2,1)S(1)} %copy-done.38), channel_id=1, source_target_pairs={{0,64},{1,65},{2,66},{3,67},{64,0},{65,1},{66,2},{67,3},{16,80},{1... | collective-permute-start | bytes 786440 | tf_op jit(solution)/shard_map/ppermute | solution.py:43
  21.3 5.5 %collective-permute-done.5 = bf16[256,512]{1,0:T(8,128)(2,1)S(1)} collective-permute-done((bf16[256,512]{1,0:T(8,128)(2,1)S(1)}, bf16[256,512]{1,0:T(8,128)(2,1)S(1)}, u32[]{:S(2)}, u32[]{:S(2)}) %collective-permute-start.5) | collective-permute-done | bytes 262176 | tf_op jit(solution)/shard_map/ppermute | solution.py:43
  26.7 2.7 %collective-permute-done.3.refs_5_ = bf16[400,512]{1,0:T(8,128)(2,1)S(1)} collective-permute-done((bf16[400,512]{1,0:T(8,128)(2,1)S(1)}, bf16[400,512]{1,0:T(8,128)(2,1)S(1)}, u32[]{:S(2)}, u32[]{:S(2)}) %collective-permute-start.3) | collective-permute-done | bytes 409632 | tf_op jit(solution)/shard_map/ppermute | solution.py:43
  29.8 0.7 pad_maximum_fusion.7
  30.5 1.6 collective-permute-start.6
  32.2 1.5 collective-permute-start.7
  33.8 5.1 %collective-permute-done.6.refs_7_ = bf16[272,512]{1,0:T(8,128)(2,1)} collective-permute-done((bf16[272,512]{1,0:T(8,128)(2,1)}, bf16[272,512]{1,0:T(8,128)(2,1)}, u32[]{:S(2)}, u32[]{:S(2)}) %collective-permute-start.6) | collective-permute-done | bytes 278560 | tf_op jit(solution)/shard_map/ppermute | solution.py:43
  38.9 1.4 assemble.1
  40.4 0.9 copy-done.23
  41.2 1.8 %collective-permute-start.9 = (bf16[256,1024]{1,0:T(8,128)(2,1)S(1)}, bf16[256,1024]{1,0:T(8,128)(2,1)S(1)}, u32[]{:S(2)}, u32[]{:S(2)}) collective-permute-start(bf16[256,1024]{1,0:T(8,128)(2,1)S(1)} %get-tuple-element.101), channel_id=1, source_target_pairs={{0,66},{1,67},{2,64},{3,65},{64,2},{65,3},{66,0},{67,1},{16,82},{1... | collective-permute-start | bytes 1572872 | tf_op jit(solution)/shard_map/ppermute | solution.py:43
  43.6 0.8 collective-permute-done.7.refs_2_
  44.4 0.9 collective-permute-start.11
  45.3 6.3 %forward.1 = (f32[256,768]{1,0:T(8,128)S(1)}, f32[256,768]{1,0:T(8,128)S(1)}, bf16[256,768]{1,0:T(8,128)(2,1)S(1)}, f32[256,128]{1,0:T(8,128)S(1)}, bf16[256,1792]{1,0:T(8,128)(2,1)}) custom-call(bf16[272,4096]{1,0:T(8,128)(2,1)S(1)} %get-tuple-element.98.refs_0_, bf16[256,1024]{1,0:T(8,128)(2,1)S(1)} %get-tuple-element.99.refs_1_, ...), custom_call_target="tpu_custom_call" | custom-call | flops 3221225472 | bytes 16777216 | tf_op jit(solution)/shard_map/forward/pallas_call | solution.py:89
  52.3 0.8 copy-done.25
  53.1 0.8 copy-done.36
  53.9 6.8 %backward.1 = (bf16[256,1536]{1,0:T(8,128)(2,1)S(1)}, bf16[256,128]{1,0:T(8,128)(2,1)S(1)}, bf16[256,2048]{1,0:T(8,128)(2,1)S(1)}, bf16[256,3584]{1,0:T(8,128)(2,1)}) custom-call(s32[10]{0:T(128)S(1)} %stack.116.refs_0_, bf16[512,512]{1,0:T(8,128)(2,1)S(1)} %pad_maximum_fusion.3.refs_1_, bf16[512,512]{1,0:T(8,128)(2,1)S(1)} %collective-permute-done.7.refs_2_, ...), custom_call_target="tpu_custom_call" | custom-call | flops 1610612736 | bytes 8388608 | tf_op jit(solution)/shard_map/backward/pallas_call | solution.py:89
  61.3 1.0 copy-done.19
  63.0 1.5 collective-permute-start.16
  64.5 5.2 %branch_rows.1 = (bf16[512,512]{1,0:T(8,128)(2,1)S(1)}, bf16[512,512]{1,0:T(8,128)(2,1)S(1)}, bf16[256,512]{1,0:T(8,128)(2,1)S(1)}, bf16[256,512]{1,0:T(8,128)(2...) custom-call(s32[8]{0:T(128)S(1)} %stack.105.refs_0_, ...), custom_call_target="tpu_custom_call" | custom-call | flops 1610612736 | bytes 8388608 | tf_op jit(solution)/shard_map/branch_rows/pallas_call | solution.py:89
  70.4 0.7 copy-done.14
  71.1 1.0 copy-done.3
  72.1 4.8 %down_terms.1 = (bf16[1024,384]{1,0:T(8,128)(2,1)S(1)}, bf16[1024,384]{1,0:T(8,128)(2,1)S(1)}, bf16[512,384]{1,0:T(8,128)(2,1)S(1)}, bf16[512,384]{1,0:T(8,128)(...) custom-call(s32[8]{0:T(128)S(1)} %stack.121.refs_0_, bf16[256,2048]{1,0:T(8,128)(2,1)S(1)} %copy-done.20, ...), custom_call_target="tpu_custom_call" | custom-call | flops 1610612736 | bytes 8388608 | tf_op jit(solution)/shard_map/down_terms/pallas_call | solution.py:89
  76.9 2.8 %collective-permute-start.19 = (bf16[1024,384]{1,0:T(8,128)(2,1)S(1)}, bf16[1024,384]{1,0:T(8,128)(2,1)S(1)}, u32[]{:S(2)}, u32[]{:S(2)}) collective-permute-start(bf16[1024,384]{1,0:T(8,128)(2,1)S(1)} %get-tuple-element.131), channel_id=1, source_target_pairs={{0,12},{1,13},{2,14},{3,15},{64,76},{65,77},{66,78},{67,79},{16,28... | collective-permute-start | bytes 2359304 | tf_op jit(solution)/shard_map/ppermute | solution.py:43
  79.9 1.7 collective-permute-start.13
  81.6 7.1 %pair_rows.1 = (bf16[512,640]{1,0:T(8,128)(2,1)S(1)}, bf16[512,640]{1,0:T(8,128)(2,1)S(1)}, bf16[256,640]{1,0:T(8,128)(2,1)S(1)}, bf16[256,640]{1,0:T(8,128)(2,1...) custom-call(s32[8]{0:T(128)S(1)} %stack.105.refs_0_, ...), custom_call_target="tpu_custom_call" | custom-call | flops 3221225472 | bytes 16777216 | tf_op jit(solution)/shard_map/pair_rows/pallas_call | solution.py:89
  88.7 0.7 copy-done.6
  89.5 0.7 copy-done.8
  90.2 4.0 %collective-permute-done.13 = bf16[512,512]{1,0:T(8,128)(2,1)S(1)} collective-permute-done((bf16[512,512]{1,0:T(8,128)(2,1)S(1)}, bf16[512,512]{1,0:T(8,128)(2,1)S(1)}, u32[]{:S(2)}, u32[]{:S(2)}) %collective-permute-start.13) | collective-permute-done | bytes 524320 | tf_op jit(solution)/shard_map/ppermute | solution.py:43
  94.4 2.9 %collective-permute-done.19 = bf16[1024,384]{1,0:T(8,128)(2,1)S(1)} collective-permute-done((bf16[1024,384]{1,0:T(8,128)(2,1)S(1)}, bf16[1024,384]{1,0:T(8,128)(2,1)S(1)}, u32[]{:S(2)}, u32[]{:S(2)}) %collective-permute-start.19) | collective-permute-done | bytes 786464 | tf_op jit(solution)/shard_map/ppermute | solution.py:43
  97.4 1.2 collective-permute-done.18
  98.6 1.2 pad_maximum_fusion
  100.6 1.5 collective-permute-start.23
  102.8 1.1 add_convert_fusion.3
  104.2 1.1 add_convert_fusion.4
  105.3 1.7 %collective-permute-start.21 = (bf16[512,384]{1,0:T(8,128)(2,1)S(1)}, bf16[512,384]{1,0:T(8,128)(2,1)S(1)}, u32[]{:S(2)}, u32[]{:S(2)}) collective-permute-start(bf16[512,384]{1,0:T(8,128)(2,1)S(1)} %add_convert_fusion.4), channel_id=1, source_target_pairs={{0,12},{1,13},{2,14},{3,15},{64,76},{65,77},{66,78},{67,79},{16,28... | collective-permute-start | bytes 1179656 | tf_op jit(solution)/shard_map/ppermute | solution.py:43
  107.8 6.8 %pair_terms.1 = (bf16[512,768]{1,0:T(8,128)(2,1)S(1)}, bf16[512,768]{1,0:T(8,128)(2,1)S(1)}, bf16[256,768]{1,0:T(8,128)(2,1)S(1)}, bf16[256,768]{1,0:T(8,128)(2,...) custom-call(s32[8]{0:T(128)S(1)} %stack.121.refs_0_, bf16[256,1024]{1,0:T(8,128)(2,1)S(1)} %copy-done.24, ...), custom_call_target="tpu_custom_call" | custom-call | flops 3221225472 | bytes 8388608 | tf_op jit(solution)/shard_map/pair_terms/pallas_call | solution.py:89
  114.9 2.6 %collective-permute-done.21 = bf16[512,384]{1,0:T(8,128)(2,1)S(1)} collective-permute-done((bf16[512,384]{1,0:T(8,128)(2,1)S(1)}, bf16[512,384]{1,0:T(8,128)(2,1)S(1)}, u32[]{:S(2)}, u32[]{:S(2)}) %collective-permute-start.21) | collective-permute-done | bytes 393248 | tf_op jit(solution)/shard_map/ppermute | solution.py:43
  118.0 2.3 %collective-permute-done.24 = bf16[512,640]{1,0:T(8,128)(2,1)S(1)} collective-permute-done((bf16[512,640]{1,0:T(8,128)(2,1)}, bf16[512,640]{1,0:T(8,128)(2,1)S(1)}, u32[]{:S(2)}, u32[]{:S(2)}) %collective-permute-start.24) | collective-permute-done | bytes 655392 | tf_op jit(solution)/shard_map/ppermute | solution.py:43
  120.6 1.0 collective-permute-start.25
  122.1 0.8 collective-permute-start.35
  122.9 1.7 %collective-permute-start.30 = (bf16[512,768]{1,0:T(8,128)(2,1)S(1)}, bf16[512,768]{1,0:T(8,128)(2,1)S(1)}, u32[]{:S(2)}, u32[]{:S(2)}) collective-permute-start(bf16[512,768]{1,0:T(8,128)(2,1)S(1)} %get-tuple-element.164), channel_id=1, source_target_pairs={{0,12},{1,13},{2,14},{3,15},{64,76},{65,77},{66,78},{67,79},{16,28... | collective-permute-start | bytes 2359304 | tf_op jit(solution)/shard_map/ppermute | solution.py:43
  124.7 4.8 %collective-permute-done.26 = bf16[256,640]{1,0:T(8,128)(2,1)S(1)} collective-permute-done((bf16[256,640]{1,0:T(8,128)(2,1)S(1)}, bf16[256,640]{1,0:T(8,128)(2,1)S(1)}, u32[]{:S(2)}, u32[]{:S(2)}) %collective-permute-start.26) | collective-permute-done | bytes 327712 | tf_op jit(solution)/shard_map/ppermute | solution.py:43
  129.5 1.4 collective-permute-done.25
  131.0 0.8 collective-permute-start.28
  132.3 9.8 %collective-permute-done.30 = bf16[512,768]{1,0:T(8,128)(2,1)S(1)} collective-permute-done((bf16[512,768]{1,0:T(8,128)(2,1)S(1)}, bf16[512,768]{1,0:T(8,128)(2,1)S(1)}, u32[]{:S(2)}, u32[]{:S(2)}) %collective-permute-start.30) | collective-permute-done | bytes 786464 | tf_op jit(solution)/shard_map/ppermute | solution.py:43
  142.2 2.2 %collective-permute-start.31 = (bf16[256,640]{1,0:T(8,128)(2,1)S(1)}, bf16[256,640]{1,0:T(8,128)(2,1)S(1)}, u32[]{:S(2)}, u32[]{:S(2)}) collective-permute-start(bf16[256,640]{1,0:T(8,128)(2,1)S(1)} %get-tuple-element.165), channel_id=1, source_target_pairs={{0,64},{1,65},{2,66},{3,67},{64,0},{65,1},{66,2},{67,3},{16,80},{1... | collective-permute-start | bytes 983048 | tf_op jit(solution)/shard_map/ppermute | solution.py:43
  144.8 1.9 %collective-permute-start.36 = (bf16[256,768]{1,0:T(8,128)(2,1)S(1)}, bf16[256,768]{1,0:T(8,128)(2,1)S(1)}, u32[]{:S(2)}, u32[]{:S(2)}) collective-permute-start(bf16[256,768]{1,0:T(8,128)(2,1)S(1)} %add_convert_fusion.2), channel_id=1, source_target_pairs={{0,12},{1,13},{2,14},{3,15},{64,76},{65,77},{66,78},{67,79},{16,28... | collective-permute-start | bytes 1179656 | tf_op jit(solution)/shard_map/ppermute | solution.py:43
  146.6 4.4 %collective-permute-done.31 = bf16[256,640]{1,0:T(8,128)(2,1)S(1)} collective-permute-done((bf16[256,640]{1,0:T(8,128)(2,1)S(1)}, bf16[256,640]{1,0:T(8,128)(2,1)S(1)}, u32[]{:S(2)}, u32[]{:S(2)}) %collective-permute-start.31) | collective-permute-done | bytes 327712 | tf_op jit(solution)/shard_map/ppermute | solution.py:43
  151.2 0.9 fusion.3
  152.2 1.0 collective-permute-done.33
  153.2 1.2 collective-permute-start.34
  154.6 2.1 %collective-permute-start.32 = (bf16[256,512]{1,0:T(8,128)(2,1)S(1)}, bf16[256,512]{1,0:T(8,128)(2,1)S(1)}, u32[]{:S(2)}, u32[]{:S(2)}) collective-permute-start(bf16[256,512]{1,0:T(8,128)(2,1)S(1)} %select_convert_fusion.2), channel_id=1, source_target_pairs={{0,64},{1,65},{2,66},{3,67},{64,0},{65,1},{66,2},{67,3},{16,80},{1... | collective-permute-start | bytes 786440 | tf_op jit(solution)/shard_map/ppermute | solution.py:43
  157.3 3.2 %collective-permute-done.38 = f32[1,512]{1,0:T(1,128)S(1)} collective-permute-done((f32[1,512]{1,0:T(1,128)S(1)}, f32[1,512]{1,0:T(1,128)S(1)}, u32[]{:S(2)}, u32[]{:S(2)}) %collective-permute-start.38) | collective-permute-done | bytes 2080 | tf_op jit(solution)/shard_map/ppermute | solution.py:43
  160.5 1.2 collective-permute-start.39
  161.7 1.1 pad_maximum_fusion.1
  162.9 2.8 %collective-permute-done.39 = f32[1,512]{1,0:T(1,128)S(1)} collective-permute-done((f32[1,512]{1,0:T(1,128)S(1)}, f32[1,512]{1,0:T(1,128)S(1)}, u32[]{:S(2)}, u32[]{:S(2)}) %collective-permute-start.39) | collective-permute-done | bytes 2080 | tf_op jit(solution)/shard_map/ppermute | solution.py:43
  166.2 0.9 add_convert_fusion.7
  (148 shorter events, 11.5 us)
Async XLA Ops:
  1.3 17.2 %copy-start.38 = (bf16[256,512]{1,0:T(8,128)(2,1)S(1)}, bf16[256,512]{1,0:T(8,128)(2,1)}, u32[]{:S(2)}) copy-start(bf16[256,512]{1,0:T(8,128)(2,1)} %param.7) | copy-start | bytes 786436
  2.3 9.1 %collective-permute-start.1 = (bf16[272,512]{1,0:T(8,128)(2,1)S(1)}, bf16[272,512]{1,0:T(8,128)(2,1)S(1)}, u32[]{:S(2)}, u32[]{:S(2)}) collective-permute-start(bf16[272,512]{1,0:T(8,128)(2,1)S(1)} %pad_maximum_fusion.6.refs_1_), channel_id=1, source_target_pairs={{0,48},{1,49},{2,50},{3,51},{64,112},{65,113},{66,114},{67,115},{1... | collective-permute-start | bytes 835592 | tf_op jit(solution)/shard_map/ppermute | solution.py:43
  5.5 10.2 %collective-permute-start.2 = (bf16[272,512]{1,0:T(8,128)(2,1)S(1)}, bf16[272,512]{1,0:T(8,128)(2,1)S(1)}, u32[]{:S(2)}, u32[]{:S(2)}) collective-permute-start(bf16[272,512]{1,0:T(8,128)(2,1)S(1)} %pad_maximum_fusion.6.refs_1_), channel_id=1, source_target_pairs={{0,64},{1,65},{2,66},{3,67},{64,0},{65,1},{66,2},{67,3},{16,80},{1... | collective-permute-start | bytes 835592 | tf_op jit(solution)/shard_map/ppermute | solution.py:43
  9.4 9.0 %collective-permute-start = (bf16[272,512]{1,0:T(8,128)(2,1)S(1)}, bf16[272,512]{1,0:T(8,128)(2,1)S(1)}, u32[]{:S(2)}, u32[]{:S(2)}) collective-permute-start(bf16[272,512]{1,0:T(8,128)(2,1)S(1)} %pad_maximum_fusion.6.refs_1_), channel_id=1, source_target_pairs={{0,16},{1,17},{2,18},{3,19},{64,80},{65,81},{66,82},{67,83},{16,32... | collective-permute-start | bytes 835592 | tf_op jit(solution)/shard_map/ppermute | solution.py:43
  15.8 13.7 %collective-permute-start.4 = (bf16[416,512]{1,0:T(8,128)(2,1)S(1)}, bf16[416,512]{1,0:T(8,128)(2,1)S(1)}, u32[]{:S(2)}, u32[]{:S(2)}) collective-permute-start(bf16[416,512]{1,0:T(8,128)(2,1)S(1)} %pad_maximum_fusion.4), channel_id=1, source_target_pairs={{0,48},{1,49},{2,50},{3,51},{64,112},{65,113},{66,114},{67,115},{1... | collective-permute-start | bytes 1277960 | tf_op jit(solution)/shard_map/ppermute | solution.py:43
  18.5 11.0 %collective-permute-start.3 = (bf16[400,512]{1,0:T(8,128)(2,1)S(1)}, bf16[400,512]{1,0:T(8,128)(2,1)S(1)}, u32[]{:S(2)}, u32[]{:S(2)}) collective-permute-start(bf16[400,512]{1,0:T(8,128)(2,1)S(1)} %pad_maximum_fusion.5), channel_id=1, source_target_pairs={{0,16},{1,17},{2,18},{3,19},{64,80},{65,81},{66,82},{67,83},{16,32... | collective-permute-start | bytes 1228808 | tf_op jit(solution)/shard_map/ppermute | solution.py:43
  18.6 8.1 %collective-permute-start.5 = (bf16[256,512]{1,0:T(8,128)(2,1)S(1)}, bf16[256,512]{1,0:T(8,128)(2,1)S(1)}, u32[]{:S(2)}, u32[]{:S(2)}) collective-permute-start(bf16[256,512]{1,0:T(8,128)(2,1)S(1)} %copy-done.38), channel_id=1, source_target_pairs={{0,64},{1,65},{2,66},{3,67},{64,0},{65,1},{66,2},{67,3},{16,80},{1... | collective-permute-start | bytes 786440 | tf_op jit(solution)/shard_map/ppermute | solution.py:43
  29.5 13.6 %collective-permute-start.8 = (bf16[512,512]{1,0:T(8,128)(2,1)S(1)}, bf16[512,512]{1,0:T(8,128)(2,1)S(1)}, u32[]{:S(2)}, u32[]{:S(2)}) collective-permute-start(bf16[512,512]{1,0:T(8,128)(2,1)S(1)} %pad_maximum_fusion.3.refs_1_), channel_id=1, source_target_pairs={{0,48},{1,49},{2,50},{3,51},{64,112},{65,113},{66,114},{67,115},{1... | collective-permute-start | bytes 1572872 | tf_op jit(solution)/shard_map/ppermute | solution.py:43
  30.5 8.4 %collective-permute-start.6 = (bf16[272,512]{1,0:T(8,128)(2,1)}, bf16[272,512]{1,0:T(8,128)(2,1)}, u32[]{:S(2)}, u32[]{:S(2)}) collective-permute-start(bf16[272,512]{1,0:T(8,128)(2,1)} %pad_maximum_fusion.7), channel_id=1, source_target_pairs={{0,64},{1,65},{2,66},{3,67},{64,0},{65,1},{66,2},{67,3},{16,80},{1... | collective-permute-start | bytes 835592 | tf_op jit(solution)/shard_map/ppermute | solution.py:43
  32.2 12.2 %collective-permute-start.7 = (bf16[512,512]{1,0:T(8,128)(2,1)S(1)}, bf16[512,512]{1,0:T(8,128)(2,1)S(1)}, u32[]{:S(2)}, u32[]{:S(2)}) collective-permute-start(bf16[512,512]{1,0:T(8,128)(2,1)S(1)} %pad_maximum_fusion.3.refs_1_), channel_id=1, source_target_pairs={{0,16},{1,17},{2,18},{3,19},{64,80},{65,81},{66,82},{67,83},{16,32... | collective-permute-start | bytes 1572872 | tf_op jit(solution)/shard_map/ppermute | solution.py:43
  41.2 11.0 %collective-permute-start.9 = (bf16[256,1024]{1,0:T(8,128)(2,1)S(1)}, bf16[256,1024]{1,0:T(8,128)(2,1)S(1)}, u32[]{:S(2)}, u32[]{:S(2)}) collective-permute-start(bf16[256,1024]{1,0:T(8,128)(2,1)S(1)} %get-tuple-element.101), channel_id=1, source_target_pairs={{0,66},{1,67},{2,64},{3,65},{64,2},{65,3},{66,0},{67,1},{16,82},{1... | collective-permute-start | bytes 1572872 | tf_op jit(solution)/shard_map/ppermute | solution.py:43
  43.0 10.0 %collective-permute-start.10 = (bf16[256,1024]{1,0:T(8,128)(2,1)S(1)}, bf16[256,1024]{1,0:T(8,128)(2,1)S(1)}, u32[]{:S(2)}, u32[]{:S(2)}) collective-permute-start(bf16[256,1024]{1,0:T(8,128)(2,1)S(1)} %get-tuple-element.102), channel_id=1, source_target_pairs={{0,2},{1,3},{2,0},{3,1},{64,66},{65,67},{66,64},{67,65},{16,18},{1... | collective-permute-start | bytes 1572872 | tf_op jit(solution)/shard_map/ppermute | solution.py:43
  43.1 10.0 %collective-permute-start.12 = (bf16[256,512]{1,0:T(8,128)(2,1)S(1)}, bf16[256,512]{1,0:T(8,128)(2,1)S(1)}, u32[]{:S(2)}, u32[]{:S(2)}) collective-permute-start(bf16[256,512]{1,0:T(8,128)(2,1)S(1)} %pad_maximum_fusion.9), channel_id=1, source_target_pairs={{0,48},{1,49},{2,50},{3,51},{64,112},{65,113},{66,114},{67,115},{1... | collective-permute-start | bytes 786440 | tf_op jit(solution)/shard_map/ppermute | solution.py:43
  44.4 8.6 %collective-permute-start.11 = (bf16[256,512]{1,0:T(8,128)(2,1)S(1)}, bf16[256,512]{1,0:T(8,128)(2,1)S(1)}, u32[]{:S(2)}, u32[]{:S(2)}) collective-permute-start(bf16[256,512]{1,0:T(8,128)(2,1)S(1)} %pad_maximum_fusion.8), channel_id=1, source_target_pairs={{0,16},{1,17},{2,18},{3,19},{64,80},{65,81},{66,82},{67,83},{16,32... | collective-permute-start | bytes 786440 | tf_op jit(solution)/shard_map/ppermute | solution.py:43
  51.7 12.8 %copy-start.2 = (bf16[256,768]{1,0:T(8,128)(2,1)}, bf16[256,768]{1,0:T(8,128)(2,1)S(1)}, u32[]{:S(2)}) copy-start(bf16[256,768]{1,0:T(8,128)(2,1)S(1)} %get-tuple-element.108.refs_1_.refs_3_) | copy-start | bytes 1179652
  62.3 8.8 %collective-permute-start.17 = (bf16[256,3584]{1,0:T(8,128)(2,1)}, bf16[256,3584]{1,0:T(8,128)(2,1)}, u32[]{:S(2)}, u32[]{:S(2)}) collective-permute-start(bf16[256,3584]{1,0:T(8,128)(2,1)} %get-tuple-element.120), channel_id=1, source_target_pairs={{0,1},{1,0},{2,3},{3,2},{64,65},{65,64},{66,67},{67,66},{16,17},{1... | collective-permute-start | bytes 5505032 | tf_op jit(solution)/shard_map/ppermute | solution.py:43
  62.3 8.8 %collective-permute-start.15 = (bf16[256,1792]{1,0:T(8,128)(2,1)}, bf16[256,1792]{1,0:T(8,128)(2,1)}, u32[]{:S(2)}, u32[]{:S(2)}) collective-permute-start(bf16[256,1792]{1,0:T(8,128)(2,1)} %get-tuple-element.117), channel_id=1, source_target_pairs={{0,1},{1,0},{2,3},{3,2},{64,65},{65,64},{66,67},{67,66},{16,17},{1... | collective-permute-start | bytes 2752520 | tf_op jit(solution)/shard_map/ppermute | solution.py:43
  63.0 31.4 %collective-permute-start.16 = (bf16[256,1536]{1,0:T(8,128)(2,1)S(1)}, bf16[256,1536]{1,0:T(8,128)(2,1)S(1)}, u32[]{:S(2)}, u32[]{:S(2)}) collective-permute-start(bf16[256,1536]{1,0:T(8,128)(2,1)S(1)} %get-tuple-element.122.refs_1_.refs_5_), channel_id=1, source_target_pairs={{0,2},{1,3},{2,0},{3,1},{64,66},{65,67},{66,64},{67,65},{16,18},{1... | collective-permute-start | bytes 2359304 | tf_op jit(solution)/shard_map/ppermute | solution.py:43
  72.1 9.6 %copy-start.17 = (bf16[256,128]{1,0:T(8,128)(2,1)S(1)}, bf16[256,128]{1,0:T(8,128)(2,1)}, u32[]{:S(2)}) copy-start(bf16[256,128]{1,0:T(8,128)(2,1)} %copy-done.16) | copy-start | bytes 196612
  76.9 11.9 %copy-start = (bf16[512,384]{1,0:T(8,128)(2,1)}, bf16[512,384]{1,0:T(8,128)(2,1)S(1)}, u32[]{:S(2)}) copy-start(bf16[512,384]{1,0:T(8,128)(2,1)S(1)} %get-tuple-element.173) | copy-start | bytes 1179652
  76.9 20.5 %collective-permute-start.19 = (bf16[1024,384]{1,0:T(8,128)(2,1)S(1)}, bf16[1024,384]{1,0:T(8,128)(2,1)S(1)}, u32[]{:S(2)}, u32[]{:S(2)}) collective-permute-start(bf16[1024,384]{1,0:T(8,128)(2,1)S(1)} %get-tuple-element.131), channel_id=1, source_target_pairs={{0,12},{1,13},{2,14},{3,15},{64,76},{65,77},{66,78},{67,79},{16,28... | collective-permute-start | bytes 2359304 | tf_op jit(solution)/shard_map/ppermute | solution.py:43
  79.7 18.9 %collective-permute-start.18 = (bf16[1024,384]{1,0:T(8,128)(2,1)S(1)}, bf16[1024,384]{1,0:T(8,128)(2,1)S(1)}, u32[]{:S(2)}, u32[]{:S(2)}) collective-permute-start(bf16[1024,384]{1,0:T(8,128)(2,1)S(1)} %get-tuple-element.121), channel_id=1, source_target_pairs={{0,4},{1,5},{2,6},{3,7},{64,68},{65,69},{66,70},{67,71},{16,20},{1... | collective-permute-start | bytes 2359304 | tf_op jit(solution)/shard_map/ppermute | solution.py:43
  79.9 14.3 %collective-permute-start.13 = (bf16[512,512]{1,0:T(8,128)(2,1)S(1)}, bf16[512,512]{1,0:T(8,128)(2,1)S(1)}, u32[]{:S(2)}, u32[]{:S(2)}) collective-permute-start(bf16[512,512]{1,0:T(8,128)(2,1)S(1)} %get-tuple-element.112), channel_id=1, source_target_pairs={{0,48},{1,49},{2,50},{3,51},{64,112},{65,113},{66,114},{67,115},{1... | collective-permute-start | bytes 1572872 | tf_op jit(solution)/shard_map/ppermute | solution.py:43
  81.6 12.8 %collective-permute-start.14 = (bf16[512,512]{1,0:T(8,128)(2,1)S(1)}, bf16[512,512]{1,0:T(8,128)(2,1)S(1)}, u32[]{:S(2)}, u32[]{:S(2)}) collective-permute-start(bf16[512,512]{1,0:T(8,128)(2,1)S(1)} %get-tuple-element.115), channel_id=1, source_target_pairs={{0,16},{1,17},{2,18},{3,19},{64,80},{65,81},{66,82},{67,83},{16,0}... | collective-permute-start | bytes 1572872 | tf_op jit(solution)/shard_map/ppermute | solution.py:43
  81.6 17.0 %copy-start.37 = (bf16[256,1024]{1,0:T(8,128)(2,1)S(1)}, bf16[256,1024]{1,0:T(8,128)(2,1)}, u32[]{:S(2)}) copy-start(bf16[256,1024]{1,0:T(8,128)(2,1)} %copy-done.36) | copy-start | bytes 1572868
  90.2 7.2 %copy-start.22 = (bf16[512,640]{1,0:T(8,128)(2,1)}, bf16[512,640]{1,0:T(8,128)(2,1)S(1)}, u32[]{:S(2)}) copy-start(bf16[512,640]{1,0:T(8,128)(2,1)S(1)} %get-tuple-element.150) | copy-start | bytes 1966084
  90.2 8.4 %copy-start.21 = (bf16[512,640]{1,0:T(8,128)(2,1)}, bf16[512,640]{1,0:T(8,128)(2,1)S(1)}, u32[]{:S(2)}) copy-start(bf16[512,640]{1,0:T(8,128)(2,1)S(1)} %get-tuple-element.130) | copy-start | bytes 1966084
  90.2 9.7 %copy-start.4 = (bf16[256,640]{1,0:T(8,128)(2,1)}, bf16[256,640]{1,0:T(8,128)(2,1)S(1)}, u32[]{:S(2)}) copy-start(bf16[256,640]{1,0:T(8,128)(2,1)S(1)} %get-tuple-element.162) | copy-start | bytes 983044
  90.2 9.7 %copy-start.10 = (bf16[256,640]{1,0:T(8,128)(2,1)}, bf16[256,640]{1,0:T(8,128)(2,1)S(1)}, u32[]{:S(2)}) copy-start(bf16[256,640]{1,0:T(8,128)(2,1)S(1)} %get-tuple-element.153) | copy-start | bytes 983044
  99.9 7.8 %collective-permute-start.20 = (bf16[256,2560]{1,0:T(8,128)(2,1)}, bf16[256,2560]{1,0:T(8,128)(2,1)}, u32[]{:S(2)}, u32[]{:S(2)}) collective-permute-start(bf16[256,2560]{1,0:T(8,128)(2,1)} %pad_maximum_fusion), channel_id=1, source_target_pairs={{0,1},{1,0},{2,3},{3,2},{64,65},{65,64},{66,67},{67,66},{16,17},{1... | collective-permute-start | bytes 3932168 | tf_op jit(solution)/shard_map/ppermute | solution.py:43
  100.6 7.2 %copy-start.24 = (bf16[256,1024]{1,0:T(8,128)(2,1)S(1)}, bf16[256,1024]{1,0:T(8,128)(2,1)}, u32[]{:S(2)}) copy-start(bf16[256,1024]{1,0:T(8,128)(2,1)} %copy-done.23) | copy-start | bytes 1572868
  100.6 7.2 %copy-start.26 = (bf16[256,1024]{1,0:T(8,128)(2,1)S(1)}, bf16[256,1024]{1,0:T(8,128)(2,1)}, u32[]{:S(2)}) copy-start(bf16[256,1024]{1,0:T(8,128)(2,1)} %copy-done.25) | copy-start | bytes 1572868
  100.6 19.8 %collective-permute-start.23 = (bf16[512,640]{1,0:T(8,128)(2,1)}, bf16[512,640]{1,0:T(8,128)(2,1)S(1)}, u32[]{:S(2)}, u32[]{:S(2)}) collective-permute-start(bf16[512,640]{1,0:T(8,128)(2,1)} %copy-done.21), channel_id=1, source_target_pairs={{0,16},{1,17},{2,18},{3,19},{64,80},{65,81},{66,82},{67,83},{16,0}... | collective-permute-start | bytes 1966088 | tf_op jit(solution)/shard_map/ppermute | solution.py:43
  102.1 18.3 %collective-permute-start.24 = (bf16[512,640]{1,0:T(8,128)(2,1)}, bf16[512,640]{1,0:T(8,128)(2,1)S(1)}, u32[]{:S(2)}, u32[]{:S(2)}) collective-permute-start(bf16[512,640]{1,0:T(8,128)(2,1)} %copy-done.22), channel_id=1, source_target_pairs={{0,48},{1,49},{2,50},{3,51},{64,112},{65,113},{66,114},{67,115},{1... | collective-permute-start | bytes 1966088 | tf_op jit(solution)/shard_map/ppermute | solution.py:43
  103.9 11.0 %collective-permute-start.22 = (bf16[512,384]{1,0:T(8,128)(2,1)S(1)}, bf16[512,384]{1,0:T(8,128)(2,1)S(1)}, u32[]{:S(2)}, u32[]{:S(2)}) collective-permute-start(bf16[512,384]{1,0:T(8,128)(2,1)S(1)} %add_convert_fusion.3), channel_id=1, source_target_pairs={{0,4},{1,5},{2,6},{3,7},{64,68},{65,69},{66,70},{67,71},{16,20},{1... | collective-permute-start | bytes 1179656 | tf_op jit(solution)/shard_map/ppermute | solution.py:43
  105.3 12.2 %collective-permute-start.21 = (bf16[512,384]{1,0:T(8,128)(2,1)S(1)}, bf16[512,384]{1,0:T(8,128)(2,1)S(1)}, u32[]{:S(2)}, u32[]{:S(2)}) collective-permute-start(bf16[512,384]{1,0:T(8,128)(2,1)S(1)} %add_convert_fusion.4), channel_id=1, source_target_pairs={{0,12},{1,13},{2,14},{3,15},{64,76},{65,77},{66,78},{67,79},{16,28... | collective-permute-start | bytes 1179656 | tf_op jit(solution)/shard_map/ppermute | solution.py:43
  107.8 12.6 %copy-start.11 = (bf16[256,640]{1,0:T(8,128)(2,1)S(1)}, bf16[256,640]{1,0:T(8,128)(2,1)}, u32[]{:S(2)}) copy-start(bf16[256,640]{1,0:T(8,128)(2,1)} %copy-done.10) | copy-start | bytes 983044
  107.8 12.8 %copy-start.9 = (bf16[256,640]{1,0:T(8,128)(2,1)S(1)}, bf16[256,640]{1,0:T(8,128)(2,1)}, u32[]{:S(2)}) copy-start(bf16[256,640]{1,0:T(8,128)(2,1)} %copy-done.8) | copy-start | bytes 983044
  114.5 7.1 %copy-start.1 = (bf16[512,384]{1,0:T(8,128)(2,1)S(1)}, bf16[512,384]{1,0:T(8,128)(2,1)}, u32[]{:S(2)}) copy-start(bf16[512,384]{1,0:T(8,128)(2,1)} %copy-done) | copy-start | bytes 1179652
  114.6 7.1 %copy-start.33 = (bf16[1024,384]{1,0:T(8,128)(2,1)S(1)}, bf16[1024,384]{1,0:T(8,128)(2,1)}, u32[]{:S(2)}) copy-start(bf16[1024,384]{1,0:T(8,128)(2,1)} %copy-done.32) | copy-start | bytes 2359300
  114.6 7.1 %copy-start.35 = (bf16[1024,384]{1,0:T(8,128)(2,1)S(1)}, bf16[1024,384]{1,0:T(8,128)(2,1)}, u32[]{:S(2)}) copy-start(bf16[1024,384]{1,0:T(8,128)(2,1)} %copy-done.34) | copy-start | bytes 2359300
  117.5 24.7 %collective-permute-start.29 = (bf16[512,768]{1,0:T(8,128)(2,1)S(1)}, bf16[512,768]{1,0:T(8,128)(2,1)S(1)}, u32[]{:S(2)}, u32[]{:S(2)}) collective-permute-start(bf16[512,768]{1,0:T(8,128)(2,1)S(1)} %get-tuple-element.147), channel_id=1, source_target_pairs={{0,4},{1,5},{2,6},{3,7},{64,68},{65,69},{66,70},{67,71},{16,20},{1... | collective-permute-start | bytes 2359304 | tf_op jit(solution)/shard_map/ppermute | solution.py:43
  120.4 9.1 %collective-permute-start.26 = (bf16[256,640]{1,0:T(8,128)(2,1)S(1)}, bf16[256,640]{1,0:T(8,128)(2,1)S(1)}, u32[]{:S(2)}, u32[]{:S(2)}) collective-permute-start(bf16[256,640]{1,0:T(8,128)(2,1)S(1)} %add_convert_fusion.5), channel_id=1, source_target_pairs={{0,16},{1,17},{2,18},{3,19},{64,80},{65,81},{66,82},{67,83},{16,0}... | collective-permute-start | bytes 983048 | tf_op jit(solution)/shard_map/ppermute | solution.py:43
  120.6 10.3 %collective-permute-start.25 = (bf16[256,640]{1,0:T(8,128)(2,1)S(1)}, bf16[256,640]{1,0:T(8,128)(2,1)S(1)}, u32[]{:S(2)}, u32[]{:S(2)}) collective-permute-start(bf16[256,640]{1,0:T(8,128)(2,1)S(1)} %add_convert_fusion.6), channel_id=1, source_target_pairs={{0,48},{1,49},{2,50},{3,51},{64,112},{65,113},{66,114},{67,115},{1... | collective-permute-start | bytes 983048 | tf_op jit(solution)/shard_map/ppermute | solution.py:43
  121.9 9.0 %copy-start.15 = (bf16[256,512]{1,0:T(8,128)(2,1)S(1)}, bf16[256,512]{1,0:T(8,128)(2,1)}, u32[]{:S(2)}) copy-start(bf16[256,512]{1,0:T(8,128)(2,1)} %copy-done.14) | copy-start | bytes 786436
  122.0 9.0 %copy-start.30 = (bf16[512,512]{1,0:T(8,128)(2,1)S(1)}, bf16[512,512]{1,0:T(8,128)(2,1)}, u32[]{:S(2)}) copy-start(bf16[512,512]{1,0:T(8,128)(2,1)} %copy-done.29) | copy-start | bytes 1572868
  122.0 9.8 %copy-start.13 = (bf16[256,512]{1,0:T(8,128)(2,1)S(1)}, bf16[256,512]{1,0:T(8,128)(2,1)}, u32[]{:S(2)}) copy-start(bf16[256,512]{1,0:T(8,128)(2,1)} %copy-done.12) | copy-start | bytes 786436
  122.0 9.8 %copy-start.28 = (bf16[512,512]{1,0:T(8,128)(2,1)S(1)}, bf16[512,512]{1,0:T(8,128)(2,1)}, u32[]{:S(2)}) copy-start(bf16[512,512]{1,0:T(8,128)(2,1)} %copy-done.27) | copy-start | bytes 1572868
  122.0 10.0 %copy-start.5 = (bf16[256,640]{1,0:T(8,128)(2,1)S(1)}, bf16[256,640]{1,0:T(8,128)(2,1)}, u32[]{:S(2)}) copy-start(bf16[256,640]{1,0:T(8,128)(2,1)} %copy-done.4) | copy-start | bytes 983044
  122.0 10.0 %copy-start.7 = (bf16[256,640]{1,0:T(8,128)(2,1)S(1)}, bf16[256,640]{1,0:T(8,128)(2,1)}, u32[]{:S(2)}) copy-start(bf16[256,640]{1,0:T(8,128)(2,1)} %copy-done.6) | copy-start | bytes 983044
  122.1 10.2 %collective-permute-start.35 = (bf16[256,768]{1,0:T(8,128)(2,1)S(1)}, bf16[256,768]{1,0:T(8,128)(2,1)S(1)}, u32[]{:S(2)}, u32[]{:S(2)}) collective-permute-start(bf16[256,768]{1,0:T(8,128)(2,1)S(1)} %select_convert_fusion), channel_id=1, source_target_pairs={{0,2},{1,3},{2,0},{3,1},{64,66},{65,67},{66,64},{67,65},{16,18},{1... | collective-permute-start | bytes 1179656 | tf_op jit(solution)/shard_map/ppermute | solution.py:43
  122.9 19.3 %collective-permute-start.30 = (bf16[512,768]{1,0:T(8,128)(2,1)S(1)}, bf16[512,768]{1,0:T(8,128)(2,1)S(1)}, u32[]{:S(2)}, u32[]{:S(2)}) collective-permute-start(bf16[512,768]{1,0:T(8,128)(2,1)S(1)} %get-tuple-element.164), channel_id=1, source_target_pairs={{0,12},{1,13},{2,14},{3,15},{64,76},{65,77},{66,78},{67,79},{16,28... | collective-permute-start | bytes 2359304 | tf_op jit(solution)/shard_map/ppermute | solution.py:43
  131.0 23.4 %collective-permute-start.28 = (bf16[256,512]{1,0:T(8,128)(2,1)S(1)}, bf16[256,512]{1,0:T(8,128)(2,1)S(1)}, u32[]{:S(2)}, u32[]{:S(2)}) collective-permute-start(bf16[256,512]{1,0:T(8,128)(2,1)S(1)} %add_convert_fusion.8), channel_id=1, source_target_pairs={{0,48},{1,49},{2,50},{3,51},{64,112},{65,113},{66,114},{67,115},{1... | collective-permute-start | bytes 786440 | tf_op jit(solution)/shard_map/ppermute | solution.py:43
  131.8 22.6 %collective-permute-start.27 = (bf16[256,512]{1,0:T(8,128)(2,1)S(1)}, bf16[256,512]{1,0:T(8,128)(2,1)S(1)}, u32[]{:S(2)}, u32[]{:S(2)}) collective-permute-start(bf16[256,512]{1,0:T(8,128)(2,1)S(1)} %add_convert_fusion.9), channel_id=1, source_target_pairs={{0,16},{1,17},{2,18},{3,19},{64,80},{65,81},{66,82},{67,83},{16,0}... | collective-permute-start | bytes 786440 | tf_op jit(solution)/shard_map/ppermute | solution.py:43
  142.2 8.8 %collective-permute-start.31 = (bf16[256,640]{1,0:T(8,128)(2,1)S(1)}, bf16[256,640]{1,0:T(8,128)(2,1)S(1)}, u32[]{:S(2)}, u32[]{:S(2)}) collective-permute-start(bf16[256,640]{1,0:T(8,128)(2,1)S(1)} %get-tuple-element.165), channel_id=1, source_target_pairs={{0,64},{1,65},{2,66},{3,67},{64,0},{65,1},{66,2},{67,3},{16,80},{1... | collective-permute-start | bytes 983048 | tf_op jit(solution)/shard_map/ppermute | solution.py:43
  144.5 6.7 %copy-start.31 = (bf16[256,512]{1,0:T(8,128)(2,1)S(1)}, bf16[256,512]{1,0:T(8,128)(2,1)}, u32[]{:S(2)}) copy-start(bf16[256,512]{1,0:T(8,128)(2,1)} %param.4) | copy-start | bytes 786436
  144.5 6.7 %copy-start.39 = (f32[512]{0:T(512)S(1)}, f32[512]{0:T(512)}, u32[]{:S(2)}) copy-start(f32[512]{0:T(512)} %convert_element_type.219) | copy-start | bytes 6148
  144.6 12.3 %collective-permute-start.37 = (bf16[256,768]{1,0:T(8,128)(2,1)S(1)}, bf16[256,768]{1,0:T(8,128)(2,1)S(1)}, u32[]{:S(2)}, u32[]{:S(2)}) collective-permute-start(bf16[256,768]{1,0:T(8,128)(2,1)S(1)} %add_convert_fusion.1), channel_id=1, source_target_pairs={{0,4},{1,5},{2,6},{3,7},{64,68},{65,69},{66,70},{67,71},{16,20},{1... | collective-permute-start | bytes 1179656 | tf_op jit(solution)/shard_map/ppermute | solution.py:43
  144.8 12.1 %collective-permute-start.36 = (bf16[256,768]{1,0:T(8,128)(2,1)S(1)}, bf16[256,768]{1,0:T(8,128)(2,1)S(1)}, u32[]{:S(2)}, u32[]{:S(2)}) collective-permute-start(bf16[256,768]{1,0:T(8,128)(2,1)S(1)} %add_convert_fusion.2), channel_id=1, source_target_pairs={{0,12},{1,13},{2,14},{3,15},{64,76},{65,77},{66,78},{67,79},{16,28... | collective-permute-start | bytes 1179656 | tf_op jit(solution)/shard_map/ppermute | solution.py:43
  152.1 1.2 collective-permute-start.33
  153.2 3.6 %collective-permute-start.34 = (f32[1,512]{1,0:T(1,128)S(1)}, f32[1,512]{1,0:T(1,128)S(1)}, u32[]{:S(2)}, u32[]{:S(2)}) collective-permute-start(f32[1,512]{1,0:T(1,128)S(1)} %add.216), channel_id=1, source_target_pairs={{0,2},{1,3},{2,0},{3,1},{64,66},{65,67},{66,64},{67,65},{16,18},{1... | collective-permute-start | bytes 6152 | tf_op jit(solution)/shard_map/ppermute | solution.py:43
  154.6 11.6 %collective-permute-start.32 = (bf16[256,512]{1,0:T(8,128)(2,1)S(1)}, bf16[256,512]{1,0:T(8,128)(2,1)S(1)}, u32[]{:S(2)}, u32[]{:S(2)}) collective-permute-start(bf16[256,512]{1,0:T(8,128)(2,1)S(1)} %select_convert_fusion.2), channel_id=1, source_target_pairs={{0,64},{1,65},{2,66},{3,67},{64,0},{65,1},{66,2},{67,3},{16,80},{1... | collective-permute-start | bytes 786440 | tf_op jit(solution)/shard_map/ppermute | solution.py:43
  156.8 3.7 %collective-permute-start.38 = (f32[1,512]{1,0:T(1,128)S(1)}, f32[1,512]{1,0:T(1,128)S(1)}, u32[]{:S(2)}, u32[]{:S(2)}) collective-permute-start(f32[1,512]{1,0:T(1,128)S(1)} %add.217), channel_id=1, source_target_pairs={{0,4},{1,5},{2,6},{3,7},{64,68},{65,69},{66,70},{67,71},{16,20},{1... | collective-permute-start | bytes 6152 | tf_op jit(solution)/shard_map/ppermute | solution.py:43
  160.5 5.1 %collective-permute-start.39 = (f32[1,512]{1,0:T(1,128)S(1)}, f32[1,512]{1,0:T(1,128)S(1)}, u32[]{:S(2)}, u32[]{:S(2)}) collective-permute-start(f32[1,512]{1,0:T(1,128)S(1)} %add.224), channel_id=1, source_target_pairs={{0,8},{1,9},{2,10},{3,11},{64,72},{65,73},{66,74},{67,75},{16,24},... | collective-permute-start | bytes 6152 | tf_op jit(solution)/shard_map/ppermute | solution.py:43
  (17 other events, 31.8 us)

commit v10 on v9

--- a/solution.py
+++ b/solution.py
@@ -352,8 +352,8 @@
     low, high = finish(branch_terms, branch_got, branch_last)
     upper = z_hi == 1
     mine = jnp.where(upper, d_high, d_low)
-    theirs = send(after(jnp.where(upper, d_low, d_high).astype(bf16), *pair_got), "z+2")
-    mine = after(mine, *pair_got) + theirs.astype(f32)
+    theirs = send(jnp.where(upper, d_low, d_high).astype(bf16), "z+2")
+    mine = mine + theirs.astype(f32)
     theirs = send(after(jnp.where(upper, low, high).astype(bf16), theirs), "z+2")
     branch = (jnp.where(upper, high, low) + theirs.astype(f32)).astype(bf16)
     d_normed, products = mine[:, :512], mine[:, 512:513] / width

time: 167 us -> 171 us (1.024)
  starting transfers between devices: 42.2 us -> 45.5 us
  local copies, waits for them, and re-layouts: 9.1 us -> 11.2 us
    ppermute x40, starting transfers between devices: 42.2 us -> 45.5 us  [send(): return lax.ppermute(value, AXES, pairs(moves[move]))]
    unnamed x82, local copies, waits for them, and re-layouts: 8.08 us -> 10.2 us
  transfers between devices with their start and end apart: 40 -> 40, of which waited for: 23 -> 24; matrix products, arithmetic and copies ran while one was open for 6% -> 5% of each run, Pallas kernels for 19% -> 18%
where the time goes in v10:
time: 171 us; the launch traced here: 170 us
  waiting for transfers between devices  62.6 us (37%)
  starting transfers between devices  45.5 us (27%)
  Pallas kernels  38.1 us (22%)
  other arithmetic  11.8 us (7%)
  local copies, waits for them, and re-layouts  11.2 us (7%)
    ppermute x40, waiting for transfers between devices, send(): return lax.ppermute(value, AXES, pairs(moves[move]))  62.6 us
    ppermute x40, starting transfers between devices, send(): return lax.ppermute(value, AXES, pairs(moves[move]))  45.5 us
    pallas_call x7, Pallas kernels, call(): pl.pallas_call(whole, in_specs=[pl.BlockSpec(memory_space=space) for spac...  38.1 us
    unnamed x82, local copies, waits for them, and re-layouts  10.2 us
  transfers between devices with their start and end apart: 40, of which 24 were waited for; matrix products, arithmetic and copies ran while one was open for 5% of the time, Pallas kernels for 18%

profile of v10, /device:TPU:0, one launch (start us, length us, event | category | flops | bytes accessed | tf_op | source)
XLA Modules:
  0.0 170.4 jit_solution(16725272910631588114)
XLA Ops:
  1.3 1.0 pad_maximum_fusion.6.refs_1_
  2.3 3.2 %collective-permute-start.1 = (bf16[272,512]{1,0:T(8,128)(2,1)S(1)}, bf16[272,512]{1,0:T(8,128)(2,1)S(1)}, u32[]{:S(2)}, u32[]{:S(2)}) collective-permute-start(bf16[272,512]{1,0:T(8,128)(2,1)S(1)} %pad_maximum_fusion.6.refs_1_), channel_id=1, source_target_pairs={{0,48},{1,49},{2,50},{3,51},{64,112},{65,113},{66,114},{67,115},{1... | collective-permute-start | bytes 835592 | tf_op jit(solution)/shard_map/ppermute | solution.py:43
  5.5 3.9 %collective-permute-start.2 = (bf16[272,512]{1,0:T(8,128)(2,1)S(1)}, bf16[272,512]{1,0:T(8,128)(2,1)S(1)}, u32[]{:S(2)}, u32[]{:S(2)}) collective-permute-start(bf16[272,512]{1,0:T(8,128)(2,1)S(1)} %pad_maximum_fusion.6.refs_1_), channel_id=1, source_target_pairs={{0,64},{1,65},{2,66},{3,67},{64,0},{65,1},{66,2},{67,3},{16,80},{1... | collective-permute-start | bytes 835592 | tf_op jit(solution)/shard_map/ppermute | solution.py:43
  9.4 2.0 %collective-permute-done.1.refs_3_ = bf16[272,512]{1,0:T(8,128)(2,1)S(1)} collective-permute-done((bf16[272,512]{1,0:T(8,128)(2,1)S(1)}, bf16[272,512]{1,0:T(8,128)(2,1)S(1)}, u32[]{:S(2)}, u32[]{:S(2)}) %collective-permute-start.1) | collective-permute-done | bytes 278560 | tf_op jit(solution)/shard_map/ppermute | solution.py:43
  11.4 4.3 %collective-permute-done.2.refs_4_ = bf16[272,512]{1,0:T(8,128)(2,1)S(1)} collective-permute-done((bf16[272,512]{1,0:T(8,128)(2,1)S(1)}, bf16[272,512]{1,0:T(8,128)(2,1)S(1)}, u32[]{:S(2)}, u32[]{:S(2)}) %collective-permute-start.2) | collective-permute-done | bytes 278560 | tf_op jit(solution)/shard_map/ppermute | solution.py:43
  15.8 0.8 collective-permute-start.4
  16.6 1.8 %collective-permute-done.refs_2_ = bf16[272,512]{1,0:T(8,128)(2,1)S(1)} collective-permute-done((bf16[272,512]{1,0:T(8,128)(2,1)S(1)}, bf16[272,512]{1,0:T(8,128)(2,1)S(1)}, u32[]{:S(2)}, u32[]{:S(2)}) %collective-permute-start) | collective-permute-done | bytes 278560 | tf_op jit(solution)/shard_map/ppermute | solution.py:43
  18.6 2.7 %collective-permute-start.5 = (bf16[256,512]{1,0:T(8,128)(2,1)S(1)}, bf16[256,512]{1,0:T(8,128)(2,1)S(1)}, u32[]{:S(2)}, u32[]{:S(2)}) collective-permute-start(bf16[256,512]{1,0:T(8,128)(2,1)S(1)} %copy-done.39), channel_id=1, source_target_pairs={{0,64},{1,65},{2,66},{3,67},{64,0},{65,1},{66,2},{67,3},{16,80},{1... | collective-permute-start | bytes 786440 | tf_op jit(solution)/shard_map/ppermute | solution.py:43
  21.3 5.5 %collective-permute-done.5 = bf16[256,512]{1,0:T(8,128)(2,1)S(1)} collective-permute-done((bf16[256,512]{1,0:T(8,128)(2,1)S(1)}, bf16[256,512]{1,0:T(8,128)(2,1)S(1)}, u32[]{:S(2)}, u32[]{:S(2)}) %collective-permute-start.5) | collective-permute-done | bytes 262176 | tf_op jit(solution)/shard_map/ppermute | solution.py:43
  26.7 2.7 %collective-permute-done.3.refs_5_ = bf16[400,512]{1,0:T(8,128)(2,1)S(1)} collective-permute-done((bf16[400,512]{1,0:T(8,128)(2,1)S(1)}, bf16[400,512]{1,0:T(8,128)(2,1)S(1)}, u32[]{:S(2)}, u32[]{:S(2)}) %collective-permute-start.3) | collective-permute-done | bytes 409632 | tf_op jit(solution)/shard_map/ppermute | solution.py:43
  29.8 0.7 pad_maximum_fusion.7
  30.5 1.6 collective-permute-start.6
  32.2 1.5 collective-permute-start.7
  33.8 5.1 %collective-permute-done.6.refs_7_ = bf16[272,512]{1,0:T(8,128)(2,1)} collective-permute-done((bf16[272,512]{1,0:T(8,128)(2,1)}, bf16[272,512]{1,0:T(8,128)(2,1)}, u32[]{:S(2)}, u32[]{:S(2)}) %collective-permute-start.6) | collective-permute-done | bytes 278560 | tf_op jit(solution)/shard_map/ppermute | solution.py:43
  38.9 1.4 assemble.1
  41.0 0.9 copy-done.24
  41.9 1.8 %collective-permute-start.9 = (bf16[256,1024]{1,0:T(8,128)(2,1)S(1)}, bf16[256,1024]{1,0:T(8,128)(2,1)S(1)}, u32[]{:S(2)}, u32[]{:S(2)}) collective-permute-start(bf16[256,1024]{1,0:T(8,128)(2,1)S(1)} %get-tuple-element.99), channel_id=1, source_target_pairs={{0,66},{1,67},{2,64},{3,65},{64,2},{65,3},{66,0},{67,1},{16,82},{1... | collective-permute-start | bytes 1572872 | tf_op jit(solution)/shard_map/ppermute | solution.py:43
  44.4 1.5 collective-permute-start.11
  46.0 6.4 %forward.1 = (f32[256,768]{1,0:T(8,128)S(1)}, f32[256,768]{1,0:T(8,128)S(1)}, bf16[256,768]{1,0:T(8,128)(2,1)S(1)}, f32[256,128]{1,0:T(8,128)S(1)}, bf16[256,1792]{1,0:T(8,128)(2,1)}) custom-call(bf16[272,4096]{1,0:T(8,128)(2,1)S(1)} %get-tuple-element.96.refs_0_, bf16[256,1024]{1,0:T(8,128)(2,1)S(1)} %get-tuple-element.97.refs_1_, ...), custom_call_target="tpu_custom_call" | custom-call | flops 3221225472 | bytes 16777216 | tf_op jit(solution)/shard_map/forward/pallas_call | solution.py:89
  52.9 0.8 copy-done.26
  53.7 0.8 copy-done.37
  54.5 6.8 %backward.1 = (bf16[256,1536]{1,0:T(8,128)(2,1)S(1)}, bf16[256,128]{1,0:T(8,128)(2,1)S(1)}, bf16[256,2048]{1,0:T(8,128)(2,1)S(1)}, bf16[256,3584]{1,0:T(8,128)(2,1)}) custom-call(s32[10]{0:T(128)S(1)} %stack.116.refs_0_, bf16[512,512]{1,0:T(8,128)(2,1)S(1)} %pad_maximum_fusion.3.refs_1_, bf16[512,512]{1,0:T(8,128)(2,1)S(1)} %collective-permute-done.7.refs_2_, ...), custom_call_target="tpu_custom_call" | custom-call | flops 1610612736 | bytes 8388608 | tf_op jit(solution)/shard_map/backward/pallas_call | solution.py:89
  62.0 1.0 copy-done.17
  63.6 1.5 collective-permute-start.16
  65.2 1.0 copy-done.6
  66.2 5.2 %branch_rows.1 = (bf16[512,512]{1,0:T(8,128)(2,1)S(1)}, bf16[512,512]{1,0:T(8,128)(2,1)S(1)}, bf16[256,512]{1,0:T(8,128)(2,1)S(1)}, bf16[256,512]{1,0:T(8,128)(2...) custom-call(s32[8]{0:T(128)S(1)} %stack.105.refs_0_, bf16[256,768]{1,0:T(8,128)(2,1)S(1)} %copy-done.6, ...), custom_call_target="tpu_custom_call" | custom-call | flops 1610612736 | bytes 8388608 | tf_op jit(solution)/shard_map/branch_rows/pallas_call | solution.py:89
  72.0 1.0 copy-done.19
  73.0 1.2 copy-done.20
  74.2 4.5 %down_terms.1 = (bf16[1024,384]{1,0:T(8,128)(2,1)S(1)}, bf16[1024,384]{1,0:T(8,128)(2,1)S(1)}, bf16[512,384]{1,0:T(8,128)(2,1)S(1)}, bf16[512,384]{1,0:T(8,128)(...) custom-call(s32[8]{0:T(128)S(1)} %stack.121.refs_0_, bf16[256,2048]{1,0:T(8,128)(2,1)S(1)} %copy-done.18, ...), custom_call_target="tpu_custom_call" | custom-call | flops 1610612736 | bytes 8388608 | tf_op jit(solution)/shard_map/down_terms/pallas_call | solution.py:89
  78.8 2.8 %collective-permute-start.19 = (bf16[1024,384]{1,0:T(8,128)(2,1)S(1)}, bf16[1024,384]{1,0:T(8,128)(2,1)S(1)}, u32[]{:S(2)}, u32[]{:S(2)}) collective-permute-start(bf16[1024,384]{1,0:T(8,128)(2,1)S(1)} %get-tuple-element.129), channel_id=1, source_target_pairs={{0,12},{1,13},{2,14},{3,15},{64,76},{65,77},{66,78},{67,79},{16,28... | collective-permute-start | bytes 2359304 | tf_op jit(solution)/shard_map/ppermute | solution.py:43
  81.8 1.7 collective-permute-start.13
  83.5 7.1 %pair_rows.1 = (bf16[512,640]{1,0:T(8,128)(2,1)S(1)}, bf16[512,640]{1,0:T(8,128)(2,1)S(1)}, bf16[256,640]{1,0:T(8,128)(2,1)S(1)}, bf16[256,640]{1,0:T(8,128)(2,1...) custom-call(s32[8]{0:T(128)S(1)} %stack.105.refs_0_, ...), custom_call_target="tpu_custom_call" | custom-call | flops 3221225472 | bytes 16777216 | tf_op jit(solution)/shard_map/pair_rows/pallas_call | solution.py:89
  92.1 4.0 %collective-permute-done.13 = bf16[512,512]{1,0:T(8,128)(2,1)S(1)} collective-permute-done((bf16[512,512]{1,0:T(8,128)(2,1)S(1)}, bf16[512,512]{1,0:T(8,128)(2,1)S(1)}, u32[]{:S(2)}, u32[]{:S(2)}) %collective-permute-start.13) | collective-permute-done | bytes 524320 | tf_op jit(solution)/shard_map/ppermute | solution.py:43
  96.3 3.0 %collective-permute-done.19 = bf16[1024,384]{1,0:T(8,128)(2,1)S(1)} collective-permute-done((bf16[1024,384]{1,0:T(8,128)(2,1)S(1)}, bf16[1024,384]{1,0:T(8,128)(2,1)S(1)}, u32[]{:S(2)}, u32[]{:S(2)}) %collective-permute-start.19) | collective-permute-done | bytes 786464 | tf_op jit(solution)/shard_map/ppermute | solution.py:43
  99.2 1.2 collective-permute-done.18
  100.5 1.2 pad_maximum_fusion
  101.9 1.6 collective-permute-start.23
  104.1 1.2 add_convert_fusion.3
  105.7 1.1 add_convert_fusion.4
  106.8 2.4 %collective-permute-start.21 = (bf16[512,384]{1,0:T(8,128)(2,1)S(1)}, bf16[512,384]{1,0:T(8,128)(2,1)S(1)}, u32[]{:S(2)}, u32[]{:S(2)}) collective-permute-start(bf16[512,384]{1,0:T(8,128)(2,1)S(1)} %add_convert_fusion.4), channel_id=1, source_target_pairs={{0,12},{1,13},{2,14},{3,15},{64,76},{65,77},{66,78},{67,79},{16,28... | collective-permute-start | bytes 1179656 | tf_op jit(solution)/shard_map/ppermute | solution.py:43
  110.0 6.7 %pair_terms.1 = (bf16[512,768]{1,0:T(8,128)(2,1)S(1)}, bf16[512,768]{1,0:T(8,128)(2,1)S(1)}, bf16[256,768]{1,0:T(8,128)(2,1)S(1)}, bf16[256,768]{1,0:T(8,128)(2,...) custom-call(s32[8]{0:T(128)S(1)} %stack.121.refs_0_, bf16[256,1024]{1,0:T(8,128)(2,1)S(1)} %copy-done.25, ...), custom_call_target="tpu_custom_call" | custom-call | flops 3221225472 | bytes 8388608 | tf_op jit(solution)/shard_map/pair_terms/pallas_call | solution.py:89
  116.7 2.3 %collective-permute-done.21 = bf16[512,384]{1,0:T(8,128)(2,1)S(1)} collective-permute-done((bf16[512,384]{1,0:T(8,128)(2,1)S(1)}, bf16[512,384]{1,0:T(8,128)(2,1)S(1)}, u32[]{:S(2)}, u32[]{:S(2)}) %collective-permute-start.21) | collective-permute-done | bytes 393248 | tf_op jit(solution)/shard_map/ppermute | solution.py:43
  119.6 2.2 %collective-permute-done.24 = bf16[512,640]{1,0:T(8,128)(2,1)S(1)} collective-permute-done((bf16[512,640]{1,0:T(8,128)(2,1)}, bf16[512,640]{1,0:T(8,128)(2,1)S(1)}, u32[]{:S(2)}, u32[]{:S(2)}) %collective-permute-start.24) | collective-permute-done | bytes 655392 | tf_op jit(solution)/shard_map/ppermute | solution.py:43
  122.0 1.0 collective-permute-start.25
  123.8 2.4 %collective-permute-start.34 = (bf16[512,768]{1,0:T(8,128)(2,1)S(1)}, bf16[512,768]{1,0:T(8,128)(2,1)S(1)}, u32[]{:S(2)}, u32[]{:S(2)}) collective-permute-start(bf16[512,768]{1,0:T(8,128)(2,1)S(1)} %get-tuple-element.165), channel_id=1, source_target_pairs={{0,12},{1,13},{2,14},{3,15},{64,76},{65,77},{66,78},{67,79},{16,28... | collective-permute-start | bytes 2359304 | tf_op jit(solution)/shard_map/ppermute | solution.py:43
  126.2 4.7 %collective-permute-done.26 = bf16[256,640]{1,0:T(8,128)(2,1)S(1)} collective-permute-done((bf16[256,640]{1,0:T(8,128)(2,1)S(1)}, bf16[256,640]{1,0:T(8,128)(2,1)S(1)}, u32[]{:S(2)}, u32[]{:S(2)}) %collective-permute-start.26) | collective-permute-done | bytes 327712 | tf_op jit(solution)/shard_map/ppermute | solution.py:43
  130.9 1.4 collective-permute-done.25
  132.6 1.9 %collective-permute-start.29 = (bf16[256,640]{1,0:T(8,128)(2,1)S(1)}, bf16[256,640]{1,0:T(8,128)(2,1)S(1)}, u32[]{:S(2)}, u32[]{:S(2)}) collective-permute-start(bf16[256,640]{1,0:T(8,128)(2,1)S(1)} %select_convert_fusion.1), channel_id=1, source_target_pairs={{0,64},{1,65},{2,66},{3,67},{64,0},{65,1},{66,2},{67,3},{16,80},{1... | collective-permute-start | bytes 983048 | tf_op jit(solution)/shard_map/ppermute | solution.py:43
  134.5 0.8 collective-permute-start.28
  135.4 6.9 %collective-permute-done.29 = bf16[256,640]{1,0:T(8,128)(2,1)S(1)} collective-permute-done((bf16[256,640]{1,0:T(8,128)(2,1)S(1)}, bf16[256,640]{1,0:T(8,128)(2,1)S(1)}, u32[]{:S(2)}, u32[]{:S(2)}) %collective-permute-start.29) | collective-permute-done | bytes 327712 | tf_op jit(solution)/shard_map/ppermute | solution.py:43
  143.3 0.9 fusion.3
  144.2 4.5 %collective-permute-done.27 = bf16[256,512]{1,0:T(8,128)(2,1)S(1)} collective-permute-done((bf16[256,512]{1,0:T(8,128)(2,1)S(1)}, bf16[256,512]{1,0:T(8,128)(2,1)S(1)}, u32[]{:S(2)}, u32[]{:S(2)}) %collective-permute-start.27) | collective-permute-done | bytes 262176 | tf_op jit(solution)/shard_map/ppermute | solution.py:43
  148.8 1.9 %collective-permute-start.30 = (bf16[256,512]{1,0:T(8,128)(2,1)S(1)}, bf16[256,512]{1,0:T(8,128)(2,1)S(1)}, u32[]{:S(2)}, u32[]{:S(2)}) collective-permute-start(bf16[256,512]{1,0:T(8,128)(2,1)S(1)} %select_convert_fusion.2), channel_id=1, source_target_pairs={{0,64},{1,65},{2,66},{3,67},{64,0},{65,1},{66,2},{67,3},{16,80},{1... | collective-permute-start | bytes 786440 | tf_op jit(solution)/shard_map/ppermute | solution.py:43
  150.7 0.8 collective-permute-start.32
  152.1 2.2 %collective-permute-start.36 = (bf16[256,768]{1,0:T(8,128)(2,1)S(1)}, bf16[256,768]{1,0:T(8,128)(2,1)S(1)}, u32[]{:S(2)}, u32[]{:S(2)}) collective-permute-start(bf16[256,768]{1,0:T(8,128)(2,1)S(1)} %add_convert_fusion.2), channel_id=1, source_target_pairs={{0,12},{1,13},{2,14},{3,15},{64,76},{65,77},{66,78},{67,79},{16,28... | collective-permute-start | bytes 1179656 | tf_op jit(solution)/shard_map/ppermute | solution.py:43
  154.4 1.4 collective-permute-done.32
  155.8 1.0 collective-permute-done.30
  156.8 0.9 add_convert_fusion.7
  157.7 1.8 %collective-permute-done.37 = bf16[256,768]{1,0:T(8,128)(2,1)S(1)} collective-permute-done((bf16[256,768]{1,0:T(8,128)(2,1)S(1)}, bf16[256,768]{1,0:T(8,128)(2,1)S(1)}, u32[]{:S(2)}, u32[]{:S(2)}) %collective-permute-start.37) | collective-permute-done | bytes 393248 | tf_op jit(solution)/shard_map/ppermute | solution.py:43
  159.5 1.7 collective-permute-done.36
  162.0 2.7 %collective-permute-done.38 = f32[1,512]{1,0:T(1,128)S(1)} collective-permute-done((f32[1,512]{1,0:T(1,128)S(1)}, f32[1,512]{1,0:T(1,128)S(1)}, u32[]{:S(2)}, u32[]{:S(2)}) %collective-permute-start.38) | collective-permute-done | bytes 2080 | tf_op jit(solution)/shard_map/ppermute | solution.py:43
  164.7 2.3 %collective-permute-start.39 = (f32[1,512]{1,0:T(1,128)S(1)}, f32[1,512]{1,0:T(1,128)S(1)}, u32[]{:S(2)}, u32[]{:S(2)}) collective-permute-start(f32[1,512]{1,0:T(1,128)S(1)} %add.224), channel_id=1, source_target_pairs={{0,8},{1,9},{2,10},{3,11},{64,72},{65,73},{66,74},{67,75},{16,24},... | collective-permute-start | bytes 6152 | tf_op jit(solution)/shard_map/ppermute | solution.py:43
  167.1 1.1 pad_maximum_fusion.1
  168.2 1.6 collective-permute-done.39
  (148 shorter events, 14.3 us)
Async XLA Ops:
  1.3 17.2 %copy-start.39 = (bf16[256,512]{1,0:T(8,128)(2,1)S(1)}, bf16[256,512]{1,0:T(8,128)(2,1)}, u32[]{:S(2)}) copy-start(bf16[256,512]{1,0:T(8,128)(2,1)} %param.7) | copy-start | bytes 786436
  2.3 9.1 %collective-permute-start.1 = (bf16[272,512]{1,0:T(8,128)(2,1)S(1)}, bf16[272,512]{1,0:T(8,128)(2,1)S(1)}, u32[]{:S(2)}, u32[]{:S(2)}) collective-permute-start(bf16[272,512]{1,0:T(8,128)(2,1)S(1)} %pad_maximum_fusion.6.refs_1_), channel_id=1, source_target_pairs={{0,48},{1,49},{2,50},{3,51},{64,112},{65,113},{66,114},{67,115},{1... | collective-permute-start | bytes 835592 | tf_op jit(solution)/shard_map/ppermute | solution.py:43
  5.5 10.2 %collective-permute-start.2 = (bf16[272,512]{1,0:T(8,128)(2,1)S(1)}, bf16[272,512]{1,0:T(8,128)(2,1)S(1)}, u32[]{:S(2)}, u32[]{:S(2)}) collective-permute-start(bf16[272,512]{1,0:T(8,128)(2,1)S(1)} %pad_maximum_fusion.6.refs_1_), channel_id=1, source_target_pairs={{0,64},{1,65},{2,66},{3,67},{64,0},{65,1},{66,2},{67,3},{16,80},{1... | collective-permute-start | bytes 835592 | tf_op jit(solution)/shard_map/ppermute | solution.py:43
  9.4 9.0 %collective-permute-start = (bf16[272,512]{1,0:T(8,128)(2,1)S(1)}, bf16[272,512]{1,0:T(8,128)(2,1)S(1)}, u32[]{:S(2)}, u32[]{:S(2)}) collective-permute-start(bf16[272,512]{1,0:T(8,128)(2,1)S(1)} %pad_maximum_fusion.6.refs_1_), channel_id=1, source_target_pairs={{0,16},{1,17},{2,18},{3,19},{64,80},{65,81},{66,82},{67,83},{16,32... | collective-permute-start | bytes 835592 | tf_op jit(solution)/shard_map/ppermute | solution.py:43
  15.8 13.7 %collective-permute-start.4 = (bf16[416,512]{1,0:T(8,128)(2,1)S(1)}, bf16[416,512]{1,0:T(8,128)(2,1)S(1)}, u32[]{:S(2)}, u32[]{:S(2)}) collective-permute-start(bf16[416,512]{1,0:T(8,128)(2,1)S(1)} %pad_maximum_fusion.4), channel_id=1, source_target_pairs={{0,48},{1,49},{2,50},{3,51},{64,112},{65,113},{66,114},{67,115},{1... | collective-permute-start | bytes 1277960 | tf_op jit(solution)/shard_map/ppermute | solution.py:43
  18.5 11.0 %collective-permute-start.3 = (bf16[400,512]{1,0:T(8,128)(2,1)S(1)}, bf16[400,512]{1,0:T(8,128)(2,1)S(1)}, u32[]{:S(2)}, u32[]{:S(2)}) collective-permute-start(bf16[400,512]{1,0:T(8,128)(2,1)S(1)} %pad_maximum_fusion.5), channel_id=1, source_target_pairs={{0,16},{1,17},{2,18},{3,19},{64,80},{65,81},{66,82},{67,83},{16,32... | collective-permute-start | bytes 1228808 | tf_op jit(solution)/shard_map/ppermute | solution.py:43
  18.6 8.1 %collective-permute-start.5 = (bf16[256,512]{1,0:T(8,128)(2,1)S(1)}, bf16[256,512]{1,0:T(8,128)(2,1)S(1)}, u32[]{:S(2)}, u32[]{:S(2)}) collective-permute-start(bf16[256,512]{1,0:T(8,128)(2,1)S(1)} %copy-done.39), channel_id=1, source_target_pairs={{0,64},{1,65},{2,66},{3,67},{64,0},{65,1},{66,2},{67,3},{16,80},{1... | collective-permute-start | bytes 786440 | tf_op jit(solution)/shard_map/ppermute | solution.py:43
  29.5 14.2 %collective-permute-start.8 = (bf16[512,512]{1,0:T(8,128)(2,1)S(1)}, bf16[512,512]{1,0:T(8,128)(2,1)S(1)}, u32[]{:S(2)}, u32[]{:S(2)}) collective-permute-start(bf16[512,512]{1,0:T(8,128)(2,1)S(1)} %pad_maximum_fusion.3.refs_1_), channel_id=1, source_target_pairs={{0,48},{1,49},{2,50},{3,51},{64,112},{65,113},{66,114},{67,115},{1... | collective-permute-start | bytes 1572872 | tf_op jit(solution)/shard_map/ppermute | solution.py:43
  30.5 8.4 %collective-permute-start.6 = (bf16[272,512]{1,0:T(8,128)(2,1)}, bf16[272,512]{1,0:T(8,128)(2,1)}, u32[]{:S(2)}, u32[]{:S(2)}) collective-permute-start(bf16[272,512]{1,0:T(8,128)(2,1)} %pad_maximum_fusion.7), channel_id=1, source_target_pairs={{0,64},{1,65},{2,66},{3,67},{64,0},{65,1},{66,2},{67,3},{16,80},{1... | collective-permute-start | bytes 835592 | tf_op jit(solution)/shard_map/ppermute | solution.py:43
  32.2 12.2 %collective-permute-start.7 = (bf16[512,512]{1,0:T(8,128)(2,1)S(1)}, bf16[512,512]{1,0:T(8,128)(2,1)S(1)}, u32[]{:S(2)}, u32[]{:S(2)}) collective-permute-start(bf16[512,512]{1,0:T(8,128)(2,1)S(1)} %pad_maximum_fusion.3.refs_1_), channel_id=1, source_target_pairs={{0,16},{1,17},{2,18},{3,19},{64,80},{65,81},{66,82},{67,83},{16,32... | collective-permute-start | bytes 1572872 | tf_op jit(solution)/shard_map/ppermute | solution.py:43
  41.9 11.0 %collective-permute-start.9 = (bf16[256,1024]{1,0:T(8,128)(2,1)S(1)}, bf16[256,1024]{1,0:T(8,128)(2,1)S(1)}, u32[]{:S(2)}, u32[]{:S(2)}) collective-permute-start(bf16[256,1024]{1,0:T(8,128)(2,1)S(1)} %get-tuple-element.99), channel_id=1, source_target_pairs={{0,66},{1,67},{2,64},{3,65},{64,2},{65,3},{66,0},{67,1},{16,82},{1... | collective-permute-start | bytes 1572872 | tf_op jit(solution)/shard_map/ppermute | solution.py:43
  43.7 10.0 %collective-permute-start.10 = (bf16[256,1024]{1,0:T(8,128)(2,1)S(1)}, bf16[256,1024]{1,0:T(8,128)(2,1)S(1)}, u32[]{:S(2)}, u32[]{:S(2)}) collective-permute-start(bf16[256,1024]{1,0:T(8,128)(2,1)S(1)} %get-tuple-element.100), channel_id=1, source_target_pairs={{0,2},{1,3},{2,0},{3,1},{64,66},{65,67},{66,64},{67,65},{16,18},{1... | collective-permute-start | bytes 1572872 | tf_op jit(solution)/shard_map/ppermute | solution.py:43
  43.8 10.0 %collective-permute-start.12 = (bf16[256,512]{1,0:T(8,128)(2,1)S(1)}, bf16[256,512]{1,0:T(8,128)(2,1)S(1)}, u32[]{:S(2)}, u32[]{:S(2)}) collective-permute-start(bf16[256,512]{1,0:T(8,128)(2,1)S(1)} %pad_maximum_fusion.9), channel_id=1, source_target_pairs={{0,48},{1,49},{2,50},{3,51},{64,112},{65,113},{66,114},{67,115},{1... | collective-permute-start | bytes 786440 | tf_op jit(solution)/shard_map/ppermute | solution.py:43
  44.4 9.3 %collective-permute-start.11 = (bf16[256,512]{1,0:T(8,128)(2,1)S(1)}, bf16[256,512]{1,0:T(8,128)(2,1)S(1)}, u32[]{:S(2)}, u32[]{:S(2)}) collective-permute-start(bf16[256,512]{1,0:T(8,128)(2,1)S(1)} %pad_maximum_fusion.8), channel_id=1, source_target_pairs={{0,16},{1,17},{2,18},{3,19},{64,80},{65,81},{66,82},{67,83},{16,32... | collective-permute-start | bytes 786440 | tf_op jit(solution)/shard_map/ppermute | solution.py:43
  52.3 9.0 %copy-start.5 = (bf16[256,768]{1,0:T(8,128)(2,1)}, bf16[256,768]{1,0:T(8,128)(2,1)S(1)}, u32[]{:S(2)}) copy-start(bf16[256,768]{1,0:T(8,128)(2,1)S(1)} %get-tuple-element.106.refs_1_.refs_3_) | copy-start | bytes 1179652
  63.0 10.0 %collective-permute-start.17 = (bf16[256,3584]{1,0:T(8,128)(2,1)}, bf16[256,3584]{1,0:T(8,128)(2,1)}, u32[]{:S(2)}, u32[]{:S(2)}) collective-permute-start(bf16[256,3584]{1,0:T(8,128)(2,1)} %get-tuple-element.118), channel_id=1, source_target_pairs={{0,1},{1,0},{2,3},{3,2},{64,65},{65,64},{66,67},{67,66},{16,17},{1... | collective-permute-start | bytes 5505032 | tf_op jit(solution)/shard_map/ppermute | solution.py:43
  63.0 9.1 %collective-permute-start.15 = (bf16[256,1792]{1,0:T(8,128)(2,1)}, bf16[256,1792]{1,0:T(8,128)(2,1)S(1)}, u32[]{:S(2)}, u32[]{:S(2)}) collective-permute-start(bf16[256,1792]{1,0:T(8,128)(2,1)} %get-tuple-element.115), channel_id=1, source_target_pairs={{0,1},{1,0},{2,3},{3,2},{64,65},{65,64},{66,67},{67,66},{16,17},{1... | collective-permute-start | bytes 2752520 | tf_op jit(solution)/shard_map/ppermute | solution.py:43
  63.6 32.6 %collective-permute-start.16 = (bf16[256,1536]{1,0:T(8,128)(2,1)S(1)}, bf16[256,1536]{1,0:T(8,128)(2,1)S(1)}, u32[]{:S(2)}, u32[]{:S(2)}) collective-permute-start(bf16[256,1536]{1,0:T(8,128)(2,1)S(1)} %get-tuple-element.120.refs_1_.refs_5_), channel_id=1, source_target_pairs={{0,2},{1,3},{2,0},{3,1},{64,66},{65,67},{66,64},{67,65},{16,18},{1... | collective-permute-start | bytes 2359304 | tf_op jit(solution)/shard_map/ppermute | solution.py:43
  66.2 6.8 %copy-start.7 = (bf16[256,768]{1,0:T(8,128)(2,1)S(1)}, bf16[256,768]{1,0:T(8,128)(2,1)}, u32[]{:S(2)}) copy-start(bf16[256,768]{1,0:T(8,128)(2,1)} %copy-done.5) | copy-start | bytes 1179652
  66.2 6.8 %copy-start.18 = (bf16[256,2048]{1,0:T(8,128)(2,1)S(1)}, bf16[256,2048]{1,0:T(8,128)(2,1)}, u32[]{:S(2)}) copy-start(bf16[256,2048]{1,0:T(8,128)(2,1)} %copy-done.17) | copy-start | bytes 3145732
  72.0 11.5 %copy-start.15 = (bf16[256,128]{1,0:T(8,128)(2,1)S(1)}, bf16[256,128]{1,0:T(8,128)(2,1)}, u32[]{:S(2)}) copy-start(bf16[256,128]{1,0:T(8,128)(2,1)} %copy-done.14) | copy-start | bytes 196612
  78.7 11.9 %copy-start = (bf16[512,384]{1,0:T(8,128)(2,1)}, bf16[512,384]{1,0:T(8,128)(2,1)S(1)}, u32[]{:S(2)}) copy-start(bf16[512,384]{1,0:T(8,128)(2,1)S(1)} %get-tuple-element.141) | copy-start | bytes 1179652
  78.7 11.9 %copy-start.1 = (bf16[512,384]{1,0:T(8,128)(2,1)}, bf16[512,384]{1,0:T(8,128)(2,1)S(1)}, u32[]{:S(2)}) copy-start(bf16[512,384]{1,0:T(8,128)(2,1)S(1)} %get-tuple-element.168) | copy-start | bytes 1179652
  78.8 11.9 %copy-start.3 = (bf16[512,384]{1,0:T(8,128)(2,1)}, bf16[512,384]{1,0:T(8,128)(2,1)S(1)}, u32[]{:S(2)}) copy-start(bf16[512,384]{1,0:T(8,128)(2,1)S(1)} %get-tuple-element.169) | copy-start | bytes 1179652
  78.8 20.5 %collective-permute-start.19 = (bf16[1024,384]{1,0:T(8,128)(2,1)S(1)}, bf16[1024,384]{1,0:T(8,128)(2,1)S(1)}, u32[]{:S(2)}, u32[]{:S(2)}) collective-permute-start(bf16[1024,384]{1,0:T(8,128)(2,1)S(1)} %get-tuple-element.129), channel_id=1, source_target_pairs={{0,12},{1,13},{2,14},{3,15},{64,76},{65,77},{66,78},{67,79},{16,28... | collective-permute-start | bytes 2359304 | tf_op jit(solution)/shard_map/ppermute | solution.py:43
  81.6 18.9 %collective-permute-start.18 = (bf16[1024,384]{1,0:T(8,128)(2,1)S(1)}, bf16[1024,384]{1,0:T(8,128)(2,1)S(1)}, u32[]{:S(2)}, u32[]{:S(2)}) collective-permute-start(bf16[1024,384]{1,0:T(8,128)(2,1)S(1)} %get-tuple-element.119), channel_id=1, source_target_pairs={{0,4},{1,5},{2,6},{3,7},{64,68},{65,69},{66,70},{67,71},{16,20},{1... | collective-permute-start | bytes 2359304 | tf_op jit(solution)/shard_map/ppermute | solution.py:43
  81.8 14.3 %collective-permute-start.13 = (bf16[512,512]{1,0:T(8,128)(2,1)S(1)}, bf16[512,512]{1,0:T(8,128)(2,1)S(1)}, u32[]{:S(2)}, u32[]{:S(2)}) collective-permute-start(bf16[512,512]{1,0:T(8,128)(2,1)S(1)} %get-tuple-element.110), channel_id=1, source_target_pairs={{0,48},{1,49},{2,50},{3,51},{64,112},{65,113},{66,114},{67,115},{1... | collective-permute-start | bytes 1572872 | tf_op jit(solution)/shard_map/ppermute | solution.py:43
  83.5 12.8 %collective-permute-start.14 = (bf16[512,512]{1,0:T(8,128)(2,1)S(1)}, bf16[512,512]{1,0:T(8,128)(2,1)S(1)}, u32[]{:S(2)}, u32[]{:S(2)}) collective-permute-start(bf16[512,512]{1,0:T(8,128)(2,1)S(1)} %get-tuple-element.113), channel_id=1, source_target_pairs={{0,16},{1,17},{2,18},{3,19},{64,80},{65,81},{66,82},{67,83},{16,0}... | collective-permute-start | bytes 1572872 | tf_op jit(solution)/shard_map/ppermute | solution.py:43
  83.5 17.0 %copy-start.38 = (bf16[256,1024]{1,0:T(8,128)(2,1)S(1)}, bf16[256,1024]{1,0:T(8,128)(2,1)}, u32[]{:S(2)}) copy-start(bf16[256,1024]{1,0:T(8,128)(2,1)} %copy-done.37) | copy-start | bytes 1572868
  92.1 7.2 %copy-start.22 = (bf16[512,640]{1,0:T(8,128)(2,1)}, bf16[512,640]{1,0:T(8,128)(2,1)S(1)}, u32[]{:S(2)}) copy-start(bf16[512,640]{1,0:T(8,128)(2,1)S(1)} %get-tuple-element.128) | copy-start | bytes 1966084
  92.1 7.2 %copy-start.23 = (bf16[512,640]{1,0:T(8,128)(2,1)}, bf16[512,640]{1,0:T(8,128)(2,1)S(1)}, u32[]{:S(2)}) copy-start(bf16[512,640]{1,0:T(8,128)(2,1)S(1)} %get-tuple-element.148) | copy-start | bytes 1966084
  96.3 5.6 %copy-start.40 = (bf16[512]{0:T(512)(128)(2,1)S(1)}, bf16[512]{0:T(512)(128)(2,1)}, u32[]{:S(2)}) copy-start(bf16[512]{0:T(512)(128)(2,1)} %param.5) | copy-start | bytes 3076
  101.8 8.1 %collective-permute-start.20 = (bf16[256,2560]{1,0:T(8,128)(2,1)}, bf16[256,2560]{1,0:T(8,128)(2,1)}, u32[]{:S(2)}, u32[]{:S(2)}) collective-permute-start(bf16[256,2560]{1,0:T(8,128)(2,1)} %pad_maximum_fusion), channel_id=1, source_target_pairs={{0,1},{1,0},{2,3},{3,2},{64,65},{65,64},{66,67},{67,66},{16,17},{1... | collective-permute-start | bytes 3932168 | tf_op jit(solution)/shard_map/ppermute | solution.py:43
  101.8 8.1 %copy-start.21 = (bf16[256,1792]{1,0:T(8,128)(2,1)S(1)}, bf16[256,1792]{1,0:T(8,128)(2,1)}, u32[]{:S(2)}) copy-start(bf16[256,1792]{1,0:T(8,128)(2,1)} %copy-done.19) | copy-start | bytes 2752516
  101.8 8.1 %copy-start.25 = (bf16[256,1024]{1,0:T(8,128)(2,1)S(1)}, bf16[256,1024]{1,0:T(8,128)(2,1)}, u32[]{:S(2)}) copy-start(bf16[256,1024]{1,0:T(8,128)(2,1)} %copy-done.24) | copy-start | bytes 1572868
  101.9 8.1 %copy-start.27 = (bf16[256,1024]{1,0:T(8,128)(2,1)S(1)}, bf16[256,1024]{1,0:T(8,128)(2,1)}, u32[]{:S(2)}) copy-start(bf16[256,1024]{1,0:T(8,128)(2,1)} %copy-done.26) | copy-start | bytes 1572868
  101.9 19.9 %collective-permute-start.23 = (bf16[512,640]{1,0:T(8,128)(2,1)}, bf16[512,640]{1,0:T(8,128)(2,1)S(1)}, u32[]{:S(2)}, u32[]{:S(2)}) collective-permute-start(bf16[512,640]{1,0:T(8,128)(2,1)} %copy-done.22), channel_id=1, source_target_pairs={{0,16},{1,17},{2,18},{3,19},{64,80},{65,81},{66,82},{67,83},{16,0}... | collective-permute-start | bytes 1966088 | tf_op jit(solution)/shard_map/ppermute | solution.py:43
  103.5 18.3 %collective-permute-start.24 = (bf16[512,640]{1,0:T(8,128)(2,1)}, bf16[512,640]{1,0:T(8,128)(2,1)S(1)}, u32[]{:S(2)}, u32[]{:S(2)}) collective-permute-start(bf16[512,640]{1,0:T(8,128)(2,1)} %copy-done.23), channel_id=1, source_target_pairs={{0,48},{1,49},{2,50},{3,51},{64,112},{65,113},{66,114},{67,115},{1... | collective-permute-start | bytes 1966088 | tf_op jit(solution)/shard_map/ppermute | solution.py:43
  105.4 11.4 %collective-permute-start.22 = (bf16[512,384]{1,0:T(8,128)(2,1)S(1)}, bf16[512,384]{1,0:T(8,128)(2,1)S(1)}, u32[]{:S(2)}, u32[]{:S(2)}) collective-permute-start(bf16[512,384]{1,0:T(8,128)(2,1)S(1)} %add_convert_fusion.3), channel_id=1, source_target_pairs={{0,4},{1,5},{2,6},{3,7},{64,68},{65,69},{66,70},{67,71},{16,20},{1... | collective-permute-start | bytes 1179656 | tf_op jit(solution)/shard_map/ppermute | solution.py:43
  106.8 12.2 %collective-permute-start.21 = (bf16[512,384]{1,0:T(8,128)(2,1)S(1)}, bf16[512,384]{1,0:T(8,128)(2,1)S(1)}, u32[]{:S(2)}, u32[]{:S(2)}) collective-permute-start(bf16[512,384]{1,0:T(8,128)(2,1)S(1)} %add_convert_fusion.4), channel_id=1, source_target_pairs={{0,12},{1,13},{2,14},{3,15},{64,76},{65,77},{66,78},{67,79},{16,28... | collective-permute-start | bytes 1179656 | tf_op jit(solution)/shard_map/ppermute | solution.py:43
  109.9 11.8 %copy-start.11 = (bf16[256,640]{1,0:T(8,128)(2,1)S(1)}, bf16[256,640]{1,0:T(8,128)(2,1)}, u32[]{:S(2)}) copy-start(bf16[256,640]{1,0:T(8,128)(2,1)} %copy-done.10) | copy-start | bytes 983044
  110.0 12.0 %copy-start.9 = (bf16[256,640]{1,0:T(8,128)(2,1)S(1)}, bf16[256,640]{1,0:T(8,128)(2,1)}, u32[]{:S(2)}) copy-start(bf16[256,640]{1,0:T(8,128)(2,1)} %copy-done.8) | copy-start | bytes 983044
  110.0 13.1 %copy-start.36 = (bf16[1024,384]{1,0:T(8,128)(2,1)S(1)}, bf16[1024,384]{1,0:T(8,128)(2,1)}, u32[]{:S(2)}) copy-start(bf16[1024,384]{1,0:T(8,128)(2,1)} %copy-done.35) | copy-start | bytes 2359300
  116.7 6.4 %copy-start.2 = (bf16[512,384]{1,0:T(8,128)(2,1)S(1)}, bf16[512,384]{1,0:T(8,128)(2,1)}, u32[]{:S(2)}) copy-start(bf16[512,384]{1,0:T(8,128)(2,1)} %copy-done.1) | copy-start | bytes 1179652
  116.7 6.4 %copy-start.4 = (bf16[512,384]{1,0:T(8,128)(2,1)S(1)}, bf16[512,384]{1,0:T(8,128)(2,1)}, u32[]{:S(2)}) copy-start(bf16[512,384]{1,0:T(8,128)(2,1)} %copy-done.3) | copy-start | bytes 1179652
  116.7 6.3 %copy-start.34 = (bf16[1024,384]{1,0:T(8,128)(2,1)S(1)}, bf16[1024,384]{1,0:T(8,128)(2,1)}, u32[]{:S(2)}) copy-start(bf16[1024,384]{1,0:T(8,128)(2,1)} %copy-done.33) | copy-start | bytes 2359300
  119.0 32.5 %collective-permute-start.33 = (bf16[512,768]{1,0:T(8,128)(2,1)S(1)}, bf16[512,768]{1,0:T(8,128)(2,1)S(1)}, u32[]{:S(2)}, u32[]{:S(2)}) collective-permute-start(bf16[512,768]{1,0:T(8,128)(2,1)S(1)} %get-tuple-element.145), channel_id=1, source_target_pairs={{0,4},{1,5},{2,6},{3,7},{64,68},{65,69},{66,70},{67,71},{16,20},{1... | collective-permute-start | bytes 2359304 | tf_op jit(solution)/shard_map/ppermute | solution.py:43
  121.8 9.1 %collective-permute-start.26 = (bf16[256,640]{1,0:T(8,128)(2,1)S(1)}, bf16[256,640]{1,0:T(8,128)(2,1)S(1)}, u32[]{:S(2)}, u32[]{:S(2)}) collective-permute-start(bf16[256,640]{1,0:T(8,128)(2,1)S(1)} %add_convert_fusion.5), channel_id=1, source_target_pairs={{0,16},{1,17},{2,18},{3,19},{64,80},{65,81},{66,82},{67,83},{16,0}... | collective-permute-start | bytes 983048 | tf_op jit(solution)/shard_map/ppermute | solution.py:43
  122.0 10.3 %collective-permute-start.25 = (bf16[256,640]{1,0:T(8,128)(2,1)S(1)}, bf16[256,640]{1,0:T(8,128)(2,1)S(1)}, u32[]{:S(2)}, u32[]{:S(2)}) collective-permute-start(bf16[256,640]{1,0:T(8,128)(2,1)S(1)} %add_convert_fusion.6), channel_id=1, source_target_pairs={{0,48},{1,49},{2,50},{3,51},{64,112},{65,113},{66,114},{67,115},{1... | collective-permute-start | bytes 983048 | tf_op jit(solution)/shard_map/ppermute | solution.py:43
  123.4 11.1 %copy-start.13 = (bf16[256,512]{1,0:T(8,128)(2,1)S(1)}, bf16[256,512]{1,0:T(8,128)(2,1)}, u32[]{:S(2)}) copy-start(bf16[256,512]{1,0:T(8,128)(2,1)} %copy-done.12) | copy-start | bytes 786436
  123.4 11.0 %copy-start.31 = (bf16[512,512]{1,0:T(8,128)(2,1)S(1)}, bf16[512,512]{1,0:T(8,128)(2,1)}, u32[]{:S(2)}) copy-start(bf16[512,512]{1,0:T(8,128)(2,1)} %copy-done.30) | copy-start | bytes 1572868
  123.4 28.1 %collective-permute-start.35 = (bf16[256,768]{1,0:T(8,128)(2,1)S(1)}, bf16[256,768]{1,0:T(8,128)(2,1)S(1)}, u32[]{:S(2)}, u32[]{:S(2)}) collective-permute-start(bf16[256,768]{1,0:T(8,128)(2,1)S(1)} %select_convert_fusion), channel_id=1, source_target_pairs={{0,2},{1,3},{2,0},{3,1},{64,66},{65,67},{66,64},{67,65},{16,18},{1... | collective-permute-start | bytes 1179656 | tf_op jit(solution)/shard_map/ppermute | solution.py:43
  123.8 27.7 %collective-permute-start.34 = (bf16[512,768]{1,0:T(8,128)(2,1)S(1)}, bf16[512,768]{1,0:T(8,128)(2,1)S(1)}, u32[]{:S(2)}, u32[]{:S(2)}) collective-permute-start(bf16[512,768]{1,0:T(8,128)(2,1)S(1)} %get-tuple-element.165), channel_id=1, source_target_pairs={{0,12},{1,13},{2,14},{3,15},{64,76},{65,77},{66,78},{67,79},{16,28... | collective-permute-start | bytes 2359304 | tf_op jit(solution)/shard_map/ppermute | solution.py:43
  132.6 9.7 %collective-permute-start.29 = (bf16[256,640]{1,0:T(8,128)(2,1)S(1)}, bf16[256,640]{1,0:T(8,128)(2,1)S(1)}, u32[]{:S(2)}, u32[]{:S(2)}) collective-permute-start(bf16[256,640]{1,0:T(8,128)(2,1)S(1)} %select_convert_fusion.1), channel_id=1, source_target_pairs={{0,64},{1,65},{2,66},{3,67},{64,0},{65,1},{66,2},{67,3},{16,80},{1... | collective-permute-start | bytes 983048 | tf_op jit(solution)/shard_map/ppermute | solution.py:43
  134.5 9.6 %collective-permute-start.28 = (bf16[256,512]{1,0:T(8,128)(2,1)S(1)}, bf16[256,512]{1,0:T(8,128)(2,1)S(1)}, u32[]{:S(2)}, u32[]{:S(2)}) collective-permute-start(bf16[256,512]{1,0:T(8,128)(2,1)S(1)} %add_convert_fusion.8), channel_id=1, source_target_pairs={{0,48},{1,49},{2,50},{3,51},{64,112},{65,113},{66,114},{67,115},{1... | collective-permute-start | bytes 786440 | tf_op jit(solution)/shard_map/ppermute | solution.py:43
  135.4 7.9 %copy-start.32 = (bf16[256,512]{1,0:T(8,128)(2,1)S(1)}, bf16[256,512]{1,0:T(8,128)(2,1)}, u32[]{:S(2)}) copy-start(bf16[256,512]{1,0:T(8,128)(2,1)} %param.4) | copy-start | bytes 786436
  142.2 6.4 %collective-permute-start.27 = (bf16[256,512]{1,0:T(8,128)(2,1)S(1)}, bf16[256,512]{1,0:T(8,128)(2,1)S(1)}, u32[]{:S(2)}, u32[]{:S(2)}) collective-permute-start(bf16[256,512]{1,0:T(8,128)(2,1)S(1)} %add_convert_fusion.9), channel_id=1, source_target_pairs={{0,16},{1,17},{2,18},{3,19},{64,80},{65,81},{66,82},{67,83},{16,0}... | collective-permute-start | bytes 786440 | tf_op jit(solution)/shard_map/ppermute | solution.py:43
  144.1 6.6 %collective-permute-start.31 = (f32[1,512]{1,0:T(1,128)S(1)}, f32[1,512]{1,0:T(1,128)S(1)}, u32[]{:S(2)}, u32[]{:S(2)}) collective-permute-start(f32[1,512]{1,0:T(1,128)S(1)} %bitcast.32), channel_id=1, source_target_pairs={{0,1},{1,0},{2,3},{3,2},{64,65},{65,64},{66,67},{67,66},{16,17},{1... | collective-permute-start | bytes 6152 | tf_op jit(solution)/shard_map/ppermute | solution.py:43
  148.8 8.0 %collective-permute-start.30 = (bf16[256,512]{1,0:T(8,128)(2,1)S(1)}, bf16[256,512]{1,0:T(8,128)(2,1)S(1)}, u32[]{:S(2)}, u32[]{:S(2)}) collective-permute-start(bf16[256,512]{1,0:T(8,128)(2,1)S(1)} %select_convert_fusion.2), channel_id=1, source_target_pairs={{0,64},{1,65},{2,66},{3,67},{64,0},{65,1},{66,2},{67,3},{16,80},{1... | collective-permute-start | bytes 786440 | tf_op jit(solution)/shard_map/ppermute | solution.py:43
  150.7 5.0 %collective-permute-start.32 = (f32[1,512]{1,0:T(1,128)S(1)}, f32[1,512]{1,0:T(1,128)S(1)}, u32[]{:S(2)}, u32[]{:S(2)}) collective-permute-start(f32[1,512]{1,0:T(1,128)S(1)} %add.216), channel_id=1, source_target_pairs={{0,2},{1,3},{2,0},{3,1},{64,66},{65,67},{66,64},{67,65},{16,18},{1... | collective-permute-start | bytes 6152 | tf_op jit(solution)/shard_map/ppermute | solution.py:43
  151.6 7.9 %collective-permute-start.37 = (bf16[256,768]{1,0:T(8,128)(2,1)S(1)}, bf16[256,768]{1,0:T(8,128)(2,1)S(1)}, u32[]{:S(2)}, u32[]{:S(2)}) collective-permute-start(bf16[256,768]{1,0:T(8,128)(2,1)S(1)} %add_convert_fusion.1), channel_id=1, source_target_pairs={{0,4},{1,5},{2,6},{3,7},{64,68},{65,69},{66,70},{67,71},{16,20},{1... | collective-permute-start | bytes 1179656 | tf_op jit(solution)/shard_map/ppermute | solution.py:43
  152.1 9.1 %collective-permute-start.36 = (bf16[256,768]{1,0:T(8,128)(2,1)S(1)}, bf16[256,768]{1,0:T(8,128)(2,1)S(1)}, u32[]{:S(2)}, u32[]{:S(2)}) collective-permute-start(bf16[256,768]{1,0:T(8,128)(2,1)S(1)} %add_convert_fusion.2), channel_id=1, source_target_pairs={{0,12},{1,13},{2,14},{3,15},{64,76},{65,77},{66,78},{67,79},{16,28... | collective-permute-start | bytes 1179656 | tf_op jit(solution)/shard_map/ppermute | solution.py:43
  161.1 3.6 %collective-permute-start.38 = (f32[1,512]{1,0:T(1,128)S(1)}, f32[1,512]{1,0:T(1,128)S(1)}, u32[]{:S(2)}, u32[]{:S(2)}) collective-permute-start(f32[1,512]{1,0:T(1,128)S(1)} %add.217), channel_id=1, source_target_pairs={{0,4},{1,5},{2,6},{3,7},{64,68},{65,69},{66,70},{67,71},{16,20},{1... | collective-permute-start | bytes 6152 | tf_op jit(solution)/shard_map/ppermute | solution.py:43
  164.7 5.1 %collective-permute-start.39 = (f32[1,512]{1,0:T(1,128)S(1)}, f32[1,512]{1,0:T(1,128)S(1)}, u32[]{:S(2)}, u32[]{:S(2)}) collective-permute-start(f32[1,512]{1,0:T(1,128)S(1)} %add.224), channel_id=1, source_target_pairs={{0,8},{1,9},{2,10},{3,11},{64,72},{65,73},{66,74},{67,75},{16,24},... | collective-permute-start | bytes 6152 | tf_op jit(solution)/shard_map/ppermute | solution.py:43
  (17 other events, 24.2 us)

commit v11 on v9

--- a/solution.py
+++ b/solution.py
@@ -361,10 +361,11 @@
     x_own = inputs.astype(f32)
     d_input = (d_normed * gain.astype(f32) - inv[:, :1] * products * x_own).astype(bf16)
     d_gain = jnp.sum(d_normed * x_own, axis=0, keepdims=True)
-    for move in ("c", "z^1", "x^1", "x+2"):
-        if move == "x^1":
-            d_gain = after(d_gain, *pair_last)
+    for move in ("c", "z^1"):
         d_gain = d_gain + send(d_gain, move)
+    d_gain = after(d_gain, *pair_last)
+    beside, across, opposite = send(d_gain, "x^1"), send(d_gain, "x^3"), send(d_gain, "x+2")
+    d_gain = (d_gain + beside) + (across + opposite)
 
     gain_rows = lax.dynamic_slice(gains, (0, s * 256), (1, 256)).astype(f32).reshape(256, 1)
     d_weights = jnp.stack(

time: 167 us -> 166 us (level)
  waiting for transfers between devices: 64.1 us -> 60 us
  starting transfers between devices: 42.2 us -> 44.5 us
    ppermute x40 -> x41, waiting for transfers between devices: 64.1 us -> 60 us  [send(): return lax.ppermute(value, AXES, pairs(moves[move]))]
    ppermute x40 -> x41, starting transfers between devices: 42.2 us -> 44.5 us  [send(): return lax.ppermute(value, AXES, pairs(moves[move]))]
  transfers between devices with their start and end apart: 40 -> 41, of which waited for: 23 -> 24; matrix products, arithmetic and copies ran while one was open for 6% -> 6% of each run, Pallas kernels for 19% -> 19%
where the time goes in v11:
time: 166 us; the launch traced here: 165 us
  waiting for transfers between devices  60 us (36%)
  starting transfers between devices  44.5 us (27%)
  Pallas kernels  38.4 us (23%)
  other arithmetic  12.1 us (7%)
  local copies, waits for them, and re-layouts  9.06 us (5%)
    ppermute x41, waiting for transfers between devices, send(): return lax.ppermute(value, AXES, pairs(moves[move]))  60 us
    ppermute x41, starting transfers between devices, send(): return lax.ppermute(value, AXES, pairs(moves[move]))  44.5 us
    pallas_call x7, Pallas kernels, call(): pl.pallas_call(whole, in_specs=[pl.BlockSpec(memory_space=space) for spac...  38.4 us
    unnamed x82, local copies, waits for them, and re-layouts  8.04 us
  transfers between devices with their start and end apart: 41, of which 24 were waited for; matrix products, arithmetic and copies ran while one was open for 6% of the time, Pallas kernels for 19%

profile of v11, /device:TPU:0, one launch (start us, length us, event | category | flops | bytes accessed | tf_op | source)
XLA Modules:
  0.0 165.2 jit_solution(2760642937164330557)
XLA Ops:
  1.3 1.0 pad_maximum_fusion.6.refs_1_
  2.3 3.2 %collective-permute-start.1 = (bf16[272,512]{1,0:T(8,128)(2,1)S(1)}, bf16[272,512]{1,0:T(8,128)(2,1)S(1)}, u32[]{:S(2)}, u32[]{:S(2)}) collective-permute-start(bf16[272,512]{1,0:T(8,128)(2,1)S(1)} %pad_maximum_fusion.6.refs_1_), channel_id=1, source_target_pairs={{0,48},{1,49},{2,50},{3,51},{64,112},{65,113},{66,114},{67,115},{1... | collective-permute-start | bytes 835592 | tf_op jit(solution)/shard_map/ppermute | solution.py:43
  5.5 3.9 %collective-permute-start.2 = (bf16[272,512]{1,0:T(8,128)(2,1)S(1)}, bf16[272,512]{1,0:T(8,128)(2,1)S(1)}, u32[]{:S(2)}, u32[]{:S(2)}) collective-permute-start(bf16[272,512]{1,0:T(8,128)(2,1)S(1)} %pad_maximum_fusion.6.refs_1_), channel_id=1, source_target_pairs={{0,64},{1,65},{2,66},{3,67},{64,0},{65,1},{66,2},{67,3},{16,80},{1... | collective-permute-start | bytes 835592 | tf_op jit(solution)/shard_map/ppermute | solution.py:43
  9.4 2.0 %collective-permute-done.1.refs_3_ = bf16[272,512]{1,0:T(8,128)(2,1)S(1)} collective-permute-done((bf16[272,512]{1,0:T(8,128)(2,1)S(1)}, bf16[272,512]{1,0:T(8,128)(2,1)S(1)}, u32[]{:S(2)}, u32[]{:S(2)}) %collective-permute-start.1) | collective-permute-done | bytes 278560 | tf_op jit(solution)/shard_map/ppermute | solution.py:43
  11.4 4.3 %collective-permute-done.2.refs_4_ = bf16[272,512]{1,0:T(8,128)(2,1)S(1)} collective-permute-done((bf16[272,512]{1,0:T(8,128)(2,1)S(1)}, bf16[272,512]{1,0:T(8,128)(2,1)S(1)}, u32[]{:S(2)}, u32[]{:S(2)}) %collective-permute-start.2) | collective-permute-done | bytes 278560 | tf_op jit(solution)/shard_map/ppermute | solution.py:43
  15.8 0.8 collective-permute-start.4
  16.6 1.8 %collective-permute-done.refs_2_ = bf16[272,512]{1,0:T(8,128)(2,1)S(1)} collective-permute-done((bf16[272,512]{1,0:T(8,128)(2,1)S(1)}, bf16[272,512]{1,0:T(8,128)(2,1)S(1)}, u32[]{:S(2)}, u32[]{:S(2)}) %collective-permute-start) | collective-permute-done | bytes 278560 | tf_op jit(solution)/shard_map/ppermute | solution.py:43
  18.6 2.7 %collective-permute-start.5 = (bf16[256,512]{1,0:T(8,128)(2,1)S(1)}, bf16[256,512]{1,0:T(8,128)(2,1)S(1)}, u32[]{:S(2)}, u32[]{:S(2)}) collective-permute-start(bf16[256,512]{1,0:T(8,128)(2,1)S(1)} %copy-done.38), channel_id=1, source_target_pairs={{0,64},{1,65},{2,66},{3,67},{64,0},{65,1},{66,2},{67,3},{16,80},{1... | collective-permute-start | bytes 786440 | tf_op jit(solution)/shard_map/ppermute | solution.py:43
  21.3 5.5 %collective-permute-done.5 = bf16[256,512]{1,0:T(8,128)(2,1)S(1)} collective-permute-done((bf16[256,512]{1,0:T(8,128)(2,1)S(1)}, bf16[256,512]{1,0:T(8,128)(2,1)S(1)}, u32[]{:S(2)}, u32[]{:S(2)}) %collective-permute-start.5) | collective-permute-done | bytes 262176 | tf_op jit(solution)/shard_map/ppermute | solution.py:43
  26.7 2.7 %collective-permute-done.3.refs_5_ = bf16[400,512]{1,0:T(8,128)(2,1)S(1)} collective-permute-done((bf16[400,512]{1,0:T(8,128)(2,1)S(1)}, bf16[400,512]{1,0:T(8,128)(2,1)S(1)}, u32[]{:S(2)}, u32[]{:S(2)}) %collective-permute-start.3) | collective-permute-done | bytes 409632 | tf_op jit(solution)/shard_map/ppermute | solution.py:43
  29.8 0.7 pad_maximum_fusion.7
  30.5 1.6 collective-permute-start.6
  32.2 1.5 collective-permute-start.7
  33.8 5.1 %collective-permute-done.6.refs_7_ = bf16[272,512]{1,0:T(8,128)(2,1)} collective-permute-done((bf16[272,512]{1,0:T(8,128)(2,1)}, bf16[272,512]{1,0:T(8,128)(2,1)}, u32[]{:S(2)}, u32[]{:S(2)}) %collective-permute-start.6) | collective-permute-done | bytes 278560 | tf_op jit(solution)/shard_map/ppermute | solution.py:43
  38.9 1.4 assemble.1
  40.4 0.8 copy-done.23
  41.2 1.8 %collective-permute-start.9 = (bf16[256,1024]{1,0:T(8,128)(2,1)S(1)}, bf16[256,1024]{1,0:T(8,128)(2,1)S(1)}, u32[]{:S(2)}, u32[]{:S(2)}) collective-permute-start(bf16[256,1024]{1,0:T(8,128)(2,1)S(1)} %get-tuple-element.101), channel_id=1, source_target_pairs={{0,66},{1,67},{2,64},{3,65},{64,2},{65,3},{66,0},{67,1},{16,82},{1... | collective-permute-start | bytes 1572872 | tf_op jit(solution)/shard_map/ppermute | solution.py:43
  43.6 0.8 collective-permute-done.7.refs_2_
  44.4 0.9 collective-permute-start.11
  45.3 6.3 %forward.1 = (f32[256,768]{1,0:T(8,128)S(1)}, f32[256,768]{1,0:T(8,128)S(1)}, bf16[256,768]{1,0:T(8,128)(2,1)S(1)}, f32[256,128]{1,0:T(8,128)S(1)}, bf16[256,1792]{1,0:T(8,128)(2,1)}) custom-call(bf16[272,4096]{1,0:T(8,128)(2,1)S(1)} %get-tuple-element.98.refs_0_, bf16[256,1024]{1,0:T(8,128)(2,1)S(1)} %get-tuple-element.99.refs_1_, ...), custom_call_target="tpu_custom_call" | custom-call | flops 3221225472 | bytes 16777216 | tf_op jit(solution)/shard_map/forward/pallas_call | solution.py:89
  52.2 0.8 copy-done.25
  53.1 0.8 copy-done.36
  53.8 6.8 %backward.1 = (bf16[256,1536]{1,0:T(8,128)(2,1)S(1)}, bf16[256,128]{1,0:T(8,128)(2,1)S(1)}, bf16[256,2048]{1,0:T(8,128)(2,1)S(1)}, bf16[256,3584]{1,0:T(8,128)(2,1)}) custom-call(s32[10]{0:T(128)S(1)} %stack.116.refs_0_, bf16[512,512]{1,0:T(8,128)(2,1)S(1)} %pad_maximum_fusion.3.refs_1_, bf16[512,512]{1,0:T(8,128)(2,1)S(1)} %collective-permute-done.7.refs_2_, ...), custom_call_target="tpu_custom_call" | custom-call | flops 1610612736 | bytes 8388608 | tf_op jit(solution)/shard_map/backward/pallas_call | solution.py:89
  61.3 1.0 copy-done.19
  63.0 1.5 collective-permute-start.16
  64.4 5.2 %branch_rows.1 = (bf16[512,512]{1,0:T(8,128)(2,1)S(1)}, bf16[512,512]{1,0:T(8,128)(2,1)S(1)}, bf16[256,512]{1,0:T(8,128)(2,1)S(1)}, bf16[256,512]{1,0:T(8,128)(2...) custom-call(s32[8]{0:T(128)S(1)} %stack.105.refs_0_, ...), custom_call_target="tpu_custom_call" | custom-call | flops 1610612736 | bytes 8388608 | tf_op jit(solution)/shard_map/branch_rows/pallas_call | solution.py:89
  70.3 0.7 copy-done.14
  71.0 1.0 copy-done.3
  72.0 4.8 %down_terms.1 = (bf16[1024,384]{1,0:T(8,128)(2,1)S(1)}, bf16[1024,384]{1,0:T(8,128)(2,1)S(1)}, bf16[512,384]{1,0:T(8,128)(2,1)S(1)}, bf16[512,384]{1,0:T(8,128)(...) custom-call(s32[8]{0:T(128)S(1)} %stack.121.refs_0_, bf16[256,2048]{1,0:T(8,128)(2,1)S(1)} %copy-done.20, ...), custom_call_target="tpu_custom_call" | custom-call | flops 1610612736 | bytes 8388608 | tf_op jit(solution)/shard_map/down_terms/pallas_call | solution.py:89
  76.8 2.8 %collective-permute-start.19 = (bf16[1024,384]{1,0:T(8,128)(2,1)S(1)}, bf16[1024,384]{1,0:T(8,128)(2,1)S(1)}, u32[]{:S(2)}, u32[]{:S(2)}) collective-permute-start(bf16[1024,384]{1,0:T(8,128)(2,1)S(1)} %get-tuple-element.131), channel_id=1, source_target_pairs={{0,12},{1,13},{2,14},{3,15},{64,76},{65,77},{66,78},{67,79},{16,28... | collective-permute-start | bytes 2359304 | tf_op jit(solution)/shard_map/ppermute | solution.py:43
  79.9 1.7 %collective-permute-start.13 = (bf16[512,512]{1,0:T(8,128)(2,1)S(1)}, bf16[512,512]{1,0:T(8,128)(2,1)S(1)}, u32[]{:S(2)}, u32[]{:S(2)}) collective-permute-start(bf16[512,512]{1,0:T(8,128)(2,1)S(1)} %get-tuple-element.112), channel_id=1, source_target_pairs={{0,48},{1,49},{2,50},{3,51},{64,112},{65,113},{66,114},{67,115},{1... | collective-permute-start | bytes 1572872 | tf_op jit(solution)/shard_map/ppermute | solution.py:43
  81.6 7.1 %pair_rows.1 = (bf16[512,640]{1,0:T(8,128)(2,1)S(1)}, bf16[512,640]{1,0:T(8,128)(2,1)S(1)}, bf16[256,640]{1,0:T(8,128)(2,1)S(1)}, bf16[256,640]{1,0:T(8,128)(2,1...) custom-call(s32[8]{0:T(128)S(1)} %stack.105.refs_0_, ...), custom_call_target="tpu_custom_call" | custom-call | flops 3221225472 | bytes 16777216 | tf_op jit(solution)/shard_map/pair_rows/pallas_call | solution.py:89
  88.7 0.7 copy-done.6
  89.4 0.7 copy-done.8
  90.2 4.0 %collective-permute-done.13 = bf16[512,512]{1,0:T(8,128)(2,1)S(1)} collective-permute-done((bf16[512,512]{1,0:T(8,128)(2,1)S(1)}, bf16[512,512]{1,0:T(8,128)(2,1)S(1)}, u32[]{:S(2)}, u32[]{:S(2)}) %collective-permute-start.13) | collective-permute-done | bytes 524320 | tf_op jit(solution)/shard_map/ppermute | solution.py:43
  94.4 2.9 %collective-permute-done.19 = bf16[1024,384]{1,0:T(8,128)(2,1)S(1)} collective-permute-done((bf16[1024,384]{1,0:T(8,128)(2,1)S(1)}, bf16[1024,384]{1,0:T(8,128)(2,1)S(1)}, u32[]{:S(2)}, u32[]{:S(2)}) %collective-permute-start.19) | collective-permute-done | bytes 786464 | tf_op jit(solution)/shard_map/ppermute | solution.py:43
  97.3 1.2 collective-permute-done.18
  98.6 1.3 pad_maximum_fusion
  100.6 1.5 collective-permute-start.23
  102.8 1.1 add_convert_fusion.3
  104.2 1.1 add_convert_fusion.4
  105.3 1.7 %collective-permute-start.21 = (bf16[512,384]{1,0:T(8,128)(2,1)S(1)}, bf16[512,384]{1,0:T(8,128)(2,1)S(1)}, u32[]{:S(2)}, u32[]{:S(2)}) collective-permute-start(bf16[512,384]{1,0:T(8,128)(2,1)S(1)} %add_convert_fusion.4), channel_id=1, source_target_pairs={{0,12},{1,13},{2,14},{3,15},{64,76},{65,77},{66,78},{67,79},{16,28... | collective-permute-start | bytes 1179656 | tf_op jit(solution)/shard_map/ppermute | solution.py:43
  107.7 6.8 %pair_terms.1 = (bf16[512,768]{1,0:T(8,128)(2,1)S(1)}, bf16[512,768]{1,0:T(8,128)(2,1)S(1)}, bf16[256,768]{1,0:T(8,128)(2,1)S(1)}, bf16[256,768]{1,0:T(8,128)(2,...) custom-call(s32[8]{0:T(128)S(1)} %stack.121.refs_0_, bf16[256,1024]{1,0:T(8,128)(2,1)S(1)} %copy-done.24, ...), custom_call_target="tpu_custom_call" | custom-call | flops 3221225472 | bytes 8388608 | tf_op jit(solution)/shard_map/pair_terms/pallas_call | solution.py:89
  114.9 2.6 %collective-permute-done.21 = bf16[512,384]{1,0:T(8,128)(2,1)S(1)} collective-permute-done((bf16[512,384]{1,0:T(8,128)(2,1)S(1)}, bf16[512,384]{1,0:T(8,128)(2,1)S(1)}, u32[]{:S(2)}, u32[]{:S(2)}) %collective-permute-start.21) | collective-permute-done | bytes 393248 | tf_op jit(solution)/shard_map/ppermute | solution.py:43
  118.0 2.3 %collective-permute-done.24 = bf16[512,640]{1,0:T(8,128)(2,1)S(1)} collective-permute-done((bf16[512,640]{1,0:T(8,128)(2,1)}, bf16[512,640]{1,0:T(8,128)(2,1)S(1)}, u32[]{:S(2)}, u32[]{:S(2)}) %collective-permute-start.24) | collective-permute-done | bytes 655392 | tf_op jit(solution)/shard_map/ppermute | solution.py:43
  120.6 1.0 collective-permute-start.25
  122.1 0.8 collective-permute-start.35
  122.9 1.7 %collective-permute-start.30 = (bf16[512,768]{1,0:T(8,128)(2,1)S(1)}, bf16[512,768]{1,0:T(8,128)(2,1)S(1)}, u32[]{:S(2)}, u32[]{:S(2)}) collective-permute-start(bf16[512,768]{1,0:T(8,128)(2,1)S(1)} %get-tuple-element.164), channel_id=1, source_target_pairs={{0,12},{1,13},{2,14},{3,15},{64,76},{65,77},{66,78},{67,79},{16,28... | collective-permute-start | bytes 2359304 | tf_op jit(solution)/shard_map/ppermute | solution.py:43
  124.7 4.8 %collective-permute-done.26 = bf16[256,640]{1,0:T(8,128)(2,1)S(1)} collective-permute-done((bf16[256,640]{1,0:T(8,128)(2,1)S(1)}, bf16[256,640]{1,0:T(8,128)(2,1)S(1)}, u32[]{:S(2)}, u32[]{:S(2)}) %collective-permute-start.26) | collective-permute-done | bytes 327712 | tf_op jit(solution)/shard_map/ppermute | solution.py:43
  129.5 1.4 collective-permute-done.25
  131.0 0.8 collective-permute-start.28
  132.3 9.9 %collective-permute-done.30 = bf16[512,768]{1,0:T(8,128)(2,1)S(1)} collective-permute-done((bf16[512,768]{1,0:T(8,128)(2,1)S(1)}, bf16[512,768]{1,0:T(8,128)(2,1)S(1)}, u32[]{:S(2)}, u32[]{:S(2)}) %collective-permute-start.30) | collective-permute-done | bytes 786464 | tf_op jit(solution)/shard_map/ppermute | solution.py:43
  142.2 2.2 %collective-permute-start.31 = (bf16[256,640]{1,0:T(8,128)(2,1)S(1)}, bf16[256,640]{1,0:T(8,128)(2,1)S(1)}, u32[]{:S(2)}, u32[]{:S(2)}) collective-permute-start(bf16[256,640]{1,0:T(8,128)(2,1)S(1)} %get-tuple-element.165), channel_id=1, source_target_pairs={{0,64},{1,65},{2,66},{3,67},{64,0},{65,1},{66,2},{67,3},{16,80},{1... | collective-permute-start | bytes 983048 | tf_op jit(solution)/shard_map/ppermute | solution.py:43
  144.7 1.8 %collective-permute-start.36 = (bf16[256,768]{1,0:T(8,128)(2,1)S(1)}, bf16[256,768]{1,0:T(8,128)(2,1)S(1)}, u32[]{:S(2)}, u32[]{:S(2)}) collective-permute-start(bf16[256,768]{1,0:T(8,128)(2,1)S(1)} %add_convert_fusion.2), channel_id=1, source_target_pairs={{0,12},{1,13},{2,14},{3,15},{64,76},{65,77},{66,78},{67,79},{16,28... | collective-permute-start | bytes 1179656 | tf_op jit(solution)/shard_map/ppermute | solution.py:43
  146.6 4.4 %collective-permute-done.31 = bf16[256,640]{1,0:T(8,128)(2,1)S(1)} collective-permute-done((bf16[256,640]{1,0:T(8,128)(2,1)S(1)}, bf16[256,640]{1,0:T(8,128)(2,1)S(1)}, u32[]{:S(2)}, u32[]{:S(2)}) %collective-permute-start.31) | collective-permute-done | bytes 327712 | tf_op jit(solution)/shard_map/ppermute | solution.py:43
  151.2 0.9 fusion.3
  152.2 1.0 collective-permute-done.33
  153.2 1.2 collective-permute-start.34
  154.6 2.1 %collective-permute-start.32 = (bf16[256,512]{1,0:T(8,128)(2,1)S(1)}, bf16[256,512]{1,0:T(8,128)(2,1)S(1)}, u32[]{:S(2)}, u32[]{:S(2)}) collective-permute-start(bf16[256,512]{1,0:T(8,128)(2,1)S(1)} %select_convert_fusion.2), channel_id=1, source_target_pairs={{0,64},{1,65},{2,66},{3,67},{64,0},{65,1},{66,2},{67,3},{16,80},{1... | collective-permute-start | bytes 786440 | tf_op jit(solution)/shard_map/ppermute | solution.py:43
  157.1 1.6 collective-permute-start.39
  158.7 1.7 %collective-permute-start.38 = (f32[1,512]{1,0:T(1,128)S(1)}, f32[1,512]{1,0:T(1,128)S(1)}, u32[]{:S(2)}, u32[]{:S(2)}) collective-permute-start(f32[1,512]{1,0:T(1,128)S(1)} %add.220), channel_id=1, source_target_pairs={{0,4},{1,5},{2,6},{3,7},{64,68},{65,69},{66,70},{67,71},{16,20},{1... | collective-permute-start | bytes 6152 | tf_op jit(solution)/shard_map/ppermute | solution.py:43
  160.8 1.1 pad_maximum_fusion.1
  162.9 1.4 collective-permute-done.32
  164.3 0.9 add_convert_fusion.7
  (149 shorter events, 12.1 us)
Async XLA Ops:
  1.3 17.2 %copy-start.38 = (bf16[256,512]{1,0:T(8,128)(2,1)S(1)}, bf16[256,512]{1,0:T(8,128)(2,1)}, u32[]{:S(2)}) copy-start(bf16[256,512]{1,0:T(8,128)(2,1)} %param.7) | copy-start | bytes 786436
  2.3 9.1 %collective-permute-start.1 = (bf16[272,512]{1,0:T(8,128)(2,1)S(1)}, bf16[272,512]{1,0:T(8,128)(2,1)S(1)}, u32[]{:S(2)}, u32[]{:S(2)}) collective-permute-start(bf16[272,512]{1,0:T(8,128)(2,1)S(1)} %pad_maximum_fusion.6.refs_1_), channel_id=1, source_target_pairs={{0,48},{1,49},{2,50},{3,51},{64,112},{65,113},{66,114},{67,115},{1... | collective-permute-start | bytes 835592 | tf_op jit(solution)/shard_map/ppermute | solution.py:43
  5.5 10.2 %collective-permute-start.2 = (bf16[272,512]{1,0:T(8,128)(2,1)S(1)}, bf16[272,512]{1,0:T(8,128)(2,1)S(1)}, u32[]{:S(2)}, u32[]{:S(2)}) collective-permute-start(bf16[272,512]{1,0:T(8,128)(2,1)S(1)} %pad_maximum_fusion.6.refs_1_), channel_id=1, source_target_pairs={{0,64},{1,65},{2,66},{3,67},{64,0},{65,1},{66,2},{67,3},{16,80},{1... | collective-permute-start | bytes 835592 | tf_op jit(solution)/shard_map/ppermute | solution.py:43
  9.4 9.0 %collective-permute-start = (bf16[272,512]{1,0:T(8,128)(2,1)S(1)}, bf16[272,512]{1,0:T(8,128)(2,1)S(1)}, u32[]{:S(2)}, u32[]{:S(2)}) collective-permute-start(bf16[272,512]{1,0:T(8,128)(2,1)S(1)} %pad_maximum_fusion.6.refs_1_), channel_id=1, source_target_pairs={{0,16},{1,17},{2,18},{3,19},{64,80},{65,81},{66,82},{67,83},{16,32... | collective-permute-start | bytes 835592 | tf_op jit(solution)/shard_map/ppermute | solution.py:43
  15.8 13.7 %collective-permute-start.4 = (bf16[416,512]{1,0:T(8,128)(2,1)S(1)}, bf16[416,512]{1,0:T(8,128)(2,1)S(1)}, u32[]{:S(2)}, u32[]{:S(2)}) collective-permute-start(bf16[416,512]{1,0:T(8,128)(2,1)S(1)} %pad_maximum_fusion.4), channel_id=1, source_target_pairs={{0,48},{1,49},{2,50},{3,51},{64,112},{65,113},{66,114},{67,115},{1... | collective-permute-start | bytes 1277960 | tf_op jit(solution)/shard_map/ppermute | solution.py:43
  18.5 11.0 %collective-permute-start.3 = (bf16[400,512]{1,0:T(8,128)(2,1)S(1)}, bf16[400,512]{1,0:T(8,128)(2,1)S(1)}, u32[]{:S(2)}, u32[]{:S(2)}) collective-permute-start(bf16[400,512]{1,0:T(8,128)(2,1)S(1)} %pad_maximum_fusion.5), channel_id=1, source_target_pairs={{0,16},{1,17},{2,18},{3,19},{64,80},{65,81},{66,82},{67,83},{16,32... | collective-permute-start | bytes 1228808 | tf_op jit(solution)/shard_map/ppermute | solution.py:43
  18.6 8.1 %collective-permute-start.5 = (bf16[256,512]{1,0:T(8,128)(2,1)S(1)}, bf16[256,512]{1,0:T(8,128)(2,1)S(1)}, u32[]{:S(2)}, u32[]{:S(2)}) collective-permute-start(bf16[256,512]{1,0:T(8,128)(2,1)S(1)} %copy-done.38), channel_id=1, source_target_pairs={{0,64},{1,65},{2,66},{3,67},{64,0},{65,1},{66,2},{67,3},{16,80},{1... | collective-permute-start | bytes 786440 | tf_op jit(solution)/shard_map/ppermute | solution.py:43
  29.5 13.5 %collective-permute-start.8 = (bf16[512,512]{1,0:T(8,128)(2,1)S(1)}, bf16[512,512]{1,0:T(8,128)(2,1)S(1)}, u32[]{:S(2)}, u32[]{:S(2)}) collective-permute-start(bf16[512,512]{1,0:T(8,128)(2,1)S(1)} %pad_maximum_fusion.3.refs_1_), channel_id=1, source_target_pairs={{0,48},{1,49},{2,50},{3,51},{64,112},{65,113},{66,114},{67,115},{1... | collective-permute-start | bytes 1572872 | tf_op jit(solution)/shard_map/ppermute | solution.py:43
  30.5 8.4 %collective-permute-start.6 = (bf16[272,512]{1,0:T(8,128)(2,1)}, bf16[272,512]{1,0:T(8,128)(2,1)}, u32[]{:S(2)}, u32[]{:S(2)}) collective-permute-start(bf16[272,512]{1,0:T(8,128)(2,1)} %pad_maximum_fusion.7), channel_id=1, source_target_pairs={{0,64},{1,65},{2,66},{3,67},{64,0},{65,1},{66,2},{67,3},{16,80},{1... | collective-permute-start | bytes 835592 | tf_op jit(solution)/shard_map/ppermute | solution.py:43
  32.2 12.2 %collective-permute-start.7 = (bf16[512,512]{1,0:T(8,128)(2,1)S(1)}, bf16[512,512]{1,0:T(8,128)(2,1)S(1)}, u32[]{:S(2)}, u32[]{:S(2)}) collective-permute-start(bf16[512,512]{1,0:T(8,128)(2,1)S(1)} %pad_maximum_fusion.3.refs_1_), channel_id=1, source_target_pairs={{0,16},{1,17},{2,18},{3,19},{64,80},{65,81},{66,82},{67,83},{16,32... | collective-permute-start | bytes 1572872 | tf_op jit(solution)/shard_map/ppermute | solution.py:43
  41.2 11.0 %collective-permute-start.9 = (bf16[256,1024]{1,0:T(8,128)(2,1)S(1)}, bf16[256,1024]{1,0:T(8,128)(2,1)S(1)}, u32[]{:S(2)}, u32[]{:S(2)}) collective-permute-start(bf16[256,1024]{1,0:T(8,128)(2,1)S(1)} %get-tuple-element.101), channel_id=1, source_target_pairs={{0,66},{1,67},{2,64},{3,65},{64,2},{65,3},{66,0},{67,1},{16,82},{1... | collective-permute-start | bytes 1572872 | tf_op jit(solution)/shard_map/ppermute | solution.py:43
  43.0 10.0 %collective-permute-start.10 = (bf16[256,1024]{1,0:T(8,128)(2,1)S(1)}, bf16[256,1024]{1,0:T(8,128)(2,1)S(1)}, u32[]{:S(2)}, u32[]{:S(2)}) collective-permute-start(bf16[256,1024]{1,0:T(8,128)(2,1)S(1)} %get-tuple-element.102), channel_id=1, source_target_pairs={{0,2},{1,3},{2,0},{3,1},{64,66},{65,67},{66,64},{67,65},{16,18},{1... | collective-permute-start | bytes 1572872 | tf_op jit(solution)/shard_map/ppermute | solution.py:43
  43.1 10.0 %collective-permute-start.12 = (bf16[256,512]{1,0:T(8,128)(2,1)S(1)}, bf16[256,512]{1,0:T(8,128)(2,1)S(1)}, u32[]{:S(2)}, u32[]{:S(2)}) collective-permute-start(bf16[256,512]{1,0:T(8,128)(2,1)S(1)} %pad_maximum_fusion.9), channel_id=1, source_target_pairs={{0,48},{1,49},{2,50},{3,51},{64,112},{65,113},{66,114},{67,115},{1... | collective-permute-start | bytes 786440 | tf_op jit(solution)/shard_map/ppermute | solution.py:43
  44.4 8.6 %collective-permute-start.11 = (bf16[256,512]{1,0:T(8,128)(2,1)S(1)}, bf16[256,512]{1,0:T(8,128)(2,1)S(1)}, u32[]{:S(2)}, u32[]{:S(2)}) collective-permute-start(bf16[256,512]{1,0:T(8,128)(2,1)S(1)} %pad_maximum_fusion.8), channel_id=1, source_target_pairs={{0,16},{1,17},{2,18},{3,19},{64,80},{65,81},{66,82},{67,83},{16,32... | collective-permute-start | bytes 786440 | tf_op jit(solution)/shard_map/ppermute | solution.py:43
  51.6 12.8 %copy-start.2 = (bf16[256,768]{1,0:T(8,128)(2,1)}, bf16[256,768]{1,0:T(8,128)(2,1)S(1)}, u32[]{:S(2)}) copy-start(bf16[256,768]{1,0:T(8,128)(2,1)S(1)} %get-tuple-element.108.refs_1_.refs_3_) | copy-start | bytes 1179652
  62.3 8.8 %collective-permute-start.17 = (bf16[256,3584]{1,0:T(8,128)(2,1)}, bf16[256,3584]{1,0:T(8,128)(2,1)}, u32[]{:S(2)}, u32[]{:S(2)}) collective-permute-start(bf16[256,3584]{1,0:T(8,128)(2,1)} %get-tuple-element.120), channel_id=1, source_target_pairs={{0,1},{1,0},{2,3},{3,2},{64,65},{65,64},{66,67},{67,66},{16,17},{1... | collective-permute-start | bytes 5505032 | tf_op jit(solution)/shard_map/ppermute | solution.py:43
  62.3 8.8 %collective-permute-start.15 = (bf16[256,1792]{1,0:T(8,128)(2,1)}, bf16[256,1792]{1,0:T(8,128)(2,1)}, u32[]{:S(2)}, u32[]{:S(2)}) collective-permute-start(bf16[256,1792]{1,0:T(8,128)(2,1)} %get-tuple-element.117), channel_id=1, source_target_pairs={{0,1},{1,0},{2,3},{3,2},{64,65},{65,64},{66,67},{67,66},{16,17},{1... | collective-permute-start | bytes 2752520 | tf_op jit(solution)/shard_map/ppermute | solution.py:43
  63.0 31.4 %collective-permute-start.16 = (bf16[256,1536]{1,0:T(8,128)(2,1)S(1)}, bf16[256,1536]{1,0:T(8,128)(2,1)S(1)}, u32[]{:S(2)}, u32[]{:S(2)}) collective-permute-start(bf16[256,1536]{1,0:T(8,128)(2,1)S(1)} %get-tuple-element.122.refs_1_.refs_5_), channel_id=1, source_target_pairs={{0,2},{1,3},{2,0},{3,1},{64,66},{65,67},{66,64},{67,65},{16,18},{1... | collective-permute-start | bytes 2359304 | tf_op jit(solution)/shard_map/ppermute | solution.py:43
  72.0 9.6 %copy-start.17 = (bf16[256,128]{1,0:T(8,128)(2,1)S(1)}, bf16[256,128]{1,0:T(8,128)(2,1)}, u32[]{:S(2)}) copy-start(bf16[256,128]{1,0:T(8,128)(2,1)} %copy-done.16) | copy-start | bytes 196612
  76.8 11.9 %copy-start = (bf16[512,384]{1,0:T(8,128)(2,1)}, bf16[512,384]{1,0:T(8,128)(2,1)S(1)}, u32[]{:S(2)}) copy-start(bf16[512,384]{1,0:T(8,128)(2,1)S(1)} %get-tuple-element.173) | copy-start | bytes 1179652
  76.8 20.5 %collective-permute-start.19 = (bf16[1024,384]{1,0:T(8,128)(2,1)S(1)}, bf16[1024,384]{1,0:T(8,128)(2,1)S(1)}, u32[]{:S(2)}, u32[]{:S(2)}) collective-permute-start(bf16[1024,384]{1,0:T(8,128)(2,1)S(1)} %get-tuple-element.131), channel_id=1, source_target_pairs={{0,12},{1,13},{2,14},{3,15},{64,76},{65,77},{66,78},{67,79},{16,28... | collective-permute-start | bytes 2359304 | tf_op jit(solution)/shard_map/ppermute | solution.py:43
  79.7 18.9 %collective-permute-start.18 = (bf16[1024,384]{1,0:T(8,128)(2,1)S(1)}, bf16[1024,384]{1,0:T(8,128)(2,1)S(1)}, u32[]{:S(2)}, u32[]{:S(2)}) collective-permute-start(bf16[1024,384]{1,0:T(8,128)(2,1)S(1)} %get-tuple-element.121), channel_id=1, source_target_pairs={{0,4},{1,5},{2,6},{3,7},{64,68},{65,69},{66,70},{67,71},{16,20},{1... | collective-permute-start | bytes 2359304 | tf_op jit(solution)/shard_map/ppermute | solution.py:43
  79.9 14.3 %collective-permute-start.13 = (bf16[512,512]{1,0:T(8,128)(2,1)S(1)}, bf16[512,512]{1,0:T(8,128)(2,1)S(1)}, u32[]{:S(2)}, u32[]{:S(2)}) collective-permute-start(bf16[512,512]{1,0:T(8,128)(2,1)S(1)} %get-tuple-element.112), channel_id=1, source_target_pairs={{0,48},{1,49},{2,50},{3,51},{64,112},{65,113},{66,114},{67,115},{1... | collective-permute-start | bytes 1572872 | tf_op jit(solution)/shard_map/ppermute | solution.py:43
  81.6 12.8 %collective-permute-start.14 = (bf16[512,512]{1,0:T(8,128)(2,1)S(1)}, bf16[512,512]{1,0:T(8,128)(2,1)S(1)}, u32[]{:S(2)}, u32[]{:S(2)}) collective-permute-start(bf16[512,512]{1,0:T(8,128)(2,1)S(1)} %get-tuple-element.115), channel_id=1, source_target_pairs={{0,16},{1,17},{2,18},{3,19},{64,80},{65,81},{66,82},{67,83},{16,0}... | collective-permute-start | bytes 1572872 | tf_op jit(solution)/shard_map/ppermute | solution.py:43
  81.6 17.0 %copy-start.37 = (bf16[256,1024]{1,0:T(8,128)(2,1)S(1)}, bf16[256,1024]{1,0:T(8,128)(2,1)}, u32[]{:S(2)}) copy-start(bf16[256,1024]{1,0:T(8,128)(2,1)} %copy-done.36) | copy-start | bytes 1572868
  90.1 7.2 %copy-start.22 = (bf16[512,640]{1,0:T(8,128)(2,1)}, bf16[512,640]{1,0:T(8,128)(2,1)S(1)}, u32[]{:S(2)}) copy-start(bf16[512,640]{1,0:T(8,128)(2,1)S(1)} %get-tuple-element.150) | copy-start | bytes 1966084
  90.1 8.4 %copy-start.21 = (bf16[512,640]{1,0:T(8,128)(2,1)}, bf16[512,640]{1,0:T(8,128)(2,1)S(1)}, u32[]{:S(2)}) copy-start(bf16[512,640]{1,0:T(8,128)(2,1)S(1)} %get-tuple-element.130) | copy-start | bytes 1966084
  90.1 9.7 %copy-start.4 = (bf16[256,640]{1,0:T(8,128)(2,1)}, bf16[256,640]{1,0:T(8,128)(2,1)S(1)}, u32[]{:S(2)}) copy-start(bf16[256,640]{1,0:T(8,128)(2,1)S(1)} %get-tuple-element.162) | copy-start | bytes 983044
  90.2 9.7 %copy-start.10 = (bf16[256,640]{1,0:T(8,128)(2,1)}, bf16[256,640]{1,0:T(8,128)(2,1)S(1)}, u32[]{:S(2)}) copy-start(bf16[256,640]{1,0:T(8,128)(2,1)S(1)} %get-tuple-element.153) | copy-start | bytes 983044
  99.9 7.8 %collective-permute-start.20 = (bf16[256,2560]{1,0:T(8,128)(2,1)}, bf16[256,2560]{1,0:T(8,128)(2,1)}, u32[]{:S(2)}, u32[]{:S(2)}) collective-permute-start(bf16[256,2560]{1,0:T(8,128)(2,1)} %pad_maximum_fusion), channel_id=1, source_target_pairs={{0,1},{1,0},{2,3},{3,2},{64,65},{65,64},{66,67},{67,66},{16,17},{1... | collective-permute-start | bytes 3932168 | tf_op jit(solution)/shard_map/ppermute | solution.py:43
  100.5 7.2 %copy-start.24 = (bf16[256,1024]{1,0:T(8,128)(2,1)S(1)}, bf16[256,1024]{1,0:T(8,128)(2,1)}, u32[]{:S(2)}) copy-start(bf16[256,1024]{1,0:T(8,128)(2,1)} %copy-done.23) | copy-start | bytes 1572868
  100.6 7.2 %copy-start.26 = (bf16[256,1024]{1,0:T(8,128)(2,1)S(1)}, bf16[256,1024]{1,0:T(8,128)(2,1)}, u32[]{:S(2)}) copy-start(bf16[256,1024]{1,0:T(8,128)(2,1)} %copy-done.25) | copy-start | bytes 1572868
  100.6 19.8 %collective-permute-start.23 = (bf16[512,640]{1,0:T(8,128)(2,1)}, bf16[512,640]{1,0:T(8,128)(2,1)S(1)}, u32[]{:S(2)}, u32[]{:S(2)}) collective-permute-start(bf16[512,640]{1,0:T(8,128)(2,1)} %copy-done.21), channel_id=1, source_target_pairs={{0,16},{1,17},{2,18},{3,19},{64,80},{65,81},{66,82},{67,83},{16,0}... | collective-permute-start | bytes 1966088 | tf_op jit(solution)/shard_map/ppermute | solution.py:43
  102.1 18.3 %collective-permute-start.24 = (bf16[512,640]{1,0:T(8,128)(2,1)}, bf16[512,640]{1,0:T(8,128)(2,1)S(1)}, u32[]{:S(2)}, u32[]{:S(2)}) collective-permute-start(bf16[512,640]{1,0:T(8,128)(2,1)} %copy-done.22), channel_id=1, source_target_pairs={{0,48},{1,49},{2,50},{3,51},{64,112},{65,113},{66,114},{67,115},{1... | collective-permute-start | bytes 1966088 | tf_op jit(solution)/shard_map/ppermute | solution.py:43
  103.9 11.0 %collective-permute-start.22 = (bf16[512,384]{1,0:T(8,128)(2,1)S(1)}, bf16[512,384]{1,0:T(8,128)(2,1)S(1)}, u32[]{:S(2)}, u32[]{:S(2)}) collective-permute-start(bf16[512,384]{1,0:T(8,128)(2,1)S(1)} %add_convert_fusion.3), channel_id=1, source_target_pairs={{0,4},{1,5},{2,6},{3,7},{64,68},{65,69},{66,70},{67,71},{16,20},{1... | collective-permute-start | bytes 1179656 | tf_op jit(solution)/shard_map/ppermute | solution.py:43
  105.3 12.2 %collective-permute-start.21 = (bf16[512,384]{1,0:T(8,128)(2,1)S(1)}, bf16[512,384]{1,0:T(8,128)(2,1)S(1)}, u32[]{:S(2)}, u32[]{:S(2)}) collective-permute-start(bf16[512,384]{1,0:T(8,128)(2,1)S(1)} %add_convert_fusion.4), channel_id=1, source_target_pairs={{0,12},{1,13},{2,14},{3,15},{64,76},{65,77},{66,78},{67,79},{16,28... | collective-permute-start | bytes 1179656 | tf_op jit(solution)/shard_map/ppermute | solution.py:43
  107.7 12.6 %copy-start.11 = (bf16[256,640]{1,0:T(8,128)(2,1)S(1)}, bf16[256,640]{1,0:T(8,128)(2,1)}, u32[]{:S(2)}) copy-start(bf16[256,640]{1,0:T(8,128)(2,1)} %copy-done.10) | copy-start | bytes 983044
  107.7 12.8 %copy-start.9 = (bf16[256,640]{1,0:T(8,128)(2,1)S(1)}, bf16[256,640]{1,0:T(8,128)(2,1)}, u32[]{:S(2)}) copy-start(bf16[256,640]{1,0:T(8,128)(2,1)} %copy-done.8) | copy-start | bytes 983044
  114.5 7.1 %copy-start.1 = (bf16[512,384]{1,0:T(8,128)(2,1)S(1)}, bf16[512,384]{1,0:T(8,128)(2,1)}, u32[]{:S(2)}) copy-start(bf16[512,384]{1,0:T(8,128)(2,1)} %copy-done) | copy-start | bytes 1179652
  114.5 7.1 %copy-start.33 = (bf16[1024,384]{1,0:T(8,128)(2,1)S(1)}, bf16[1024,384]{1,0:T(8,128)(2,1)}, u32[]{:S(2)}) copy-start(bf16[1024,384]{1,0:T(8,128)(2,1)} %copy-done.32) | copy-start | bytes 2359300
  114.5 7.1 %copy-start.35 = (bf16[1024,384]{1,0:T(8,128)(2,1)S(1)}, bf16[1024,384]{1,0:T(8,128)(2,1)}, u32[]{:S(2)}) copy-start(bf16[1024,384]{1,0:T(8,128)(2,1)} %copy-done.34) | copy-start | bytes 2359300
  117.5 24.7 %collective-permute-start.29 = (bf16[512,768]{1,0:T(8,128)(2,1)S(1)}, bf16[512,768]{1,0:T(8,128)(2,1)S(1)}, u32[]{:S(2)}, u32[]{:S(2)}) collective-permute-start(bf16[512,768]{1,0:T(8,128)(2,1)S(1)} %get-tuple-element.147), channel_id=1, source_target_pairs={{0,4},{1,5},{2,6},{3,7},{64,68},{65,69},{66,70},{67,71},{16,20},{1... | collective-permute-start | bytes 2359304 | tf_op jit(solution)/shard_map/ppermute | solution.py:43
  120.4 9.1 %collective-permute-start.26 = (bf16[256,640]{1,0:T(8,128)(2,1)S(1)}, bf16[256,640]{1,0:T(8,128)(2,1)S(1)}, u32[]{:S(2)}, u32[]{:S(2)}) collective-permute-start(bf16[256,640]{1,0:T(8,128)(2,1)S(1)} %add_convert_fusion.5), channel_id=1, source_target_pairs={{0,16},{1,17},{2,18},{3,19},{64,80},{65,81},{66,82},{67,83},{16,0}... | collective-permute-start | bytes 983048 | tf_op jit(solution)/shard_map/ppermute | solution.py:43
  120.6 10.3 %collective-permute-start.25 = (bf16[256,640]{1,0:T(8,128)(2,1)S(1)}, bf16[256,640]{1,0:T(8,128)(2,1)S(1)}, u32[]{:S(2)}, u32[]{:S(2)}) collective-permute-start(bf16[256,640]{1,0:T(8,128)(2,1)S(1)} %add_convert_fusion.6), channel_id=1, source_target_pairs={{0,48},{1,49},{2,50},{3,51},{64,112},{65,113},{66,114},{67,115},{1... | collective-permute-start | bytes 983048 | tf_op jit(solution)/shard_map/ppermute | solution.py:43
  121.9 9.0 %copy-start.15 = (bf16[256,512]{1,0:T(8,128)(2,1)S(1)}, bf16[256,512]{1,0:T(8,128)(2,1)}, u32[]{:S(2)}) copy-start(bf16[256,512]{1,0:T(8,128)(2,1)} %copy-done.14) | copy-start | bytes 786436
  121.9 9.0 %copy-start.30 = (bf16[512,512]{1,0:T(8,128)(2,1)S(1)}, bf16[512,512]{1,0:T(8,128)(2,1)}, u32[]{:S(2)}) copy-start(bf16[512,512]{1,0:T(8,128)(2,1)} %copy-done.29) | copy-start | bytes 1572868
  122.0 9.8 %copy-start.13 = (bf16[256,512]{1,0:T(8,128)(2,1)S(1)}, bf16[256,512]{1,0:T(8,128)(2,1)}, u32[]{:S(2)}) copy-start(bf16[256,512]{1,0:T(8,128)(2,1)} %copy-done.12) | copy-start | bytes 786436
  122.0 9.8 %copy-start.28 = (bf16[512,512]{1,0:T(8,128)(2,1)S(1)}, bf16[512,512]{1,0:T(8,128)(2,1)}, u32[]{:S(2)}) copy-start(bf16[512,512]{1,0:T(8,128)(2,1)} %copy-done.27) | copy-start | bytes 1572868
  122.0 10.0 %copy-start.5 = (bf16[256,640]{1,0:T(8,128)(2,1)S(1)}, bf16[256,640]{1,0:T(8,128)(2,1)}, u32[]{:S(2)}) copy-start(bf16[256,640]{1,0:T(8,128)(2,1)} %copy-done.4) | copy-start | bytes 983044
  122.0 10.0 %copy-start.7 = (bf16[256,640]{1,0:T(8,128)(2,1)S(1)}, bf16[256,640]{1,0:T(8,128)(2,1)}, u32[]{:S(2)}) copy-start(bf16[256,640]{1,0:T(8,128)(2,1)} %copy-done.6) | copy-start | bytes 983044
  122.1 10.2 %collective-permute-start.35 = (bf16[256,768]{1,0:T(8,128)(2,1)S(1)}, bf16[256,768]{1,0:T(8,128)(2,1)S(1)}, u32[]{:S(2)}, u32[]{:S(2)}) collective-permute-start(bf16[256,768]{1,0:T(8,128)(2,1)S(1)} %select_convert_fusion), channel_id=1, source_target_pairs={{0,2},{1,3},{2,0},{3,1},{64,66},{65,67},{66,64},{67,65},{16,18},{1... | collective-permute-start | bytes 1179656 | tf_op jit(solution)/shard_map/ppermute | solution.py:43
  122.9 19.2 %collective-permute-start.30 = (bf16[512,768]{1,0:T(8,128)(2,1)S(1)}, bf16[512,768]{1,0:T(8,128)(2,1)S(1)}, u32[]{:S(2)}, u32[]{:S(2)}) collective-permute-start(bf16[512,768]{1,0:T(8,128)(2,1)S(1)} %get-tuple-element.164), channel_id=1, source_target_pairs={{0,12},{1,13},{2,14},{3,15},{64,76},{65,77},{66,78},{67,79},{16,28... | collective-permute-start | bytes 2359304 | tf_op jit(solution)/shard_map/ppermute | solution.py:43
  131.0 23.4 %collective-permute-start.28 = (bf16[256,512]{1,0:T(8,128)(2,1)S(1)}, bf16[256,512]{1,0:T(8,128)(2,1)S(1)}, u32[]{:S(2)}, u32[]{:S(2)}) collective-permute-start(bf16[256,512]{1,0:T(8,128)(2,1)S(1)} %add_convert_fusion.8), channel_id=1, source_target_pairs={{0,48},{1,49},{2,50},{3,51},{64,112},{65,113},{66,114},{67,115},{1... | collective-permute-start | bytes 786440 | tf_op jit(solution)/shard_map/ppermute | solution.py:43
  131.8 22.6 %collective-permute-start.27 = (bf16[256,512]{1,0:T(8,128)(2,1)S(1)}, bf16[256,512]{1,0:T(8,128)(2,1)S(1)}, u32[]{:S(2)}, u32[]{:S(2)}) collective-permute-start(bf16[256,512]{1,0:T(8,128)(2,1)S(1)} %add_convert_fusion.9), channel_id=1, source_target_pairs={{0,16},{1,17},{2,18},{3,19},{64,80},{65,81},{66,82},{67,83},{16,0}... | collective-permute-start | bytes 786440 | tf_op jit(solution)/shard_map/ppermute | solution.py:43
  142.2 8.8 %collective-permute-start.31 = (bf16[256,640]{1,0:T(8,128)(2,1)S(1)}, bf16[256,640]{1,0:T(8,128)(2,1)S(1)}, u32[]{:S(2)}, u32[]{:S(2)}) collective-permute-start(bf16[256,640]{1,0:T(8,128)(2,1)S(1)} %get-tuple-element.165), channel_id=1, source_target_pairs={{0,64},{1,65},{2,66},{3,67},{64,0},{65,1},{66,2},{67,3},{16,80},{1... | collective-permute-start | bytes 983048 | tf_op jit(solution)/shard_map/ppermute | solution.py:43
  144.5 6.7 %copy-start.31 = (bf16[256,512]{1,0:T(8,128)(2,1)S(1)}, bf16[256,512]{1,0:T(8,128)(2,1)}, u32[]{:S(2)}) copy-start(bf16[256,512]{1,0:T(8,128)(2,1)} %param.4) | copy-start | bytes 786436
  144.5 12.3 %collective-permute-start.37 = (bf16[256,768]{1,0:T(8,128)(2,1)S(1)}, bf16[256,768]{1,0:T(8,128)(2,1)S(1)}, u32[]{:S(2)}, u32[]{:S(2)}) collective-permute-start(bf16[256,768]{1,0:T(8,128)(2,1)S(1)} %add_convert_fusion.1), channel_id=1, source_target_pairs={{0,4},{1,5},{2,6},{3,7},{64,68},{65,69},{66,70},{67,71},{16,20},{1... | collective-permute-start | bytes 1179656 | tf_op jit(solution)/shard_map/ppermute | solution.py:43
  144.7 12.1 %collective-permute-start.36 = (bf16[256,768]{1,0:T(8,128)(2,1)S(1)}, bf16[256,768]{1,0:T(8,128)(2,1)S(1)}, u32[]{:S(2)}, u32[]{:S(2)}) collective-permute-start(bf16[256,768]{1,0:T(8,128)(2,1)S(1)} %add_convert_fusion.2), channel_id=1, source_target_pairs={{0,12},{1,13},{2,14},{3,15},{64,76},{65,77},{66,78},{67,79},{16,28... | collective-permute-start | bytes 1179656 | tf_op jit(solution)/shard_map/ppermute | solution.py:43
  152.1 1.2 collective-permute-start.33
  153.2 3.6 %collective-permute-start.34 = (f32[1,512]{1,0:T(1,128)S(1)}, f32[1,512]{1,0:T(1,128)S(1)}, u32[]{:S(2)}, u32[]{:S(2)}) collective-permute-start(f32[1,512]{1,0:T(1,128)S(1)} %add.219), channel_id=1, source_target_pairs={{0,2},{1,3},{2,0},{3,1},{64,66},{65,67},{66,64},{67,65},{16,18},{1... | collective-permute-start | bytes 6152 | tf_op jit(solution)/shard_map/ppermute | solution.py:43
  154.6 9.7 %collective-permute-start.32 = (bf16[256,512]{1,0:T(8,128)(2,1)S(1)}, bf16[256,512]{1,0:T(8,128)(2,1)S(1)}, u32[]{:S(2)}, u32[]{:S(2)}) collective-permute-start(bf16[256,512]{1,0:T(8,128)(2,1)S(1)} %select_convert_fusion.2), channel_id=1, source_target_pairs={{0,64},{1,65},{2,66},{3,67},{64,0},{65,1},{66,2},{67,3},{16,80},{1... | collective-permute-start | bytes 786440 | tf_op jit(solution)/shard_map/ppermute | solution.py:43
  156.8 5.2 %collective-permute-start.40 = (f32[1,512]{1,0:T(1,128)S(1)}, f32[1,512]{1,0:T(1,128)S(1)}, u32[]{:S(2)}, u32[]{:S(2)}) collective-permute-start(f32[1,512]{1,0:T(1,128)S(1)} %add.220), channel_id=1, source_target_pairs={{0,8},{1,9},{2,10},{3,11},{64,72},{65,73},{66,74},{67,75},{16,24},... | collective-permute-start | bytes 6152 | tf_op jit(solution)/shard_map/ppermute | solution.py:43
  157.1 4.9 %collective-permute-start.39 = (f32[1,512]{1,0:T(1,128)S(1)}, f32[1,512]{1,0:T(1,128)S(1)}, u32[]{:S(2)}, u32[]{:S(2)}) collective-permute-start(f32[1,512]{1,0:T(1,128)S(1)} %add.220), channel_id=1, source_target_pairs={{0,12},{1,13},{2,14},{3,15},{64,76},{65,77},{66,78},{67,79},{16,28... | collective-permute-start | bytes 6152 | tf_op jit(solution)/shard_map/ppermute | solution.py:43
  158.7 3.6 %collective-permute-start.38 = (f32[1,512]{1,0:T(1,128)S(1)}, f32[1,512]{1,0:T(1,128)S(1)}, u32[]{:S(2)}, u32[]{:S(2)}) collective-permute-start(f32[1,512]{1,0:T(1,128)S(1)} %add.220), channel_id=1, source_target_pairs={{0,4},{1,5},{2,6},{3,7},{64,68},{65,69},{66,70},{67,71},{16,20},{1... | collective-permute-start | bytes 6152 | tf_op jit(solution)/shard_map/ppermute | solution.py:43
  (18 other events, 38.5 us)

commit v12 on v11

--- a/solution.py
+++ b/solution.py
@@ -322,11 +322,11 @@
     cot_pieces = (after(cot_pieces[0], x_same, x_cross), *cot_pieces[1:])
     d_pair, products, cot_mine, core_two = backward(spot, cot_pieces, w3, gate, up_val, inv)
     core_two = send(core_two, "c")
-    branch_terms = branch_rows(order(y), after(hidden, d_pair), w3)
     pair_z = send(d_pair, "z^1")
-    down_terms = outer("down_terms", order(x), [(after(cot_mine, branch_terms[0]), 0), (core_two, 0)], [(hidden, 0), (core_one, 1024)], 512, 384)
+    down_terms = outer("down_terms", order(x), [(cot_mine, 0), (core_two, 0)], [(hidden, 0), (core_one, 1024)], 512, 384)
+    branch_terms = branch_rows(order(y), after(hidden, down_terms[0]), w3)
     branch_got = [send(value, move) for value, move in zip(branch_terms[0:2], ("y^1", "y^3"))]
-    d_terms = pair_rows(order(y), after(d_pair, down_terms[0]), products, w3)
+    d_terms = pair_rows(order(y), after(d_pair, branch_terms[0]), products, w3)
     down_got, _, down_last = halve(down_terms, "x")
     d_terms = lax.optimization_barrier((*d_terms, *branch_got))[:6]
     d_got = [send(value, move) for value, move in zip(d_terms[0:2], ("y^1", "y^3"))]

time: 166 us -> 170 us (1.024)
  local copies, waits for them, and re-layouts: 9.06 us -> 11.9 us
    unnamed x82 -> x76, local copies, waits for them, and re-layouts: 8.04 us -> 10.8 us
  transfers between devices with their start and end apart: 41 -> 41, of which waited for: 24 -> 23; matrix products, arithmetic and copies ran while one was open for 6% -> 6% of each run, Pallas kernels for 19% -> 19%
where the time goes in v12:
time: 170 us
  waiting for transfers between devices  59.1 us (35%)
  starting transfers between devices  45.8 us (27%)
  Pallas kernels  38.8 us (23%)
  other arithmetic  13.2 us (8%)
  local copies, waits for them, and re-layouts  11.9 us (7%)
    ppermute x41, waiting for transfers between devices, send(): return lax.ppermute(value, AXES, pairs(moves[move]))  59.1 us
    ppermute x41, starting transfers between devices, send(): return lax.ppermute(value, AXES, pairs(moves[move]))  45.8 us
    pallas_call x7, Pallas kernels, call(): pl.pallas_call(whole, in_specs=[pl.BlockSpec(memory_space=space) for spac...  38.8 us
    unnamed x76, local copies, waits for them, and re-layouts  10.8 us
  transfers between devices with their start and end apart: 41, of which 23 were waited for; matrix products, arithmetic and copies ran while one was open for 6% of the time, Pallas kernels for 19%

profile of v12, /device:TPU:0, one launch (start us, length us, event | category | flops | bytes accessed | tf_op | source)
XLA Modules:
  0.0 169.9 jit_solution(4397703815893350198)
XLA Ops:
  1.3 1.0 pad_maximum_fusion.6.refs_1_
  2.3 3.2 %collective-permute-start.1 = (bf16[272,512]{1,0:T(8,128)(2,1)S(1)}, bf16[272,512]{1,0:T(8,128)(2,1)S(1)}, u32[]{:S(2)}, u32[]{:S(2)}) collective-permute-start(bf16[272,512]{1,0:T(8,128)(2,1)S(1)} %pad_maximum_fusion.6.refs_1_), channel_id=1, source_target_pairs={{0,48},{1,49},{2,50},{3,51},{64,112},{65,113},{66,114},{67,115},{1... | collective-permute-start | bytes 835592 | tf_op jit(solution)/shard_map/ppermute | solution.py:43
  5.5 3.9 %collective-permute-start.2 = (bf16[272,512]{1,0:T(8,128)(2,1)S(1)}, bf16[272,512]{1,0:T(8,128)(2,1)S(1)}, u32[]{:S(2)}, u32[]{:S(2)}) collective-permute-start(bf16[272,512]{1,0:T(8,128)(2,1)S(1)} %pad_maximum_fusion.6.refs_1_), channel_id=1, source_target_pairs={{0,64},{1,65},{2,66},{3,67},{64,0},{65,1},{66,2},{67,3},{16,80},{1... | collective-permute-start | bytes 835592 | tf_op jit(solution)/shard_map/ppermute | solution.py:43
  9.4 2.0 %collective-permute-done.1.refs_3_ = bf16[272,512]{1,0:T(8,128)(2,1)S(1)} collective-permute-done((bf16[272,512]{1,0:T(8,128)(2,1)S(1)}, bf16[272,512]{1,0:T(8,128)(2,1)S(1)}, u32[]{:S(2)}, u32[]{:S(2)}) %collective-permute-start.1) | collective-permute-done | bytes 278560 | tf_op jit(solution)/shard_map/ppermute | solution.py:43
  11.4 4.3 %collective-permute-done.2.refs_4_ = bf16[272,512]{1,0:T(8,128)(2,1)S(1)} collective-permute-done((bf16[272,512]{1,0:T(8,128)(2,1)S(1)}, bf16[272,512]{1,0:T(8,128)(2,1)S(1)}, u32[]{:S(2)}, u32[]{:S(2)}) %collective-permute-start.2) | collective-permute-done | bytes 278560 | tf_op jit(solution)/shard_map/ppermute | solution.py:43
  15.8 0.8 collective-permute-start.4
  16.6 1.8 %collective-permute-done.refs_2_ = bf16[272,512]{1,0:T(8,128)(2,1)S(1)} collective-permute-done((bf16[272,512]{1,0:T(8,128)(2,1)S(1)}, bf16[272,512]{1,0:T(8,128)(2,1)S(1)}, u32[]{:S(2)}, u32[]{:S(2)}) %collective-permute-start) | collective-permute-done | bytes 278560 | tf_op jit(solution)/shard_map/ppermute | solution.py:43
  18.6 2.7 %collective-permute-start.5 = (bf16[256,512]{1,0:T(8,128)(2,1)S(1)}, bf16[256,512]{1,0:T(8,128)(2,1)S(1)}, u32[]{:S(2)}, u32[]{:S(2)}) collective-permute-start(bf16[256,512]{1,0:T(8,128)(2,1)S(1)} %copy-done.35), channel_id=1, source_target_pairs={{0,64},{1,65},{2,66},{3,67},{64,0},{65,1},{66,2},{67,3},{16,80},{1... | collective-permute-start | bytes 786440 | tf_op jit(solution)/shard_map/ppermute | solution.py:43
  21.3 5.5 %collective-permute-done.5 = bf16[256,512]{1,0:T(8,128)(2,1)S(1)} collective-permute-done((bf16[256,512]{1,0:T(8,128)(2,1)S(1)}, bf16[256,512]{1,0:T(8,128)(2,1)S(1)}, u32[]{:S(2)}, u32[]{:S(2)}) %collective-permute-start.5) | collective-permute-done | bytes 262176 | tf_op jit(solution)/shard_map/ppermute | solution.py:43
  26.7 2.7 %collective-permute-done.3.refs_5_ = bf16[400,512]{1,0:T(8,128)(2,1)S(1)} collective-permute-done((bf16[400,512]{1,0:T(8,128)(2,1)S(1)}, bf16[400,512]{1,0:T(8,128)(2,1)S(1)}, u32[]{:S(2)}, u32[]{:S(2)}) %collective-permute-start.3) | collective-permute-done | bytes 409632 | tf_op jit(solution)/shard_map/ppermute | solution.py:43
  30.5 1.6 collective-permute-start.6
  32.2 1.5 collective-permute-start.7
  33.8 5.1 %collective-permute-done.6.refs_7_ = bf16[272,512]{1,0:T(8,128)(2,1)} collective-permute-done((bf16[272,512]{1,0:T(8,128)(2,1)}, bf16[272,512]{1,0:T(8,128)(2,1)}, u32[]{:S(2)}, u32[]{:S(2)}) %collective-permute-start.6) | collective-permute-done | bytes 278560 | tf_op jit(solution)/shard_map/ppermute | solution.py:43
  38.9 1.4 assemble.1
  40.4 0.8 copy-done.24
  41.2 1.8 %collective-permute-start.9 = (bf16[256,1024]{1,0:T(8,128)(2,1)S(1)}, bf16[256,1024]{1,0:T(8,128)(2,1)S(1)}, u32[]{:S(2)}, u32[]{:S(2)}) collective-permute-start(bf16[256,1024]{1,0:T(8,128)(2,1)S(1)} %get-tuple-element.100), channel_id=1, source_target_pairs={{0,66},{1,67},{2,64},{3,65},{64,2},{65,3},{66,0},{67,1},{16,82},{1... | collective-permute-start | bytes 1572872 | tf_op jit(solution)/shard_map/ppermute | solution.py:43
  43.6 0.8 collective-permute-done.7.refs_2_
  44.4 0.8 collective-permute-start.11
  45.3 6.3 %forward.1 = (f32[256,768]{1,0:T(8,128)S(1)}, f32[256,768]{1,0:T(8,128)S(1)}, bf16[256,768]{1,0:T(8,128)(2,1)S(1)}, f32[256,128]{1,0:T(8,128)S(1)}, bf16[256,1792]{1,0:T(8,128)(2,1)}) custom-call(bf16[272,4096]{1,0:T(8,128)(2,1)S(1)} %get-tuple-element.97.refs_0_, bf16[256,1024]{1,0:T(8,128)(2,1)S(1)} %get-tuple-element.98.refs_1_, ...), custom_call_target="tpu_custom_call" | custom-call | flops 3221225472 | bytes 16777216 | tf_op jit(solution)/shard_map/forward/pallas_call | solution.py:89
  51.6 0.8 copy-done.2
  52.8 0.8 copy-done.33
  53.6 6.8 %backward.1 = (bf16[256,1536]{1,0:T(8,128)(2,1)S(1)}, bf16[256,128]{1,0:T(8,128)(2,1)S(1)}, bf16[256,2048]{1,0:T(8,128)(2,1)S(1)}, bf16[256,3584]{1,0:T(8,128)(2,1)}) custom-call(s32[10]{0:T(128)S(1)} %stack.116.refs_0_, bf16[512,512]{1,0:T(8,128)(2,1)S(1)} %pad_maximum_fusion.3.refs_1_, bf16[512,512]{1,0:T(8,128)(2,1)S(1)} %collective-permute-done.7.refs_2_, ...), custom_call_target="tpu_custom_call" | custom-call | flops 1610612736 | bytes 8388608 | tf_op jit(solution)/shard_map/backward/pallas_call | solution.py:89
  61.1 1.0 copy-done.20
  62.6 1.6 collective-permute-start.17
  64.3 3.2 %collective-permute-done.14.refs_4_.refs_3_ = bf16[256,1792]{1,0:T(8,128)(2,1)} collective-permute-done((bf16[256,1792]{1,0:T(8,128)(2,1)}, bf16[256,1792]{1,0:T(8,128)(2,1)}, u32[]{:S(2)}, u32[]{:S(2)}) %collective-permute-start.14) | collective-permute-done | bytes 917536 | tf_op jit(solution)/shard_map/ppermute | solution.py:43
  67.5 1.0 copy-done.3
  68.5 1.2 copy-done.21
  69.7 5.1 %down_terms.1 = (bf16[1024,384]{1,0:T(8,128)(2,1)}, bf16[1024,384]{1,0:T(8,128)(2,1)}, bf16[512,384]{1,0:T(8,128)(2,1)S(1)}, bf16[512,384]{1,0:T(8,128)(2,1)S(1)...) custom-call(s32[8]{0:T(128)S(1)} %stack.121.refs_0_, bf16[256,2048]{1,0:T(8,128)(2,1)S(1)} %copy-done.21, ...), custom_call_target="tpu_custom_call" | custom-call | flops 1610612736 | bytes 8388608 | tf_op jit(solution)/shard_map/down_terms/pallas_call | solution.py:89
  75.6 2.8 %collective-permute-start.19 = (bf16[1024,384]{1,0:T(8,128)(2,1)}, bf16[1024,384]{1,0:T(8,128)(2,1)}, u32[]{:S(2)}, u32[]{:S(2)}) collective-permute-start(bf16[1024,384]{1,0:T(8,128)(2,1)} %get-tuple-element.129), channel_id=1, source_target_pairs={{0,12},{1,13},{2,14},{3,15},{64,76},{65,77},{66,78},{67,79},{16,28... | collective-permute-start | bytes 2359304 | tf_op jit(solution)/shard_map/ppermute | solution.py:43
  78.7 1.0 copy-done.4
  79.7 5.2 %branch_rows.1 = (bf16[512,512]{1,0:T(8,128)(2,1)S(1)}, bf16[512,512]{1,0:T(8,128)(2,1)S(1)}, bf16[256,512]{1,0:T(8,128)(2,1)S(1)}, bf16[256,512]{1,0:T(8,128)(2...) custom-call(s32[8]{0:T(128)S(1)} %stack.105.refs_0_, bf16[256,768]{1,0:T(8,128)(2,1)S(1)} %copy-done.4, ...), custom_call_target="tpu_custom_call" | custom-call | flops 1610612736 | bytes 8388608 | tf_op jit(solution)/shard_map/branch_rows/pallas_call | solution.py:89
  86.2 2.1 %collective-permute-start.15 = (bf16[512,512]{1,0:T(8,128)(2,1)S(1)}, bf16[512,512]{1,0:T(8,128)(2,1)S(1)}, u32[]{:S(2)}, u32[]{:S(2)}) collective-permute-start(bf16[512,512]{1,0:T(8,128)(2,1)S(1)} %get-tuple-element.114), channel_id=1, source_target_pairs={{0,48},{1,49},{2,50},{3,51},{64,112},{65,113},{66,114},{67,115},{1... | collective-permute-start | bytes 1572872 | tf_op jit(solution)/shard_map/ppermute | solution.py:43
  88.3 7.1 %pair_rows.1 = (bf16[512,640]{1,0:T(8,128)(2,1)S(1)}, bf16[512,640]{1,0:T(8,128)(2,1)S(1)}, bf16[256,640]{1,0:T(8,128)(2,1)S(1)}, bf16[256,640]{1,0:T(8,128)(2,1...) custom-call(s32[8]{0:T(128)S(1)} %stack.105.refs_0_, ...), custom_call_target="tpu_custom_call" | custom-call | flops 3221225472 | bytes 16777216 | tf_op jit(solution)/shard_map/pair_rows/pallas_call | solution.py:89
  96.2 0.7 copy-done.9
  96.9 4.0 %collective-permute-done.15 = bf16[512,512]{1,0:T(8,128)(2,1)S(1)} collective-permute-done((bf16[512,512]{1,0:T(8,128)(2,1)S(1)}, bf16[512,512]{1,0:T(8,128)(2,1)S(1)}, u32[]{:S(2)}, u32[]{:S(2)}) %collective-permute-start.15) | collective-permute-done | bytes 524320 | tf_op jit(solution)/shard_map/ppermute | solution.py:43
  101.6 1.2 pad_maximum_fusion
  103.8 1.6 collective-permute-start.24
  105.4 1.1 add_convert_fusion.3
  106.5 1.8 %collective-permute-start.22 = (bf16[512,384]{1,0:T(8,128)(2,1)S(1)}, bf16[512,384]{1,0:T(8,128)(2,1)S(1)}, u32[]{:S(2)}, u32[]{:S(2)}) collective-permute-start(bf16[512,384]{1,0:T(8,128)(2,1)S(1)} %add_convert_fusion.3), channel_id=1, source_target_pairs={{0,4},{1,5},{2,6},{3,7},{64,68},{65,69},{66,70},{67,71},{16,20},{1... | collective-permute-start | bytes 1179656 | tf_op jit(solution)/shard_map/ppermute | solution.py:43
  108.3 1.1 add_convert_fusion.4
  109.4 0.8 collective-permute-start.21
  110.9 6.8 %pair_terms.1 = (bf16[512,768]{1,0:T(8,128)(2,1)S(1)}, bf16[512,768]{1,0:T(8,128)(2,1)S(1)}, bf16[256,768]{1,0:T(8,128)(2,1)S(1)}, bf16[256,768]{1,0:T(8,128)(2,...) custom-call(s32[8]{0:T(128)S(1)} %stack.121.refs_0_, bf16[256,1024]{1,0:T(8,128)(2,1)S(1)} %copy-done.25, ...), custom_call_target="tpu_custom_call" | custom-call | flops 3221225472 | bytes 8388608 | tf_op jit(solution)/shard_map/pair_terms/pallas_call | solution.py:89
  117.6 3.9 %collective-permute-done.21 = bf16[512,384]{1,0:T(8,128)(2,1)S(1)} collective-permute-done((bf16[512,384]{1,0:T(8,128)(2,1)S(1)}, bf16[512,384]{1,0:T(8,128)(2,1)S(1)}, u32[]{:S(2)}, u32[]{:S(2)}) %collective-permute-start.21) | collective-permute-done | bytes 393248 | tf_op jit(solution)/shard_map/ppermute | solution.py:43
  122.1 0.8 collective-permute-start.26
  123.0 1.7 %collective-permute-start.25 = (bf16[256,640]{1,0:T(8,128)(2,1)S(1)}, bf16[256,640]{1,0:T(8,128)(2,1)S(1)}, u32[]{:S(2)}, u32[]{:S(2)}) collective-permute-start(bf16[256,640]{1,0:T(8,128)(2,1)S(1)} %add_convert_fusion.6), channel_id=1, source_target_pairs={{0,48},{1,49},{2,50},{3,51},{64,112},{65,113},{66,114},{67,115},{1... | collective-permute-start | bytes 983048 | tf_op jit(solution)/shard_map/ppermute | solution.py:43
  124.7 1.4 convert_add_fusion
  126.2 1.3 collective-permute-start.35
  127.5 1.0 collective-permute-start.30
  128.5 2.7 %collective-permute-done.26 = bf16[256,640]{1,0:T(8,128)(2,1)S(1)} collective-permute-done((bf16[256,640]{1,0:T(8,128)(2,1)S(1)}, bf16[256,640]{1,0:T(8,128)(2,1)S(1)}, u32[]{:S(2)}, u32[]{:S(2)}) %collective-permute-start.26) | collective-permute-done | bytes 327712 | tf_op jit(solution)/shard_map/ppermute | solution.py:43
  131.2 1.6 collective-permute-done.25
  132.9 1.7 collective-permute-start.28
  135.0 0.9 collective-permute-done.35
  135.9 10.9 %collective-permute-done.30 = bf16[512,768]{1,0:T(8,128)(2,1)S(1)} collective-permute-done((bf16[512,768]{1,0:T(8,128)(2,1)S(1)}, bf16[512,768]{1,0:T(8,128)(2,1)S(1)}, u32[]{:S(2)}, u32[]{:S(2)}) %collective-permute-start.30) | collective-permute-done | bytes 786464 | tf_op jit(solution)/shard_map/ppermute | solution.py:43
  146.9 1.8 %collective-permute-start.31 = (bf16[256,640]{1,0:T(8,128)(2,1)S(1)}, bf16[256,640]{1,0:T(8,128)(2,1)S(1)}, u32[]{:S(2)}, u32[]{:S(2)}) collective-permute-start(bf16[256,640]{1,0:T(8,128)(2,1)S(1)} %get-tuple-element.163), channel_id=1, source_target_pairs={{0,64},{1,65},{2,66},{3,67},{64,0},{65,1},{66,2},{67,3},{16,80},{1... | collective-permute-start | bytes 983048 | tf_op jit(solution)/shard_map/ppermute | solution.py:43
  149.6 1.0 collective-permute-start.36
  150.5 5.2 %collective-permute-done.31 = bf16[256,640]{1,0:T(8,128)(2,1)S(1)} collective-permute-done((bf16[256,640]{1,0:T(8,128)(2,1)S(1)}, bf16[256,640]{1,0:T(8,128)(2,1)S(1)}, u32[]{:S(2)}, u32[]{:S(2)}) %collective-permute-start.31) | collective-permute-done | bytes 327712 | tf_op jit(solution)/shard_map/ppermute | solution.py:43
  156.0 0.9 fusion.3
  157.0 1.0 collective-permute-done.33
  158.4 3.2 %collective-permute-start.32 = (bf16[256,512]{1,0:T(8,128)(2,1)S(1)}, bf16[256,512]{1,0:T(8,128)(2,1)S(1)}, u32[]{:S(2)}, u32[]{:S(2)}) collective-permute-start(bf16[256,512]{1,0:T(8,128)(2,1)S(1)} %select_convert_fusion.2), channel_id=1, source_target_pairs={{0,64},{1,65},{2,66},{3,67},{64,0},{65,1},{66,2},{67,3},{16,80},{1... | collective-permute-start | bytes 786440 | tf_op jit(solution)/shard_map/ppermute | solution.py:43
  161.6 1.0 collective-permute-start.40
  162.7 2.1 %collective-permute-start.39 = (f32[1,512]{1,0:T(1,128)S(1)}, f32[1,512]{1,0:T(1,128)S(1)}, u32[]{:S(2)}, u32[]{:S(2)}) collective-permute-start(f32[1,512]{1,0:T(1,128)S(1)} %add.220), channel_id=1, source_target_pairs={{0,12},{1,13},{2,14},{3,15},{64,76},{65,77},{66,78},{67,79},{16,28... | collective-permute-start | bytes 6152 | tf_op jit(solution)/shard_map/ppermute | solution.py:43
  165.6 1.1 pad_maximum_fusion.1
  167.5 0.9 collective-permute-done.38
  168.9 0.9 add_convert_fusion.7
  (143 shorter events, 14.8 us)
Async XLA Ops:
  1.3 17.2 %copy-start.35 = (bf16[256,512]{1,0:T(8,128)(2,1)S(1)}, bf16[256,512]{1,0:T(8,128)(2,1)}, u32[]{:S(2)}) copy-start(bf16[256,512]{1,0:T(8,128)(2,1)} %param.7) | copy-start | bytes 786436
  2.3 9.1 %collective-permute-start.1 = (bf16[272,512]{1,0:T(8,128)(2,1)S(1)}, bf16[272,512]{1,0:T(8,128)(2,1)S(1)}, u32[]{:S(2)}, u32[]{:S(2)}) collective-permute-start(bf16[272,512]{1,0:T(8,128)(2,1)S(1)} %pad_maximum_fusion.6.refs_1_), channel_id=1, source_target_pairs={{0,48},{1,49},{2,50},{3,51},{64,112},{65,113},{66,114},{67,115},{1... | collective-permute-start | bytes 835592 | tf_op jit(solution)/shard_map/ppermute | solution.py:43
  5.5 10.2 %collective-permute-start.2 = (bf16[272,512]{1,0:T(8,128)(2,1)S(1)}, bf16[272,512]{1,0:T(8,128)(2,1)S(1)}, u32[]{:S(2)}, u32[]{:S(2)}) collective-permute-start(bf16[272,512]{1,0:T(8,128)(2,1)S(1)} %pad_maximum_fusion.6.refs_1_), channel_id=1, source_target_pairs={{0,64},{1,65},{2,66},{3,67},{64,0},{65,1},{66,2},{67,3},{16,80},{1... | collective-permute-start | bytes 835592 | tf_op jit(solution)/shard_map/ppermute | solution.py:43
  9.4 9.0 %collective-permute-start = (bf16[272,512]{1,0:T(8,128)(2,1)S(1)}, bf16[272,512]{1,0:T(8,128)(2,1)S(1)}, u32[]{:S(2)}, u32[]{:S(2)}) collective-permute-start(bf16[272,512]{1,0:T(8,128)(2,1)S(1)} %pad_maximum_fusion.6.refs_1_), channel_id=1, source_target_pairs={{0,16},{1,17},{2,18},{3,19},{64,80},{65,81},{66,82},{67,83},{16,32... | collective-permute-start | bytes 835592 | tf_op jit(solution)/shard_map/ppermute | solution.py:43
  15.8 13.7 %collective-permute-start.4 = (bf16[416,512]{1,0:T(8,128)(2,1)S(1)}, bf16[416,512]{1,0:T(8,128)(2,1)S(1)}, u32[]{:S(2)}, u32[]{:S(2)}) collective-permute-start(bf16[416,512]{1,0:T(8,128)(2,1)S(1)} %pad_maximum_fusion.4), channel_id=1, source_target_pairs={{0,48},{1,49},{2,50},{3,51},{64,112},{65,113},{66,114},{67,115},{1... | collective-permute-start | bytes 1277960 | tf_op jit(solution)/shard_map/ppermute | solution.py:43
  18.5 11.0 %collective-permute-start.3 = (bf16[400,512]{1,0:T(8,128)(2,1)S(1)}, bf16[400,512]{1,0:T(8,128)(2,1)S(1)}, u32[]{:S(2)}, u32[]{:S(2)}) collective-permute-start(bf16[400,512]{1,0:T(8,128)(2,1)S(1)} %pad_maximum_fusion.5), channel_id=1, source_target_pairs={{0,16},{1,17},{2,18},{3,19},{64,80},{65,81},{66,82},{67,83},{16,32... | collective-permute-start | bytes 1228808 | tf_op jit(solution)/shard_map/ppermute | solution.py:43
  18.6 8.1 %collective-permute-start.5 = (bf16[256,512]{1,0:T(8,128)(2,1)S(1)}, bf16[256,512]{1,0:T(8,128)(2,1)S(1)}, u32[]{:S(2)}, u32[]{:S(2)}) collective-permute-start(bf16[256,512]{1,0:T(8,128)(2,1)S(1)} %copy-done.35), channel_id=1, source_target_pairs={{0,64},{1,65},{2,66},{3,67},{64,0},{65,1},{66,2},{67,3},{16,80},{1... | collective-permute-start | bytes 786440 | tf_op jit(solution)/shard_map/ppermute | solution.py:43
  29.5 13.5 %collective-permute-start.8 = (bf16[512,512]{1,0:T(8,128)(2,1)S(1)}, bf16[512,512]{1,0:T(8,128)(2,1)S(1)}, u32[]{:S(2)}, u32[]{:S(2)}) collective-permute-start(bf16[512,512]{1,0:T(8,128)(2,1)S(1)} %pad_maximum_fusion.3.refs_1_), channel_id=1, source_target_pairs={{0,48},{1,49},{2,50},{3,51},{64,112},{65,113},{66,114},{67,115},{1... | collective-permute-start | bytes 1572872 | tf_op jit(solution)/shard_map/ppermute | solution.py:43
  30.5 8.4 %collective-permute-start.6 = (bf16[272,512]{1,0:T(8,128)(2,1)}, bf16[272,512]{1,0:T(8,128)(2,1)}, u32[]{:S(2)}, u32[]{:S(2)}) collective-permute-start(bf16[272,512]{1,0:T(8,128)(2,1)} %pad_maximum_fusion.7), channel_id=1, source_target_pairs={{0,64},{1,65},{2,66},{3,67},{64,0},{65,1},{66,2},{67,3},{16,80},{1... | collective-permute-start | bytes 835592 | tf_op jit(solution)/shard_map/ppermute | solution.py:43
  32.2 12.2 %collective-permute-start.7 = (bf16[512,512]{1,0:T(8,128)(2,1)S(1)}, bf16[512,512]{1,0:T(8,128)(2,1)S(1)}, u32[]{:S(2)}, u32[]{:S(2)}) collective-permute-start(bf16[512,512]{1,0:T(8,128)(2,1)S(1)} %pad_maximum_fusion.3.refs_1_), channel_id=1, source_target_pairs={{0,16},{1,17},{2,18},{3,19},{64,80},{65,81},{66,82},{67,83},{16,32... | collective-permute-start | bytes 1572872 | tf_op jit(solution)/shard_map/ppermute | solution.py:43
  41.2 1.8 %copy-start.19 = (bf16[16,4096]{1,0:T(8,128)(2,1)}, bf16[16,4096]{1,0:T(8,128)(2,1)S(1)}, u32[]{:S(2)}) copy-start(bf16[16,4096]{1,0:T(8,128)(2,1)S(1)} %get-tuple-element.180) | copy-start | bytes 393220
  41.2 11.2 %collective-permute-start.9 = (bf16[256,1024]{1,0:T(8,128)(2,1)S(1)}, bf16[256,1024]{1,0:T(8,128)(2,1)S(1)}, u32[]{:S(2)}, u32[]{:S(2)}) collective-permute-start(bf16[256,1024]{1,0:T(8,128)(2,1)S(1)} %get-tuple-element.100), channel_id=1, source_target_pairs={{0,66},{1,67},{2,64},{3,65},{64,2},{65,3},{66,0},{67,1},{16,82},{1... | collective-permute-start | bytes 1572872 | tf_op jit(solution)/shard_map/ppermute | solution.py:43
  43.0 9.8 %collective-permute-start.10 = (bf16[256,1024]{1,0:T(8,128)(2,1)S(1)}, bf16[256,1024]{1,0:T(8,128)(2,1)S(1)}, u32[]{:S(2)}, u32[]{:S(2)}) collective-permute-start(bf16[256,1024]{1,0:T(8,128)(2,1)S(1)} %get-tuple-element.101), channel_id=1, source_target_pairs={{0,2},{1,3},{2,0},{3,1},{64,66},{65,67},{66,64},{67,65},{16,18},{1... | collective-permute-start | bytes 1572872 | tf_op jit(solution)/shard_map/ppermute | solution.py:43
  43.0 9.8 %collective-permute-start.12 = (bf16[256,512]{1,0:T(8,128)(2,1)S(1)}, bf16[256,512]{1,0:T(8,128)(2,1)S(1)}, u32[]{:S(2)}, u32[]{:S(2)}) collective-permute-start(bf16[256,512]{1,0:T(8,128)(2,1)S(1)} %pad_maximum_fusion.9), channel_id=1, source_target_pairs={{0,48},{1,49},{2,50},{3,51},{64,112},{65,113},{66,114},{67,115},{1... | collective-permute-start | bytes 786440 | tf_op jit(solution)/shard_map/ppermute | solution.py:43
  44.4 8.4 %collective-permute-start.11 = (bf16[256,512]{1,0:T(8,128)(2,1)S(1)}, bf16[256,512]{1,0:T(8,128)(2,1)S(1)}, u32[]{:S(2)}, u32[]{:S(2)}) collective-permute-start(bf16[256,512]{1,0:T(8,128)(2,1)S(1)} %pad_maximum_fusion.8), channel_id=1, source_target_pairs={{0,16},{1,17},{2,18},{3,19},{64,80},{65,81},{66,82},{67,83},{16,32... | collective-permute-start | bytes 786440 | tf_op jit(solution)/shard_map/ppermute | solution.py:43
  52.4 8.0 %copy-start.26 = (bf16[256,1024]{1,0:T(8,128)(2,1)}, bf16[256,1024]{1,0:T(8,128)(2,1)S(1)}, u32[]{:S(2)}) copy-start(bf16[256,1024]{1,0:T(8,128)(2,1)S(1)} %collective-permute-done.9.refs_2_) | copy-start | bytes 1572868
  62.0 5.4 %collective-permute-start.13 = (bf16[256,3584]{1,0:T(8,128)(2,1)}, bf16[256,3584]{1,0:T(8,128)(2,1)}, u32[]{:S(2)}, u32[]{:S(2)}) collective-permute-start(bf16[256,3584]{1,0:T(8,128)(2,1)} %get-tuple-element.107), channel_id=1, source_target_pairs={{0,1},{1,0},{2,3},{3,2},{64,65},{65,64},{66,67},{67,66},{16,17},{1... | collective-permute-start | bytes 5505032 | tf_op jit(solution)/shard_map/ppermute | solution.py:43
  62.0 5.4 %collective-permute-start.14 = (bf16[256,1792]{1,0:T(8,128)(2,1)}, bf16[256,1792]{1,0:T(8,128)(2,1)}, u32[]{:S(2)}, u32[]{:S(2)}) collective-permute-start(bf16[256,1792]{1,0:T(8,128)(2,1)} %get-tuple-element.108), channel_id=1, source_target_pairs={{0,1},{1,0},{2,3},{3,2},{64,65},{65,64},{66,67},{67,66},{16,17},{1... | collective-permute-start | bytes 2752520 | tf_op jit(solution)/shard_map/ppermute | solution.py:43
  62.6 38.9 %collective-permute-start.17 = (bf16[256,1536]{1,0:T(8,128)(2,1)S(1)}, bf16[256,1536]{1,0:T(8,128)(2,1)S(1)}, u32[]{:S(2)}, u32[]{:S(2)}) collective-permute-start(bf16[256,1536]{1,0:T(8,128)(2,1)S(1)} %get-tuple-element.120.refs_1_.refs_5_), channel_id=1, source_target_pairs={{0,2},{1,3},{2,0},{3,1},{64,66},{65,67},{66,64},{67,65},{16,18},{1... | collective-permute-start | bytes 2359304 | tf_op jit(solution)/shard_map/ppermute | solution.py:43
  75.6 25.9 %collective-permute-start.19 = (bf16[1024,384]{1,0:T(8,128)(2,1)}, bf16[1024,384]{1,0:T(8,128)(2,1)}, u32[]{:S(2)}, u32[]{:S(2)}) collective-permute-start(bf16[1024,384]{1,0:T(8,128)(2,1)} %get-tuple-element.129), channel_id=1, source_target_pairs={{0,12},{1,13},{2,14},{3,15},{64,76},{65,77},{66,78},{67,79},{16,28... | collective-permute-start | bytes 2359304 | tf_op jit(solution)/shard_map/ppermute | solution.py:43
  78.3 23.2 %collective-permute-start.18 = (bf16[1024,384]{1,0:T(8,128)(2,1)}, bf16[1024,384]{1,0:T(8,128)(2,1)}, u32[]{:S(2)}, u32[]{:S(2)}) collective-permute-start(bf16[1024,384]{1,0:T(8,128)(2,1)} %get-tuple-element.109), channel_id=1, source_target_pairs={{0,4},{1,5},{2,6},{3,7},{64,68},{65,69},{66,70},{67,71},{16,20},{1... | collective-permute-start | bytes 2359304 | tf_op jit(solution)/shard_map/ppermute | solution.py:43
  79.7 8.7 %copy-start.18 = (bf16[256,128]{1,0:T(8,128)(2,1)S(1)}, bf16[256,128]{1,0:T(8,128)(2,1)}, u32[]{:S(2)}) copy-start(bf16[256,128]{1,0:T(8,128)(2,1)} %copy-done.17) | copy-start | bytes 196612
  86.2 14.7 %collective-permute-start.15 = (bf16[512,512]{1,0:T(8,128)(2,1)S(1)}, bf16[512,512]{1,0:T(8,128)(2,1)S(1)}, u32[]{:S(2)}, u32[]{:S(2)}) collective-permute-start(bf16[512,512]{1,0:T(8,128)(2,1)S(1)} %get-tuple-element.114), channel_id=1, source_target_pairs={{0,48},{1,49},{2,50},{3,51},{64,112},{65,113},{66,114},{67,115},{1... | collective-permute-start | bytes 1572872 | tf_op jit(solution)/shard_map/ppermute | solution.py:43
  88.3 13.2 %collective-permute-start.16 = (bf16[512,512]{1,0:T(8,128)(2,1)S(1)}, bf16[512,512]{1,0:T(8,128)(2,1)S(1)}, u32[]{:S(2)}, u32[]{:S(2)}) collective-permute-start(bf16[512,512]{1,0:T(8,128)(2,1)S(1)} %get-tuple-element.117), channel_id=1, source_target_pairs={{0,16},{1,17},{2,18},{3,19},{64,80},{65,81},{66,82},{67,83},{16,0}... | collective-permute-start | bytes 1572872 | tf_op jit(solution)/shard_map/ppermute | solution.py:43
  88.3 13.2 %copy-start.34 = (bf16[256,1024]{1,0:T(8,128)(2,1)S(1)}, bf16[256,1024]{1,0:T(8,128)(2,1)}, u32[]{:S(2)}) copy-start(bf16[256,1024]{1,0:T(8,128)(2,1)} %copy-done.33) | copy-start | bytes 1572868
  96.9 4.6 %copy-start.22 = (bf16[512,640]{1,0:T(8,128)(2,1)}, bf16[512,640]{1,0:T(8,128)(2,1)S(1)}, u32[]{:S(2)}) copy-start(bf16[512,640]{1,0:T(8,128)(2,1)S(1)} %get-tuple-element.128) | copy-start | bytes 1966084
  96.9 4.6 %copy-start.23 = (bf16[512,640]{1,0:T(8,128)(2,1)}, bf16[512,640]{1,0:T(8,128)(2,1)S(1)}, u32[]{:S(2)}) copy-start(bf16[512,640]{1,0:T(8,128)(2,1)S(1)} %get-tuple-element.148) | copy-start | bytes 1966084
  96.9 5.9 %copy-start.5 = (bf16[256,640]{1,0:T(8,128)(2,1)}, bf16[256,640]{1,0:T(8,128)(2,1)S(1)}, u32[]{:S(2)}) copy-start(bf16[256,640]{1,0:T(8,128)(2,1)S(1)} %get-tuple-element.160) | copy-start | bytes 983044
  96.9 5.9 %copy-start.11 = (bf16[256,640]{1,0:T(8,128)(2,1)}, bf16[256,640]{1,0:T(8,128)(2,1)S(1)}, u32[]{:S(2)}) copy-start(bf16[256,640]{1,0:T(8,128)(2,1)S(1)} %get-tuple-element.151) | copy-start | bytes 983044
  100.9 1.9 %copy-start.28 = (bf16[512,512]{1,0:T(8,128)(2,1)}, bf16[512,512]{1,0:T(8,128)(2,1)S(1)}, u32[]{:S(2)}) copy-start(bf16[512,512]{1,0:T(8,128)(2,1)S(1)} %collective-permute-done.15) | copy-start | bytes 1572868
  102.8 8.1 %collective-permute-start.20 = (bf16[256,2560]{1,0:T(8,128)(2,1)}, bf16[256,2560]{1,0:T(8,128)(2,1)}, u32[]{:S(2)}, u32[]{:S(2)}) collective-permute-start(bf16[256,2560]{1,0:T(8,128)(2,1)} %pad_maximum_fusion), channel_id=1, source_target_pairs={{0,1},{1,0},{2,3},{3,2},{64,65},{65,64},{66,67},{67,66},{16,17},{1... | collective-permute-start | bytes 3932168 | tf_op jit(solution)/shard_map/ppermute | solution.py:43
  103.5 7.4 %copy-start.25 = (bf16[256,1024]{1,0:T(8,128)(2,1)S(1)}, bf16[256,1024]{1,0:T(8,128)(2,1)}, u32[]{:S(2)}) copy-start(bf16[256,1024]{1,0:T(8,128)(2,1)} %copy-done.24) | copy-start | bytes 1572868
  103.5 7.4 %copy-start.27 = (bf16[256,1024]{1,0:T(8,128)(2,1)S(1)}, bf16[256,1024]{1,0:T(8,128)(2,1)}, u32[]{:S(2)}) copy-start(bf16[256,1024]{1,0:T(8,128)(2,1)} %copy-done.26) | copy-start | bytes 1572868
  103.5 18.5 %collective-permute-start.23 = (bf16[512,640]{1,0:T(8,128)(2,1)}, bf16[512,640]{1,0:T(8,128)(2,1)S(1)}, u32[]{:S(2)}, u32[]{:S(2)}) collective-permute-start(bf16[512,640]{1,0:T(8,128)(2,1)} %copy-done.22), channel_id=1, source_target_pairs={{0,16},{1,17},{2,18},{3,19},{64,80},{65,81},{66,82},{67,83},{16,0}... | collective-permute-start | bytes 1966088 | tf_op jit(solution)/shard_map/ppermute | solution.py:43
  103.8 18.3 %collective-permute-start.24 = (bf16[512,640]{1,0:T(8,128)(2,1)}, bf16[512,640]{1,0:T(8,128)(2,1)S(1)}, u32[]{:S(2)}, u32[]{:S(2)}) collective-permute-start(bf16[512,640]{1,0:T(8,128)(2,1)} %copy-done.23), channel_id=1, source_target_pairs={{0,48},{1,49},{2,50},{3,51},{64,112},{65,113},{66,114},{67,115},{1... | collective-permute-start | bytes 1966088 | tf_op jit(solution)/shard_map/ppermute | solution.py:43
  106.5 11.2 %collective-permute-start.22 = (bf16[512,384]{1,0:T(8,128)(2,1)S(1)}, bf16[512,384]{1,0:T(8,128)(2,1)S(1)}, u32[]{:S(2)}, u32[]{:S(2)}) collective-permute-start(bf16[512,384]{1,0:T(8,128)(2,1)S(1)} %add_convert_fusion.3), channel_id=1, source_target_pairs={{0,4},{1,5},{2,6},{3,7},{64,68},{65,69},{66,70},{67,71},{16,20},{1... | collective-permute-start | bytes 1179656 | tf_op jit(solution)/shard_map/ppermute | solution.py:43
  109.4 12.2 %collective-permute-start.21 = (bf16[512,384]{1,0:T(8,128)(2,1)S(1)}, bf16[512,384]{1,0:T(8,128)(2,1)S(1)}, u32[]{:S(2)}, u32[]{:S(2)}) collective-permute-start(bf16[512,384]{1,0:T(8,128)(2,1)S(1)} %add_convert_fusion.4), channel_id=1, source_target_pairs={{0,12},{1,13},{2,14},{3,15},{64,76},{65,77},{66,78},{67,79},{16,28... | collective-permute-start | bytes 1179656 | tf_op jit(solution)/shard_map/ppermute | solution.py:43
  110.8 11.2 %copy-start.12 = (bf16[256,640]{1,0:T(8,128)(2,1)S(1)}, bf16[256,640]{1,0:T(8,128)(2,1)}, u32[]{:S(2)}) copy-start(bf16[256,640]{1,0:T(8,128)(2,1)} %copy-done.11) | copy-start | bytes 983044
  110.8 12.0 %copy-start.10 = (bf16[256,640]{1,0:T(8,128)(2,1)S(1)}, bf16[256,640]{1,0:T(8,128)(2,1)}, u32[]{:S(2)}) copy-start(bf16[256,640]{1,0:T(8,128)(2,1)} %copy-done.9) | copy-start | bytes 983044
  117.6 7.1 %copy-start.1 = (bf16[512,384]{1,0:T(8,128)(2,1)S(1)}, bf16[512,384]{1,0:T(8,128)(2,1)}, u32[]{:S(2)}) copy-start(bf16[512,384]{1,0:T(8,128)(2,1)} %copy-done) | copy-start | bytes 1179652
  121.5 25.3 %collective-permute-start.29 = (bf16[512,768]{1,0:T(8,128)(2,1)S(1)}, bf16[512,768]{1,0:T(8,128)(2,1)S(1)}, u32[]{:S(2)}, u32[]{:S(2)}) collective-permute-start(bf16[512,768]{1,0:T(8,128)(2,1)S(1)} %get-tuple-element.145), channel_id=1, source_target_pairs={{0,4},{1,5},{2,6},{3,7},{64,68},{65,69},{66,70},{67,71},{16,20},{1... | collective-permute-start | bytes 2359304 | tf_op jit(solution)/shard_map/ppermute | solution.py:43
  122.1 9.1 %collective-permute-start.26 = (bf16[256,640]{1,0:T(8,128)(2,1)S(1)}, bf16[256,640]{1,0:T(8,128)(2,1)S(1)}, u32[]{:S(2)}, u32[]{:S(2)}) collective-permute-start(bf16[256,640]{1,0:T(8,128)(2,1)S(1)} %add_convert_fusion.5), channel_id=1, source_target_pairs={{0,16},{1,17},{2,18},{3,19},{64,80},{65,81},{66,82},{67,83},{16,0}... | collective-permute-start | bytes 983048 | tf_op jit(solution)/shard_map/ppermute | solution.py:43
  123.0 9.9 %collective-permute-start.25 = (bf16[256,640]{1,0:T(8,128)(2,1)S(1)}, bf16[256,640]{1,0:T(8,128)(2,1)S(1)}, u32[]{:S(2)}, u32[]{:S(2)}) collective-permute-start(bf16[256,640]{1,0:T(8,128)(2,1)S(1)} %add_convert_fusion.6), channel_id=1, source_target_pairs={{0,48},{1,49},{2,50},{3,51},{64,112},{65,113},{66,114},{67,115},{1... | collective-permute-start | bytes 983048 | tf_op jit(solution)/shard_map/ppermute | solution.py:43
  126.1 6.8 %copy-start.16 = (bf16[256,512]{1,0:T(8,128)(2,1)S(1)}, bf16[256,512]{1,0:T(8,128)(2,1)}, u32[]{:S(2)}) copy-start(bf16[256,512]{1,0:T(8,128)(2,1)} %copy-done.15) | copy-start | bytes 786436
  126.1 6.8 %copy-start.31 = (bf16[512,512]{1,0:T(8,128)(2,1)S(1)}, bf16[512,512]{1,0:T(8,128)(2,1)}, u32[]{:S(2)}) copy-start(bf16[512,512]{1,0:T(8,128)(2,1)} %copy-done.30) | copy-start | bytes 1572868
  126.1 8.5 %copy-start.14 = (bf16[256,512]{1,0:T(8,128)(2,1)S(1)}, bf16[256,512]{1,0:T(8,128)(2,1)}, u32[]{:S(2)}) copy-start(bf16[256,512]{1,0:T(8,128)(2,1)} %copy-done.13) | copy-start | bytes 786436
  126.1 8.5 %copy-start.29 = (bf16[512,512]{1,0:T(8,128)(2,1)S(1)}, bf16[512,512]{1,0:T(8,128)(2,1)}, u32[]{:S(2)}) copy-start(bf16[512,512]{1,0:T(8,128)(2,1)} %copy-done.28) | copy-start | bytes 1572868
  126.1 8.6 %copy-start.6 = (bf16[256,640]{1,0:T(8,128)(2,1)S(1)}, bf16[256,640]{1,0:T(8,128)(2,1)}, u32[]{:S(2)}) copy-start(bf16[256,640]{1,0:T(8,128)(2,1)} %copy-done.5) | copy-start | bytes 983044
  126.1 8.6 %copy-start.8 = (bf16[256,640]{1,0:T(8,128)(2,1)S(1)}, bf16[256,640]{1,0:T(8,128)(2,1)}, u32[]{:S(2)}) copy-start(bf16[256,640]{1,0:T(8,128)(2,1)} %copy-done.7) | copy-start | bytes 983044
  126.2 9.7 %collective-permute-start.35 = (bf16[256,768]{1,0:T(8,128)(2,1)S(1)}, bf16[256,768]{1,0:T(8,128)(2,1)S(1)}, u32[]{:S(2)}, u32[]{:S(2)}) collective-permute-start(bf16[256,768]{1,0:T(8,128)(2,1)S(1)} %select_convert_fusion), channel_id=1, source_target_pairs={{0,2},{1,3},{2,0},{3,1},{64,66},{65,67},{66,64},{67,65},{16,18},{1... | collective-permute-start | bytes 1179656 | tf_op jit(solution)/shard_map/ppermute | solution.py:43
  127.5 19.4 %collective-permute-start.30 = (bf16[512,768]{1,0:T(8,128)(2,1)S(1)}, bf16[512,768]{1,0:T(8,128)(2,1)S(1)}, u32[]{:S(2)}, u32[]{:S(2)}) collective-permute-start(bf16[512,768]{1,0:T(8,128)(2,1)S(1)} %get-tuple-element.162), channel_id=1, source_target_pairs={{0,12},{1,13},{2,14},{3,15},{64,76},{65,77},{66,78},{67,79},{16,28... | collective-permute-start | bytes 2359304 | tf_op jit(solution)/shard_map/ppermute | solution.py:43
  132.9 25.3 %collective-permute-start.28 = (bf16[256,512]{1,0:T(8,128)(2,1)S(1)}, bf16[256,512]{1,0:T(8,128)(2,1)S(1)}, u32[]{:S(2)}, u32[]{:S(2)}) collective-permute-start(bf16[256,512]{1,0:T(8,128)(2,1)S(1)} %add_convert_fusion.8), channel_id=1, source_target_pairs={{0,48},{1,49},{2,50},{3,51},{64,112},{65,113},{66,114},{67,115},{1... | collective-permute-start | bytes 786440 | tf_op jit(solution)/shard_map/ppermute | solution.py:43
  134.6 23.5 %collective-permute-start.27 = (bf16[256,512]{1,0:T(8,128)(2,1)S(1)}, bf16[256,512]{1,0:T(8,128)(2,1)S(1)}, u32[]{:S(2)}, u32[]{:S(2)}) collective-permute-start(bf16[256,512]{1,0:T(8,128)(2,1)S(1)} %add_convert_fusion.9), channel_id=1, source_target_pairs={{0,16},{1,17},{2,18},{3,19},{64,80},{65,81},{66,82},{67,83},{16,0}... | collective-permute-start | bytes 786440 | tf_op jit(solution)/shard_map/ppermute | solution.py:43
  146.9 8.9 %collective-permute-start.31 = (bf16[256,640]{1,0:T(8,128)(2,1)S(1)}, bf16[256,640]{1,0:T(8,128)(2,1)S(1)}, u32[]{:S(2)}, u32[]{:S(2)}) collective-permute-start(bf16[256,640]{1,0:T(8,128)(2,1)S(1)} %get-tuple-element.163), channel_id=1, source_target_pairs={{0,64},{1,65},{2,66},{3,67},{64,0},{65,1},{66,2},{67,3},{16,80},{1... | collective-permute-start | bytes 983048 | tf_op jit(solution)/shard_map/ppermute | solution.py:43
  148.8 7.2 %copy-start.32 = (bf16[256,512]{1,0:T(8,128)(2,1)S(1)}, bf16[256,512]{1,0:T(8,128)(2,1)}, u32[]{:S(2)}) copy-start(bf16[256,512]{1,0:T(8,128)(2,1)} %param.4) | copy-start | bytes 786436
  148.8 7.2 %copy-start.36 = (f32[512]{0:T(512)S(1)}, f32[512]{0:T(512)}, u32[]{:S(2)}) copy-start(f32[512]{0:T(512)} %convert_element_type.219) | copy-start | bytes 6148
  148.8 12.8 %collective-permute-start.37 = (bf16[256,768]{1,0:T(8,128)(2,1)S(1)}, bf16[256,768]{1,0:T(8,128)(2,1)S(1)}, u32[]{:S(2)}, u32[]{:S(2)}) collective-permute-start(bf16[256,768]{1,0:T(8,128)(2,1)S(1)} %add_convert_fusion.1), channel_id=1, source_target_pairs={{0,4},{1,5},{2,6},{3,7},{64,68},{65,69},{66,70},{67,71},{16,20},{1... | collective-permute-start | bytes 1179656 | tf_op jit(solution)/shard_map/ppermute | solution.py:43
  149.6 12.1 %collective-permute-start.36 = (bf16[256,768]{1,0:T(8,128)(2,1)S(1)}, bf16[256,768]{1,0:T(8,128)(2,1)S(1)}, u32[]{:S(2)}, u32[]{:S(2)}) collective-permute-start(bf16[256,768]{1,0:T(8,128)(2,1)S(1)} %add_convert_fusion.2), channel_id=1, source_target_pairs={{0,12},{1,13},{2,14},{3,15},{64,76},{65,77},{66,78},{67,79},{16,28... | collective-permute-start | bytes 1179656 | tf_op jit(solution)/shard_map/ppermute | solution.py:43
  156.9 1.2 collective-permute-start.33
  158.0 3.6 %collective-permute-start.34 = (f32[1,512]{1,0:T(1,128)S(1)}, f32[1,512]{1,0:T(1,128)S(1)}, u32[]{:S(2)}, u32[]{:S(2)}) collective-permute-start(f32[1,512]{1,0:T(1,128)S(1)} %add.219), channel_id=1, source_target_pairs={{0,2},{1,3},{2,0},{3,1},{64,66},{65,67},{66,64},{67,65},{16,18},{1... | collective-permute-start | bytes 6152 | tf_op jit(solution)/shard_map/ppermute | solution.py:43
  158.4 10.5 %collective-permute-start.32 = (bf16[256,512]{1,0:T(8,128)(2,1)S(1)}, bf16[256,512]{1,0:T(8,128)(2,1)S(1)}, u32[]{:S(2)}, u32[]{:S(2)}) collective-permute-start(bf16[256,512]{1,0:T(8,128)(2,1)S(1)} %select_convert_fusion.2), channel_id=1, source_target_pairs={{0,64},{1,65},{2,66},{3,67},{64,0},{65,1},{66,2},{67,3},{16,80},{1... | collective-permute-start | bytes 786440 | tf_op jit(solution)/shard_map/ppermute | solution.py:43
  161.6 5.2 %collective-permute-start.40 = (f32[1,512]{1,0:T(1,128)S(1)}, f32[1,512]{1,0:T(1,128)S(1)}, u32[]{:S(2)}, u32[]{:S(2)}) collective-permute-start(f32[1,512]{1,0:T(1,128)S(1)} %add.220), channel_id=1, source_target_pairs={{0,8},{1,9},{2,10},{3,11},{64,72},{65,73},{66,74},{67,75},{16,24},... | collective-permute-start | bytes 6152 | tf_op jit(solution)/shard_map/ppermute | solution.py:43
  162.7 4.8 %collective-permute-start.39 = (f32[1,512]{1,0:T(1,128)S(1)}, f32[1,512]{1,0:T(1,128)S(1)}, u32[]{:S(2)}, u32[]{:S(2)}) collective-permute-start(f32[1,512]{1,0:T(1,128)S(1)} %add.220), channel_id=1, source_target_pairs={{0,12},{1,13},{2,14},{3,15},{64,76},{65,77},{66,78},{67,79},{16,28... | collective-permute-start | bytes 6152 | tf_op jit(solution)/shard_map/ppermute | solution.py:43
  164.7 3.6 %collective-permute-start.38 = (f32[1,512]{1,0:T(1,128)S(1)}, f32[1,512]{1,0:T(1,128)S(1)}, u32[]{:S(2)}, u32[]{:S(2)}) collective-permute-start(f32[1,512]{1,0:T(1,128)S(1)} %add.220), channel_id=1, source_target_pairs={{0,4},{1,5},{2,6},{3,7},{64,68},{65,69},{66,70},{67,71},{16,20},{1... | collective-permute-start | bytes 6152 | tf_op jit(solution)/shard_map/ppermute | solution.py:43
  (15 other events, 13.4 us)
